TPU v7x, 32 devices: a whole 2x2x4 slice. The times are simulated.
32 devices in a mesh: groups: 2 (over x), seq: 2 (over core), mp: 8 (over z, y).
Axes of the slice: x: 2, y: 2, z: 4, core: 2. Of those that a mesh axis runs over, the one named last changes fastest.
Arguments:
- tokens_in: bfloat16 [3072, 4096], P(('groups', 'seq', 'mp')), parts along dimension 0, may hold values from -6 to 6
- out_grad: bfloat16 [3072, 14336], P('groups', ('seq', 'mp')), parts along dimension 0, may hold values from -6 to 6
- w_gate: bfloat16 [4096, 14336], P(None, ('seq', 'mp')), may hold values from -0.09375 to 0.09375
- w_up: bfloat16 [4096, 14336], P(None, ('seq', 'mp')), may hold values from -0.09375 to 0.09375
- proj_in: bfloat16 [4096, 64], replicated, may hold values from -0.09375 to 0.09375
- proj_out: bfloat16 [14336, 128], P(('seq', 'mp')), may hold values from -0.046875 to 0.046875
- lengths: int32 [16], P('groups'), parts along dimension 0, may hold values from 1 to 768, 1536 in all
- val_sketch: bfloat16 [1024, 8192], P('mp', 'seq'), may hold values from -0.0625 to 0.0625
Outputs:
- scores: float32 [16, 1024], P(('groups', 'seq'), 'mp'), parts along dimension 0
There are 2 independent parts, one for each index of `groups`. A program takes and returns all parts, laid end to end along the dimension named above; an argument that names none is the same for every part. Nothing has to cross between parts.
Inputs may be any that keep to these rules, and one draw needn't show every extreme that they name: Sequences lie end to end in token order, sequence s starting where sequence s - 1 ends; the lengths add up to 1536 and one of them is exactly 768.
All inputs are finite; a program needn't handle non-finite values.
Results may differ from a plain program's by a relative error of at most 0.003.
Values may be sent and summed in bfloat16 or wider, within the bound.
No kernel may reach another device: no remote copies, remote signals or barrier semaphores. Data moves between devices by JAX's collectives and lax.ppermute only.
A program may use at most 128 MiB of HBM per device.

v0:
```python
import jax
import jax.numpy as jnp
from jax import lax
from jax.sharding import PartitionSpec as P

eps_scale = 1e-06


def grad_rows(block_rows, w_gate, w_up, proj_out, out_grad):
    half_cols = proj_out.shape[1] // 2
    gate_pre = jnp.dot(block_rows, w_gate, preferred_element_type=jnp.float32)
    up_pre = jnp.dot(block_rows, w_up, preferred_element_type=jnp.float32)
    cotangent = out_grad.astype(jnp.float32)
    sigmoid_gate = jax.nn.sigmoid(gate_pre)
    grad_up = (cotangent * gate_pre * sigmoid_gate).astype(jnp.bfloat16)
    grad_gate = (
        cotangent * up_pre * sigmoid_gate * (1.0 + gate_pre * (1.0 - sigmoid_gate))
    ).astype(jnp.bfloat16)
    proj_gate = jnp.dot(grad_gate, proj_out[:, :half_cols], preferred_element_type=jnp.float32)
    proj_up = jnp.dot(grad_up, proj_out[:, half_cols:], preferred_element_type=jnp.float32)
    return jnp.concatenate([proj_gate, proj_up], axis=1)


def sketch_part(block_rows, first_position, proj_in, lengths, grads_block):
    row_count = block_rows.shape[0]
    acts_block = jnp.dot(block_rows, proj_in, preferred_element_type=jnp.float32)
    position = first_position + lax.iota(jnp.int32, row_count)
    seq_ends = jnp.cumsum(lengths)
    seq_starts = seq_ends - lengths
    member = (
        (position[:, None] >= seq_starts[None, :]) & (position[:, None] < seq_ends[None, :])
    ).astype(jnp.float32)
    seq_count = lengths.shape[0]
    sketch_rank = acts_block.shape[1]
    weighted = (member[:, :, None] * acts_block[:, None, :]).reshape(
        row_count, seq_count * sketch_rank
    )
    return lax.dot_general(
        weighted, grads_block, (((0,), (0,)), ((), ())), precision=lax.Precision.HIGHEST
    )


def shards(tokens_in, out_grad, w_gate, w_up, proj_in, proj_out, lengths, val_sketch):
    local_rows = tokens_in.shape[0]
    seq_count = lengths.shape[0]
    sketch_rank = proj_in.shape[1]
    proj_terms = grad_rows(
        lax.all_gather(tokens_in, ("seq", "mp"), axis=0, tiled=True),
        w_gate,
        w_up,
        proj_out,
        out_grad,
    )
    proj_grads = lax.psum_scatter(proj_terms, ("seq", "mp"), scatter_dimension=0, tiled=True)
    first_row = (lax.axis_index("seq") * lax.axis_size("mp") + lax.axis_index("mp")) * local_rows
    partial_sketch = sketch_part(tokens_in, first_row, proj_in, lengths, proj_grads)
    partial_sketch = partial_sketch.reshape(seq_count, 2 * sketch_rank * sketch_rank)
    sketch = lax.psum(partial_sketch, ("seq", "mp"))
    layered = sketch.reshape(seq_count, sketch_rank, 2, sketch_rank)
    norm_scale = jnp.sqrt(jnp.mean(layered * layered, axis=(1, 3)) + eps_scale)
    normed = (layered / norm_scale[:, None, :, None]).reshape(
        seq_count, 2 * sketch_rank * sketch_rank
    )
    own_seqs = seq_count // lax.axis_size("seq")
    full_val = lax.all_gather(val_sketch, "seq", axis=1, tiled=True)
    own_rows = lax.dynamic_slice_in_dim(normed, lax.axis_index("seq") * own_seqs, own_seqs, 0)
    scores = lax.dot_general(
        own_rows,
        full_val.astype(jnp.float32),
        (((1,), (1,)), ((), ())),
        precision=lax.Precision.HIGHEST,
    )
    return scores


def solution(mesh):
    in_specs = (
        P(("groups", "seq", "mp"), None),
        P("groups", ("seq", "mp")),
        P(None, ("seq", "mp")),
        P(None, ("seq", "mp")),
        P(),
        P(("seq", "mp"), None),
        P("groups"),
        P("mp", "seq"),
    )
    out_specs = P(("groups", "seq"), "mp")
    return jax.shard_map(shards, mesh=mesh, in_specs=in_specs, out_specs=out_specs, check_vma=False)
```

profile of v0, /device:TPU:0, one launch (start us, length us, event | category | flops | bytes accessed | tf_op | source)
XLA Modules:
  0.0 320.5 jit_solution(9285085063448715758)
XLA Ops:
  7.4 0.7 all-gather.3.cloned.1.call-update
  8.1 105.8 %all-gather.3.cloned.1.call-done = bf16[1536,4096]{1,0:T(8,128)(2,1)} async-done(((bf16[96,4096]{1,0:T(8,128)(2,1)}), bf16[1536,4096]{1,0:T(8,128)(2,1)}) %all-gather.3.cloned.1.call-update) | async-done | bytes 12582928 | tf_op jit(solution)/shard_map/all_gather | solution.py:48
  113.9 19.1 %fusion.15 = f32[1536,896]{1,0:T(8,128)} fusion(bf16[1536,4096]{1,0:T(8,128)(2,1)} %all-gather.3.cloned.1.call-done, bf16[4096,896]{1,0:T(8,128)(2,1)} %param.10), kind=kOutput, calls=%fused_computation.24 | convolution fusion | flops 11274289152 | bytes 25427968 | tf_op jit(solution)/shard_map/dot_general | solution.py:11
  133.0 5.2 %fusion.5 = f32[1536,64]{1,0:T(8,128)S(1)} fusion(f32[1536,896]{1,0:T(8,128)} %fusion.15, bf16[1536,896]{1,0:T(8,128)(2,1)} %param.9, bf16[896,128]{1,0:T(8,128)(2,1)S(1)} %copy-done.2), kind=kOutput, calls=%fused_computation.8 | convolution fusion | flops 185794560 | bytes 8880128 | tf_op jit(solution)/shard_map/dot_general | solution.py:20
  138.2 1.8 copy-done.3
  140.0 2.1 copy-done.4
  142.1 16.2 %fusion.2 = bf16[1536,896]{1,0:T(8,128)(2,1)S(1)} fusion(bf16[1536,896]{1,0:T(8,128)(2,1)} %param.9, f32[1536,896]{1,0:T(8,128)} %fusion.15, bf16[1536,4096]{1,0:T(8,128)(2,1)S(1)} %copy-done.3, bf16[4096,896]{1,0:T(8,128)(2,1)S(1)} %copy-done.4), kind=kOutput, calls=%fused_computation.4 | convolution fusion | flops 11289427968 | bytes 30932992 | tf_op jit(solution)/shard_map/dot_general | solution.py:12
  158.3 0.9 fusion.8
  159.2 1.2 pad_maximum_fusion
  160.4 0.2 reduce-window.8
  160.6 0.1 and_convert_fusion
  160.7 0.4 fusion.14
  161.1 54.2 %reduce-scatter.2.cloned.1.call-done = f32[96,128]{1,0:T(8,128)} async-done(((f32[1536,128]{1,0:T(8,128)}), f32[96,128]{1,0:T(8,128)}) %reduce-scatter.2.cloned.1.call-update) | async-done | bytes 49168 | tf_op jit(solution)/shard_map/reduce_scatter | solution.py:54
  215.3 1.1 fusion.16
  216.5 0.8 reshape.101
  217.3 0.2 all-gather.5.cloned.1.call-start
  217.5 0.3 all-gather.5.cloned.1.call-update
  217.8 89.1 %all-reduce.2.cloned.1.call-done = f32[8,8192]{1,0:T(8,128)} async-done(((f32[8,8192]{1,0:T(8,128)}), f32[8,8192]{1,0:T(8,128)}) %all-reduce.2.cloned.1.call-update) | async-done | bytes 262160 | tf_op jit(solution)/shard_map/psum | solution.py:58
  306.9 1.1 mul.62
  308.0 0.4 mul.63
  308.3 0.3 reduce_sum.9
  308.7 0.2 div.19
  308.9 0.5 div.20
  309.4 4.0 %fusion.10 = f32[4,128]{1,0:T(4,128)} fusion(bf16[128,8192]{1,0:T(8,128)(2,1)} %all-gather.5.cloned.1.call-done, f32[8,8192]{1,0:T(8,128)S(1)} %div.20, s32[]{:T(128)S(6)} %select_n.3, f32[8,8192]{1,0:T(8,128)} %all-reduce.2.cloned.1.call-done), kind=kOutput, calls=%fused_computation.14 | convolution fusion | flops 50364416 | bytes 2361348 | tf_op jit(solution)/shard_map/dot_general | solution.py:67
  (20 shorter events, 0.2 us)
Async XLA Ops:
  7.4 153.3 %copy-start = (bf16[4096,64]{0,1:T(8,128)(2,1)S(1)}, bf16[4096,64]{0,1:T(8,128)(2,1)}, u32[]{:S(2)}) copy-start(bf16[4096,64]{0,1:T(8,128)(2,1)} %param.12) | copy-start | bytes 1572868
  7.4 106.5 %all-gather.3.cloned.1.call-start = ((), (), s32[]{:S(2)}) async-start(), calls=%async_computation.1 | async-start | bytes 13369344 | tf_op jit(solution)/shard_map/all_gather | solution.py:48
  8.1 124.9 %copy-start.2 = (bf16[896,128]{1,0:T(8,128)(2,1)S(1)}, bf16[896,128]{1,0:T(8,128)(2,1)}, u32[]{:S(2)}) copy-start(bf16[896,128]{1,0:T(8,128)(2,1)} %param.13) | copy-start | bytes 688132
  8.1 207.2 %reduce-scatter.2.cloned.1.call-start = ((), (), s32[]{:S(2)}) async-start(), calls=%async_computation.2 | async-start | bytes 835584 | tf_op jit(solution)/shard_map/reduce_scatter | solution.py:54
  133.0 7.0 %copy-start.3 = (bf16[1536,4096]{1,0:T(8,128)(2,1)S(1)}, bf16[1536,4096]{1,0:T(8,128)(2,1)}, u32[]{:S(2)}) copy-start(bf16[1536,4096]{1,0:T(8,128)(2,1)} %all-gather.3.cloned.1.call-done) | copy-start | bytes 37748740
  133.0 9.1 %copy-start.4 = (bf16[4096,896]{1,0:T(8,128)(2,1)S(1)}, bf16[4096,896]{1,0:T(8,128)(2,1)}, u32[]{:S(2)}) copy-start(bf16[4096,896]{1,0:T(8,128)(2,1)} %param.11) | copy-start | bytes 22020100
  158.3 2.2 copy-start.5
  158.3 2.4 copy-start.1
  160.4 146.5 %all-reduce.2.cloned.1.call-start = ((), (), s32[]{:S(2)}) async-start(), calls=%async_computation.3 | async-start | bytes 524288 | tf_op jit(solution)/shard_map/psum | solution.py:58
  217.3 92.1 %all-gather.5.cloned.1.call-start = ((), (), s32[]{:S(2)}) async-start(), calls=%async_computation.4 | async-start | bytes 3145728 | tf_op jit(solution)/shard_map/all_gather | solution.py:65
Sparse Core Ops, SparseCore 0:
  10.4 103.4 all-gather.2
  160.5 54.7 reduce-scatter.1
  219.1 87.7 all-reduce.1
Sparse Core Ops, SparseCore 1:
  219.3 9.5 all-gather.4
where the time goes:
time: 321 us
  waiting for transfers between devices  250 us (78%)
  matrix products  46.9 us (15%)
  between operations  14.7 us (5%)
  local copies, waits for them, and re-layouts  5.72 us (2%)
    all_gather x1, waiting for transfers between devices, shards(): lax.all_gather(tokens_in, ('seq', 'mp'), axis=0, tiled=True)  106 us
    psum x1, waiting for transfers between devices, shards(): sketch = lax.psum(partial_sketch, ('seq', 'mp'))  89.1 us
    reduce_scatter x1, waiting for transfers between devices, shards(): lax.psum_scatter(proj_terms, ('seq', 'mp'), scatter_dimension=0, tiled=True)  54.2 us
    dot_general x1, matrix products, grad_rows(): gate_pre = jnp.dot(block_rows, w_gate, preferred_element_type=jnp.float32)  19.1 us
    dot_general x1, matrix products, grad_rows(): up_pre = jnp.dot(block_rows, w_up, preferred_element_type=jnp.float32)  16.2 us
  transfers between devices with their start and end apart: 4, of which 3 were waited for; matrix products, arithmetic and copies ran while one was open for 1% of the time, Pallas kernels for 0%

commit v1 on v0

v1 whole, which is shorter than its diff:
```python
import functools

import jax
import jax.numpy as jnp
import numpy as np
from jax import lax
from jax.sharding import PartitionSpec as P

eps_scale = 1e-06


def ring_order(mesh):
    n = mesh.shape["mp"]
    line = list(mesh.devices[0, 0, :])
    natural = list(range(n))
    if n < 4 or not hasattr(line[0], "coords"):
        return natural
    first, third = line[0].coords, line[2].coords
    if sum(abs(a - b) for a, b in zip(first, third)) == 1:
        return natural[0::2] + natural[1::2][::-1]
    return natural


def grad_rows(rows, cotangent, w_gate, w_up, proj_out):
    half_cols = proj_out.shape[1] // 2
    gate_pre = jnp.dot(rows, w_gate, preferred_element_type=jnp.float32)
    up_pre = jnp.dot(rows, w_up, preferred_element_type=jnp.float32)
    cotangent = cotangent.astype(jnp.float32)
    sigmoid_gate = jax.nn.sigmoid(gate_pre)
    grad_up = (cotangent * gate_pre * sigmoid_gate).astype(jnp.bfloat16)
    grad_gate = (
        cotangent * up_pre * sigmoid_gate * (1.0 + gate_pre * (1.0 - sigmoid_gate))
    ).astype(jnp.bfloat16)
    proj_gate = jnp.dot(grad_gate, proj_out[:, :half_cols], preferred_element_type=jnp.float32)
    proj_up = jnp.dot(grad_up, proj_out[:, half_cols:], preferred_element_type=jnp.float32)
    return jnp.concatenate([proj_gate, proj_up], axis=1)


def shards(order, tokens_in, out_grad, w_gate, w_up, proj_in, proj_out, lengths, val_sketch):
    n = len(order)
    rows = tokens_in.shape[0]
    seq_count = lengths.shape[0]
    rank = proj_in.shape[1]
    place = np.argsort(np.array(order)).astype(np.int32)
    at = jnp.asarray(place)[lax.axis_index("mp")]
    ring = jnp.asarray(np.array(order, np.int32))
    core = lax.axis_index("seq")
    forward = [(order[i], order[(i + 1) % n]) for i in range(n)]
    backward = [(b, a) for a, b in forward]
    send_on = functools.partial(lax.ppermute, axis_name="mp", perm=forward)
    send_back = functools.partial(lax.ppermute, axis_name="mp", perm=backward)
    swap = functools.partial(lax.ppermute, axis_name="seq", perm=[(0, 1), (1, 0)])

    seq_ends = jnp.cumsum(lengths)
    seq_starts = seq_ends - lengths

    def first_row(step, of_core):
        return (of_core * n + ring[(at + step + n) % n]) * rows

    def sketch_of(blocks, starts):
        x = jnp.concatenate(blocks, axis=0) if len(blocks) > 1 else blocks[0]
        cot, position = [], []
        for b, s in zip(blocks, starts):
            cot.append(lax.dynamic_slice_in_dim(out_grad, s, b.shape[0], 0))
            position.append(s + lax.iota(jnp.int32, b.shape[0]))
        cot = jnp.concatenate(cot, axis=0)
        position = jnp.concatenate(position, axis=0)
        grads = grad_rows(x, cot, w_gate, w_up, proj_out)
        acts = jnp.dot(x, proj_in, preferred_element_type=jnp.float32)
        member = (
            (position[:, None] >= seq_starts[None, :]) & (position[:, None] < seq_ends[None, :])
        ).astype(jnp.float32)
        weighted = (member[:, :, None] * acts[:, None, :]).reshape(-1, seq_count * rank)
        return lax.dot_general(
            weighted, grads, (((0,), (0,)), ((), ())), precision=lax.Precision.HIGHEST
        )

    other_val = swap(val_sketch)
    other = swap(tokens_in)
    on, back = tokens_in, tokens_in
    total = sketch_of([tokens_in, other], [first_row(0, core), first_row(0, 1 - core)])
    for step in range(1, n // 2):
        on, back = send_on(on), send_back(back)
        blocks = [on, back, swap(on), swap(back)]
        starts = [first_row(d, c) for c in (core, 1 - core) for d in (-step, step)]
        total = total + sketch_of(blocks, starts)
    half = rows // 2
    on, back = send_on(on[:half]), send_back(back[half:])
    blocks = [on, back, swap(on), swap(back)]
    starts = [
        first_row(n // 2, c) + d for c in (core, 1 - core) for d in (0, half)
    ]
    total = total + sketch_of(blocks, starts)

    own = seq_count // 2
    total = total.reshape(2, own, rank, 2 * rank)
    kept = lax.dynamic_index_in_dim(total, core, 0, keepdims=False)
    sent = lax.dynamic_index_in_dim(total, 1 - core, 0, keepdims=False)
    sketch = kept + swap(sent)
    bit = 1
    while bit < n:
        sketch = sketch + lax.ppermute(sketch, "mp", [(i, i ^ bit) for i in range(n)])
        bit *= 2
    layered = sketch.reshape(own, rank, 2, rank)
    norm_scale = jnp.sqrt(jnp.mean(layered * layered, axis=(1, 3)) + eps_scale)
    normed = (layered / norm_scale[:, None, :, None]).reshape(own, 2 * rank * rank)
    low = jnp.where(core == 0, val_sketch, other_val)
    high = jnp.where(core == 0, other_val, val_sketch)
    full_val = jnp.concatenate([low, high], axis=1)
    return lax.dot_general(
        normed,
        full_val.astype(jnp.float32),
        (((1,), (1,)), ((), ())),
        precision=lax.Precision.HIGHEST,
    )


def solution(mesh):
    in_specs = (
        P(("groups", "seq", "mp"), None),
        P("groups", ("seq", "mp")),
        P(None, ("seq", "mp")),
        P(None, ("seq", "mp")),
        P(),
        P(("seq", "mp"), None),
        P("groups"),
        P("mp", "seq"),
    )
    out_specs = P(("groups", "seq"), "mp")
    return jax.shard_map(
        functools.partial(shards, ring_order(mesh)),
        mesh=mesh,
        in_specs=in_specs,
        out_specs=out_specs,
        check_vma=False,
    )
```

time: 321 us -> 175 us (0.55)
  waiting for transfers between devices: 250 us -> 22 us
  matrix products: 46.9 us -> 87.2 us
  local copies, waits for them, and re-layouts: 5.72 us -> 24.5 us
  starting transfers between devices: 0.31 us -> 18.2 us
  other arithmetic: 2.83 us -> 6.06 us
    all_gather x2 -> x0, waiting for transfers between devices: 106 us -> none  [the longest x1 106 us: shards(): lax.all_gather(tokens_in, ('seq', 'mp'), axis=0, tiled=True)]
    psum x1 -> x0, waiting for transfers between devices: 89.1 us -> none  [shards(): sketch = lax.psum(partial_sketch, ('seq', 'mp'))]
    reduce_scatter x1 -> x0, waiting for transfers between devices: 54.2 us -> none  [shards(): lax.psum_scatter(proj_terms, ('seq', 'mp'), scatter_dimension=0, tiled=True)]
    dot_general x1 -> x5, matrix products: 0.88 us -> 36.9 us  [grad_rows(): jnp.dot(grad_gate, proj_out[:, :half_cols], preferred_element_type=jnp.fl...]
    ppermute x0 -> x22, waiting for transfers between devices: none -> 22 us  [the longest x3 10.4 us: shards(): lax.ppermute(sketch, 'mp', [(i, i ^ bit) for i in range(n)])]
    ppermute x0 -> x22, starting transfers between devices: none -> 18.2 us  [the longest x6 7.38 us: shards(): on, back = (send_on(on), send_back(back))]
    unnamed x12 -> x97, local copies, waits for them, and re-layouts: 3.9 us -> 12.7 us
    dynamic_slice x0 -> x4, local copies, waits for them, and re-layouts: none -> 7.8 us  [the longest x2 4.92 us: sketch_of(): cot.append(lax.dynamic_slice_in_dim(out_grad, s, b.shape[0], 0))]
  transfers between devices with their start and end apart: 4 -> 22, of which waited for: 3 -> 6; matrix products, arithmetic and copies ran while one was open for 1% -> 64% of each run, Pallas kernels for 0% -> 0%
where the time goes in v1:
time: 175 us; the launch traced here: 174 us
  matrix products  87.2 us (50%)
  local copies, waits for them, and re-layouts  24.5 us (14%)
  waiting for transfers between devices  22 us (13%)
  starting transfers between devices  18.2 us (10%)
  between operations  16.3 us (9%)
  other arithmetic  6.06 us (3%)
    dot_general x5, matrix products, grad_rows(): jnp.dot(grad_gate, proj_out[:, :half_cols], preferred_element_type=jnp.fl...  36.9 us
    dot_general x5, matrix products, grad_rows(): gate_pre = jnp.dot(rows, w_gate, preferred_element_type=jnp.float32)  28.3 us
    unnamed x97, local copies, waits for them, and re-layouts  12.7 us
    ppermute x3, waiting for transfers between devices, shards(): lax.ppermute(sketch, 'mp', [(i, i ^ bit) for i in range(n)])  10.4 us
    dot_general x5, matrix products, sketch_of(): acts = jnp.dot(x, proj_in, preferred_element_type=jnp.float32)  8.58 us
    ppermute x6, starting transfers between devices, shards(): on, back = (send_on(on), send_back(back))  7.38 us
    ppermute x3, starting transfers between devices, shards(): lax.ppermute(sketch, 'mp', [(i, i ^ bit) for i in range(n)])  5.61 us
    ppermute x6, waiting for transfers between devices, shards(): on, back = (send_on(on), send_back(back))  5.59 us
  transfers between devices with their start and end apart: 22, of which 6 were waited for; matrix products, arithmetic and copies ran while one was open for 64% of the time, Pallas kernels for 0%

profile of v1, /device:TPU:0, one launch (start us, length us, event | category | flops | bytes accessed | tf_op | source)
XLA Modules:
  0.0 174.2 jit_solution(10747774844839652818)
XLA Ops:
  0.0 3.0 %collective-permute-start.1 = (bf16[96,4096]{1,0:T(8,128)(2,1)}, bf16[96,4096]{1,0:T(8,128)(2,1)}, u32[]{:S(2)}, u32[]{:S(2)}) collective-permute-start(bf16[96,4096]{1,0:T(8,128)(2,1)} %param.10), channel_id=1, source_target_pairs={{0,2},{2,4},{4,6},{6,7},{7,5},{5,3},{3,1},{1,0},{8,10},{10,12},{12... | collective-permute-start | bytes 2359304 | tf_op jit(solution)/shard_map/ppermute | solution.py:83
  25.5 3.2 %constant_dynamic-slice_fusion.7 = (bf16[96,896]{1,0:T(8,128)(2,1)}, bf16[96,896]{1,0:T(8,128)(2,1)}, bf16[96,896]{1,0:T(8,128)(2,1)}, bf16[96,896]{1,0:T(8,128)...) fusion(bf16[1536,896]{1,0:T(8,128)(2,1)} %param.11, ...), kind=kLoop, calls=%fused_computation.146 | loop fusion | bytes 4816952 | tf_op jit(solution)/shard_map/dynamic_slice | solution.py:64
  30.7 5.9 %fusion.114 = f32[192,896]{1,0:T(8,128)} fusion(bf16[192,4096]{1,0:T(8,128)(2,1)S(1)} %constant_dynamic-update-slice_fusion, bf16[4096,896]{1,0:T(8,128)(2,1)} %param.12), kind=kOutput, calls=%fused_computation.210 | convolution fusion | flops 1409286144 | bytes 9601024 | tf_op jit(solution)/shard_map/dot_general | solution.py:26
  36.6 5.8 %fusion.29 = f32[192,64]{0,1:T(8,128)} fusion(bf16[192,4096]{1,0:T(8,128)(2,1)S(1)} %constant_dynamic-update-slice_fusion, bf16[4096,896]{1,0:T(8,128)(2,1)} %param.13, f32[192,896]{1,0:T(8,128)} %fusion.114, bf16[96,896]{1,0:T(8,128)(2,1)S(1)} %copy-done.17, bf16[96,896]{1,0:T(8,128)(2,1)S(1)} %copy-done.19, bf16[896,128]{1,0:T(8,128)(2,1)S(1)} %copy-done.31), kind=kOutput, calls=%fused_computation.43 | convolution fusion | flops 1433714688 | bytes 10223616 | tf_op jit(solution)/shard_map/dot_general | solution.py:34
  43.1 2.1 %collective-permute-start.5 = (bf16[96,4096]{1,0:T(8,128)(2,1)}, bf16[96,4096]{1,0:T(8,128)(2,1)}, u32[]{:S(2)}, u32[]{:S(2)}) collective-permute-start(bf16[96,4096]{1,0:T(8,128)(2,1)} %collective-permute-done.1), channel_id=1, source_target_pairs={{0,2},{2,4},{4,6},{6,7},{7,5},{5,3},{3,1},{1,0},{8,10},{10,12},{12... | collective-permute-start | bytes 2359304 | tf_op jit(solution)/shard_map/ppermute | solution.py:83
  49.5 6.9 %fusion.116 = f32[384,896]{1,0:T(8,128)S(1)} fusion(bf16[384,4096]{1,0:T(8,128)(2,1)S(1)} %constant_dynamic-update-slice_fusion.2, bf16[4096,896]{1,0:T(8,128)(2,1)} %param.12), kind=kOutput, calls=%fused_computation.212 | convolution fusion | flops 2818572288 | bytes 11862016 | tf_op jit(solution)/shard_map/dot_general | solution.py:26
  57.5 5.6 %collective-permute-done.5 = bf16[96,4096]{1,0:T(8,128)(2,1)} collective-permute-done((bf16[96,4096]{1,0:T(8,128)(2,1)}, bf16[96,4096]{1,0:T(8,128)(2,1)}, u32[]{:S(2)}, u32[]{:S(2)}) %collective-permute-start.5) | collective-permute-done | bytes 786464 | tf_op jit(solution)/shard_map/ppermute | solution.py:83
  63.1 2.1 %constant_dynamic-update-slice_fusion.9 = bf16[384,4096]{1,0:T(8,128)(2,1)} fusion(bf16[96,4096]{1,0:T(8,128)(2,1)} %collective-permute-done.5), kind=kLoop, calls=%fused_computation.125 | loop fusion | bytes 1572864
  67.0 8.8 %fusion.28 = f32[384,64]{0,1:T(8,128)} fusion(f32[384,896]{1,0:T(8,128)} %copy-done.38, bf16[384,4096]{1,0:T(8,128)(2,1)} %copy-done.3, bf16[4096,896]{1,0:T(8,128)(2,1)} %param.13, bf16[896,128]{1,0:T(8,128)(2,1)} %param.15, bf16[96,896]{1,0:T(8,128)(2,1)S(1)} %get-tuple-element.17, bf16[96,896]{1,0:T(8,128)(2,1)S(1)} %get-tuple-element.18, ...), kind=kOutput, calls=%fused_computation.42 | convolution fusion | flops 2868805632 | bytes 12877824 | tf_op jit(solution)/shard_map/dot_general | solution.py:34
  77.2 3.1 %fusion.115 = f32[384,64]{0,1:T(8,128)S(1)} fusion(bf16[384,4096]{1,0:T(8,128)(2,1)} %copy-done.3, bf16[4096,64]{0,1:T(8,128)(2,1)S(1)} %copy-done), kind=kOutput, calls=%fused_computation.211 | convolution fusion | flops 201326592 | bytes 3768320 | tf_op jit(solution)/shard_map/dot_general | solution.py:69
  84.1 5.8 %fusion.118 = f32[384,896]{1,0:T(8,128)S(1)} fusion(bf16[384,4096]{1,0:T(8,128)(2,1)S(1)} %constant_dynamic-update-slice_fusion.6, bf16[4096,896]{1,0:T(8,128)(2,1)} %param.12), kind=kOutput, calls=%fused_computation.214 | convolution fusion | flops 2818572288 | bytes 11862016 | tf_op jit(solution)/shard_map/dot_general | solution.py:26
  93.1 8.9 %fusion.27 = f32[384,64]{0,1:T(8,128)} fusion(f32[384,896]{1,0:T(8,128)} %copy-done.39, bf16[384,4096]{1,0:T(8,128)(2,1)} %copy-done.2, bf16[4096,896]{1,0:T(8,128)(2,1)} %param.13, bf16[896,128]{1,0:T(8,128)(2,1)} %param.15, bf16[96,896]{1,0:T(8,128)(2,1)S(1)} %get-tuple-element.13, bf16[96,896]{1,0:T(8,128)(2,1)} %get-tuple-element.14, ...), kind=kOutput, calls=%fused_computation.41 | convolution fusion | flops 2868805632 | bytes 12877824 | tf_op jit(solution)/shard_map/dot_general | solution.py:34
  109.0 5.0 %collective-permute-done.14 = bf16[48,4096]{1,0:T(8,128)(2,1)} collective-permute-done((bf16[48,4096]{1,0:T(8,128)(2,1)S(1)}, bf16[48,4096]{1,0:T(8,128)(2,1)}, u32[]{:S(2)}, u32[]{:S(2)}) %collective-permute-start.14) | collective-permute-done | bytes 393248 | tf_op jit(solution)/shard_map/ppermute | solution.py:88
  116.2 8.0 %fusion.120 = f32[384,896]{1,0:T(8,128)} fusion(bf16[384,4096]{1,0:T(8,128)(2,1)S(1)} %constant_dynamic-update-slice_fusion.10, bf16[4096,896]{1,0:T(8,128)(2,1)} %param.12), kind=kOutput, calls=%fused_computation.216 | convolution fusion | flops 2818572288 | bytes 11862016 | tf_op jit(solution)/shard_map/dot_general | solution.py:26
  124.2 8.2 %fusion.26 = f32[384,64]{0,1:T(8,128)S(1)} fusion(f32[384,896]{1,0:T(8,128)} %fusion.120, bf16[384,4096]{1,0:T(8,128)(2,1)} %copy-done.4, bf16[4096,896]{1,0:T(8,128)(2,1)} %param.13, bf16[896,128]{1,0:T(8,128)(2,1)} %param.15, bf16[96,896]{1,0:T(8,128)(2,1)S(1)} %copy-done.9, bf16[96,896]{1,0:T(8,128)(2,1)S(1)} %copy-done.10, ...), kind=kOutput, calls=%fused_computation.40 | convolution fusion | flops 2868805632 | bytes 12877824 | tf_op jit(solution)/shard_map/dot_general | solution.py:34
  132.5 3.1 %fusion.119 = f32[384,64]{0,1:T(8,128)S(1)} fusion(bf16[384,4096]{1,0:T(8,128)(2,1)} %copy-done.4, bf16[4096,64]{0,1:T(8,128)(2,1)S(1)} %copy-done), kind=kOutput, calls=%fused_computation.215 | convolution fusion | flops 201326592 | bytes 3768320 | tf_op jit(solution)/shard_map/dot_general | solution.py:69
  135.6 2.1 %fusion.46 = f32[384,64]{0,1:T(8,128)S(1)} fusion(f32[384,896]{1,0:T(8,128)} %fusion.120, bf16[896,128]{1,0:T(8,128)(2,1)S(1)} %copy-done.34, bf16[96,896]{1,0:T(8,128)(2,1)S(1)} %copy-done.9, bf16[96,896]{1,0:T(8,128)(2,1)S(1)} %copy-done.10, bf16[96,896]{1,0:T(8,128)(2,1)S(1)} %copy-done.11, bf16[96,896]{1,0:T(8,128)(2,1)S(1)} %copy-done.8), kind=kOutput, calls=%fused_computation.69 | convolution fusion | flops 48857088 | bytes 2392064 | tf_op jit(solution)/shard_map/dot_general | solution.py:35
  143.2 5.3 %fusion.30 = f32[192,64]{0,1:T(8,128)S(1)} fusion(bf16[192,4096]{1,0:T(8,128)(2,1)S(1)} %constant_dynamic-update-slice_fusion.14, bf16[4096,896]{1,0:T(8,128)(2,1)} %param.13, f32[192,896]{1,0:T(8,128)} %copy-done.37, bf16[896,128]{1,0:T(8,128)(2,1)S(1)} %copy-done.35, bf16[48,896]{1,0:T(8,128)(2,1)S(1)} %copy-done.26, bf16[48,896]{1,0:T(8,128)(2,1)S(1)} %copy-done.27, ...), kind=kOutput, calls=%fused_computation.44 | convolution fusion | flops 1434402816 | bytes 10223616 | tf_op jit(solution)/shard_map/dot_general | solution.py:34
  152.9 4.5 %collective-permute-done.18 = f32[4,64,128]{2,1,0:T(8,128)S(1)} collective-permute-done((f32[4,64,128]{2,1,0:T(8,128)S(1)}, f32[4,64,128]{2,1,0:T(8,128)S(1)}, u32[]{:S(2)}, u32[]{:S(2)}) %collective-permute-start.18) | collective-permute-done | bytes 131104 | tf_op jit(solution)/shard_map/ppermute | solution.py:102
  159.1 3.4 %collective-permute-done.19 = f32[4,64,128]{2,1,0:T(8,128)S(1)} collective-permute-done((f32[4,64,128]{2,1,0:T(8,128)S(1)}, f32[4,64,128]{2,1,0:T(8,128)S(1)}, u32[]{:S(2)}, u32[]{:S(2)}) %collective-permute-start.19) | collective-permute-done | bytes 131104 | tf_op jit(solution)/shard_map/ppermute | solution.py:102
  162.5 2.7 %collective-permute-start.20 = (f32[4,64,128]{2,1,0:T(8,128)S(1)}, f32[4,64,128]{2,1,0:T(8,128)S(1)}, u32[]{:S(2)}, u32[]{:S(2)}) collective-permute-start(f32[4,64,128]{2,1,0:T(8,128)S(1)} %add.574), channel_id=1, source_target_pairs={{0,4},{1,5},{2,6},{3,7},{4,0},{5,1},{6,2},{7,3},{8,12},{9,13},{10,... | collective-permute-start | bytes 393224 | tf_op jit(solution)/shard_map/ppermute | solution.py:102
  165.2 2.4 %broadcast_select_fusion.1 = (bf16[128,4096]{1,0:T(8,128)(2,1)S(1)}, bf16[128,4096]{1,0:T(8,128)(2,1)}) fusion(bf16[128,4096]{1,0:T(8,128)(2,1)S(1)} %copy-done.5, bf16[128,4096]{1,0:T(8,128)(2,1)} %collective-permute-done.21, pred[]{:T(512)S(6)} %eq.23), kind=kLoop, calls=%fused_computation.46 | loop fusion | flops 1048576 | bytes 4194305 | tf_op jit(solution)/shard_map/jit(_where)/select_n | solution.py:107
  167.6 2.5 %collective-permute-done.20 = f32[4,64,128]{2,1,0:T(8,128)S(1)} collective-permute-done((f32[4,64,128]{2,1,0:T(8,128)S(1)}, f32[4,64,128]{2,1,0:T(8,128)S(1)}, u32[]{:S(2)}, u32[]{:S(2)}) %collective-permute-start.20) | collective-permute-done | bytes 131104 | tf_op jit(solution)/shard_map/ppermute | solution.py:102
  170.7 3.5 %fusion = f32[4,128]{1,0:T(4,128)} fusion(bf16[128,4096]{1,0:T(8,128)(2,1)} %get-tuple-element.24, bf16[128,4096]{1,0:T(8,128)(2,1)S(1)} %get-tuple-element.23, f32[4,8192]{1,0:T(4,128)S(1)} %div.36, f32[1,4,64,128]{3,2,1,0:T(8,128)S(1)} %get-tuple-element.25), kind=kOutput, calls=%fused_computation | convolution fusion | flops 54558720 | bytes 2361344 | tf_op jit(solution)/shard_map/dot_general | solution.py:110
  (194 shorter events, 46.2 us)
Async XLA Ops:
  0.0 42.4 %copy-start = (bf16[4096,64]{0,1:T(8,128)(2,1)S(1)}, bf16[4096,64]{0,1:T(8,128)(2,1)}, u32[]{:S(2)}) copy-start(bf16[4096,64]{0,1:T(8,128)(2,1)} %param.14) | copy-start | bytes 1572868
  0.0 43.1 %collective-permute-start.1 = (bf16[96,4096]{1,0:T(8,128)(2,1)}, bf16[96,4096]{1,0:T(8,128)(2,1)}, u32[]{:S(2)}, u32[]{:S(2)}) collective-permute-start(bf16[96,4096]{1,0:T(8,128)(2,1)} %param.10), channel_id=1, source_target_pairs={{0,2},{2,4},{4,6},{6,7},{7,5},{5,3},{3,1},{1,0},{8,10},{10,12},{12... | collective-permute-start | bytes 2359304 | tf_op jit(solution)/shard_map/ppermute | solution.py:83
  3.0 43.4 %collective-permute-start.2 = (bf16[96,4096]{1,0:T(8,128)(2,1)}, bf16[96,4096]{1,0:T(8,128)(2,1)}, u32[]{:S(2)}, u32[]{:S(2)}) collective-permute-start(bf16[96,4096]{1,0:T(8,128)(2,1)} %param.10), channel_id=1, source_target_pairs={{2,0},{4,2},{6,4},{7,6},{5,7},{3,5},{1,3},{0,1},{10,8},{12,10},{14... | collective-permute-start | bytes 2359304 | tf_op jit(solution)/shard_map/ppermute | solution.py:83
  3.0 26.4 %collective-permute-start = (bf16[96,4096]{1,0:T(8,128)(2,1)}, bf16[96,4096]{1,0:T(8,128)(2,1)}, u32[]{:S(2)}, u32[]{:S(2)}) collective-permute-start(bf16[96,4096]{1,0:T(8,128)(2,1)} %param.10), channel_id=1, source_target_pairs={{0,8},{8,0},{1,9},{9,1},{2,10},{10,2},{3,11},{11,3},{4,12},{12,4},... | collective-permute-start | bytes 2359304 | tf_op jit(solution)/shard_map/ppermute | solution.py:79
  3.0 162.1 %collective-permute-start.21 = (bf16[128,4096]{1,0:T(8,128)(2,1)}, bf16[128,4096]{1,0:T(8,128)(2,1)}, u32[]{:S(2)}, u32[]{:S(2)}) collective-permute-start(bf16[128,4096]{1,0:T(8,128)(2,1)} %param.17), channel_id=1, source_target_pairs={{0,8},{8,0},{1,9},{9,1},{2,10},{10,2},{3,11},{11,3},{4,12},{12,4},... | collective-permute-start | bytes 3145736 | tf_op jit(solution)/shard_map/ppermute | solution.py:78
  43.1 20.0 %collective-permute-start.5 = (bf16[96,4096]{1,0:T(8,128)(2,1)}, bf16[96,4096]{1,0:T(8,128)(2,1)}, u32[]{:S(2)}, u32[]{:S(2)}) collective-permute-start(bf16[96,4096]{1,0:T(8,128)(2,1)} %collective-permute-done.1), channel_id=1, source_target_pairs={{0,2},{2,4},{4,6},{6,7},{7,5},{5,3},{3,1},{1,0},{8,10},{10,12},{12... | collective-permute-start | bytes 2359304 | tf_op jit(solution)/shard_map/ppermute | solution.py:83
  45.1 4.2 %collective-permute-start.3 = (bf16[96,4096]{1,0:T(8,128)(2,1)}, bf16[96,4096]{1,0:T(8,128)(2,1)S(1)}, u32[]{:S(2)}, u32[]{:S(2)}) collective-permute-start(bf16[96,4096]{1,0:T(8,128)(2,1)} %collective-permute-done.1), channel_id=1, source_target_pairs={{0,8},{8,0},{1,9},{9,1},{2,10},{10,2},{3,11},{11,3},{4,12},{12,4},... | collective-permute-start | bytes 2359304 | tf_op jit(solution)/shard_map/ppermute | solution.py:84
  46.4 29.3 %collective-permute-start.6 = (bf16[96,4096]{1,0:T(8,128)(2,1)}, bf16[96,4096]{1,0:T(8,128)(2,1)S(1)}, u32[]{:S(2)}, u32[]{:S(2)}) collective-permute-start(bf16[96,4096]{1,0:T(8,128)(2,1)} %collective-permute-done.2), channel_id=1, source_target_pairs={{2,0},{4,2},{6,4},{7,6},{5,7},{3,5},{1,3},{0,1},{10,8},{12,10},{14... | collective-permute-start | bytes 2359304 | tf_op jit(solution)/shard_map/ppermute | solution.py:83
  46.7 2.7 %collective-permute-start.4 = (bf16[96,4096]{1,0:T(8,128)(2,1)}, bf16[96,4096]{1,0:T(8,128)(2,1)S(1)}, u32[]{:S(2)}, u32[]{:S(2)}) collective-permute-start(bf16[96,4096]{1,0:T(8,128)(2,1)} %collective-permute-done.2), channel_id=1, source_target_pairs={{0,8},{8,0},{1,9},{9,1},{2,10},{10,2},{3,11},{11,3},{4,12},{12,4},... | collective-permute-start | bytes 2359304 | tf_op jit(solution)/shard_map/ppermute | solution.py:84
  65.2 16.0 %collective-permute-start.7 = (bf16[96,4096]{1,0:T(8,128)(2,1)}, bf16[96,4096]{1,0:T(8,128)(2,1)}, u32[]{:S(2)}, u32[]{:S(2)}) collective-permute-start(bf16[96,4096]{1,0:T(8,128)(2,1)} %collective-permute-done.5), channel_id=1, source_target_pairs={{0,8},{8,0},{1,9},{9,1},{2,10},{10,2},{3,11},{11,3},{4,12},{12,4},... | collective-permute-start | bytes 2359304 | tf_op jit(solution)/shard_map/ppermute | solution.py:84
  65.2 24.7 %collective-permute-start.9 = (bf16[96,4096]{1,0:T(8,128)(2,1)}, bf16[96,4096]{1,0:T(8,128)(2,1)S(1)}, u32[]{:S(2)}, u32[]{:S(2)}) collective-permute-start(bf16[96,4096]{1,0:T(8,128)(2,1)} %collective-permute-done.5), channel_id=1, source_target_pairs={{0,2},{2,4},{4,6},{6,7},{7,5},{5,3},{3,1},{1,0},{8,10},{10,12},{12... | collective-permute-start | bytes 2359304 | tf_op jit(solution)/shard_map/ppermute | solution.py:83
  75.8 6.6 %collective-permute-start.8 = (bf16[96,4096]{1,0:T(8,128)(2,1)S(1)}, bf16[96,4096]{1,0:T(8,128)(2,1)S(1)}, u32[]{:S(2)}, u32[]{:S(2)}) collective-permute-start(bf16[96,4096]{1,0:T(8,128)(2,1)S(1)} %collective-permute-done.6), channel_id=1, source_target_pairs={{0,8},{8,0},{1,9},{9,1},{2,10},{10,2},{3,11},{11,3},{4,12},{12,4},... | collective-permute-start | bytes 2359304 | tf_op jit(solution)/shard_map/ppermute | solution.py:84
  76.0 26.0 %collective-permute-start.10 = (bf16[96,4096]{1,0:T(8,128)(2,1)S(1)}, bf16[96,4096]{1,0:T(8,128)(2,1)}, u32[]{:S(2)}, u32[]{:S(2)}) collective-permute-start(bf16[96,4096]{1,0:T(8,128)(2,1)S(1)} %collective-permute-done.6), channel_id=1, source_target_pairs={{2,0},{4,2},{6,4},{7,6},{5,7},{3,5},{1,3},{0,1},{10,8},{12,10},{14... | collective-permute-start | bytes 2359304 | tf_op jit(solution)/shard_map/ppermute | solution.py:83
  90.0 18.9 %collective-permute-start.13 = (bf16[48,4096]{1,0:T(8,128)(2,1)S(1)}, bf16[48,4096]{1,0:T(8,128)(2,1)}, u32[]{:S(2)}, u32[]{:S(2)}) collective-permute-start(bf16[48,4096]{1,0:T(8,128)(2,1)S(1)} %slice.24), channel_id=1, source_target_pairs={{0,2},{2,4},{4,6},{6,7},{7,5},{5,3},{3,1},{1,0},{8,10},{10,12},{12... | collective-permute-start | bytes 1179656 | tf_op jit(solution)/shard_map/ppermute | solution.py:88
  103.1 10.9 %collective-permute-start.14 = (bf16[48,4096]{1,0:T(8,128)(2,1)S(1)}, bf16[48,4096]{1,0:T(8,128)(2,1)}, u32[]{:S(2)}, u32[]{:S(2)}) collective-permute-start(bf16[48,4096]{1,0:T(8,128)(2,1)S(1)} %slice.25), channel_id=1, source_target_pairs={{2,0},{4,2},{6,4},{7,6},{5,7},{3,5},{1,3},{0,1},{10,8},{12,10},{14... | collective-permute-start | bytes 1179656 | tf_op jit(solution)/shard_map/ppermute | solution.py:88
  107.1 8.9 %collective-permute-start.11 = (bf16[96,4096]{1,0:T(8,128)(2,1)S(1)}, bf16[96,4096]{1,0:T(8,128)(2,1)S(1)}, u32[]{:S(2)}, u32[]{:S(2)}) collective-permute-start(bf16[96,4096]{1,0:T(8,128)(2,1)S(1)} %collective-permute-done.9), channel_id=1, source_target_pairs={{0,8},{8,0},{1,9},{9,1},{2,10},{10,2},{3,11},{11,3},{4,12},{12,4},... | collective-permute-start | bytes 2359304 | tf_op jit(solution)/shard_map/ppermute | solution.py:84
  107.2 8.9 %collective-permute-start.12 = (bf16[96,4096]{1,0:T(8,128)(2,1)}, bf16[96,4096]{1,0:T(8,128)(2,1)S(1)}, u32[]{:S(2)}, u32[]{:S(2)}) collective-permute-start(bf16[96,4096]{1,0:T(8,128)(2,1)} %collective-permute-done.10), channel_id=1, source_target_pairs={{0,8},{8,0},{1,9},{9,1},{2,10},{10,2},{3,11},{11,3},{4,12},{12,4},... | collective-permute-start | bytes 2359304 | tf_op jit(solution)/shard_map/ppermute | solution.py:84
  108.9 23.6 %collective-permute-start.15 = (bf16[48,4096]{1,0:T(8,128)(2,1)}, bf16[48,4096]{1,0:T(8,128)(2,1)S(1)}, u32[]{:S(2)}, u32[]{:S(2)}) collective-permute-start(bf16[48,4096]{1,0:T(8,128)(2,1)} %collective-permute-done.13), channel_id=1, source_target_pairs={{0,8},{8,0},{1,9},{9,1},{2,10},{10,2},{3,11},{11,3},{4,12},{12,4},... | collective-permute-start | bytes 1179656 | tf_op jit(solution)/shard_map/ppermute | solution.py:89
  114.0 23.8 %collective-permute-start.16 = (bf16[48,4096]{1,0:T(8,128)(2,1)}, bf16[48,4096]{1,0:T(8,128)(2,1)}, u32[]{:S(2)}, u32[]{:S(2)}) collective-permute-start(bf16[48,4096]{1,0:T(8,128)(2,1)} %collective-permute-done.14), channel_id=1, source_target_pairs={{0,8},{8,0},{1,9},{9,1},{2,10},{10,2},{3,11},{11,3},{4,12},{12,4},... | collective-permute-start | bytes 1179656 | tf_op jit(solution)/shard_map/ppermute | solution.py:89
  149.4 15.8 %copy-start.5 = (bf16[128,4096]{1,0:T(8,128)(2,1)S(1)}, bf16[128,4096]{1,0:T(8,128)(2,1)}, u32[]{:S(2)}) copy-start(bf16[128,4096]{1,0:T(8,128)(2,1)} %param.17) | copy-start | bytes 3145732
  150.0 1.6 collective-permute-start.17
  151.6 5.8 %collective-permute-start.18 = (f32[4,64,128]{2,1,0:T(8,128)S(1)}, f32[4,64,128]{2,1,0:T(8,128)S(1)}, u32[]{:S(2)}, u32[]{:S(2)}) collective-permute-start(f32[4,64,128]{2,1,0:T(8,128)S(1)} %bitcast_add_fusion), channel_id=1, source_target_pairs={{0,1},{1,0},{2,3},{3,2},{4,5},{5,4},{6,7},{7,6},{8,9},{9,8},{10,11... | collective-permute-start | bytes 393224 | tf_op jit(solution)/shard_map/ppermute | solution.py:102
  157.5 5.0 %collective-permute-start.19 = (f32[4,64,128]{2,1,0:T(8,128)S(1)}, f32[4,64,128]{2,1,0:T(8,128)S(1)}, u32[]{:S(2)}, u32[]{:S(2)}) collective-permute-start(f32[4,64,128]{2,1,0:T(8,128)S(1)} %add.573), channel_id=1, source_target_pairs={{0,2},{1,3},{2,0},{3,1},{4,6},{5,7},{6,4},{7,5},{8,10},{9,11},{10,... | collective-permute-start | bytes 393224 | tf_op jit(solution)/shard_map/ppermute | solution.py:102
  162.5 7.6 %collective-permute-start.20 = (f32[4,64,128]{2,1,0:T(8,128)S(1)}, f32[4,64,128]{2,1,0:T(8,128)S(1)}, u32[]{:S(2)}, u32[]{:S(2)}) collective-permute-start(f32[4,64,128]{2,1,0:T(8,128)S(1)} %add.574), channel_id=1, source_target_pairs={{0,4},{1,5},{2,6},{3,7},{4,0},{5,1},{6,2},{7,3},{8,12},{9,13},{10,... | collective-permute-start | bytes 393224 | tf_op jit(solution)/shard_map/ppermute | solution.py:102
  (40 other events, 196.7 us)

commit v2 on v1

v2 whole, which is shorter than its diff:
```python
import functools

import jax
import jax.numpy as jnp
import numpy as np
from jax import lax
from jax.experimental import pallas as pl
from jax.experimental.pallas import tpu as pltpu
from jax.sharding import PartitionSpec as P

eps_scale = 1e-06
LANES = 128
CHUNK = 32
ANY = pl.BlockSpec(memory_space=pl.ANY)
VMEM = pl.BlockSpec(memory_space=pltpu.VMEM)
SMEM = pl.BlockSpec(memory_space=pltpu.SMEM)


def ring_order(mesh):
    n = mesh.shape["mp"]
    line = list(mesh.devices[0, 0, :])
    natural = list(range(n))
    if n < 4 or not hasattr(line[0], "coords"):
        return natural
    first, third = line[0].coords, line[2].coords
    if sum(abs(a - b) for a, b in zip(first, third)) == 1:
        return natural[0::2] + natural[1::2][::-1]
    return natural


def ring_table(order, rows):
    n = len(order)
    table = []
    for core in range(2):
        for m in range(n):
            p, sign = order.index(m), 1 - 2 * core

            def row(c, shift):
                return (c * n + order[(p + shift) % n]) * rows

            line = [row(core, 0), row(1 - core, 0)]
            for k in range(1, n // 2):
                line += [row(core, -sign * k), row(core, sign * k)]
                line += [row(1 - core, sign * k), row(1 - core, -sign * k)]
            line += [row(core, n // 2), row(1 - core, n // 2), core]
            table.append(line)
    return np.array(table, np.int32)


def fill_weights(w_gate, w_up, proj_in, proj_out, w, diagonal, sems):
    hidden = w_gate.shape[1]
    copies = [
        pltpu.make_async_copy(w_gate, w.at[:, pl.ds(0, hidden)], sems.at[0]),
        pltpu.make_async_copy(w_up, w.at[:, pl.ds(hidden, hidden)], sems.at[1]),
    ]
    for copy in copies:
        copy.start()
    w[:, 2 * hidden :] = jnp.concatenate([proj_in[...], proj_in[...]], axis=1)
    values = proj_out[...]
    left = lax.broadcasted_iota(jnp.int32, values.shape, 1) < LANES // 2
    none = jnp.zeros_like(values)
    diagonal[:hidden, :] = jnp.where(left, values, none)
    diagonal[hidden:, :] = jnp.where(left, none, values)
    return copies


def split(value):
    high = value.astype(jnp.bfloat16)
    return high, (value - high.astype(jnp.float32)).astype(jnp.bfloat16)


def step_kernel(count, place, first, last, table, lengths, *refs):
    blocks = refs[:count]
    out_grad, at = refs[count], count + 1
    if first:
        weights, at = refs[at : at + 4], at + 4
    else:
        (before, w, diagonal), at = refs[at : at + 3], at + 3
    outs, at = (refs[at : at + 2], at + 2) if last else (refs[at : at + 1], at + 1)
    if first:
        (w, diagonal), at = refs[at : at + 2], at + 2
    x, cot, pre, both, x_sem, cot_sem, w_sem = refs[at:]
    rows = blocks[0].shape[0]
    total_rows = rows * count
    hidden = out_grad.shape[1]
    seq_count = lengths.shape[0]

    x_copies, cot_copies, starts = [], [], []
    for i in range(count):
        here = pl.ds(i * rows, rows)
        starts.append(table[place + i])
        source = out_grad.at[pl.ds(pl.multiple_of(starts[i], 16), rows)]
        x_copies.append(pltpu.make_async_copy(blocks[i], x.at[here], x_sem.at[i]))
        cot_copies.append(pltpu.make_async_copy(source, cot.at[here], cot_sem.at[i]))
    for copy in x_copies + cot_copies:
        copy.start()
    if first:
        for copy in fill_weights(*weights, w, diagonal, w_sem):
            copy.wait()
    for copy in x_copies:
        copy.wait()
    pre[...] = jnp.dot(x[...], w[...], preferred_element_type=jnp.float32)
    for copy in cot_copies:
        copy.wait()

    def chunk(i, _):
        here = pl.ds(pl.multiple_of(i * CHUNK, CHUNK), CHUNK)
        gate = pre[here, :hidden]
        up = pre[here, hidden : 2 * hidden]
        cotangent = cot[here, :].astype(jnp.float32)
        sig = 0.5 * (1.0 + jnp.tanh(0.5 * gate))
        scaled = cotangent * sig
        both[here, hidden:] = (scaled * gate).astype(jnp.bfloat16)
        both[here, :hidden] = (scaled * up * (1.0 + gate * (1.0 - sig))).astype(jnp.bfloat16)
        return 0

    lax.fori_loop(0, total_rows // CHUNK, chunk, 0)
    grads = jnp.dot(both[...], diagonal[...], preferred_element_type=jnp.float32)
    grads_high, grads_low = split(grads)
    grads_both = jnp.concatenate([grads_high, grads_low], axis=1)

    acts = pre[:, 2 * hidden :]
    position = []
    for i in range(count):
        position.append(starts[i] + lax.broadcasted_iota(jnp.int32, (rows, LANES), 0))
    position = jnp.concatenate(position, axis=0)
    low = lax.broadcasted_iota(jnp.int32, (1, LANES), 1) < LANES // 2
    ends = []
    for s in range(seq_count):
        ends.append(lengths[s] + (ends[-1] if s else 0))
    groups = seq_count // 2
    highs, lows = [], []
    for g in range(groups):
        begin = jnp.where(low, ends[2 * g - 1] if g else 0, ends[2 * g])
        end = jnp.where(low, ends[2 * g], ends[2 * g + 1])
        weighted = jnp.where((position >= begin) & (position < end), acts, 0.0)
        high, rest = split(weighted)
        highs.append(high)
        lows.append(rest)
    over_rows = (((0,), (0,)), ((), ()))
    main = lax.dot_general(
        jnp.concatenate(highs, axis=1),
        grads_both,
        over_rows,
        preferred_element_type=jnp.float32,
    )
    rest = lax.dot_general(
        jnp.concatenate(lows, axis=1), grads_high, over_rows, preferred_element_type=jnp.float32
    )
    part = main[:, :LANES] + main[:, LANES:] + rest
    if not first:
        part += before[...]
    if not last:
        outs[0][...] = part
        return
    kept, sent = outs
    core = table[table.shape[0] - 1]
    half = part.shape[0] // 2
    upper, lower = part[:half, :], part[half:, :]
    kept[...] = jnp.where(core == 0, upper, lower)
    sent[...] = jnp.where(core == 0, lower, upper)


def step_sketch(blocks, place, state, table, lengths, out_grad, weights, last=False):
    count = len(blocks)
    rows, width = blocks[0].shape
    total_rows = count * rows
    hidden = out_grad.shape[1]
    columns = 2 * hidden + LANES
    first = state is None
    out_rows = lengths.shape[0] * LANES // 2
    operands = [table, lengths, *blocks, out_grad]
    specs = [SMEM, SMEM] + [ANY] * (count + 1)
    if first:
        operands += weights
        specs += [ANY, ANY, VMEM, VMEM]
    else:
        operands += state
        specs += [VMEM, VMEM, VMEM]
    out_shape = [jax.ShapeDtypeStruct((out_rows, LANES), jnp.float32)]
    if last:
        out_shape = [jax.ShapeDtypeStruct((out_rows // 2, LANES), jnp.float32)] * 2
    if first:
        out_shape += [
            pltpu.VMEM((width, columns), jnp.bfloat16),
            jax.ShapeDtypeStruct((2 * hidden, LANES), jnp.bfloat16),
        ]
    outs = pl.pallas_call(
        functools.partial(step_kernel, count, place, first, last),
        out_shape=out_shape,
        in_specs=specs,
        out_specs=[VMEM] * len(out_shape),
        scratch_shapes=[
            pltpu.VMEM((total_rows, width), jnp.bfloat16),
            pltpu.VMEM((total_rows, hidden), jnp.bfloat16),
            pltpu.VMEM((total_rows, columns), jnp.float32),
            pltpu.VMEM((total_rows, 2 * hidden), jnp.bfloat16),
            pltpu.SemaphoreType.DMA((count,)),
            pltpu.SemaphoreType.DMA((count,)),
            pltpu.SemaphoreType.DMA((2,)),
        ],
        compiler_params=pltpu.CompilerParams(vmem_limit_bytes=32 * 2**20),
        cost_estimate=pl.CostEstimate(
            flops=4 * total_rows * width * columns,
            bytes_accessed=2 * total_rows * width,
            transcendentals=0,
        ),
    )(*operands)
    return outs if first or last else [*outs, *state[1:]]


def score_kernel(table, mine, theirs, val_own, val_other, scores, sketch):
    core = table[table.shape[0] - 1]
    sketch[...] = mine[...] + theirs[...]
    own, rank = scores.shape[0], sketch.shape[0] // scores.shape[0]
    half = rank // 2
    left = lax.broadcasted_iota(jnp.int32, (own, LANES), 1) < LANES // 2
    squares = jnp.zeros((own, LANES), jnp.float32)
    found = jnp.zeros((4 * own, scores.shape[1]), jnp.float32)
    for side, val in ((core, val_own), (1 - core, val_other)):
        gates, ups = [], []
        for a in range(half):
            slab = sketch[pl.ds(side * half + a, own, stride=rank), :]
            squares += slab * slab
            gates.append(jnp.where(left, slab, 0.0))
            ups.append(jnp.where(left, 0.0, slab))
        gate_high, gate_low = split(jnp.concatenate(gates, axis=1))
        up_high, up_low = split(jnp.concatenate(ups, axis=1))
        found += lax.dot_general(
            jnp.concatenate([gate_high, gate_low, up_high, up_low], axis=0),
            val[...],
            (((1,), (1,)), ((), ())),
            preferred_element_type=jnp.float32,
        )
    count = rank * LANES // 2
    gate_mean = jnp.sum(jnp.where(left, squares, 0.0), axis=1, keepdims=True) / count
    up_mean = jnp.sum(jnp.where(left, 0.0, squares), axis=1, keepdims=True) / count
    gate_part = found[:own] + found[own : 2 * own]
    up_part = found[2 * own : 3 * own] + found[3 * own :]
    scores[...] = gate_part / jnp.sqrt(gate_mean + eps_scale) + up_part / jnp.sqrt(
        up_mean + eps_scale
    )


def score(table, mine, theirs, val_own, val_other, own):
    return pl.pallas_call(
        score_kernel,
        out_shape=jax.ShapeDtypeStruct((own, val_own.shape[0]), jnp.float32),
        in_specs=[SMEM, VMEM, VMEM, VMEM, VMEM],
        out_specs=VMEM,
        scratch_shapes=[pltpu.VMEM(mine.shape, jnp.float32)],
        compiler_params=pltpu.CompilerParams(vmem_limit_bytes=16 * 2**20),
    )(table, mine, theirs, val_own, val_other)


def fast(order, tokens_in, out_grad, w_gate, w_up, proj_in, proj_out, lengths, val_sketch):
    n = len(order)
    rows = tokens_in.shape[0]
    seq_count = lengths.shape[0]
    table = ring_table(order, rows)
    device = lax.axis_index("seq") * n + lax.axis_index("mp")
    table = lax.dynamic_index_in_dim(jnp.asarray(table), device, 0, keepdims=False)
    ahead = [(order[i], order[(i + 1) % n]) for i in range(n)]
    one = ahead + [(n + b, n + a) for a, b in ahead]
    send_one = functools.partial(lax.ppermute, axis_name=("seq", "mp"), perm=one)
    send_two = functools.partial(
        lax.ppermute, axis_name=("seq", "mp"), perm=[(b, a) for a, b in one]
    )
    swap = functools.partial(lax.ppermute, axis_name="seq", perm=[(0, 1), (1, 0)])

    add = functools.partial(
        step_sketch,
        table=table,
        lengths=lengths,
        out_grad=out_grad,
        weights=[w_gate, w_up, proj_in, proj_out],
    )
    one_way, two_way = send_one(tokens_in), send_two(tokens_in)
    other = swap(tokens_in)
    other_val = swap(val_sketch)
    total, *weights = add([tokens_in, other], 0, None)
    place = 2
    for k in range(1, n // 2):
        one_way, two_way, total, other_val = lax.optimization_barrier(
            (one_way, two_way, total, other_val)
        )
        next_one = send_one(one_way)
        next_two = send_two(two_way) if k + 1 < n // 2 else None
        blocks = [one_way, two_way, swap(one_way), swap(two_way)]
        total = add(blocks, place, [total, *weights])[0]
        place += 4
        one_way, two_way = next_one, next_two
    one_way, total = lax.optimization_barrier((one_way, total))
    kept, sent = add([one_way, swap(one_way)], place, [total, *weights], last=True)

    mine, theirs = kept, swap(sent)
    bit = 1
    while bit < n:
        mine = mine + theirs
        pairs = [(i, i ^ bit) for i in range(n)]
        theirs = lax.ppermute(mine.astype(jnp.bfloat16), "mp", pairs).astype(jnp.float32)
        bit *= 2
    return score(table, mine, theirs, val_sketch, other_val, seq_count // 2)


def grad_rows(rows, cotangent, w_gate, w_up, proj_out):
    half_cols = proj_out.shape[1] // 2
    gate_pre = jnp.dot(rows, w_gate, preferred_element_type=jnp.float32)
    up_pre = jnp.dot(rows, w_up, preferred_element_type=jnp.float32)
    cotangent = cotangent.astype(jnp.float32)
    sigmoid_gate = jax.nn.sigmoid(gate_pre)
    grad_up = (cotangent * gate_pre * sigmoid_gate).astype(jnp.bfloat16)
    grad_gate = (
        cotangent * up_pre * sigmoid_gate * (1.0 + gate_pre * (1.0 - sigmoid_gate))
    ).astype(jnp.bfloat16)
    proj_gate = jnp.dot(grad_gate, proj_out[:, :half_cols], preferred_element_type=jnp.float32)
    proj_up = jnp.dot(grad_up, proj_out[:, half_cols:], preferred_element_type=jnp.float32)
    return jnp.concatenate([proj_gate, proj_up], axis=1)


def plain(order, tokens_in, out_grad, w_gate, w_up, proj_in, proj_out, lengths, val_sketch):
    n = len(order)
    rows = tokens_in.shape[0]
    seq_count = lengths.shape[0]
    rank = proj_in.shape[1]
    x = lax.all_gather(tokens_in, ("seq", "mp"), axis=0, tiled=True)
    grads = grad_rows(x, out_grad, w_gate, w_up, proj_out)
    acts = jnp.dot(x, proj_in, preferred_element_type=jnp.float32)
    ends = jnp.cumsum(lengths)
    position = lax.iota(jnp.int32, x.shape[0])[:, None]
    member = ((position >= (ends - lengths)[None, :]) & (position < ends[None, :])).astype(
        jnp.float32
    )
    weighted = (member[:, :, None] * acts[:, None, :]).reshape(x.shape[0], seq_count * rank)
    sketch = lax.dot_general(
        weighted, grads, (((0,), (0,)), ((), ())), precision=lax.Precision.HIGHEST
    )
    sketch = lax.psum(sketch, ("seq", "mp"))
    own = seq_count // lax.axis_size("seq")
    layered = sketch.reshape(seq_count, rank, 2, rank)
    layered = lax.dynamic_slice_in_dim(layered, lax.axis_index("seq") * own, own, 0)
    norm_scale = jnp.sqrt(jnp.mean(layered * layered, axis=(1, 3)) + eps_scale)
    normed = (layered / norm_scale[:, None, :, None]).reshape(own, 2 * rank * rank)
    full_val = lax.all_gather(val_sketch, "seq", axis=1, tiled=True)
    return lax.dot_general(
        normed,
        full_val.astype(jnp.float32),
        (((1,), (1,)), ((), ())),
        precision=lax.Precision.HIGHEST,
    )


def shards(order, tokens_in, out_grad, w_gate, w_up, proj_in, proj_out, lengths, val_sketch):
    n = len(order)
    rows, width = tokens_in.shape
    fits = (
        n >= 2
        and n & (n - 1) == 0
        and lax.axis_size("seq") == 2
        and rows % CHUNK == 0
        and w_gate.shape[1] % LANES == 0
        and width % LANES == 0
        and 2 * proj_in.shape[1] == LANES
        and lengths.shape[0] % 4 == 0
        and val_sketch.shape[1] == proj_in.shape[1] * LANES // 2
    )
    work = fast if fits else plain
    return work(
        order, tokens_in, out_grad, w_gate, w_up, proj_in, proj_out, lengths, val_sketch
    )


def solution(mesh):
    in_specs = (
        P(("groups", "seq", "mp"), None),
        P("groups", ("seq", "mp")),
        P(None, ("seq", "mp")),
        P(None, ("seq", "mp")),
        P(),
        P(("seq", "mp"), None),
        P("groups"),
        P("mp", "seq"),
    )
    out_specs = P(("groups", "seq"), "mp")
    return jax.shard_map(
        functools.partial(shards, ring_order(mesh)),
        mesh=mesh,
        in_specs=in_specs,
        out_specs=out_specs,
        check_vma=False,
    )
```

time: 175 us -> 108 us (0.62)
  matrix products: 87.2 us -> 0 us
  Pallas kernels: 0 us -> 51.1 us
  between operations: 16.3 us -> 0.14 us
  waiting for transfers between devices: 22 us -> 14.6 us
  other arithmetic: 6.06 us -> 0.07 us
    dot_general x26 -> x0, matrix products: 87.2 us -> none  [the longest x5 36.9 us: grad_rows(): jnp.dot(grad_gate, proj_out[:, :half_cols], preferred_element_type=jnp.fl...]
    pallas_call x0 -> x6, Pallas kernels: none -> 51.1 us  [the longest x5 49.3 us: step_sketch(): pl.pallas_call(functools.partial(step_kernel, count, place, first, last),...]
    unnamed x97 -> x19, local copies, waits for them, and re-layouts: 12.7 us -> 22.4 us
    dynamic_slice x4 -> x0, local copies, waits for them, and re-layouts: 7.8 us -> none  [the longest x2 4.92 us: sketch_of(): cot.append(lax.dynamic_slice_in_dim(out_grad, s, b.shape[0], 0))]
    ppermute x22 -> x20, waiting for transfers between devices: 22 us -> 14.6 us  [the longest x3 7.78 us: fast(): lax.ppermute(mine.astype(jnp.bfloat16), 'mp', pairs).astype(jnp.float32)]
    concatenate x5 -> x0, local copies, waits for them, and re-layouts: 2.38 us -> none  [sketch_of(): x = jnp.concatenate(blocks, axis=0) if len(blocks) > 1 else blocks[0]]
    select_n x1 -> x0, other arithmetic: 2.37 us -> none  [shards(): low = jnp.where(core == 0, val_sketch, other_val)]
    ppermute x22 -> x20, starting transfers between devices: 18.2 us -> 18.5 us  [the longest x3 6.46 us: fast(): lax.ppermute(mine.astype(jnp.bfloat16), 'mp', pairs).astype(jnp.float32)]
  transfers between devices with their start and end apart: 22 -> 20, of which waited for: 6 -> 12; matrix products, arithmetic and copies ran while one was open for 64% -> 2% of each run, Pallas kernels for 0% -> 41%
where the time goes in v2:
time: 108 us; the launch traced here: 107 us
  Pallas kernels  51.1 us (47%)
  local copies, waits for them, and re-layouts  23.1 us (21%)
  starting transfers between devices  18.5 us (17%)
  waiting for transfers between devices  14.6 us (14%)
    pallas_call x5, Pallas kernels, step_sketch(): pl.pallas_call(functools.partial(step_kernel, count, place, first, last),...  49.3 us
    unnamed x19, local copies, waits for them, and re-layouts  22.4 us
    ppermute x3, waiting for transfers between devices, fast(): lax.ppermute(mine.astype(jnp.bfloat16), 'mp', pairs).astype(jnp.float32)  7.78 us
    ppermute x3, starting transfers between devices, fast(): lax.ppermute(mine.astype(jnp.bfloat16), 'mp', pairs).astype(jnp.float32)  6.46 us
    ppermute x3, starting transfers between devices, fast(): next_one = send_one(one_way)  5.96 us
    ppermute x2, starting transfers between devices, fast(): one_way, two_way = (send_one(tokens_in), send_two(tokens_in))  3.03 us
    ppermute x6, waiting for transfers between devices, fast(): blocks = [one_way, two_way, swap(one_way), swap(two_way)]  2.92 us
  transfers between devices with their start and end apart: 20, of which 12 were waited for; matrix products, arithmetic and copies ran while one was open for 2% of the time, Pallas kernels for 41%

profile of v2, /device:TPU:0, one launch (start us, length us, event | category | flops | bytes accessed | tf_op | source)
XLA Modules:
  0.0 107.4 jit_solution(6253758306529578542)
XLA Ops:
  0.5 3.0 %collective-permute-start = (bf16[96,4096]{1,0:T(8,128)(2,1)}, bf16[96,4096]{1,0:T(8,128)(2,1)S(1)}, u32[]{:S(2)}, u32[]{:S(2)}) collective-permute-start(bf16[96,4096]{1,0:T(8,128)(2,1)} %refs_0_.1), channel_id=1, source_target_pairs={{0,2},{2,4},{4,6},{6,7},{7,5},{5,3},{3,1},{1,0},{10,8},{12,10},{14... | collective-permute-start | bytes 2359304 | tf_op jit(solution)/shard_map/ppermute | solution.py:278
  3.5 1.5 %copy.10.refs_5_ = bf16[4096,64]{1,0:T(8,128)(2,1)S(1)} copy(bf16[4096,64]{0,1:T(8,128)(2,1)} %param.13) | data formatting | bytes 1048576 | tf_op args[4]
  5.8 1.8 %copy-done.1 = bf16[1536,896]{1,0:T(8,128)(2,1)S(1)} copy-done((bf16[1536,896]{1,0:T(8,128)(2,1)S(1)}, bf16[1536,896]{1,0:T(8,128)(2,1)}, u32[]{:S(2)}) %copy-start.1) | copy-done | bytes 2752536
  7.5 1.1 %copy-done.3 = bf16[96,4096]{1,0:T(8,128)(2,1)S(1)} copy-done((bf16[96,4096]{1,0:T(8,128)(2,1)S(1)}, bf16[96,4096]{1,0:T(8,128)(2,1)}, u32[]{:S(2)}) %copy-start.3) | copy-done | bytes 786456
  10.3 11.0 %shard_map.91 = (f32[512,128]{1,0:T(8,128)S(1)}, bf16[4096,1920]{1,0:T(8,128)(2,1)S(1)}, bf16[1792,128]{1,0:T(8,128)(2,1)S(1)}) custom-call(s32[17]{0:T(128)S(1)} %dynamic-slice_bitcast_fusion.table, s32[8]{0:T(128)S(1)} %copy-done.5, bf16[96,4096]{1,0:T(8,128)(2,1)S(1)} %copy-done.3, bf16[96,4096]{1,0:T(8,128)(2,1)} %collective-permute-done.2.refs_1_, ...), custom_call_target="tpu_custom_call" | custom-call | flops 6039797760 | bytes 1572864 | tf_op jit(solution)/shard_map/pallas_call | solution.py:188
  21.3 5.4 %copy-done.6 = bf16[4096,1920]{1,0:T(8,128)(2,1)} copy-done((bf16[4096,1920]{1,0:T(8,128)(2,1)}, bf16[4096,1920]{1,0:T(8,128)(2,1)S(1)}, u32[]{:S(2)}) %copy-start.6) | copy-done | bytes 15728664
  27.3 2.0 %collective-permute-start.4 = (bf16[96,4096]{1,0:T(8,128)(2,1)S(1)}, bf16[96,4096]{1,0:T(8,128)(2,1)S(1)}, u32[]{:S(2)}, u32[]{:S(2)}) collective-permute-start(bf16[96,4096]{1,0:T(8,128)(2,1)S(1)} %collective-permute-done.refs_0_), channel_id=1, source_target_pairs={{0,2},{2,4},{4,6},{6,7},{7,5},{5,3},{3,1},{1,0},{10,8},{12,10},{14... | collective-permute-start | bytes 2359304 | tf_op jit(solution)/shard_map/ppermute | solution.py:287
  29.4 1.0 collective-permute-done.7.refs_3_
  30.4 5.5 %copy-done.7 = bf16[4096,1920]{1,0:T(8,128)(2,1)S(1)} copy-done((bf16[4096,1920]{1,0:T(8,128)(2,1)S(1)}, bf16[4096,1920]{1,0:T(8,128)(2,1)}, u32[]{:S(2)}) %copy-start.7) | copy-done | bytes 15728664
  35.9 10.9 %shard_map.92.refs_5_ = f32[512,128]{1,0:T(8,128)S(1)} custom-call(s32[17]{0:T(128)S(1)} %dynamic-slice_bitcast_fusion.table, s32[8]{0:T(128)S(1)} %copy-done.5, bf16[96,4096]{1,0:T(8,128)(2,1)S(1)} %collective-permute-done.refs_0_, bf16[96,4096]{1,0:T(8,128)(2,1)} %collective-permute-done.1.refs_1_, bf16[96,4096]{1,0:T(8,128)(2,1)S(1)} %collective-permute-done.6.refs_2_, ...), custom_call_target="tpu_custom_call" | custom-call | flops 12079595520 | bytes 3145728 | tf_op jit(solution)/shard_map/pallas_call | solution.py:188
  47.6 2.0 %collective-permute-start.8 = (bf16[96,4096]{1,0:T(8,128)(2,1)S(1)}, bf16[96,4096]{1,0:T(8,128)(2,1)S(1)}, u32[]{:S(2)}, u32[]{:S(2)}) collective-permute-start(bf16[96,4096]{1,0:T(8,128)(2,1)S(1)} %collective-permute-done.4.refs_0_), channel_id=1, source_target_pairs={{0,2},{2,4},{4,6},{6,7},{7,5},{5,3},{3,1},{1,0},{10,8},{12,10},{14... | collective-permute-start | bytes 2359304 | tf_op jit(solution)/shard_map/ppermute | solution.py:287
  50.6 5.5 %copy-done.8 = bf16[4096,1920]{1,0:T(8,128)(2,1)S(1)} copy-done((bf16[4096,1920]{1,0:T(8,128)(2,1)S(1)}, bf16[4096,1920]{1,0:T(8,128)(2,1)}, u32[]{:S(2)}) %copy-start.8) | copy-done | bytes 15728664
  56.0 10.8 %shard_map.93.refs_5_ = f32[512,128]{1,0:T(8,128)S(1)} custom-call(s32[17]{0:T(128)S(1)} %dynamic-slice_bitcast_fusion.table, s32[8]{0:T(128)S(1)} %copy-done.5, bf16[96,4096]{1,0:T(8,128)(2,1)S(1)} %collective-permute-done.4.refs_0_, bf16[96,4096]{1,0:T(8,128)(2,1)S(1)} %collective-permute-done.5.refs_1_, ...), custom_call_target="tpu_custom_call" | custom-call | flops 12079595520 | bytes 3145728 | tf_op jit(solution)/shard_map/pallas_call | solution.py:188
  68.0 2.0 %collective-permute-start.12 = (bf16[96,4096]{1,0:T(8,128)(2,1)S(1)}, bf16[96,4096]{1,0:T(8,128)(2,1)S(1)}, u32[]{:S(2)}, u32[]{:S(2)}) collective-permute-start(bf16[96,4096]{1,0:T(8,128)(2,1)S(1)} %collective-permute-done.8.refs_0_), channel_id=1, source_target_pairs={{0,2},{2,4},{4,6},{6,7},{7,5},{5,3},{3,1},{1,0},{10,8},{12,10},{14... | collective-permute-start | bytes 2359304 | tf_op jit(solution)/shard_map/ppermute | solution.py:287
  70.9 10.8 %shard_map.94.refs_3_ = f32[512,128]{1,0:T(8,128)S(1)} custom-call(s32[17]{0:T(128)S(1)} %dynamic-slice_bitcast_fusion.table, s32[8]{0:T(128)S(1)} %copy-done.5, bf16[96,4096]{1,0:T(8,128)(2,1)S(1)} %collective-permute-done.8.refs_0_, bf16[96,4096]{1,0:T(8,128)(2,1)S(1)} %collective-permute-done.9.refs_1_, ...), custom_call_target="tpu_custom_call" | custom-call | flops 12079595520 | bytes 3145728 | tf_op jit(solution)/shard_map/pallas_call | solution.py:188
  82.2 1.9 %collective-permute-done.15.refs_1_ = bf16[96,4096]{1,0:T(8,128)(2,1)S(1)} collective-permute-done((bf16[96,4096]{1,0:T(8,128)(2,1)S(1)}, bf16[96,4096]{1,0:T(8,128)(2,1)S(1)}, u32[]{:S(2)}, u32[]{:S(2)}) %collective-permute-start.15) | collective-permute-done | bytes 786464 | tf_op jit(solution)/shard_map/ppermute | solution.py:294
  84.1 5.8 %shard_map.95 = (f32[256,128]{1,0:T(8,128)S(1)}, f32[256,128]{1,0:T(8,128)S(1)}) custom-call(s32[17]{0:T(128)S(1)} %dynamic-slice_bitcast_fusion.table, s32[8]{0:T(128)S(1)} %copy-done.5, bf16[96,4096]{1,0:T(8,128)(2,1)S(1)} %collective-permute-done.12.refs_0_, bf16[96,4096]{1,0:T(8,128)(2,1)S(1)} %collective-permute-done.15.refs_1_, ...), custom_call_target="tpu_custom_call" | custom-call | flops 6039797760 | bytes 1572864 | tf_op jit(solution)/shard_map/pallas_call | solution.py:188
  91.3 2.1 %collective-permute-start.17 = (bf16[256,128]{1,0:T(8,128)(2,1)S(1)}, bf16[256,128]{1,0:T(8,128)(2,1)S(1)}, u32[]{:S(2)}, u32[]{:S(2)}) collective-permute-start(bf16[256,128]{1,0:T(8,128)(2,1)S(1)} %get-tuple-element.45), channel_id=1, source_target_pairs={{0,1},{1,0},{2,3},{3,2},{4,5},{5,4},{6,7},{7,6},{8,9},{9,8},{10,11... | collective-permute-start | bytes 196616 | tf_op jit(solution)/shard_map/ppermute | solution.py:301
  93.4 2.6 %collective-permute-done.17 = bf16[256,128]{1,0:T(8,128)(2,1)S(1)} collective-permute-done((bf16[256,128]{1,0:T(8,128)(2,1)S(1)}, bf16[256,128]{1,0:T(8,128)(2,1)S(1)}, u32[]{:S(2)}, u32[]{:S(2)}) %collective-permute-start.17) | collective-permute-done | bytes 65568 | tf_op jit(solution)/shard_map/ppermute | solution.py:301
  96.0 1.7 %collective-permute-start.18 = (bf16[256,128]{1,0:T(8,128)(2,1)S(1)}, bf16[256,128]{1,0:T(8,128)(2,1)S(1)}, u32[]{:S(2)}, u32[]{:S(2)}) collective-permute-start(bf16[256,128]{1,0:T(8,128)(2,1)S(1)} %fusion), channel_id=1, source_target_pairs={{0,2},{1,3},{2,0},{3,1},{4,6},{5,7},{6,4},{7,5},{8,10},{9,11},{10,... | collective-permute-start | bytes 196616 | tf_op jit(solution)/shard_map/ppermute | solution.py:301
  97.7 2.6 %collective-permute-done.18 = bf16[256,128]{1,0:T(8,128)(2,1)S(1)} collective-permute-done((bf16[256,128]{1,0:T(8,128)(2,1)S(1)}, bf16[256,128]{1,0:T(8,128)(2,1)S(1)}, u32[]{:S(2)}, u32[]{:S(2)}) %collective-permute-start.18) | collective-permute-done | bytes 65568 | tf_op jit(solution)/shard_map/ppermute | solution.py:301
  100.4 2.7 %collective-permute-start.19 = (bf16[256,128]{1,0:T(8,128)(2,1)S(1)}, bf16[256,128]{1,0:T(8,128)(2,1)S(1)}, u32[]{:S(2)}, u32[]{:S(2)}) collective-permute-start(bf16[256,128]{1,0:T(8,128)(2,1)S(1)} %get-tuple-element.43), channel_id=1, source_target_pairs={{0,4},{1,5},{2,6},{3,7},{4,0},{5,1},{6,2},{7,3},{8,12},{9,13},{10,... | collective-permute-start | bytes 196616 | tf_op jit(solution)/shard_map/ppermute | solution.py:301
  103.1 2.5 %collective-permute-done.19 = bf16[256,128]{1,0:T(8,128)(2,1)S(1)} collective-permute-done((bf16[256,128]{1,0:T(8,128)(2,1)S(1)}, bf16[256,128]{1,0:T(8,128)(2,1)S(1)}, u32[]{:S(2)}, u32[]{:S(2)}) %collective-permute-start.19) | collective-permute-done | bytes 65568 | tf_op jit(solution)/shard_map/ppermute | solution.py:301
  105.6 1.8 %shard_map.96 = f32[4,128]{1,0:T(4,128)} custom-call(s32[17]{0:T(128)S(1)} %dynamic-slice_bitcast_fusion.table, f32[256,128]{1,0:T(8,128)S(1)} %get-tuple-element.44.mine, f32[256,128]{1,0:T(8,128)S(1)} %convert_element_type.23.theirs, bf16[128,4096]{1,0:T(8,128)(2,1)S(1)} %copy-done, bf16[128,4096]{1,0:T(8,128)(2,1)S(1)} %collective-permute-done.3.val_other), custom_call_target="tpu_custom_call" | custom-call | tf_op jit(solution)/shard_map/pallas_call | solution.py:246
  (46 shorter events, 9.3 us)
Async XLA Ops:
  0.0 5.8 %collective-permute-start.2 = (bf16[96,4096]{1,0:T(8,128)(2,1)}, bf16[96,4096]{1,0:T(8,128)(2,1)}, u32[]{:S(2)}, u32[]{:S(2)}) collective-permute-start(bf16[96,4096]{1,0:T(8,128)(2,1)} %refs_0_.1), channel_id=1, source_target_pairs={{0,8},{8,0},{1,9},{9,1},{2,10},{10,2},{3,11},{11,3},{4,12},{12,4},... | collective-permute-start | bytes 2359304 | tf_op jit(solution)/shard_map/ppermute | solution.py:279
  0.5 26.3 %collective-permute-start.3 = (bf16[128,4096]{1,0:T(8,128)(2,1)}, bf16[128,4096]{1,0:T(8,128)(2,1)S(1)}, u32[]{:S(2)}, u32[]{:S(2)}) collective-permute-start(bf16[128,4096]{1,0:T(8,128)(2,1)} %val_own.1), channel_id=1, source_target_pairs={{0,8},{8,0},{1,9},{9,1},{2,10},{10,2},{3,11},{11,3},{4,12},{12,4},... | collective-permute-start | bytes 3145736 | tf_op jit(solution)/shard_map/ppermute | solution.py:280
  0.5 26.2 %collective-permute-start = (bf16[96,4096]{1,0:T(8,128)(2,1)}, bf16[96,4096]{1,0:T(8,128)(2,1)S(1)}, u32[]{:S(2)}, u32[]{:S(2)}) collective-permute-start(bf16[96,4096]{1,0:T(8,128)(2,1)} %refs_0_.1), channel_id=1, source_target_pairs={{0,2},{2,4},{4,6},{6,7},{7,5},{5,3},{3,1},{1,0},{10,8},{12,10},{14... | collective-permute-start | bytes 2359304 | tf_op jit(solution)/shard_map/ppermute | solution.py:278
  3.5 23.2 %collective-permute-start.1 = (bf16[96,4096]{1,0:T(8,128)(2,1)}, bf16[96,4096]{1,0:T(8,128)(2,1)}, u32[]{:S(2)}, u32[]{:S(2)}) collective-permute-start(bf16[96,4096]{1,0:T(8,128)(2,1)} %refs_0_.1), channel_id=1, source_target_pairs={{2,0},{4,2},{6,4},{7,6},{5,7},{3,5},{1,3},{0,1},{8,10},{10,12},{12... | collective-permute-start | bytes 2359304 | tf_op jit(solution)/shard_map/ppermute | solution.py:278
  10.3 20.1 %copy-start.2 = (bf16[1536,896]{1,0:T(8,128)(2,1)S(1)}, bf16[1536,896]{1,0:T(8,128)(2,1)}, u32[]{:S(2)}) copy-start(bf16[1536,896]{1,0:T(8,128)(2,1)} %refs_2_.3) | copy-start | bytes 8257540
  26.7 2.7 %collective-permute-start.6 = (bf16[96,4096]{1,0:T(8,128)(2,1)S(1)}, bf16[96,4096]{1,0:T(8,128)(2,1)S(1)}, u32[]{:S(2)}, u32[]{:S(2)}) collective-permute-start(bf16[96,4096]{1,0:T(8,128)(2,1)S(1)} %collective-permute-done.refs_0_), channel_id=1, source_target_pairs={{0,8},{8,0},{1,9},{9,1},{2,10},{10,2},{3,11},{11,3},{4,12},{12,4},... | collective-permute-start | bytes 2359304 | tf_op jit(solution)/shard_map/ppermute | solution.py:289
  26.8 3.6 %collective-permute-start.7 = (bf16[96,4096]{1,0:T(8,128)(2,1)}, bf16[96,4096]{1,0:T(8,128)(2,1)S(1)}, u32[]{:S(2)}, u32[]{:S(2)}) collective-permute-start(bf16[96,4096]{1,0:T(8,128)(2,1)} %collective-permute-done.1.refs_1_), channel_id=1, source_target_pairs={{0,8},{8,0},{1,9},{9,1},{2,10},{10,2},{3,11},{11,3},{4,12},{12,4},... | collective-permute-start | bytes 2359304 | tf_op jit(solution)/shard_map/ppermute | solution.py:289
  27.3 19.5 %collective-permute-start.4 = (bf16[96,4096]{1,0:T(8,128)(2,1)S(1)}, bf16[96,4096]{1,0:T(8,128)(2,1)S(1)}, u32[]{:S(2)}, u32[]{:S(2)}) collective-permute-start(bf16[96,4096]{1,0:T(8,128)(2,1)S(1)} %collective-permute-done.refs_0_), channel_id=1, source_target_pairs={{0,2},{2,4},{4,6},{6,7},{7,5},{5,3},{3,1},{1,0},{10,8},{12,10},{14... | collective-permute-start | bytes 2359304 | tf_op jit(solution)/shard_map/ppermute | solution.py:287
  29.3 17.8 %collective-permute-start.5 = (bf16[96,4096]{1,0:T(8,128)(2,1)}, bf16[96,4096]{1,0:T(8,128)(2,1)S(1)}, u32[]{:S(2)}, u32[]{:S(2)}) collective-permute-start(bf16[96,4096]{1,0:T(8,128)(2,1)} %collective-permute-done.1.refs_1_), channel_id=1, source_target_pairs={{2,0},{4,2},{6,4},{7,6},{5,7},{3,5},{1,3},{0,1},{8,10},{10,12},{12... | collective-permute-start | bytes 2359304 | tf_op jit(solution)/shard_map/ppermute | solution.py:288
  30.4 5.5 %copy-start.7 = (bf16[4096,1920]{1,0:T(8,128)(2,1)S(1)}, bf16[4096,1920]{1,0:T(8,128)(2,1)}, u32[]{:S(2)}) copy-start(bf16[4096,1920]{1,0:T(8,128)(2,1)} %copy-done.6) | copy-start | bytes 47185924
  47.1 2.6 %collective-permute-start.10 = (bf16[96,4096]{1,0:T(8,128)(2,1)S(1)}, bf16[96,4096]{1,0:T(8,128)(2,1)S(1)}, u32[]{:S(2)}, u32[]{:S(2)}) collective-permute-start(bf16[96,4096]{1,0:T(8,128)(2,1)S(1)} %collective-permute-done.4.refs_0_), channel_id=1, source_target_pairs={{0,8},{8,0},{1,9},{9,1},{2,10},{10,2},{3,11},{11,3},{4,12},{12,4},... | collective-permute-start | bytes 2359304 | tf_op jit(solution)/shard_map/ppermute | solution.py:289
  47.5 3.0 %collective-permute-start.11 = (bf16[96,4096]{1,0:T(8,128)(2,1)S(1)}, bf16[96,4096]{1,0:T(8,128)(2,1)S(1)}, u32[]{:S(2)}, u32[]{:S(2)}) collective-permute-start(bf16[96,4096]{1,0:T(8,128)(2,1)S(1)} %collective-permute-done.5.refs_1_), channel_id=1, source_target_pairs={{0,8},{8,0},{1,9},{9,1},{2,10},{10,2},{3,11},{11,3},{4,12},{12,4},... | collective-permute-start | bytes 2359304 | tf_op jit(solution)/shard_map/ppermute | solution.py:289
  47.6 19.4 %collective-permute-start.8 = (bf16[96,4096]{1,0:T(8,128)(2,1)S(1)}, bf16[96,4096]{1,0:T(8,128)(2,1)S(1)}, u32[]{:S(2)}, u32[]{:S(2)}) collective-permute-start(bf16[96,4096]{1,0:T(8,128)(2,1)S(1)} %collective-permute-done.4.refs_0_), channel_id=1, source_target_pairs={{0,2},{2,4},{4,6},{6,7},{7,5},{5,3},{3,1},{1,0},{10,8},{12,10},{14... | collective-permute-start | bytes 2359304 | tf_op jit(solution)/shard_map/ppermute | solution.py:287
  49.6 17.9 %collective-permute-start.9 = (bf16[96,4096]{1,0:T(8,128)(2,1)S(1)}, bf16[96,4096]{1,0:T(8,128)(2,1)S(1)}, u32[]{:S(2)}, u32[]{:S(2)}) collective-permute-start(bf16[96,4096]{1,0:T(8,128)(2,1)S(1)} %collective-permute-done.5.refs_1_), channel_id=1, source_target_pairs={{2,0},{4,2},{6,4},{7,6},{5,7},{3,5},{1,3},{0,1},{8,10},{10,12},{12... | collective-permute-start | bytes 2359304 | tf_op jit(solution)/shard_map/ppermute | solution.py:288
  50.6 5.5 %copy-start.8 = (bf16[4096,1920]{1,0:T(8,128)(2,1)S(1)}, bf16[4096,1920]{1,0:T(8,128)(2,1)}, u32[]{:S(2)}) copy-start(bf16[4096,1920]{1,0:T(8,128)(2,1)} %copy-done.6) | copy-start | bytes 47185924
  67.5 2.5 %collective-permute-start.13 = (bf16[96,4096]{1,0:T(8,128)(2,1)S(1)}, bf16[96,4096]{1,0:T(8,128)(2,1)S(1)}, u32[]{:S(2)}, u32[]{:S(2)}) collective-permute-start(bf16[96,4096]{1,0:T(8,128)(2,1)S(1)} %collective-permute-done.8.refs_0_), channel_id=1, source_target_pairs={{0,8},{8,0},{1,9},{9,1},{2,10},{10,2},{3,11},{11,3},{4,12},{12,4},... | collective-permute-start | bytes 2359304 | tf_op jit(solution)/shard_map/ppermute | solution.py:289
  67.9 3.0 %collective-permute-start.14 = (bf16[96,4096]{1,0:T(8,128)(2,1)S(1)}, bf16[96,4096]{1,0:T(8,128)(2,1)S(1)}, u32[]{:S(2)}, u32[]{:S(2)}) collective-permute-start(bf16[96,4096]{1,0:T(8,128)(2,1)S(1)} %collective-permute-done.9.refs_1_), channel_id=1, source_target_pairs={{0,8},{8,0},{1,9},{9,1},{2,10},{10,2},{3,11},{11,3},{4,12},{12,4},... | collective-permute-start | bytes 2359304 | tf_op jit(solution)/shard_map/ppermute | solution.py:289
  68.0 13.7 %collective-permute-start.12 = (bf16[96,4096]{1,0:T(8,128)(2,1)S(1)}, bf16[96,4096]{1,0:T(8,128)(2,1)S(1)}, u32[]{:S(2)}, u32[]{:S(2)}) collective-permute-start(bf16[96,4096]{1,0:T(8,128)(2,1)S(1)} %collective-permute-done.8.refs_0_), channel_id=1, source_target_pairs={{0,2},{2,4},{4,6},{6,7},{7,5},{5,3},{3,1},{1,0},{10,8},{12,10},{14... | collective-permute-start | bytes 2359304 | tf_op jit(solution)/shard_map/ppermute | solution.py:287
  81.7 23.9 %copy-start = (bf16[128,4096]{1,0:T(8,128)(2,1)S(1)}, bf16[128,4096]{1,0:T(8,128)(2,1)}, u32[]{:S(2)}) copy-start(bf16[128,4096]{1,0:T(8,128)(2,1)} %val_own.1) | copy-start | bytes 3145732
  81.8 2.4 %collective-permute-start.15 = (bf16[96,4096]{1,0:T(8,128)(2,1)S(1)}, bf16[96,4096]{1,0:T(8,128)(2,1)S(1)}, u32[]{:S(2)}, u32[]{:S(2)}) collective-permute-start(bf16[96,4096]{1,0:T(8,128)(2,1)S(1)} %collective-permute-done.12.refs_0_), channel_id=1, source_target_pairs={{0,8},{8,0},{1,9},{9,1},{2,10},{10,2},{3,11},{11,3},{4,12},{12,4},... | collective-permute-start | bytes 2359304 | tf_op jit(solution)/shard_map/ppermute | solution.py:294
  89.9 1.4 %collective-permute-start.16 = (f32[256,128]{1,0:T(8,128)S(1)}, f32[256,128]{1,0:T(8,128)S(1)}, u32[]{:S(2)}, u32[]{:S(2)}) collective-permute-start(f32[256,128]{1,0:T(8,128)S(1)} %get-tuple-element.41), channel_id=1, source_target_pairs={{0,8},{8,0},{1,9},{9,1},{2,10},{10,2},{3,11},{11,3},{4,12},{12,4},... | collective-permute-start | bytes 393224 | tf_op jit(solution)/shard_map/ppermute | solution.py:296
  91.3 4.7 %collective-permute-start.17 = (bf16[256,128]{1,0:T(8,128)(2,1)S(1)}, bf16[256,128]{1,0:T(8,128)(2,1)S(1)}, u32[]{:S(2)}, u32[]{:S(2)}) collective-permute-start(bf16[256,128]{1,0:T(8,128)(2,1)S(1)} %get-tuple-element.45), channel_id=1, source_target_pairs={{0,1},{1,0},{2,3},{3,2},{4,5},{5,4},{6,7},{7,6},{8,9},{9,8},{10,11... | collective-permute-start | bytes 196616 | tf_op jit(solution)/shard_map/ppermute | solution.py:301
  96.0 4.3 %collective-permute-start.18 = (bf16[256,128]{1,0:T(8,128)(2,1)S(1)}, bf16[256,128]{1,0:T(8,128)(2,1)S(1)}, u32[]{:S(2)}, u32[]{:S(2)}) collective-permute-start(bf16[256,128]{1,0:T(8,128)(2,1)S(1)} %fusion), channel_id=1, source_target_pairs={{0,2},{1,3},{2,0},{3,1},{4,6},{5,7},{6,4},{7,5},{8,10},{9,11},{10,... | collective-permute-start | bytes 196616 | tf_op jit(solution)/shard_map/ppermute | solution.py:301
  100.4 5.2 %collective-permute-start.19 = (bf16[256,128]{1,0:T(8,128)(2,1)S(1)}, bf16[256,128]{1,0:T(8,128)(2,1)S(1)}, u32[]{:S(2)}, u32[]{:S(2)}) collective-permute-start(bf16[256,128]{1,0:T(8,128)(2,1)S(1)} %get-tuple-element.43), channel_id=1, source_target_pairs={{0,4},{1,5},{2,6},{3,7},{4,0},{5,1},{6,2},{7,3},{8,12},{9,13},{10,... | collective-permute-start | bytes 196616 | tf_op jit(solution)/shard_map/ppermute | solution.py:301
  (5 other events, 10.0 us)

commit v3 on v2

--- a/solution.py
+++ b/solution.py
@@ -40,28 +40,35 @@
 
             line = [row(core, 0), row(1 - core, 0)]
             for k in range(1, n // 2):
-                line += [row(core, -sign * k), row(core, sign * k)]
-                line += [row(1 - core, sign * k), row(1 - core, -sign * k)]
+                line += [row(core, -sign * k), row(1 - core, sign * k)]
+                line += [row(core, sign * k), row(1 - core, -sign * k)]
             line += [row(core, n // 2), row(1 - core, n // 2), core]
             table.append(line)
     return np.array(table, np.int32)
 
 
-def fill_weights(w_gate, w_up, proj_in, proj_out, w, diagonal, sems):
-    hidden = w_gate.shape[1]
-    copies = [
-        pltpu.make_async_copy(w_gate, w.at[:, pl.ds(0, hidden)], sems.at[0]),
-        pltpu.make_async_copy(w_up, w.at[:, pl.ds(hidden, hidden)], sems.at[1]),
-    ]
-    for copy in copies:
-        copy.start()
-    w[:, 2 * hidden :] = jnp.concatenate([proj_in[...], proj_in[...]], axis=1)
+def prepare_kernel(w_gate, w_up, out_grad, proj_in, proj_out, twice, diagonal):
+    twice[...] = jnp.concatenate([proj_in[...], proj_in[...]], axis=1)
     values = proj_out[...]
+    hidden = values.shape[0]
     left = lax.broadcasted_iota(jnp.int32, values.shape, 1) < LANES // 2
     none = jnp.zeros_like(values)
     diagonal[:hidden, :] = jnp.where(left, values, none)
     diagonal[hidden:, :] = jnp.where(left, none, values)
-    return copies
+
+
+def prepare(w_gate, w_up, out_grad, proj_in, proj_out):
+    width, hidden = w_gate.shape
+    return pl.pallas_call(
+        prepare_kernel,
+        out_shape=[
+            jax.ShapeDtypeStruct((width, LANES), proj_in.dtype),
+            jax.ShapeDtypeStruct((2 * hidden, LANES), proj_out.dtype),
+        ],
+        in_specs=[VMEM] * 5,
+        out_specs=[VMEM] * 2,
+        compiler_params=pltpu.CompilerParams(vmem_limit_bytes=16 * 2**20),
+    )(w_gate, w_up, out_grad, proj_in, proj_out)
 
 
 def split(value):
@@ -69,52 +76,35 @@
     return high, (value - high.astype(jnp.float32)).astype(jnp.bfloat16)
 
 
-def step_kernel(count, place, first, last, table, lengths, *refs):
+def step_kernel(count, entry, first, last, table, lengths, *refs):
     blocks = refs[:count]
-    out_grad, at = refs[count], count + 1
-    if first:
-        weights, at = refs[at : at + 4], at + 4
-    else:
-        (before, w, diagonal), at = refs[at : at + 3], at + 3
-    outs, at = (refs[at : at + 2], at + 2) if last else (refs[at : at + 1], at + 1)
-    if first:
-        (w, diagonal), at = refs[at : at + 2], at + 2
-    x, cot, pre, both, x_sem, cot_sem, w_sem = refs[at:]
+    out_grad, w_gate, w_up, twice, diagonal = refs[count : count + 5]
+    at = count + 5
+    if not first:
+        before, at = refs[at], at + 1
+    outs, (pre, both) = refs[at:-2], refs[-2:]
     rows = blocks[0].shape[0]
     total_rows = rows * count
     hidden = out_grad.shape[1]
     seq_count = lengths.shape[0]
-
-    x_copies, cot_copies, starts = [], [], []
-    for i in range(count):
-        here = pl.ds(i * rows, rows)
-        starts.append(table[place + i])
-        source = out_grad.at[pl.ds(pl.multiple_of(starts[i], 16), rows)]
-        x_copies.append(pltpu.make_async_copy(blocks[i], x.at[here], x_sem.at[i]))
-        cot_copies.append(pltpu.make_async_copy(source, cot.at[here], cot_sem.at[i]))
-    for copy in x_copies + cot_copies:
-        copy.start()
-    if first:
-        for copy in fill_weights(*weights, w, diagonal, w_sem):
-            copy.wait()
-    for copy in x_copies:
-        copy.wait()
-    pre[...] = jnp.dot(x[...], w[...], preferred_element_type=jnp.float32)
-    for copy in cot_copies:
-        copy.wait()
-
-    def chunk(i, _):
-        here = pl.ds(pl.multiple_of(i * CHUNK, CHUNK), CHUNK)
+    starts = [table[entry + i] for i in range(count)]
+
+    for place, w in ((0, w_gate), (hidden, w_up), (2 * hidden, twice)):
+        x = jnp.concatenate([block[...] for block in blocks], axis=0)
+        pre[:, place : place + w.shape[1]] = jnp.dot(
+            x, w[...], preferred_element_type=jnp.float32
+        )
+    for i in range(total_rows // CHUNK):
+        here = slice(i * CHUNK, (i + 1) * CHUNK)
+        block, row = divmod(i * CHUNK, rows)
+        source = pl.ds(pl.multiple_of(starts[block] + row, CHUNK), CHUNK)
         gate = pre[here, :hidden]
         up = pre[here, hidden : 2 * hidden]
-        cotangent = cot[here, :].astype(jnp.float32)
+        cotangent = out_grad[source, :].astype(jnp.float32)
         sig = 0.5 * (1.0 + jnp.tanh(0.5 * gate))
         scaled = cotangent * sig
         both[here, hidden:] = (scaled * gate).astype(jnp.bfloat16)
         both[here, :hidden] = (scaled * up * (1.0 + gate * (1.0 - sig))).astype(jnp.bfloat16)
-        return 0
-
-    lax.fori_loop(0, total_rows // CHUNK, chunk, 0)
     grads = jnp.dot(both[...], diagonal[...], preferred_element_type=jnp.float32)
     grads_high, grads_low = split(grads)
     grads_both = jnp.concatenate([grads_high, grads_low], axis=1)
@@ -128,9 +118,8 @@
     ends = []
     for s in range(seq_count):
         ends.append(lengths[s] + (ends[-1] if s else 0))
-    groups = seq_count // 2
     highs, lows = [], []
-    for g in range(groups):
+    for g in range(seq_count // 2):
         begin = jnp.where(low, ends[2 * g - 1] if g else 0, ends[2 * g])
         end = jnp.where(low, ends[2 * g], ends[2 * g + 1])
         weighted = jnp.where((position >= begin) & (position < end), acts, 0.0)
@@ -161,57 +150,40 @@
     sent[...] = jnp.where(core == 0, lower, upper)
 
 
-def step_sketch(blocks, place, state, table, lengths, out_grad, weights, last=False):
+def step_sketch(blocks, entry, total, table, lengths, weights, last=False):
     count = len(blocks)
     rows, width = blocks[0].shape
     total_rows = count * rows
-    hidden = out_grad.shape[1]
+    hidden = weights[0].shape[1]
     columns = 2 * hidden + LANES
-    first = state is None
+    first = total is None
     out_rows = lengths.shape[0] * LANES // 2
-    operands = [table, lengths, *blocks, out_grad]
-    specs = [SMEM, SMEM] + [ANY] * (count + 1)
-    if first:
-        operands += weights
-        specs += [ANY, ANY, VMEM, VMEM]
-    else:
-        operands += state
-        specs += [VMEM, VMEM, VMEM]
+    operands = [*blocks, *weights] + ([] if first else [total])
     out_shape = [jax.ShapeDtypeStruct((out_rows, LANES), jnp.float32)]
     if last:
         out_shape = [jax.ShapeDtypeStruct((out_rows // 2, LANES), jnp.float32)] * 2
-    if first:
-        out_shape += [
-            pltpu.VMEM((width, columns), jnp.bfloat16),
-            jax.ShapeDtypeStruct((2 * hidden, LANES), jnp.bfloat16),
-        ]
     outs = pl.pallas_call(
-        functools.partial(step_kernel, count, place, first, last),
+        functools.partial(step_kernel, count, entry, first, last),
         out_shape=out_shape,
-        in_specs=specs,
+        in_specs=[SMEM, SMEM] + [VMEM] * len(operands),
         out_specs=[VMEM] * len(out_shape),
         scratch_shapes=[
-            pltpu.VMEM((total_rows, width), jnp.bfloat16),
-            pltpu.VMEM((total_rows, hidden), jnp.bfloat16),
             pltpu.VMEM((total_rows, columns), jnp.float32),
             pltpu.VMEM((total_rows, 2 * hidden), jnp.bfloat16),
-            pltpu.SemaphoreType.DMA((count,)),
-            pltpu.SemaphoreType.DMA((count,)),
-            pltpu.SemaphoreType.DMA((2,)),
         ],
-        compiler_params=pltpu.CompilerParams(vmem_limit_bytes=32 * 2**20),
+        compiler_params=pltpu.CompilerParams(vmem_limit_bytes=16 * 2**20),
         cost_estimate=pl.CostEstimate(
             flops=4 * total_rows * width * columns,
             bytes_accessed=2 * total_rows * width,
             transcendentals=0,
         ),
-    )(*operands)
-    return outs if first or last else [*outs, *state[1:]]
+    )(table, lengths, *operands)
+    return outs if last else outs[0]
 
 
 def score_kernel(table, mine, theirs, val_own, val_other, scores, sketch):
     core = table[table.shape[0] - 1]
-    sketch[...] = mine[...] + theirs[...]
+    sketch[...] = mine[...] + theirs[...].astype(jnp.float32)
     own, rank = scores.shape[0], sketch.shape[0] // scores.shape[0]
     half = rank // 2
     left = lax.broadcasted_iota(jnp.int32, (own, LANES), 1) < LANES // 2
@@ -268,38 +240,57 @@
     )
     swap = functools.partial(lax.ppermute, axis_name="seq", perm=[(0, 1), (1, 0)])
 
+    after = lax.optimization_barrier
+    one_way = send_one(tokens_in)
+    other, other_val = swap(tokens_in), swap(val_sketch)
+    twice, diagonal = prepare(w_gate, w_up, out_grad, proj_in, proj_out)
+    later_tokens, twice = after((tokens_in, twice))
+    two_way = send_two(later_tokens)
     add = functools.partial(
         step_sketch,
         table=table,
         lengths=lengths,
-        out_grad=out_grad,
-        weights=[w_gate, w_up, proj_in, proj_out],
-    )
-    one_way, two_way = send_one(tokens_in), send_two(tokens_in)
-    other = swap(tokens_in)
-    other_val = swap(val_sketch)
-    total, *weights = add([tokens_in, other], 0, None)
-    place = 2
+        weights=[out_grad, w_gate, w_up, twice, diagonal],
+    )
+
+    waiting = (tokens_in, other)
+    total, entry = None, 0
     for k in range(1, n // 2):
-        one_way, two_way, total, other_val = lax.optimization_barrier(
-            (one_way, two_way, total, other_val)
-        )
+        one_way, other_half = after((one_way, waiting[1]))
         next_one = send_one(one_way)
+        swapped_one = swap(one_way)
+        total = add([waiting[0], other_half], entry, total)
+        entry += 2
+        two_way, total, other_val = after((two_way, total, other_val))
         next_two = send_two(two_way) if k + 1 < n // 2 else None
-        blocks = [one_way, two_way, swap(one_way), swap(two_way)]
-        total = add(blocks, place, [total, *weights])[0]
-        place += 4
+        swapped_two = swap(two_way)
+        _, swapped_one = after((two_way, swapped_one))
+        total = add([one_way, swapped_one], entry, total)
+        entry += 2
+        next_one, total = after((next_one, total))
+        waiting = (two_way, swapped_two)
         one_way, two_way = next_one, next_two
-    one_way, total = lax.optimization_barrier((one_way, total))
-    kept, sent = add([one_way, swap(one_way)], place, [total, *weights], last=True)
+    total = add(waiting, entry, total)
+    entry += 2
+    kept, sent = add([one_way, swap(one_way)], entry, total, last=True)
 
     mine, theirs = kept, swap(sent)
     bit = 1
     while bit < n:
         mine = mine + theirs
-        pairs = [(i, i ^ bit) for i in range(n)]
-        theirs = lax.ppermute(mine.astype(jnp.bfloat16), "mp", pairs).astype(jnp.float32)
-        bit *= 2
+        sent = mine.astype(jnp.bfloat16)
+        exchange = [bit]
+        if bit == 1 and n >= 8:
+            exchange = [1, 2, 3]
+        got = [
+            lax.ppermute(sent, "mp", [(i, i ^ flip) for i in range(n)]) for flip in exchange
+        ]
+        for part in got[:-1]:
+            mine = mine + part.astype(jnp.float32)
+        theirs = got[-1]
+        bit = exchange[-1] + 1 if len(exchange) > 1 else 2 * bit
+        if bit < n:
+            theirs = theirs.astype(jnp.float32)
     return score(table, mine, theirs, val_sketch, other_val, seq_count // 2)
 
 

time: 108 us -> 99.1 us (0.918)
  Pallas kernels: 51.1 us -> 43.7 us
  local copies, waits for them, and re-layouts: 23.1 us -> 20.9 us
  starting transfers between devices: 18.5 us -> 20.2 us
  waiting for transfers between devices: 14.6 us -> 13.5 us
    pallas_call x5 -> x9, Pallas kernels: 49.3 us -> 41.9 us  [the longest x8 41.5 us: step_sketch(): pl.pallas_call(functools.partial(step_kernel, count, entry, first, last),...]
    ppermute x14 -> x15, waiting for transfers between devices: 12.6 us -> 6.61 us  [the longest x4 5.57 us: fast(): lax.ppermute(sent, 'mp', [(i, i ^ flip) for i in range(n)])]
    ppermute x14 -> x15, starting transfers between devices: 12 us -> 15 us  [the longest x4 7.26 us: fast(): lax.ppermute(sent, 'mp', [(i, i ^ flip) for i in range(n)])]
    ppermute x3, waiting for transfers between devices: 0.11 us -> 3.04 us  [fast(): next_one = send_one(one_way)]
    unnamed x19 -> x25, local copies, waits for them, and re-layouts: 22.4 us -> 20.2 us
    ppermute x2, waiting for transfers between devices: 0.81 us -> 2.49 us  [fast(): next_two = send_two(two_way) if k + 1 < n // 2 else None]
    ppermute x3, starting transfers between devices: 5.96 us -> 4.53 us  [fast(): next_one = send_one(one_way)]
  transfers between devices with their start and end apart: 20 -> 21, of which waited for: 12 -> 8; matrix products, arithmetic and copies ran while one was open for 2% -> 2% of each run, Pallas kernels for 41% -> 37%
where the time goes in v3:
time: 99.1 us; the launch traced here: 98.5 us
  Pallas kernels  43.7 us (44%)
  local copies, waits for them, and re-layouts  20.9 us (21%)
  starting transfers between devices  20.2 us (20%)
  waiting for transfers between devices  13.5 us (14%)
    pallas_call x8, Pallas kernels, step_sketch(): pl.pallas_call(functools.partial(step_kernel, count, entry, first, last),...  41.5 us
    unnamed x25, local copies, waits for them, and re-layouts  20.2 us
    ppermute x4, starting transfers between devices, fast(): lax.ppermute(sent, 'mp', [(i, i ^ flip) for i in range(n)])  7.26 us
    ppermute x4, waiting for transfers between devices, fast(): lax.ppermute(sent, 'mp', [(i, i ^ flip) for i in range(n)])  5.57 us
    ppermute x3, starting transfers between devices, fast(): next_one = send_one(one_way)  4.53 us
    ppermute x3, waiting for transfers between devices, fast(): next_one = send_one(one_way)  3.04 us
    ppermute x3, starting transfers between devices, fast(): swapped_one = swap(one_way)  3.04 us
    ppermute x1, starting transfers between devices, fast(): one_way = send_one(tokens_in)  3.02 us
  transfers between devices with their start and end apart: 21, of which 8 were waited for; matrix products, arithmetic and copies ran while one was open for 2% of the time, Pallas kernels for 37%

profile of v3, /device:TPU:0, one launch (start us, length us, event | category | flops | bytes accessed | tf_op | source)
XLA Modules:
  0.0 98.5 jit_solution(8115194822291914330)
XLA Ops:
  0.0 3.0 %collective-permute-start = (bf16[96,4096]{1,0:T(8,128)(2,1)}, bf16[96,4096]{1,0:T(8,128)(2,1)}, u32[]{:S(2)}, u32[]{:S(2)}) collective-permute-start(bf16[96,4096]{1,0:T(8,128)(2,1)} %refs_0_.1), channel_id=1, source_target_pairs={{0,2},{2,4},{4,6},{6,7},{7,5},{5,3},{3,1},{1,0},{10,8},{12,10},{14... | collective-permute-start | bytes 2359304 | tf_op jit(solution)/shard_map/ppermute | solution.py:244
  5.1 3.1 %copy-done = bf16[4096,896]{1,0:T(8,128)(2,1)S(1)} copy-done((bf16[4096,896]{1,0:T(8,128)(2,1)S(1)}, bf16[4096,896]{1,0:T(8,128)(2,1)}, u32[]{:S(2)}) %copy-start) | copy-done | bytes 7340056
  8.2 3.1 %copy-done.2 = bf16[4096,896]{1,0:T(8,128)(2,1)S(1)} copy-done((bf16[4096,896]{1,0:T(8,128)(2,1)S(1)}, bf16[4096,896]{1,0:T(8,128)(2,1)}, u32[]{:S(2)}) %copy-start.2) | copy-done | bytes 7340056
  11.3 1.8 %copy-done.4 = bf16[1536,896]{1,0:T(8,128)(2,1)S(1)} copy-done((bf16[1536,896]{1,0:T(8,128)(2,1)S(1)}, bf16[1536,896]{1,0:T(8,128)(2,1)}, u32[]{:S(2)}) %copy-start.4) | copy-done | bytes 2752536
  18.8 3.1 %copy-done.1 = bf16[4096,896]{1,0:T(8,128)(2,1)S(1)} copy-done((bf16[4096,896]{1,0:T(8,128)(2,1)S(1)}, bf16[4096,896]{1,0:T(8,128)(2,1)}, u32[]{:S(2)}) %copy-start.1) | copy-done | bytes 7340056
  21.9 3.1 %copy-done.3 = bf16[4096,896]{1,0:T(8,128)(2,1)S(1)} copy-done((bf16[4096,896]{1,0:T(8,128)(2,1)S(1)}, bf16[4096,896]{1,0:T(8,128)(2,1)}, u32[]{:S(2)}) %copy-start.3) | copy-done | bytes 7340056
  25.0 1.8 %copy-done.5 = bf16[1536,896]{1,0:T(8,128)(2,1)S(1)} copy-done((bf16[1536,896]{1,0:T(8,128)(2,1)S(1)}, bf16[1536,896]{1,0:T(8,128)(2,1)}, u32[]{:S(2)}) %copy-start.5) | copy-done | bytes 2752536
  27.8 5.8 %shard_map.92.refs_7_ = f32[512,128]{1,0:T(8,128)S(1)} custom-call(s32[17]{0:T(128)S(1)} %dynamic-slice_bitcast_fusion.table, s32[8]{0:T(128)S(1)} %copy-done.11, bf16[96,4096]{1,0:T(8,128)(2,1)} %refs_0_.1, bf16[96,4096]{1,0:T(8,128)(2,1)} %collective-permute-done.1.refs_1_, bf16[1536,896]{1,0:T(8,128)(2,1)S(1)} %copy-done.5, ...), custom_call_target="tpu_custom_call" | custom-call | flops 6039797760 | bytes 1572864 | tf_op jit(solution)/shard_map/pallas_call | solution.py:165
  34.8 5.6 %shard_map.93.refs_7_ = f32[512,128]{1,0:T(8,128)S(1)} custom-call(s32[17]{0:T(128)S(1)} %dynamic-slice_bitcast_fusion.table, s32[8]{0:T(128)S(1)} %copy-done.11, bf16[96,4096]{1,0:T(8,128)(2,1)} %collective-permute-done.refs_0_, bf16[96,4096]{1,0:T(8,128)(2,1)S(1)} %collective-permute-done.5.refs_1_, bf16[1536,896]{1,0:T(8,128)(2,1)S(1)} %copy-done.5, ...), custom_call_target="tpu_custom_call" | custom-call | flops 6039797760 | bytes 1572864 | tf_op jit(solution)/shard_map/pallas_call | solution.py:165
  40.3 1.7 %collective-permute-start.9 = (bf16[96,4096]{1,0:T(8,128)(2,1)S(1)}, bf16[96,4096]{1,0:T(8,128)(2,1)S(1)}, u32[]{:S(2)}, u32[]{:S(2)}) collective-permute-start(bf16[96,4096]{1,0:T(8,128)(2,1)S(1)} %collective-permute-done.2.refs_0_), channel_id=1, source_target_pairs={{0,8},{8,0},{1,9},{9,1},{2,10},{10,2},{3,11},{11,3},{4,12},{12,4},... | collective-permute-start | bytes 2359304 | tf_op jit(solution)/shard_map/ppermute | solution.py:261
  42.1 1.6 %collective-permute-start.7 = (bf16[96,4096]{1,0:T(8,128)(2,1)S(1)}, bf16[96,4096]{1,0:T(8,128)(2,1)S(1)}, u32[]{:S(2)}, u32[]{:S(2)}) collective-permute-start(bf16[96,4096]{1,0:T(8,128)(2,1)S(1)} %collective-permute-done.2.refs_0_), channel_id=1, source_target_pairs={{0,2},{2,4},{4,6},{6,7},{7,5},{5,3},{3,1},{1,0},{10,8},{12,10},{14... | collective-permute-start | bytes 2359304 | tf_op jit(solution)/shard_map/ppermute | solution.py:260
  43.7 4.9 %shard_map.94.refs_7_ = f32[512,128]{1,0:T(8,128)S(1)} custom-call(s32[17]{0:T(128)S(1)} %dynamic-slice_bitcast_fusion.table, s32[8]{0:T(128)S(1)} %copy-done.11, bf16[96,4096]{1,0:T(8,128)(2,1)S(1)} %collective-permute-done.3.refs_0_, bf16[96,4096]{1,0:T(8,128)(2,1)S(1)} %collective-permute-done.6.refs_1_, bf16[1536,896]{1,0:T(8,128)(2,1)S(1)} %copy-done.5, ...), custom_call_target="tpu_custom_call" | custom-call | flops 6039797760 | bytes 1572864 | tf_op jit(solution)/shard_map/pallas_call | solution.py:165
  49.2 5.0 %shard_map.95.refs_7_ = f32[512,128]{1,0:T(8,128)S(1)} custom-call(s32[17]{0:T(128)S(1)} %dynamic-slice_bitcast_fusion.table, s32[8]{0:T(128)S(1)} %copy-done.11, bf16[96,4096]{1,0:T(8,128)(2,1)S(1)} %collective-permute-done.2.refs_0_, bf16[96,4096]{1,0:T(8,128)(2,1)S(1)} %collective-permute-done.9.refs_1_, bf16[1536,896]{1,0:T(8,128)(2,1)S(1)} %copy-done.5, ...), custom_call_target="tpu_custom_call" | custom-call | flops 6039797760 | bytes 1572864 | tf_op jit(solution)/shard_map/pallas_call | solution.py:165
  54.2 3.0 %collective-permute-done.7.refs_0_ = bf16[96,4096]{1,0:T(8,128)(2,1)S(1)} collective-permute-done((bf16[96,4096]{1,0:T(8,128)(2,1)S(1)}, bf16[96,4096]{1,0:T(8,128)(2,1)S(1)}, u32[]{:S(2)}, u32[]{:S(2)}) %collective-permute-start.7) | collective-permute-done | bytes 786464 | tf_op jit(solution)/shard_map/ppermute | solution.py:260
  59.0 4.9 %shard_map.96.refs_7_ = f32[512,128]{1,0:T(8,128)S(1)} custom-call(s32[17]{0:T(128)S(1)} %dynamic-slice_bitcast_fusion.table, s32[8]{0:T(128)S(1)} %copy-done.11, bf16[96,4096]{1,0:T(8,128)(2,1)S(1)} %collective-permute-done.8.refs_0_, bf16[96,4096]{1,0:T(8,128)(2,1)S(1)} %collective-permute-done.10.refs_1_, bf16[1536,896]{1,0:T(8,128)(2,1)S(1)} %copy-done.5, ...), custom_call_target="tpu_custom_call" | custom-call | flops 6039797760 | bytes 1572864 | tf_op jit(solution)/shard_map/pallas_call | solution.py:165
  64.0 2.5 %collective-permute-done.12.refs_0_ = bf16[96,4096]{1,0:T(8,128)(2,1)S(1)} collective-permute-done((bf16[96,4096]{1,0:T(8,128)(2,1)S(1)}, bf16[96,4096]{1,0:T(8,128)(2,1)S(1)}, u32[]{:S(2)}, u32[]{:S(2)}) %collective-permute-start.12) | collective-permute-done | bytes 786464 | tf_op jit(solution)/shard_map/ppermute | solution.py:265
  66.5 5.0 %shard_map.97.refs_7_ = f32[512,128]{1,0:T(8,128)S(1)} custom-call(s32[17]{0:T(128)S(1)} %dynamic-slice_bitcast_fusion.table, s32[8]{0:T(128)S(1)} %copy-done.11, bf16[96,4096]{1,0:T(8,128)(2,1)S(1)} %collective-permute-done.7.refs_0_, bf16[96,4096]{1,0:T(8,128)(2,1)S(1)} %collective-permute-done.13.refs_1_, bf16[1536,896]{1,0:T(8,128)(2,1)S(1)} %copy-done.5, ...), custom_call_target="tpu_custom_call" | custom-call | flops 6039797760 | bytes 1572864 | tf_op jit(solution)/shard_map/pallas_call | solution.py:165
  72.1 5.0 %shard_map.98.refs_7_ = f32[512,128]{1,0:T(8,128)S(1)} custom-call(s32[17]{0:T(128)S(1)} %dynamic-slice_bitcast_fusion.table, s32[8]{0:T(128)S(1)} %copy-done.11, bf16[96,4096]{1,0:T(8,128)(2,1)S(1)} %collective-permute-done.12.refs_0_, bf16[96,4096]{1,0:T(8,128)(2,1)S(1)} %collective-permute-done.15.refs_1_, bf16[1536,896]{1,0:T(8,128)(2,1)S(1)} %copy-done.5, ...), custom_call_target="tpu_custom_call" | custom-call | flops 6039797760 | bytes 1572864 | tf_op jit(solution)/shard_map/pallas_call | solution.py:165
  77.1 5.3 %shard_map.99 = (f32[256,128]{1,0:T(8,128)S(1)}, f32[256,128]{1,0:T(8,128)S(1)}) custom-call(s32[17]{0:T(128)S(1)} %dynamic-slice_bitcast_fusion.table, s32[8]{0:T(128)S(1)} %copy-done.11, bf16[96,4096]{1,0:T(8,128)(2,1)S(1)} %collective-permute-done.11.refs_0_, bf16[96,4096]{1,0:T(8,128)(2,1)S(1)} %collective-permute-done.14.refs_1_, ...), custom_call_target="tpu_custom_call" | custom-call | flops 6039797760 | bytes 1572864 | tf_op jit(solution)/shard_map/pallas_call | solution.py:165
  85.3 2.0 %collective-permute-start.19 = (bf16[256,128]{1,0:T(8,128)(2,1)S(1)}, bf16[256,128]{1,0:T(8,128)(2,1)S(1)}, u32[]{:S(2)}, u32[]{:S(2)}) collective-permute-start(bf16[256,128]{1,0:T(8,128)(2,1)S(1)} %get-tuple-element.67), channel_id=1, source_target_pairs={{0,3},{1,2},{2,1},{3,0},{4,7},{5,6},{6,5},{7,4},{8,11},{9,10},{10,... | collective-permute-start | bytes 196616 | tf_op jit(solution)/shard_map/ppermute | solution.py:286
  88.2 2.5 %collective-permute-done.19 = bf16[256,128]{1,0:T(8,128)(2,1)S(1)} collective-permute-done((bf16[256,128]{1,0:T(8,128)(2,1)S(1)}, bf16[256,128]{1,0:T(8,128)(2,1)S(1)}, u32[]{:S(2)}, u32[]{:S(2)}) %collective-permute-start.19) | collective-permute-done | bytes 65568 | tf_op jit(solution)/shard_map/ppermute | solution.py:286
  90.7 3.7 %collective-permute-start.20 = (bf16[256,128]{1,0:T(8,128)(2,1)S(1)}, bf16[256,128]{1,0:T(8,128)(2,1)S(1)}, u32[]{:S(2)}, u32[]{:S(2)}) collective-permute-start(bf16[256,128]{1,0:T(8,128)(2,1)S(1)} %get-tuple-element.65), channel_id=1, source_target_pairs={{0,4},{1,5},{2,6},{3,7},{4,0},{5,1},{6,2},{7,3},{8,12},{9,13},{10,... | collective-permute-start | bytes 196616 | tf_op jit(solution)/shard_map/ppermute | solution.py:286
  94.4 2.2 %collective-permute-done.20.theirs = bf16[256,128]{1,0:T(8,128)(2,1)S(1)} collective-permute-done((bf16[256,128]{1,0:T(8,128)(2,1)S(1)}, bf16[256,128]{1,0:T(8,128)(2,1)S(1)}, u32[]{:S(2)}, u32[]{:S(2)}) %collective-permute-start.20) | collective-permute-done | bytes 65568 | tf_op jit(solution)/shard_map/ppermute | solution.py:286
  96.7 1.8 %shard_map.100 = f32[4,128]{1,0:T(4,128)} custom-call(s32[17]{0:T(128)S(1)} %dynamic-slice_bitcast_fusion.table, f32[256,128]{1,0:T(8,128)S(1)} %get-tuple-element.66.mine, bf16[256,128]{1,0:T(8,128)(2,1)S(1)} %collective-permute-done.20.theirs, bf16[128,4096]{1,0:T(8,128)(2,1)S(1)} %copy-done.6, bf16[128,4096]{1,0:T(8,128)(2,1)S(1)} %collective-permute-done.4.val_other), custom_call_target="tpu_custom_call" | custom-call | tf_op jit(solution)/shard_map/pallas_call | solution.py:218
  (56 shorter events, 16.7 us)
Async XLA Ops:
  0.0 16.4 %collective-permute-start = (bf16[96,4096]{1,0:T(8,128)(2,1)}, bf16[96,4096]{1,0:T(8,128)(2,1)}, u32[]{:S(2)}, u32[]{:S(2)}) collective-permute-start(bf16[96,4096]{1,0:T(8,128)(2,1)} %refs_0_.1), channel_id=1, source_target_pairs={{0,2},{2,4},{4,6},{6,7},{7,5},{5,3},{3,1},{1,0},{10,8},{12,10},{14... | collective-permute-start | bytes 2359304 | tf_op jit(solution)/shard_map/ppermute | solution.py:244
  3.0 13.4 %collective-permute-start.1 = (bf16[96,4096]{1,0:T(8,128)(2,1)}, bf16[96,4096]{1,0:T(8,128)(2,1)}, u32[]{:S(2)}, u32[]{:S(2)}) collective-permute-start(bf16[96,4096]{1,0:T(8,128)(2,1)} %refs_0_.1), channel_id=1, source_target_pairs={{0,8},{8,0},{1,9},{9,1},{2,10},{10,2},{3,11},{11,3},{4,12},{12,4},... | collective-permute-start | bytes 2359304 | tf_op jit(solution)/shard_map/ppermute | solution.py:245
  3.0 31.6 %collective-permute-start.4 = (bf16[128,4096]{1,0:T(8,128)(2,1)}, bf16[128,4096]{1,0:T(8,128)(2,1)S(1)}, u32[]{:S(2)}, u32[]{:S(2)}) collective-permute-start(bf16[128,4096]{1,0:T(8,128)(2,1)} %val_own.1), channel_id=1, source_target_pairs={{0,8},{8,0},{1,9},{9,1},{2,10},{10,2},{3,11},{11,3},{4,12},{12,4},... | collective-permute-start | bytes 3145736 | tf_op jit(solution)/shard_map/ppermute | solution.py:245
  14.0 4.8 %copy-start.11 = (s32[8]{0:T(128)S(1)}, s32[8]{0:T(128)}, u32[]{:S(2)}) copy-start(s32[8]{0:T(128)} %lengths.15) | copy-start | bytes 100
  15.2 19.4 %collective-permute-start.3 = (bf16[96,4096]{1,0:T(8,128)(2,1)}, bf16[96,4096]{1,0:T(8,128)(2,1)S(1)}, u32[]{:S(2)}, u32[]{:S(2)}) collective-permute-start(bf16[96,4096]{1,0:T(8,128)(2,1)} %refs_0_.1), channel_id=1, source_target_pairs={{2,0},{4,2},{6,4},{7,6},{5,7},{3,5},{1,3},{0,1},{8,10},{10,12},{12... | collective-permute-start | bytes 2359304 | tf_op jit(solution)/shard_map/ppermute | solution.py:248
  16.4 18.3 %collective-permute-start.5 = (bf16[96,4096]{1,0:T(8,128)(2,1)}, bf16[96,4096]{1,0:T(8,128)(2,1)S(1)}, u32[]{:S(2)}, u32[]{:S(2)}) collective-permute-start(bf16[96,4096]{1,0:T(8,128)(2,1)} %collective-permute-done.refs_0_), channel_id=1, source_target_pairs={{0,8},{8,0},{1,9},{9,1},{2,10},{10,2},{3,11},{11,3},{4,12},{12,4},... | collective-permute-start | bytes 2359304 | tf_op jit(solution)/shard_map/ppermute | solution.py:261
  17.2 23.1 %collective-permute-start.2 = (bf16[96,4096]{1,0:T(8,128)(2,1)}, bf16[96,4096]{1,0:T(8,128)(2,1)S(1)}, u32[]{:S(2)}, u32[]{:S(2)}) collective-permute-start(bf16[96,4096]{1,0:T(8,128)(2,1)} %collective-permute-done.refs_0_), channel_id=1, source_target_pairs={{0,2},{2,4},{4,6},{6,7},{7,5},{5,3},{3,1},{1,0},{10,8},{12,10},{14... | collective-permute-start | bytes 2359304 | tf_op jit(solution)/shard_map/ppermute | solution.py:260
  27.8 7.0 %copy-start.10 = (bf16[1792,128]{1,0:T(8,128)(2,1)S(1)}, bf16[1792,128]{1,0:T(8,128)(2,1)}, u32[]{:S(2)}) copy-start(bf16[1792,128]{1,0:T(8,128)(2,1)} %copy-done.8) | copy-start | bytes 1376260
  34.6 5.7 %collective-permute-start.6 = (bf16[96,4096]{1,0:T(8,128)(2,1)S(1)}, bf16[96,4096]{1,0:T(8,128)(2,1)S(1)}, u32[]{:S(2)}, u32[]{:S(2)}) collective-permute-start(bf16[96,4096]{1,0:T(8,128)(2,1)S(1)} %collective-permute-done.3.refs_0_), channel_id=1, source_target_pairs={{0,8},{8,0},{1,9},{9,1},{2,10},{10,2},{3,11},{11,3},{4,12},{12,4},... | collective-permute-start | bytes 2359304 | tf_op jit(solution)/shard_map/ppermute | solution.py:266
  34.6 14.0 %collective-permute-start.8 = (bf16[96,4096]{1,0:T(8,128)(2,1)S(1)}, bf16[96,4096]{1,0:T(8,128)(2,1)S(1)}, u32[]{:S(2)}, u32[]{:S(2)}) collective-permute-start(bf16[96,4096]{1,0:T(8,128)(2,1)S(1)} %collective-permute-done.3.refs_0_), channel_id=1, source_target_pairs={{2,0},{4,2},{6,4},{7,6},{5,7},{3,5},{1,3},{0,1},{8,10},{10,12},{12... | collective-permute-start | bytes 2359304 | tf_op jit(solution)/shard_map/ppermute | solution.py:265
  40.3 8.8 %collective-permute-start.9 = (bf16[96,4096]{1,0:T(8,128)(2,1)S(1)}, bf16[96,4096]{1,0:T(8,128)(2,1)S(1)}, u32[]{:S(2)}, u32[]{:S(2)}) collective-permute-start(bf16[96,4096]{1,0:T(8,128)(2,1)S(1)} %collective-permute-done.2.refs_0_), channel_id=1, source_target_pairs={{0,8},{8,0},{1,9},{9,1},{2,10},{10,2},{3,11},{11,3},{4,12},{12,4},... | collective-permute-start | bytes 2359304 | tf_op jit(solution)/shard_map/ppermute | solution.py:261
  42.1 15.2 %collective-permute-start.7 = (bf16[96,4096]{1,0:T(8,128)(2,1)S(1)}, bf16[96,4096]{1,0:T(8,128)(2,1)S(1)}, u32[]{:S(2)}, u32[]{:S(2)}) collective-permute-start(bf16[96,4096]{1,0:T(8,128)(2,1)S(1)} %collective-permute-done.2.refs_0_), channel_id=1, source_target_pairs={{0,2},{2,4},{4,6},{6,7},{7,5},{5,3},{3,1},{1,0},{10,8},{12,10},{14... | collective-permute-start | bytes 2359304 | tf_op jit(solution)/shard_map/ppermute | solution.py:260
  48.7 8.6 %collective-permute-start.10 = (bf16[96,4096]{1,0:T(8,128)(2,1)S(1)}, bf16[96,4096]{1,0:T(8,128)(2,1)S(1)}, u32[]{:S(2)}, u32[]{:S(2)}) collective-permute-start(bf16[96,4096]{1,0:T(8,128)(2,1)S(1)} %collective-permute-done.8.refs_0_), channel_id=1, source_target_pairs={{0,8},{8,0},{1,9},{9,1},{2,10},{10,2},{3,11},{11,3},{4,12},{12,4},... | collective-permute-start | bytes 2359304 | tf_op jit(solution)/shard_map/ppermute | solution.py:266
  48.7 17.7 %collective-permute-start.12 = (bf16[96,4096]{1,0:T(8,128)(2,1)S(1)}, bf16[96,4096]{1,0:T(8,128)(2,1)S(1)}, u32[]{:S(2)}, u32[]{:S(2)}) collective-permute-start(bf16[96,4096]{1,0:T(8,128)(2,1)S(1)} %collective-permute-done.8.refs_0_), channel_id=1, source_target_pairs={{2,0},{4,2},{6,4},{7,6},{5,7},{3,5},{1,3},{0,1},{8,10},{10,12},{12... | collective-permute-start | bytes 2359304 | tf_op jit(solution)/shard_map/ppermute | solution.py:265
  57.2 9.3 %collective-permute-start.13 = (bf16[96,4096]{1,0:T(8,128)(2,1)S(1)}, bf16[96,4096]{1,0:T(8,128)(2,1)S(1)}, u32[]{:S(2)}, u32[]{:S(2)}) collective-permute-start(bf16[96,4096]{1,0:T(8,128)(2,1)S(1)} %collective-permute-done.7.refs_0_), channel_id=1, source_target_pairs={{0,8},{8,0},{1,9},{9,1},{2,10},{10,2},{3,11},{11,3},{4,12},{12,4},... | collective-permute-start | bytes 2359304 | tf_op jit(solution)/shard_map/ppermute | solution.py:261
  57.7 13.7 %collective-permute-start.11 = (bf16[96,4096]{1,0:T(8,128)(2,1)S(1)}, bf16[96,4096]{1,0:T(8,128)(2,1)S(1)}, u32[]{:S(2)}, u32[]{:S(2)}) collective-permute-start(bf16[96,4096]{1,0:T(8,128)(2,1)S(1)} %collective-permute-done.7.refs_0_), channel_id=1, source_target_pairs={{0,2},{2,4},{4,6},{6,7},{7,5},{5,3},{3,1},{1,0},{10,8},{12,10},{14... | collective-permute-start | bytes 2359304 | tf_op jit(solution)/shard_map/ppermute | solution.py:260
  66.5 5.6 %collective-permute-start.15 = (bf16[96,4096]{1,0:T(8,128)(2,1)S(1)}, bf16[96,4096]{1,0:T(8,128)(2,1)S(1)}, u32[]{:S(2)}, u32[]{:S(2)}) collective-permute-start(bf16[96,4096]{1,0:T(8,128)(2,1)S(1)} %collective-permute-done.12.refs_0_), channel_id=1, source_target_pairs={{0,8},{8,0},{1,9},{9,1},{2,10},{10,2},{3,11},{11,3},{4,12},{12,4},... | collective-permute-start | bytes 2359304 | tf_op jit(solution)/shard_map/ppermute | solution.py:266
  71.5 5.6 %collective-permute-start.14 = (bf16[96,4096]{1,0:T(8,128)(2,1)S(1)}, bf16[96,4096]{1,0:T(8,128)(2,1)S(1)}, u32[]{:S(2)}, u32[]{:S(2)}) collective-permute-start(bf16[96,4096]{1,0:T(8,128)(2,1)S(1)} %collective-permute-done.11.refs_0_), channel_id=1, source_target_pairs={{0,8},{8,0},{1,9},{9,1},{2,10},{10,2},{3,11},{11,3},{4,12},{12,4},... | collective-permute-start | bytes 2359304 | tf_op jit(solution)/shard_map/ppermute | solution.py:275
  77.1 19.6 %copy-start.6 = (bf16[128,4096]{1,0:T(8,128)(2,1)S(1)}, bf16[128,4096]{1,0:T(8,128)(2,1)}, u32[]{:S(2)}) copy-start(bf16[128,4096]{1,0:T(8,128)(2,1)} %val_own.1) | copy-start | bytes 3145732
  82.4 1.4 %collective-permute-start.16 = (f32[256,128]{1,0:T(8,128)S(1)}, f32[256,128]{1,0:T(8,128)S(1)}, u32[]{:S(2)}, u32[]{:S(2)}) collective-permute-start(f32[256,128]{1,0:T(8,128)S(1)} %get-tuple-element.63), channel_id=1, source_target_pairs={{0,8},{8,0},{1,9},{9,1},{2,10},{10,2},{3,11},{11,3},{4,12},{12,4},... | collective-permute-start | bytes 393224 | tf_op jit(solution)/shard_map/ppermute | solution.py:277
  83.8 4.3 %collective-permute-start.17 = (bf16[256,128]{1,0:T(8,128)(2,1)S(1)}, bf16[256,128]{1,0:T(8,128)(2,1)S(1)}, u32[]{:S(2)}, u32[]{:S(2)}) collective-permute-start(bf16[256,128]{1,0:T(8,128)(2,1)S(1)} %get-tuple-element.67), channel_id=1, source_target_pairs={{0,1},{1,0},{2,3},{3,2},{4,5},{5,4},{6,7},{7,6},{8,9},{9,8},{10,11... | collective-permute-start | bytes 196616 | tf_op jit(solution)/shard_map/ppermute | solution.py:286
  83.9 4.3 %collective-permute-start.18 = (bf16[256,128]{1,0:T(8,128)(2,1)S(1)}, bf16[256,128]{1,0:T(8,128)(2,1)S(1)}, u32[]{:S(2)}, u32[]{:S(2)}) collective-permute-start(bf16[256,128]{1,0:T(8,128)(2,1)S(1)} %get-tuple-element.67), channel_id=1, source_target_pairs={{0,2},{1,3},{2,0},{3,1},{4,6},{5,7},{6,4},{7,5},{8,10},{9,11},{10,... | collective-permute-start | bytes 196616 | tf_op jit(solution)/shard_map/ppermute | solution.py:286
  85.3 5.4 %collective-permute-start.19 = (bf16[256,128]{1,0:T(8,128)(2,1)S(1)}, bf16[256,128]{1,0:T(8,128)(2,1)S(1)}, u32[]{:S(2)}, u32[]{:S(2)}) collective-permute-start(bf16[256,128]{1,0:T(8,128)(2,1)S(1)} %get-tuple-element.67), channel_id=1, source_target_pairs={{0,3},{1,2},{2,1},{3,0},{4,7},{5,6},{6,5},{7,4},{8,11},{9,10},{10,... | collective-permute-start | bytes 196616 | tf_op jit(solution)/shard_map/ppermute | solution.py:286
  90.7 6.0 %collective-permute-start.20 = (bf16[256,128]{1,0:T(8,128)(2,1)S(1)}, bf16[256,128]{1,0:T(8,128)(2,1)S(1)}, u32[]{:S(2)}, u32[]{:S(2)}) collective-permute-start(bf16[256,128]{1,0:T(8,128)(2,1)S(1)} %get-tuple-element.65), channel_id=1, source_target_pairs={{0,4},{1,5},{2,6},{3,7},{4,0},{5,1},{6,2},{7,3},{8,12},{9,13},{10,... | collective-permute-start | bytes 196616 | tf_op jit(solution)/shard_map/ppermute | solution.py:286
  (9 other events, 18.7 us)

commit v4 on v3

--- a/solution.py
+++ b/solution.py
@@ -47,7 +47,7 @@
     return np.array(table, np.int32)
 
 
-def prepare_kernel(w_gate, w_up, out_grad, proj_in, proj_out, twice, diagonal):
+def prepare_kernel(table, lengths, w_gate, w_up, out_grad, proj_in, proj_out, twice, diagonal):
     twice[...] = jnp.concatenate([proj_in[...], proj_in[...]], axis=1)
     values = proj_out[...]
     hidden = values.shape[0]
@@ -57,7 +57,7 @@
     diagonal[hidden:, :] = jnp.where(left, none, values)
 
 
-def prepare(w_gate, w_up, out_grad, proj_in, proj_out):
+def prepare(table, lengths, w_gate, w_up, out_grad, proj_in, proj_out):
     width, hidden = w_gate.shape
     return pl.pallas_call(
         prepare_kernel,
@@ -65,10 +65,10 @@
             jax.ShapeDtypeStruct((width, LANES), proj_in.dtype),
             jax.ShapeDtypeStruct((2 * hidden, LANES), proj_out.dtype),
         ],
-        in_specs=[VMEM] * 5,
+        in_specs=[SMEM, SMEM] + [VMEM] * 5,
         out_specs=[VMEM] * 2,
         compiler_params=pltpu.CompilerParams(vmem_limit_bytes=16 * 2**20),
-    )(w_gate, w_up, out_grad, proj_in, proj_out)
+    )(table, lengths, w_gate, w_up, out_grad, proj_in, proj_out)
 
 
 def split(value):
@@ -243,9 +243,9 @@
     after = lax.optimization_barrier
     one_way = send_one(tokens_in)
     other, other_val = swap(tokens_in), swap(val_sketch)
-    twice, diagonal = prepare(w_gate, w_up, out_grad, proj_in, proj_out)
-    later_tokens, twice = after((tokens_in, twice))
+    later_tokens, table = after((tokens_in, table))
     two_way = send_two(later_tokens)
+    twice, diagonal = prepare(table, lengths, w_gate, w_up, out_grad, proj_in, proj_out)
     add = functools.partial(
         step_sketch,
         table=table,

time: 99.1 us -> 94.7 us (0.956)
  local copies, waits for them, and re-layouts: 20.9 us -> 11.8 us
  waiting for transfers between devices: 13.5 us -> 16.2 us
  starting transfers between devices: 20.2 us -> 21.9 us
    unnamed x25 -> x15, local copies, waits for them, and re-layouts: 20.2 us -> 11.1 us
    ppermute x2, starting transfers between devices: 0.57 us -> 3.62 us  [fast(): next_two = send_two(two_way) if k + 1 < n // 2 else None]
    ppermute x3, starting transfers between devices: 3.04 us -> 0.08 us  [fast(): swapped_one = swap(one_way)]
    ppermute x1, waiting for transfers between devices: 0.01 us -> 2.56 us  [fast(): one_way = send_one(tokens_in)]
    ppermute x4, waiting for transfers between devices: 5.57 us -> 7.64 us  [fast(): lax.ppermute(sent, 'mp', [(i, i ^ flip) for i in range(n)])]
    ppermute x2, waiting for transfers between devices: 2.49 us -> 1.31 us  [fast(): next_two = send_two(two_way) if k + 1 < n // 2 else None]
    ppermute x3, starting transfers between devices: 4.53 us -> 5.63 us  [fast(): next_one = send_one(one_way)]
    ppermute x1, waiting for transfers between devices: 1.01 us -> 0.01 us  [fast(): two_way = send_two(later_tokens)]
  transfers between devices with their start and end apart: 21 -> 21, of which waited for: 8 -> 10; matrix products, arithmetic and copies ran while one was open for 2% -> 2% of each run, Pallas kernels for 37% -> 39%
where the time goes in v4:
time: 94.7 us; the launch traced here: 94.3 us
  Pallas kernels  44.2 us (47%)
  starting transfers between devices  21.9 us (23%)
  waiting for transfers between devices  16.2 us (17%)
  local copies, waits for them, and re-layouts  11.8 us (12%)
    pallas_call x8, Pallas kernels, step_sketch(): pl.pallas_call(functools.partial(step_kernel, count, entry, first, last),...  41.5 us
    unnamed x15, local copies, waits for them, and re-layouts  11.1 us
    ppermute x4, waiting for transfers between devices, fast(): lax.ppermute(sent, 'mp', [(i, i ^ flip) for i in range(n)])  7.64 us
    ppermute x4, starting transfers between devices, fast(): lax.ppermute(sent, 'mp', [(i, i ^ flip) for i in range(n)])  7.08 us
    ppermute x3, starting transfers between devices, fast(): next_one = send_one(one_way)  5.63 us
    ppermute x3, waiting for transfers between devices, fast(): next_one = send_one(one_way)  3.65 us
    ppermute x2, starting transfers between devices, fast(): next_two = send_two(two_way) if k + 1 < n // 2 else None  3.62 us
    ppermute x1, starting transfers between devices, fast(): one_way = send_one(tokens_in)  3.02 us
  transfers between devices with their start and end apart: 21, of which 10 were waited for; matrix products, arithmetic and copies ran while one was open for 2% of the time, Pallas kernels for 39%

profile of v4, /device:TPU:0, one launch (start us, length us, event | category | flops | bytes accessed | tf_op | source)
XLA Modules:
  0.0 94.3 jit_solution(10413907302724801123)
XLA Ops:
  0.0 3.0 %collective-permute-start = (bf16[96,4096]{1,0:T(8,128)(2,1)}, bf16[96,4096]{1,0:T(8,128)(2,1)S(1)}, u32[]{:S(2)}, u32[]{:S(2)}) collective-permute-start(bf16[96,4096]{1,0:T(8,128)(2,1)} %refs_0_.1), channel_id=1, source_target_pairs={{0,2},{2,4},{4,6},{6,7},{7,5},{5,3},{3,1},{1,0},{10,8},{12,10},{14... | collective-permute-start | bytes 2359304 | tf_op jit(solution)/shard_map/ppermute | solution.py:244
  6.3 3.1 %copy-done = bf16[4096,896]{1,0:T(8,128)(2,1)S(1)} copy-done((bf16[4096,896]{1,0:T(8,128)(2,1)S(1)}, bf16[4096,896]{1,0:T(8,128)(2,1)}, u32[]{:S(2)}) %copy-start) | copy-done | bytes 7340056
  9.4 3.1 %copy-done.1 = bf16[4096,896]{1,0:T(8,128)(2,1)S(1)} copy-done((bf16[4096,896]{1,0:T(8,128)(2,1)S(1)}, bf16[4096,896]{1,0:T(8,128)(2,1)}, u32[]{:S(2)}) %copy-start.1) | copy-done | bytes 7340056
  12.5 1.8 %copy-done.2 = bf16[1536,896]{1,0:T(8,128)(2,1)S(1)} copy-done((bf16[1536,896]{1,0:T(8,128)(2,1)S(1)}, bf16[1536,896]{1,0:T(8,128)(2,1)}, u32[]{:S(2)}) %copy-start.2) | copy-done | bytes 2752536
  16.8 2.6 %collective-permute-done.refs_0_ = bf16[96,4096]{1,0:T(8,128)(2,1)S(1)} collective-permute-done((bf16[96,4096]{1,0:T(8,128)(2,1)}, bf16[96,4096]{1,0:T(8,128)(2,1)S(1)}, u32[]{:S(2)}, u32[]{:S(2)}) %collective-permute-start) | collective-permute-done | bytes 786464 | tf_op jit(solution)/shard_map/ppermute | solution.py:244
  19.4 2.4 %collective-permute-start.2 = (bf16[96,4096]{1,0:T(8,128)(2,1)S(1)}, bf16[96,4096]{1,0:T(8,128)(2,1)S(1)}, u32[]{:S(2)}, u32[]{:S(2)}) collective-permute-start(bf16[96,4096]{1,0:T(8,128)(2,1)S(1)} %collective-permute-done.refs_0_), channel_id=1, source_target_pairs={{0,2},{2,4},{4,6},{6,7},{7,5},{5,3},{3,1},{1,0},{10,8},{12,10},{14... | collective-permute-start | bytes 2359304 | tf_op jit(solution)/shard_map/ppermute | solution.py:260
  21.8 5.6 %shard_map.92.refs_7_ = f32[512,128]{1,0:T(8,128)S(1)} custom-call(s32[17]{0:T(128)S(1)} %dynamic-slice_bitcast_fusion.table, s32[8]{0:T(128)S(1)} %copy-done.5, bf16[96,4096]{1,0:T(8,128)(2,1)S(1)} %copy-done.6, bf16[96,4096]{1,0:T(8,128)(2,1)} %collective-permute-done.1.refs_1_, bf16[1536,896]{1,0:T(8,128)(2,1)S(1)} %copy-done.2, ...), custom_call_target="tpu_custom_call" | custom-call | flops 6039797760 | bytes 1572864 | tf_op jit(solution)/shard_map/pallas_call | solution.py:165
  28.1 1.6 %collective-permute-start.8 = (bf16[96,4096]{1,0:T(8,128)(2,1)}, bf16[96,4096]{1,0:T(8,128)(2,1)S(1)}, u32[]{:S(2)}, u32[]{:S(2)}) collective-permute-start(bf16[96,4096]{1,0:T(8,128)(2,1)} %collective-permute-done.3.refs_0_), channel_id=1, source_target_pairs={{2,0},{4,2},{6,4},{7,6},{5,7},{3,5},{1,3},{0,1},{8,10},{10,12},{12... | collective-permute-start | bytes 2359304 | tf_op jit(solution)/shard_map/ppermute | solution.py:265
  29.7 5.0 %shard_map.93.refs_7_ = f32[512,128]{1,0:T(8,128)S(1)} custom-call(s32[17]{0:T(128)S(1)} %dynamic-slice_bitcast_fusion.table, s32[8]{0:T(128)S(1)} %copy-done.5, bf16[96,4096]{1,0:T(8,128)(2,1)S(1)} %collective-permute-done.refs_0_, bf16[96,4096]{1,0:T(8,128)(2,1)S(1)} %collective-permute-done.5.refs_1_, bf16[1536,896]{1,0:T(8,128)(2,1)S(1)} %copy-done.2, ...), custom_call_target="tpu_custom_call" | custom-call | flops 6039797760 | bytes 1572864 | tf_op jit(solution)/shard_map/pallas_call | solution.py:165
  36.4 5.6 %shard_map.94.refs_7_ = f32[512,128]{1,0:T(8,128)S(1)} custom-call(s32[17]{0:T(128)S(1)} %dynamic-slice_bitcast_fusion.table, s32[8]{0:T(128)S(1)} %copy-done.5, bf16[96,4096]{1,0:T(8,128)(2,1)} %collective-permute-done.3.refs_0_, bf16[96,4096]{1,0:T(8,128)(2,1)S(1)} %collective-permute-done.6.refs_1_, bf16[1536,896]{1,0:T(8,128)(2,1)S(1)} %copy-done.2, ...), custom_call_target="tpu_custom_call" | custom-call | flops 6039797760 | bytes 1572864 | tf_op jit(solution)/shard_map/pallas_call | solution.py:165
  42.7 2.0 %collective-permute-start.12 = (bf16[96,4096]{1,0:T(8,128)(2,1)S(1)}, bf16[96,4096]{1,0:T(8,128)(2,1)S(1)}, u32[]{:S(2)}, u32[]{:S(2)}) collective-permute-start(bf16[96,4096]{1,0:T(8,128)(2,1)S(1)} %collective-permute-done.8.refs_0_), channel_id=1, source_target_pairs={{2,0},{4,2},{6,4},{7,6},{5,7},{3,5},{1,3},{0,1},{8,10},{10,12},{12... | collective-permute-start | bytes 2359304 | tf_op jit(solution)/shard_map/ppermute | solution.py:265
  44.7 5.0 %shard_map.95.refs_7_ = f32[512,128]{1,0:T(8,128)S(1)} custom-call(s32[17]{0:T(128)S(1)} %dynamic-slice_bitcast_fusion.table, s32[8]{0:T(128)S(1)} %copy-done.5, bf16[96,4096]{1,0:T(8,128)(2,1)S(1)} %collective-permute-done.2.refs_0_, bf16[96,4096]{1,0:T(8,128)(2,1)S(1)} %collective-permute-done.9.refs_1_, bf16[1536,896]{1,0:T(8,128)(2,1)S(1)} %copy-done.2, ...), custom_call_target="tpu_custom_call" | custom-call | flops 6039797760 | bytes 1572864 | tf_op jit(solution)/shard_map/pallas_call | solution.py:165
  49.7 2.2 %collective-permute-done.7.refs_0_ = bf16[96,4096]{1,0:T(8,128)(2,1)S(1)} collective-permute-done((bf16[96,4096]{1,0:T(8,128)(2,1)S(1)}, bf16[96,4096]{1,0:T(8,128)(2,1)S(1)}, u32[]{:S(2)}, u32[]{:S(2)}) %collective-permute-start.7) | collective-permute-done | bytes 786464 | tf_op jit(solution)/shard_map/ppermute | solution.py:260
  51.9 1.7 %collective-permute-start.11 = (bf16[96,4096]{1,0:T(8,128)(2,1)S(1)}, bf16[96,4096]{1,0:T(8,128)(2,1)S(1)}, u32[]{:S(2)}, u32[]{:S(2)}) collective-permute-start(bf16[96,4096]{1,0:T(8,128)(2,1)S(1)} %collective-permute-done.7.refs_0_), channel_id=1, source_target_pairs={{0,2},{2,4},{4,6},{6,7},{7,5},{5,3},{3,1},{1,0},{10,8},{12,10},{14... | collective-permute-start | bytes 2359304 | tf_op jit(solution)/shard_map/ppermute | solution.py:260
  53.6 5.0 %shard_map.96.refs_7_ = f32[512,128]{1,0:T(8,128)S(1)} custom-call(s32[17]{0:T(128)S(1)} %dynamic-slice_bitcast_fusion.table, s32[8]{0:T(128)S(1)} %copy-done.5, bf16[96,4096]{1,0:T(8,128)(2,1)S(1)} %collective-permute-done.8.refs_0_, bf16[96,4096]{1,0:T(8,128)(2,1)S(1)} %collective-permute-done.10.refs_1_, bf16[1536,896]{1,0:T(8,128)(2,1)S(1)} %copy-done.2, ...), custom_call_target="tpu_custom_call" | custom-call | flops 6039797760 | bytes 1572864 | tf_op jit(solution)/shard_map/pallas_call | solution.py:165
  59.4 5.0 %shard_map.97.refs_7_ = f32[512,128]{1,0:T(8,128)S(1)} custom-call(s32[17]{0:T(128)S(1)} %dynamic-slice_bitcast_fusion.table, s32[8]{0:T(128)S(1)} %copy-done.5, bf16[96,4096]{1,0:T(8,128)(2,1)S(1)} %collective-permute-done.7.refs_0_, bf16[96,4096]{1,0:T(8,128)(2,1)S(1)} %collective-permute-done.13.refs_1_, bf16[1536,896]{1,0:T(8,128)(2,1)S(1)} %copy-done.2, ...), custom_call_target="tpu_custom_call" | custom-call | flops 6039797760 | bytes 1572864 | tf_op jit(solution)/shard_map/pallas_call | solution.py:165
  65.9 5.0 %shard_map.98.refs_7_ = f32[512,128]{1,0:T(8,128)S(1)} custom-call(s32[17]{0:T(128)S(1)} %dynamic-slice_bitcast_fusion.table, s32[8]{0:T(128)S(1)} %copy-done.5, bf16[96,4096]{1,0:T(8,128)(2,1)S(1)} %collective-permute-done.12.refs_0_, bf16[96,4096]{1,0:T(8,128)(2,1)S(1)} %collective-permute-done.15.refs_1_, bf16[1536,896]{1,0:T(8,128)(2,1)S(1)} %copy-done.2, ...), custom_call_target="tpu_custom_call" | custom-call | flops 6039797760 | bytes 1572864 | tf_op jit(solution)/shard_map/pallas_call | solution.py:165
  70.9 5.3 %shard_map.99 = (f32[256,128]{1,0:T(8,128)S(1)}, f32[256,128]{1,0:T(8,128)S(1)}) custom-call(s32[17]{0:T(128)S(1)} %dynamic-slice_bitcast_fusion.table, s32[8]{0:T(128)S(1)} %copy-done.5, bf16[96,4096]{1,0:T(8,128)(2,1)S(1)} %collective-permute-done.11.refs_0_, bf16[96,4096]{1,0:T(8,128)(2,1)S(1)} %collective-permute-done.14.refs_1_, ...), custom_call_target="tpu_custom_call" | custom-call | flops 6039797760 | bytes 1572864 | tf_op jit(solution)/shard_map/pallas_call | solution.py:165
  77.7 2.1 %collective-permute-start.17 = (bf16[256,128]{1,0:T(8,128)(2,1)S(1)}, bf16[256,128]{1,0:T(8,128)(2,1)S(1)}, u32[]{:S(2)}, u32[]{:S(2)}) collective-permute-start(bf16[256,128]{1,0:T(8,128)(2,1)S(1)} %get-tuple-element.67), channel_id=1, source_target_pairs={{0,1},{1,0},{2,3},{3,2},{4,5},{5,4},{6,7},{7,6},{8,9},{9,8},{10,11... | collective-permute-start | bytes 196616 | tf_op jit(solution)/shard_map/ppermute | solution.py:286
  82.5 2.2 %collective-permute-done.18 = bf16[256,128]{1,0:T(8,128)(2,1)S(1)} collective-permute-done((bf16[256,128]{1,0:T(8,128)(2,1)S(1)}, bf16[256,128]{1,0:T(8,128)(2,1)S(1)}, u32[]{:S(2)}, u32[]{:S(2)}) %collective-permute-start.18) | collective-permute-done | bytes 65568 | tf_op jit(solution)/shard_map/ppermute | solution.py:286
  84.7 1.9 %collective-permute-done.19 = bf16[256,128]{1,0:T(8,128)(2,1)S(1)} collective-permute-done((bf16[256,128]{1,0:T(8,128)(2,1)S(1)}, bf16[256,128]{1,0:T(8,128)(2,1)S(1)}, u32[]{:S(2)}, u32[]{:S(2)}) %collective-permute-start.19) | collective-permute-done | bytes 65568 | tf_op jit(solution)/shard_map/ppermute | solution.py:286
  86.6 3.4 %collective-permute-start.20 = (bf16[256,128]{1,0:T(8,128)(2,1)S(1)}, bf16[256,128]{1,0:T(8,128)(2,1)S(1)}, u32[]{:S(2)}, u32[]{:S(2)}) collective-permute-start(bf16[256,128]{1,0:T(8,128)(2,1)S(1)} %get-tuple-element.65), channel_id=1, source_target_pairs={{0,4},{1,5},{2,6},{3,7},{4,0},{5,1},{6,2},{7,3},{8,12},{9,13},{10,... | collective-permute-start | bytes 196616 | tf_op jit(solution)/shard_map/ppermute | solution.py:286
  90.0 2.5 %collective-permute-done.20.theirs = bf16[256,128]{1,0:T(8,128)(2,1)S(1)} collective-permute-done((bf16[256,128]{1,0:T(8,128)(2,1)S(1)}, bf16[256,128]{1,0:T(8,128)(2,1)S(1)}, u32[]{:S(2)}, u32[]{:S(2)}) %collective-permute-start.20) | collective-permute-done | bytes 65568 | tf_op jit(solution)/shard_map/ppermute | solution.py:286
  92.5 1.8 %shard_map.100 = f32[4,128]{1,0:T(4,128)} custom-call(s32[17]{0:T(128)S(1)} %dynamic-slice_bitcast_fusion.table, f32[256,128]{1,0:T(8,128)S(1)} %get-tuple-element.66.mine, bf16[256,128]{1,0:T(8,128)(2,1)S(1)} %collective-permute-done.20.theirs, bf16[128,4096]{1,0:T(8,128)(2,1)S(1)} %copy-done.3, bf16[128,4096]{1,0:T(8,128)(2,1)S(1)} %collective-permute-done.4.val_other), custom_call_target="tpu_custom_call" | custom-call | tf_op jit(solution)/shard_map/pallas_call | solution.py:218
  (46 shorter events, 15.3 us)
Async XLA Ops:
  0.0 19.4 %collective-permute-start = (bf16[96,4096]{1,0:T(8,128)(2,1)}, bf16[96,4096]{1,0:T(8,128)(2,1)S(1)}, u32[]{:S(2)}, u32[]{:S(2)}) collective-permute-start(bf16[96,4096]{1,0:T(8,128)(2,1)} %refs_0_.1), channel_id=1, source_target_pairs={{0,2},{2,4},{4,6},{6,7},{7,5},{5,3},{3,1},{1,0},{10,8},{12,10},{14... | collective-permute-start | bytes 2359304 | tf_op jit(solution)/shard_map/ppermute | solution.py:244
  3.0 16.4 %collective-permute-start.1 = (bf16[96,4096]{1,0:T(8,128)(2,1)}, bf16[96,4096]{1,0:T(8,128)(2,1)}, u32[]{:S(2)}, u32[]{:S(2)}) collective-permute-start(bf16[96,4096]{1,0:T(8,128)(2,1)} %refs_0_.1), channel_id=1, source_target_pairs={{0,8},{8,0},{1,9},{9,1},{2,10},{10,2},{3,11},{11,3},{4,12},{12,4},... | collective-permute-start | bytes 2359304 | tf_op jit(solution)/shard_map/ppermute | solution.py:245
  3.0 24.4 %collective-permute-start.4 = (bf16[128,4096]{1,0:T(8,128)(2,1)}, bf16[128,4096]{1,0:T(8,128)(2,1)S(1)}, u32[]{:S(2)}, u32[]{:S(2)}) collective-permute-start(bf16[128,4096]{1,0:T(8,128)(2,1)} %val_own.1), channel_id=1, source_target_pairs={{0,8},{8,0},{1,9},{9,1},{2,10},{10,2},{3,11},{11,3},{4,12},{12,4},... | collective-permute-start | bytes 3145736 | tf_op jit(solution)/shard_map/ppermute | solution.py:245
  4.2 23.2 %collective-permute-start.3 = (bf16[96,4096]{1,0:T(8,128)(2,1)}, bf16[96,4096]{1,0:T(8,128)(2,1)}, u32[]{:S(2)}, u32[]{:S(2)}) collective-permute-start(bf16[96,4096]{1,0:T(8,128)(2,1)} %refs_0_.1), channel_id=1, source_target_pairs={{2,0},{4,2},{6,4},{7,6},{5,7},{3,5},{1,3},{0,1},{8,10},{10,12},{12... | collective-permute-start | bytes 2359304 | tf_op jit(solution)/shard_map/ppermute | solution.py:247
  6.3 3.1 %copy-start = (bf16[4096,896]{1,0:T(8,128)(2,1)S(1)}, bf16[4096,896]{1,0:T(8,128)(2,1)}, u32[]{:S(2)}) copy-start(bf16[4096,896]{1,0:T(8,128)(2,1)} %refs_3_.15) | copy-start | bytes 22020100
  15.9 5.9 %copy-start.6 = (bf16[96,4096]{1,0:T(8,128)(2,1)S(1)}, bf16[96,4096]{1,0:T(8,128)(2,1)}, u32[]{:S(2)}) copy-start(bf16[96,4096]{1,0:T(8,128)(2,1)} %refs_0_.1) | copy-start | bytes 2359300
  19.4 10.3 %collective-permute-start.5 = (bf16[96,4096]{1,0:T(8,128)(2,1)S(1)}, bf16[96,4096]{1,0:T(8,128)(2,1)S(1)}, u32[]{:S(2)}, u32[]{:S(2)}) collective-permute-start(bf16[96,4096]{1,0:T(8,128)(2,1)S(1)} %collective-permute-done.refs_0_), channel_id=1, source_target_pairs={{0,8},{8,0},{1,9},{9,1},{2,10},{10,2},{3,11},{11,3},{4,12},{12,4},... | collective-permute-start | bytes 2359304 | tf_op jit(solution)/shard_map/ppermute | solution.py:261
  19.4 15.4 %collective-permute-start.2 = (bf16[96,4096]{1,0:T(8,128)(2,1)S(1)}, bf16[96,4096]{1,0:T(8,128)(2,1)S(1)}, u32[]{:S(2)}, u32[]{:S(2)}) collective-permute-start(bf16[96,4096]{1,0:T(8,128)(2,1)S(1)} %collective-permute-done.refs_0_), channel_id=1, source_target_pairs={{0,2},{2,4},{4,6},{6,7},{7,5},{5,3},{3,1},{1,0},{10,8},{12,10},{14... | collective-permute-start | bytes 2359304 | tf_op jit(solution)/shard_map/ppermute | solution.py:260
  27.4 7.3 %collective-permute-start.6 = (bf16[96,4096]{1,0:T(8,128)(2,1)}, bf16[96,4096]{1,0:T(8,128)(2,1)S(1)}, u32[]{:S(2)}, u32[]{:S(2)}) collective-permute-start(bf16[96,4096]{1,0:T(8,128)(2,1)} %collective-permute-done.3.refs_0_), channel_id=1, source_target_pairs={{0,8},{8,0},{1,9},{9,1},{2,10},{10,2},{3,11},{11,3},{4,12},{12,4},... | collective-permute-start | bytes 2359304 | tf_op jit(solution)/shard_map/ppermute | solution.py:266
  28.1 14.5 %collective-permute-start.8 = (bf16[96,4096]{1,0:T(8,128)(2,1)}, bf16[96,4096]{1,0:T(8,128)(2,1)S(1)}, u32[]{:S(2)}, u32[]{:S(2)}) collective-permute-start(bf16[96,4096]{1,0:T(8,128)(2,1)} %collective-permute-done.3.refs_0_), channel_id=1, source_target_pairs={{2,0},{4,2},{6,4},{7,6},{5,7},{3,5},{1,3},{0,1},{8,10},{10,12},{12... | collective-permute-start | bytes 2359304 | tf_op jit(solution)/shard_map/ppermute | solution.py:265
  34.8 9.9 %collective-permute-start.9 = (bf16[96,4096]{1,0:T(8,128)(2,1)S(1)}, bf16[96,4096]{1,0:T(8,128)(2,1)S(1)}, u32[]{:S(2)}, u32[]{:S(2)}) collective-permute-start(bf16[96,4096]{1,0:T(8,128)(2,1)S(1)} %collective-permute-done.2.refs_0_), channel_id=1, source_target_pairs={{0,8},{8,0},{1,9},{9,1},{2,10},{10,2},{3,11},{11,3},{4,12},{12,4},... | collective-permute-start | bytes 2359304 | tf_op jit(solution)/shard_map/ppermute | solution.py:261
  34.9 17.0 %collective-permute-start.7 = (bf16[96,4096]{1,0:T(8,128)(2,1)S(1)}, bf16[96,4096]{1,0:T(8,128)(2,1)S(1)}, u32[]{:S(2)}, u32[]{:S(2)}) collective-permute-start(bf16[96,4096]{1,0:T(8,128)(2,1)S(1)} %collective-permute-done.2.refs_0_), channel_id=1, source_target_pairs={{0,2},{2,4},{4,6},{6,7},{7,5},{5,3},{3,1},{1,0},{10,8},{12,10},{14... | collective-permute-start | bytes 2359304 | tf_op jit(solution)/shard_map/ppermute | solution.py:260
  42.7 9.2 %collective-permute-start.10 = (bf16[96,4096]{1,0:T(8,128)(2,1)S(1)}, bf16[96,4096]{1,0:T(8,128)(2,1)S(1)}, u32[]{:S(2)}, u32[]{:S(2)}) collective-permute-start(bf16[96,4096]{1,0:T(8,128)(2,1)S(1)} %collective-permute-done.8.refs_0_), channel_id=1, source_target_pairs={{0,8},{8,0},{1,9},{9,1},{2,10},{10,2},{3,11},{11,3},{4,12},{12,4},... | collective-permute-start | bytes 2359304 | tf_op jit(solution)/shard_map/ppermute | solution.py:266
  42.7 16.6 %collective-permute-start.12 = (bf16[96,4096]{1,0:T(8,128)(2,1)S(1)}, bf16[96,4096]{1,0:T(8,128)(2,1)S(1)}, u32[]{:S(2)}, u32[]{:S(2)}) collective-permute-start(bf16[96,4096]{1,0:T(8,128)(2,1)S(1)} %collective-permute-done.8.refs_0_), channel_id=1, source_target_pairs={{2,0},{4,2},{6,4},{7,6},{5,7},{3,5},{1,3},{0,1},{8,10},{10,12},{12... | collective-permute-start | bytes 2359304 | tf_op jit(solution)/shard_map/ppermute | solution.py:265
  51.9 7.5 %collective-permute-start.13 = (bf16[96,4096]{1,0:T(8,128)(2,1)S(1)}, bf16[96,4096]{1,0:T(8,128)(2,1)S(1)}, u32[]{:S(2)}, u32[]{:S(2)}) collective-permute-start(bf16[96,4096]{1,0:T(8,128)(2,1)S(1)} %collective-permute-done.7.refs_0_), channel_id=1, source_target_pairs={{0,8},{8,0},{1,9},{9,1},{2,10},{10,2},{3,11},{11,3},{4,12},{12,4},... | collective-permute-start | bytes 2359304 | tf_op jit(solution)/shard_map/ppermute | solution.py:261
  51.9 13.9 %collective-permute-start.11 = (bf16[96,4096]{1,0:T(8,128)(2,1)S(1)}, bf16[96,4096]{1,0:T(8,128)(2,1)S(1)}, u32[]{:S(2)}, u32[]{:S(2)}) collective-permute-start(bf16[96,4096]{1,0:T(8,128)(2,1)S(1)} %collective-permute-done.7.refs_0_), channel_id=1, source_target_pairs={{0,2},{2,4},{4,6},{6,7},{7,5},{5,3},{3,1},{1,0},{10,8},{12,10},{14... | collective-permute-start | bytes 2359304 | tf_op jit(solution)/shard_map/ppermute | solution.py:260
  59.3 6.6 %collective-permute-start.15 = (bf16[96,4096]{1,0:T(8,128)(2,1)S(1)}, bf16[96,4096]{1,0:T(8,128)(2,1)S(1)}, u32[]{:S(2)}, u32[]{:S(2)}) collective-permute-start(bf16[96,4096]{1,0:T(8,128)(2,1)S(1)} %collective-permute-done.12.refs_0_), channel_id=1, source_target_pairs={{0,8},{8,0},{1,9},{9,1},{2,10},{10,2},{3,11},{11,3},{4,12},{12,4},... | collective-permute-start | bytes 2359304 | tf_op jit(solution)/shard_map/ppermute | solution.py:266
  65.9 5.0 %collective-permute-start.14 = (bf16[96,4096]{1,0:T(8,128)(2,1)S(1)}, bf16[96,4096]{1,0:T(8,128)(2,1)S(1)}, u32[]{:S(2)}, u32[]{:S(2)}) collective-permute-start(bf16[96,4096]{1,0:T(8,128)(2,1)S(1)} %collective-permute-done.11.refs_0_), channel_id=1, source_target_pairs={{0,8},{8,0},{1,9},{9,1},{2,10},{10,2},{3,11},{11,3},{4,12},{12,4},... | collective-permute-start | bytes 2359304 | tf_op jit(solution)/shard_map/ppermute | solution.py:275
  70.9 21.7 %copy-start.3 = (bf16[128,4096]{1,0:T(8,128)(2,1)S(1)}, bf16[128,4096]{1,0:T(8,128)(2,1)}, u32[]{:S(2)}) copy-start(bf16[128,4096]{1,0:T(8,128)(2,1)} %val_own.1) | copy-start | bytes 3145732
  76.1 1.6 %collective-permute-start.16 = (f32[256,128]{1,0:T(8,128)S(1)}, f32[256,128]{1,0:T(8,128)S(1)}, u32[]{:S(2)}, u32[]{:S(2)}) collective-permute-start(f32[256,128]{1,0:T(8,128)S(1)} %get-tuple-element.63), channel_id=1, source_target_pairs={{0,8},{8,0},{1,9},{9,1},{2,10},{10,2},{3,11},{11,3},{4,12},{12,4},... | collective-permute-start | bytes 393224 | tf_op jit(solution)/shard_map/ppermute | solution.py:277
  77.7 4.7 %collective-permute-start.17 = (bf16[256,128]{1,0:T(8,128)(2,1)S(1)}, bf16[256,128]{1,0:T(8,128)(2,1)S(1)}, u32[]{:S(2)}, u32[]{:S(2)}) collective-permute-start(bf16[256,128]{1,0:T(8,128)(2,1)S(1)} %get-tuple-element.67), channel_id=1, source_target_pairs={{0,1},{1,0},{2,3},{3,2},{4,5},{5,4},{6,7},{7,6},{8,9},{9,8},{10,11... | collective-permute-start | bytes 196616 | tf_op jit(solution)/shard_map/ppermute | solution.py:286
  79.9 4.8 %collective-permute-start.18 = (bf16[256,128]{1,0:T(8,128)(2,1)S(1)}, bf16[256,128]{1,0:T(8,128)(2,1)S(1)}, u32[]{:S(2)}, u32[]{:S(2)}) collective-permute-start(bf16[256,128]{1,0:T(8,128)(2,1)S(1)} %get-tuple-element.67), channel_id=1, source_target_pairs={{0,2},{1,3},{2,0},{3,1},{4,6},{5,7},{6,4},{7,5},{8,10},{9,11},{10,... | collective-permute-start | bytes 196616 | tf_op jit(solution)/shard_map/ppermute | solution.py:286
  81.4 5.2 %collective-permute-start.19 = (bf16[256,128]{1,0:T(8,128)(2,1)S(1)}, bf16[256,128]{1,0:T(8,128)(2,1)S(1)}, u32[]{:S(2)}, u32[]{:S(2)}) collective-permute-start(bf16[256,128]{1,0:T(8,128)(2,1)S(1)} %get-tuple-element.67), channel_id=1, source_target_pairs={{0,3},{1,2},{2,1},{3,0},{4,7},{5,6},{6,5},{7,4},{8,11},{9,10},{10,... | collective-permute-start | bytes 196616 | tf_op jit(solution)/shard_map/ppermute | solution.py:286
  86.6 5.9 %collective-permute-start.20 = (bf16[256,128]{1,0:T(8,128)(2,1)S(1)}, bf16[256,128]{1,0:T(8,128)(2,1)S(1)}, u32[]{:S(2)}, u32[]{:S(2)}) collective-permute-start(bf16[256,128]{1,0:T(8,128)(2,1)S(1)} %get-tuple-element.65), channel_id=1, source_target_pairs={{0,4},{1,5},{2,6},{3,7},{4,0},{5,1},{6,2},{7,3},{8,12},{9,13},{10,... | collective-permute-start | bytes 196616 | tf_op jit(solution)/shard_map/ppermute | solution.py:286
  (4 other events, 6.5 us)

commit v5 on v4

--- a/solution.py
+++ b/solution.py
@@ -47,72 +47,32 @@
     return np.array(table, np.int32)
 
 
-def prepare_kernel(table, lengths, w_gate, w_up, out_grad, proj_in, proj_out, twice, diagonal):
-    twice[...] = jnp.concatenate([proj_in[...], proj_in[...]], axis=1)
-    values = proj_out[...]
-    hidden = values.shape[0]
-    left = lax.broadcasted_iota(jnp.int32, values.shape, 1) < LANES // 2
-    none = jnp.zeros_like(values)
-    diagonal[:hidden, :] = jnp.where(left, values, none)
-    diagonal[hidden:, :] = jnp.where(left, none, values)
-
-
-def prepare(table, lengths, w_gate, w_up, out_grad, proj_in, proj_out):
-    width, hidden = w_gate.shape
-    return pl.pallas_call(
-        prepare_kernel,
-        out_shape=[
-            jax.ShapeDtypeStruct((width, LANES), proj_in.dtype),
-            jax.ShapeDtypeStruct((2 * hidden, LANES), proj_out.dtype),
-        ],
-        in_specs=[SMEM, SMEM] + [VMEM] * 5,
-        out_specs=[VMEM] * 2,
-        compiler_params=pltpu.CompilerParams(vmem_limit_bytes=16 * 2**20),
-    )(table, lengths, w_gate, w_up, out_grad, proj_in, proj_out)
-
-
 def split(value):
     high = value.astype(jnp.bfloat16)
     return high, (value - high.astype(jnp.float32)).astype(jnp.bfloat16)
 
 
-def step_kernel(count, entry, first, last, table, lengths, *refs):
-    blocks = refs[:count]
-    out_grad, w_gate, w_up, twice, diagonal = refs[count : count + 5]
-    at = count + 5
-    if not first:
-        before, at = refs[at], at + 1
-    outs, (pre, both) = refs[at:-2], refs[-2:]
-    rows = blocks[0].shape[0]
-    total_rows = rows * count
-    hidden = out_grad.shape[1]
-    seq_count = lengths.shape[0]
-    starts = [table[entry + i] for i in range(count)]
-
-    for place, w in ((0, w_gate), (hidden, w_up), (2 * hidden, twice)):
-        x = jnp.concatenate([block[...] for block in blocks], axis=0)
-        pre[:, place : place + w.shape[1]] = jnp.dot(
-            x, w[...], preferred_element_type=jnp.float32
-        )
-    for i in range(total_rows // CHUNK):
+def gradients(pre, cotangents, both):
+    hidden = both.shape[1] // 2
+    for i, cotangent in enumerate(cotangents):
         here = slice(i * CHUNK, (i + 1) * CHUNK)
-        block, row = divmod(i * CHUNK, rows)
-        source = pl.ds(pl.multiple_of(starts[block] + row, CHUNK), CHUNK)
         gate = pre[here, :hidden]
         up = pre[here, hidden : 2 * hidden]
-        cotangent = out_grad[source, :].astype(jnp.float32)
         sig = 0.5 * (1.0 + jnp.tanh(0.5 * gate))
-        scaled = cotangent * sig
+        scaled = cotangent().astype(jnp.float32) * sig
         both[here, hidden:] = (scaled * gate).astype(jnp.bfloat16)
         both[here, :hidden] = (scaled * up * (1.0 + gate * (1.0 - sig))).astype(jnp.bfloat16)
+
+
+def sketch_of(starts, rows, lengths, pre, both, diagonal):
     grads = jnp.dot(both[...], diagonal[...], preferred_element_type=jnp.float32)
     grads_high, grads_low = split(grads)
     grads_both = jnp.concatenate([grads_high, grads_low], axis=1)
-
-    acts = pre[:, 2 * hidden :]
+    seq_count = lengths.shape[0]
+    acts = pre[:, both.shape[1] :]
     position = []
-    for i in range(count):
-        position.append(starts[i] + lax.broadcasted_iota(jnp.int32, (rows, LANES), 0))
+    for start in starts:
+        position.append(start + lax.broadcasted_iota(jnp.int32, (rows, LANES), 0))
     position = jnp.concatenate(position, axis=0)
     low = lax.broadcasted_iota(jnp.int32, (1, LANES), 1) < LANES // 2
     ends = []
@@ -136,48 +96,147 @@
     rest = lax.dot_general(
         jnp.concatenate(lows, axis=1), grads_high, over_rows, preferred_element_type=jnp.float32
     )
-    part = main[:, :LANES] + main[:, LANES:] + rest
-    if not first:
-        part += before[...]
+    return main[:, :LANES] + main[:, LANES:] + rest
+
+
+def first_kernel(
+    table, lengths, own, other, gate_hbm, up_hbm, out_grad_hbm, proj_out_hbm, proj_in,
+    total, w, out_grad, diagonal, x, pre, both, sems, w_sems,
+):
+    rows = own.shape[0]
+    width, hidden = gate_hbm.shape
+    depth = width // w_sems.shape[0]
+    parts = []
+    for k in range(w_sems.shape[0]):
+        here = pl.ds(k * depth, depth)
+        parts.append(
+            (
+                pltpu.make_async_copy(
+                    gate_hbm.at[here], w.at[here, pl.ds(0, hidden)], w_sems.at[k, 0]
+                ),
+                pltpu.make_async_copy(
+                    up_hbm.at[here], w.at[here, pl.ds(hidden, hidden)], w_sems.at[k, 1]
+                ),
+            )
+        )
+    blocks = [
+        pltpu.make_async_copy(own, x.at[pl.ds(0, rows)], sems.at[0]),
+        pltpu.make_async_copy(other, x.at[pl.ds(rows, rows)], sems.at[1]),
+    ]
+    upper = pltpu.make_async_copy(proj_out_hbm, diagonal.at[pl.ds(0, hidden)], sems.at[2])
+    whole = pltpu.make_async_copy(out_grad_hbm, out_grad, sems.at[3])
+    for copy in blocks + [upper]:
+        copy.start()
+    for pair in parts:
+        for copy in pair:
+            copy.start()
+    whole.start()
+
+    w[:, 2 * hidden :] = jnp.concatenate([proj_in[...], proj_in[...]], axis=1)
+    upper.wait()
+    values = diagonal[:hidden, :]
+    left = lax.broadcasted_iota(jnp.int32, values.shape, 1) < LANES // 2
+    none = jnp.zeros_like(values)
+    diagonal[hidden:, :] = jnp.where(left, none, values)
+    diagonal[:hidden, :] = jnp.where(left, values, none)
+    for copy in blocks:
+        copy.wait()
+    for k, pair in enumerate(parts):
+        for copy in pair:
+            copy.wait()
+        here = slice(k * depth, (k + 1) * depth)
+        product = jnp.dot(x[:, here], w[here, :], preferred_element_type=jnp.float32)
+        pre[...] = product if k == 0 else pre[...] + product
+    whole.wait()
+    starts = [table[0], table[1]]
+    gradients(pre, cotangent_chunks(out_grad, starts, rows), both)
+    total[...] = sketch_of(starts, rows, lengths, pre, both, diagonal)
+
+
+def cotangent_chunks(out_grad, starts, rows):
+    chunks = []
+    for start in starts:
+        for row in range(0, rows, CHUNK):
+            here = pl.ds(pl.multiple_of(start + row, CHUNK), CHUNK)
+            chunks.append(lambda here=here: out_grad[here, :])
+    return chunks
+
+
+def step_kernel(entry, last, table, lengths, one, two, w, out_grad, diagonal, before, *refs):
+    outs, (pre, both) = refs[:-2], refs[-2:]
+    rows = one.shape[0]
+    starts = [table[entry], table[entry + 1]]
+    x = jnp.concatenate([one[...], two[...]], axis=0)
+    pre[...] = jnp.dot(x, w[...], preferred_element_type=jnp.float32)
+    gradients(pre, cotangent_chunks(out_grad, starts, rows), both)
+    total = before[...] + sketch_of(starts, rows, lengths, pre, both, diagonal)
     if not last:
-        outs[0][...] = part
+        outs[0][...] = total
         return
     kept, sent = outs
     core = table[table.shape[0] - 1]
-    half = part.shape[0] // 2
-    upper, lower = part[:half, :], part[half:, :]
+    half = total.shape[0] // 2
+    upper, lower = total[:half, :], total[half:, :]
     kept[...] = jnp.where(core == 0, upper, lower)
     sent[...] = jnp.where(core == 0, lower, upper)
 
 
-def step_sketch(blocks, entry, total, table, lengths, weights, last=False):
-    count = len(blocks)
+def costs(rows, width, columns):
+    return pl.CostEstimate(
+        flops=4 * rows * width * columns, bytes_accessed=2 * rows * width, transcendentals=0
+    )
+
+
+def first_step(table, lengths, own, other, w_gate, w_up, out_grad, proj_in, proj_out):
+    rows, width = own.shape
+    hidden = w_gate.shape[1]
+    columns = 2 * hidden + LANES
+    chunks = 4 if width % (4 * LANES) == 0 else 1
+    own, w_gate, w_up, out_grad, proj_out = [
+        pltpu.with_memory_space_constraint(a, pltpu.HBM)
+        for a in (own, w_gate, w_up, out_grad, proj_out)
+    ]
+    return pl.pallas_call(
+        first_kernel,
+        out_shape=[
+            jax.ShapeDtypeStruct((lengths.shape[0] * LANES // 2, LANES), jnp.float32),
+            pltpu.VMEM((width, columns), jnp.bfloat16),
+            pltpu.VMEM(out_grad.shape, jnp.bfloat16),
+            pltpu.VMEM((2 * hidden, LANES), jnp.bfloat16),
+        ],
+        in_specs=[SMEM, SMEM] + [ANY] * 6 + [VMEM],
+        out_specs=[VMEM] * 4,
+        scratch_shapes=[
+            pltpu.VMEM((2 * rows, width), jnp.bfloat16),
+            pltpu.VMEM((2 * rows, columns), jnp.float32),
+            pltpu.VMEM((2 * rows, 2 * hidden), jnp.bfloat16),
+            pltpu.SemaphoreType.DMA((4,)),
+            pltpu.SemaphoreType.DMA((chunks, 2)),
+        ],
+        compiler_params=pltpu.CompilerParams(vmem_limit_bytes=16 * 2**20),
+        cost_estimate=costs(2 * rows, width, columns),
+    )(table, lengths, own, other, w_gate, w_up, out_grad, proj_out, proj_in)
+
+
+def next_step(blocks, entry, total, table, lengths, weights, last=False):
     rows, width = blocks[0].shape
-    total_rows = count * rows
-    hidden = weights[0].shape[1]
-    columns = 2 * hidden + LANES
-    first = total is None
-    out_rows = lengths.shape[0] * LANES // 2
-    operands = [*blocks, *weights] + ([] if first else [total])
-    out_shape = [jax.ShapeDtypeStruct((out_rows, LANES), jnp.float32)]
+    w, _, diagonal = weights
+    shape = total.shape
+    out_shape = [jax.ShapeDtypeStruct(shape, jnp.float32)]
     if last:
-        out_shape = [jax.ShapeDtypeStruct((out_rows // 2, LANES), jnp.float32)] * 2
+        out_shape = [jax.ShapeDtypeStruct((shape[0] // 2, LANES), jnp.float32)] * 2
     outs = pl.pallas_call(
-        functools.partial(step_kernel, count, entry, first, last),
+        functools.partial(step_kernel, entry, last),
         out_shape=out_shape,
-        in_specs=[SMEM, SMEM] + [VMEM] * len(operands),
+        in_specs=[SMEM, SMEM] + [VMEM] * 6,
         out_specs=[VMEM] * len(out_shape),
         scratch_shapes=[
-            pltpu.VMEM((total_rows, columns), jnp.float32),
-            pltpu.VMEM((total_rows, 2 * hidden), jnp.bfloat16),
+            pltpu.VMEM((2 * rows, w.shape[1]), jnp.float32),
+            pltpu.VMEM((2 * rows, diagonal.shape[0]), jnp.bfloat16),
         ],
         compiler_params=pltpu.CompilerParams(vmem_limit_bytes=16 * 2**20),
-        cost_estimate=pl.CostEstimate(
-            flops=4 * total_rows * width * columns,
-            bytes_accessed=2 * total_rows * width,
-            transcendentals=0,
-        ),
-    )(table, lengths, *operands)
+        cost_estimate=costs(2 * rows, width, w.shape[1]),
+    )(table, lengths, *blocks, *weights, total)
     return outs if last else outs[0]
 
 
@@ -245,33 +304,22 @@
     other, other_val = swap(tokens_in), swap(val_sketch)
     later_tokens, table = after((tokens_in, table))
     two_way = send_two(later_tokens)
-    twice, diagonal = prepare(table, lengths, w_gate, w_up, out_grad, proj_in, proj_out)
-    add = functools.partial(
-        step_sketch,
-        table=table,
-        lengths=lengths,
-        weights=[out_grad, w_gate, w_up, twice, diagonal],
-    )
-
-    waiting = (tokens_in, other)
-    total, entry = None, 0
+    total, *weights = first_step(
+        table, lengths, tokens_in, other, w_gate, w_up, out_grad, proj_in, proj_out
+    )
+    add = functools.partial(next_step, table=table, lengths=lengths, weights=weights)
+
+    entry = 2
     for k in range(1, n // 2):
-        one_way, other_half = after((one_way, waiting[1]))
-        next_one = send_one(one_way)
-        swapped_one = swap(one_way)
-        total = add([waiting[0], other_half], entry, total)
-        entry += 2
+        one_way, total = after((one_way, total))
+        next_one, swapped = send_one(one_way), swap(one_way)
+        total = add([one_way, swapped], entry, total)
         two_way, total, other_val = after((two_way, total, other_val))
         next_two = send_two(two_way) if k + 1 < n // 2 else None
-        swapped_two = swap(two_way)
-        _, swapped_one = after((two_way, swapped_one))
-        total = add([one_way, swapped_one], entry, total)
-        entry += 2
-        next_one, total = after((next_one, total))
-        waiting = (two_way, swapped_two)
+        total = add([two_way, swap(two_way)], entry + 2, total)
+        entry += 4
         one_way, two_way = next_one, next_two
-    total = add(waiting, entry, total)
-    entry += 2
+    one_way, total = after((one_way, total))
     kept, sent = add([one_way, swap(one_way)], entry, total, last=True)
 
     mine, theirs = kept, swap(sent)

time: 94.7 us -> 114 us (1.20)
  waiting for transfers between devices: 16.2 us -> 47.7 us
  local copies, waits for them, and re-layouts: 11.8 us -> 2.95 us
  starting transfers between devices: 21.9 us -> 17.8 us
  Pallas kernels: 44.2 us -> 45.4 us
    ppermute x9, waiting for transfers between devices: 3.67 us -> 19.7 us  [the longest x6 17.6 us: fast(): next_one, swapped = (send_one(one_way), swap(one_way))]
    ppermute x2, waiting for transfers between devices: 1.31 us -> 10.2 us  [fast(): next_two = send_two(two_way) if k + 1 < n // 2 else None]
    unnamed x15 -> x7, local copies, waits for them, and re-layouts: 11.1 us -> 2.26 us
    ppermute x1, waiting for transfers between devices: 0.01 us -> 5.58 us  [fast(): two_way = send_two(later_tokens)]
    ppermute x1, waiting for transfers between devices: 2.56 us -> 0.01 us  [fast(): one_way = send_one(tokens_in)]
    ppermute x1, waiting for transfers between devices: 0.01 us -> 2.28 us  [fast(): kept, sent = add([one_way, swap(one_way)], entry, total, last=True)]
    ppermute x4, starting transfers between devices: 7.08 us -> 5.28 us  [fast(): lax.ppermute(sent, 'mp', [(i, i ^ flip) for i in range(n)])]
    ppermute x9, starting transfers between devices: 6.54 us -> 4.99 us  [the longest x6 4.98 us: fast(): next_one, swapped = (send_one(one_way), swap(one_way))]
  transfers between devices with their start and end apart: 21 -> 21, of which waited for: 10 -> 18; matrix products, arithmetic and copies ran while one was open for 2% -> 2% of each run, Pallas kernels for 39% -> 34%
where the time goes in v5:
time: 114 us
  waiting for transfers between devices  47.7 us (42%)
  Pallas kernels  45.4 us (40%)
  starting transfers between devices  17.8 us (16%)
  local copies, waits for them, and re-layouts  2.95 us (3%)
    pallas_call x7, Pallas kernels, next_step(): pl.pallas_call(functools.partial(step_kernel, entry, last), out_shape=out...  32.3 us
    ppermute x6, waiting for transfers between devices, fast(): next_one, swapped = (send_one(one_way), swap(one_way))  17.6 us
    pallas_call x1, Pallas kernels, first_step(): pl.pallas_call(first_kernel, out_shape=[jax.ShapeDtypeStruct((lengths.sha...  11.2 us
    ppermute x2, waiting for transfers between devices, fast(): next_two = send_two(two_way) if k + 1 < n // 2 else None  10.2 us
    ppermute x4, waiting for transfers between devices, fast(): lax.ppermute(sent, 'mp', [(i, i ^ flip) for i in range(n)])  8.69 us
    ppermute x1, waiting for transfers between devices, fast(): two_way = send_two(later_tokens)  5.58 us
    ppermute x4, starting transfers between devices, fast(): lax.ppermute(sent, 'mp', [(i, i ^ flip) for i in range(n)])  5.28 us
    ppermute x6, starting transfers between devices, fast(): next_one, swapped = (send_one(one_way), swap(one_way))  4.98 us
  transfers between devices with their start and end apart: 21, of which 18 were waited for; matrix products, arithmetic and copies ran while one was open for 2% of the time, Pallas kernels for 34%

profile of v5, /device:TPU:0, one launch (start us, length us, event | category | flops | bytes accessed | tf_op | source)
XLA Modules:
  0.0 114.0 jit_solution(13190946914534833631)
XLA Ops:
  0.5 2.6 %collective-permute-start = (bf16[96,4096]{1,0:T(8,128)(2,1)}, bf16[96,4096]{1,0:T(8,128)(2,1)S(1)}, u32[]{:S(2)}, u32[]{:S(2)}) collective-permute-start(bf16[96,4096]{1,0:T(8,128)(2,1)} %own.1), channel_id=1, source_target_pairs={{0,2},{2,4},{4,6},{6,7},{7,5},{5,3},{3,1},{1,0},{10,8},{12,10},{14... | collective-permute-start | bytes 2359304 | tf_op jit(solution)/shard_map/ppermute | solution.py:303
  6.0 11.2 %shard_map.91 = (f32[512,128]{1,0:T(8,128)S(1)}, bf16[4096,1920]{1,0:T(8,128)(2,1)S(1)}, bf16[1536,896]{1,0:T(8,128)(2,1)S(1)}, bf16[1792,128]{1,0:T(8,128)(2,1)S(1)}) custom-call(s32[17]{0:T(128)S(1)} %dynamic-slice_bitcast_fusion.table, s32[8]{0:T(128)S(1)} %copy-done.1, bf16[96,4096]{1,0:T(8,128)(2,1)} %own.1, ...), custom_call_target="tpu_custom_call" | custom-call | flops 6039797760 | bytes 1572864 | tf_op jit(solution)/shard_map/pallas_call | solution.py:199
  19.6 4.6 %shard_map.92.before = f32[512,128]{1,0:T(8,128)S(1)} custom-call(s32[17]{0:T(128)S(1)} %dynamic-slice_bitcast_fusion.table, s32[8]{0:T(128)S(1)} %copy-done.1, bf16[96,4096]{1,0:T(8,128)(2,1)S(1)} %collective-permute-done.one, bf16[96,4096]{1,0:T(8,128)(2,1)S(1)} %collective-permute-done.4.two, bf16[4096,1920]{1,0:T(8,128)(2,1)S(1)} %get-tuple-element.34.w, ...), custom_call_target="tpu_custom_call" | custom-call | flops 6039797760 | bytes 1572864 | tf_op jit(solution)/shard_map/pallas_call | solution.py:228
  24.2 5.6 %collective-permute-done.3.one = bf16[96,4096]{1,0:T(8,128)(2,1)S(1)} collective-permute-done((bf16[96,4096]{1,0:T(8,128)(2,1)S(1)}, bf16[96,4096]{1,0:T(8,128)(2,1)S(1)}, u32[]{:S(2)}, u32[]{:S(2)}) %collective-permute-start.3) | collective-permute-done | bytes 786464 | tf_op jit(solution)/shard_map/ppermute | solution.py:306
  29.8 1.6 %collective-permute-start.2 = (bf16[96,4096]{1,0:T(8,128)(2,1)S(1)}, bf16[96,4096]{1,0:T(8,128)(2,1)S(1)}, u32[]{:S(2)}, u32[]{:S(2)}) collective-permute-start(bf16[96,4096]{1,0:T(8,128)(2,1)S(1)} %collective-permute-done.one), channel_id=1, source_target_pairs={{0,2},{2,4},{4,6},{6,7},{7,5},{5,3},{3,1},{1,0},{10,8},{12,10},{14... | collective-permute-start | bytes 2359304 | tf_op jit(solution)/shard_map/ppermute | solution.py:315
  32.1 4.6 %shard_map.93.before = f32[512,128]{1,0:T(8,128)S(1)} custom-call(s32[17]{0:T(128)S(1)} %dynamic-slice_bitcast_fusion.table, s32[8]{0:T(128)S(1)} %copy-done.1, bf16[96,4096]{1,0:T(8,128)(2,1)S(1)} %collective-permute-done.3.one, bf16[96,4096]{1,0:T(8,128)(2,1)S(1)} %collective-permute-done.6.two, bf16[4096,1920]{1,0:T(8,128)(2,1)S(1)} %get-tuple-element.34.w, ...), custom_call_target="tpu_custom_call" | custom-call | flops 6039797760 | bytes 1572864 | tf_op jit(solution)/shard_map/pallas_call | solution.py:228
  36.7 5.1 %collective-permute-done.2.one = bf16[96,4096]{1,0:T(8,128)(2,1)S(1)} collective-permute-done((bf16[96,4096]{1,0:T(8,128)(2,1)S(1)}, bf16[96,4096]{1,0:T(8,128)(2,1)S(1)}, u32[]{:S(2)}, u32[]{:S(2)}) %collective-permute-start.2) | collective-permute-done | bytes 786464 | tf_op jit(solution)/shard_map/ppermute | solution.py:315
  44.1 4.6 %shard_map.94.before = f32[512,128]{1,0:T(8,128)S(1)} custom-call(s32[17]{0:T(128)S(1)} %dynamic-slice_bitcast_fusion.table, s32[8]{0:T(128)S(1)} %copy-done.1, bf16[96,4096]{1,0:T(8,128)(2,1)S(1)} %collective-permute-done.2.one, bf16[96,4096]{1,0:T(8,128)(2,1)S(1)} %collective-permute-done.9.two, bf16[4096,1920]{1,0:T(8,128)(2,1)S(1)} %get-tuple-element.34.w, ...), custom_call_target="tpu_custom_call" | custom-call | flops 6039797760 | bytes 1572864 | tf_op jit(solution)/shard_map/pallas_call | solution.py:228
  48.7 5.1 %collective-permute-done.8.one = bf16[96,4096]{1,0:T(8,128)(2,1)S(1)} collective-permute-done((bf16[96,4096]{1,0:T(8,128)(2,1)S(1)}, bf16[96,4096]{1,0:T(8,128)(2,1)S(1)}, u32[]{:S(2)}, u32[]{:S(2)}) %collective-permute-start.8) | collective-permute-done | bytes 786464 | tf_op jit(solution)/shard_map/ppermute | solution.py:318
  53.8 1.6 %collective-permute-start.7 = (bf16[96,4096]{1,0:T(8,128)(2,1)S(1)}, bf16[96,4096]{1,0:T(8,128)(2,1)S(1)}, u32[]{:S(2)}, u32[]{:S(2)}) collective-permute-start(bf16[96,4096]{1,0:T(8,128)(2,1)S(1)} %collective-permute-done.2.one), channel_id=1, source_target_pairs={{0,2},{2,4},{4,6},{6,7},{7,5},{5,3},{3,1},{1,0},{10,8},{12,10},{14... | collective-permute-start | bytes 2359304 | tf_op jit(solution)/shard_map/ppermute | solution.py:315
  56.1 4.6 %shard_map.95.before = f32[512,128]{1,0:T(8,128)S(1)} custom-call(s32[17]{0:T(128)S(1)} %dynamic-slice_bitcast_fusion.table, s32[8]{0:T(128)S(1)} %copy-done.1, bf16[96,4096]{1,0:T(8,128)(2,1)S(1)} %collective-permute-done.8.one, bf16[96,4096]{1,0:T(8,128)(2,1)S(1)} %collective-permute-done.10.two, bf16[4096,1920]{1,0:T(8,128)(2,1)S(1)} %get-tuple-element.34.w, ...), custom_call_target="tpu_custom_call" | custom-call | flops 6039797760 | bytes 1572864 | tf_op jit(solution)/shard_map/pallas_call | solution.py:228
  60.7 5.1 %collective-permute-done.7.one = bf16[96,4096]{1,0:T(8,128)(2,1)S(1)} collective-permute-done((bf16[96,4096]{1,0:T(8,128)(2,1)S(1)}, bf16[96,4096]{1,0:T(8,128)(2,1)S(1)}, u32[]{:S(2)}, u32[]{:S(2)}) %collective-permute-start.7) | collective-permute-done | bytes 786464 | tf_op jit(solution)/shard_map/ppermute | solution.py:315
  68.1 4.6 %shard_map.96.before = f32[512,128]{1,0:T(8,128)S(1)} custom-call(s32[17]{0:T(128)S(1)} %dynamic-slice_bitcast_fusion.table, s32[8]{0:T(128)S(1)} %copy-done.1, bf16[96,4096]{1,0:T(8,128)(2,1)S(1)} %collective-permute-done.7.one, bf16[96,4096]{1,0:T(8,128)(2,1)S(1)} %collective-permute-done.13.two, bf16[4096,1920]{1,0:T(8,128)(2,1)S(1)} %get-tuple-element.34.w, ...), custom_call_target="tpu_custom_call" | custom-call | flops 6039797760 | bytes 1572864 | tf_op jit(solution)/shard_map/pallas_call | solution.py:228
  72.7 5.1 %collective-permute-done.12.one = bf16[96,4096]{1,0:T(8,128)(2,1)S(1)} collective-permute-done((bf16[96,4096]{1,0:T(8,128)(2,1)S(1)}, bf16[96,4096]{1,0:T(8,128)(2,1)S(1)}, u32[]{:S(2)}, u32[]{:S(2)}) %collective-permute-start.12) | collective-permute-done | bytes 786464 | tf_op jit(solution)/shard_map/ppermute | solution.py:318
  77.8 1.6 %collective-permute-start.11 = (bf16[96,4096]{1,0:T(8,128)(2,1)S(1)}, bf16[96,4096]{1,0:T(8,128)(2,1)S(1)}, u32[]{:S(2)}, u32[]{:S(2)}) collective-permute-start(bf16[96,4096]{1,0:T(8,128)(2,1)S(1)} %collective-permute-done.7.one), channel_id=1, source_target_pairs={{0,2},{2,4},{4,6},{6,7},{7,5},{5,3},{3,1},{1,0},{10,8},{12,10},{14... | collective-permute-start | bytes 2359304 | tf_op jit(solution)/shard_map/ppermute | solution.py:315
  80.1 4.6 %shard_map.97.before = f32[512,128]{1,0:T(8,128)S(1)} custom-call(s32[17]{0:T(128)S(1)} %dynamic-slice_bitcast_fusion.table, s32[8]{0:T(128)S(1)} %copy-done.1, bf16[96,4096]{1,0:T(8,128)(2,1)S(1)} %collective-permute-done.12.one, bf16[96,4096]{1,0:T(8,128)(2,1)S(1)} %collective-permute-done.14.two, bf16[4096,1920]{1,0:T(8,128)(2,1)S(1)} %get-tuple-element.34.w, ...), custom_call_target="tpu_custom_call" | custom-call | flops 6039797760 | bytes 1572864 | tf_op jit(solution)/shard_map/pallas_call | solution.py:228
  84.7 5.1 %collective-permute-done.11.one = bf16[96,4096]{1,0:T(8,128)(2,1)S(1)} collective-permute-done((bf16[96,4096]{1,0:T(8,128)(2,1)S(1)}, bf16[96,4096]{1,0:T(8,128)(2,1)S(1)}, u32[]{:S(2)}, u32[]{:S(2)}) %collective-permute-start.11) | collective-permute-done | bytes 786464 | tf_op jit(solution)/shard_map/ppermute | solution.py:315
  89.8 2.3 %collective-permute-done.15.two = bf16[96,4096]{1,0:T(8,128)(2,1)S(1)} collective-permute-done((bf16[96,4096]{1,0:T(8,128)(2,1)S(1)}, bf16[96,4096]{1,0:T(8,128)(2,1)S(1)}, u32[]{:S(2)}, u32[]{:S(2)}) %collective-permute-start.15) | collective-permute-done | bytes 786464 | tf_op jit(solution)/shard_map/ppermute | solution.py:323
  92.1 4.6 %shard_map.98 = (f32[256,128]{1,0:T(8,128)S(1)}, f32[256,128]{1,0:T(8,128)S(1)}) custom-call(s32[17]{0:T(128)S(1)} %dynamic-slice_bitcast_fusion.table, s32[8]{0:T(128)S(1)} %copy-done.1, bf16[96,4096]{1,0:T(8,128)(2,1)S(1)} %collective-permute-done.11.one, bf16[96,4096]{1,0:T(8,128)(2,1)S(1)} %collective-permute-done.15.two, ...), custom_call_target="tpu_custom_call" | custom-call | flops 6039797760 | bytes 1572864 | tf_op jit(solution)/shard_map/pallas_call | solution.py:228
  102.5 1.7 %collective-permute-done.18 = bf16[256,128]{1,0:T(8,128)(2,1)S(1)} collective-permute-done((bf16[256,128]{1,0:T(8,128)(2,1)S(1)}, bf16[256,128]{1,0:T(8,128)(2,1)S(1)}, u32[]{:S(2)}, u32[]{:S(2)}) %collective-permute-start.18) | collective-permute-done | bytes 65568 | tf_op jit(solution)/shard_map/ppermute | solution.py:334
  104.1 2.1 %collective-permute-done.19 = bf16[256,128]{1,0:T(8,128)(2,1)S(1)} collective-permute-done((bf16[256,128]{1,0:T(8,128)(2,1)S(1)}, bf16[256,128]{1,0:T(8,128)(2,1)S(1)}, u32[]{:S(2)}, u32[]{:S(2)}) %collective-permute-start.19) | collective-permute-done | bytes 65568 | tf_op jit(solution)/shard_map/ppermute | solution.py:334
  106.3 1.7 %collective-permute-start.20 = (bf16[256,128]{1,0:T(8,128)(2,1)S(1)}, bf16[256,128]{1,0:T(8,128)(2,1)S(1)}, u32[]{:S(2)}, u32[]{:S(2)}) collective-permute-start(bf16[256,128]{1,0:T(8,128)(2,1)S(1)} %get-tuple-element.55), channel_id=1, source_target_pairs={{0,4},{1,5},{2,6},{3,7},{4,0},{5,1},{6,2},{7,3},{8,12},{9,13},{10,... | collective-permute-start | bytes 196616 | tf_op jit(solution)/shard_map/ppermute | solution.py:334
  108.0 4.1 %collective-permute-done.20.theirs = bf16[256,128]{1,0:T(8,128)(2,1)S(1)} collective-permute-done((bf16[256,128]{1,0:T(8,128)(2,1)S(1)}, bf16[256,128]{1,0:T(8,128)(2,1)S(1)}, u32[]{:S(2)}, u32[]{:S(2)}) %collective-permute-start.20) | collective-permute-done | bytes 65568 | tf_op jit(solution)/shard_map/ppermute | solution.py:334
  112.1 1.8 %shard_map.99 = f32[4,128]{1,0:T(4,128)} custom-call(s32[17]{0:T(128)S(1)} %dynamic-slice_bitcast_fusion.table, f32[256,128]{1,0:T(8,128)S(1)} %get-tuple-element.56.mine, bf16[256,128]{1,0:T(8,128)(2,1)S(1)} %collective-permute-done.20.theirs, bf16[128,4096]{1,0:T(8,128)(2,1)S(1)} %copy-done, bf16[128,4096]{1,0:T(8,128)(2,1)S(1)} %collective-permute-done.5.val_other), custom_call_target="tpu_custom_call" | custom-call | tf_op jit(solution)/shard_map/pallas_call | solution.py:277
  (37 shorter events, 18.2 us)
Async XLA Ops:
  0.0 5.3 %collective-permute-start.1 = (bf16[96,4096]{1,0:T(8,128)(2,1)}, bf16[96,4096]{1,0:T(8,128)(2,1)S(1)}, u32[]{:S(2)}, u32[]{:S(2)}) collective-permute-start(bf16[96,4096]{1,0:T(8,128)(2,1)} %own.1), channel_id=1, source_target_pairs={{0,8},{8,0},{1,9},{9,1},{2,10},{10,2},{3,11},{11,3},{4,12},{12,4},... | collective-permute-start | bytes 2359304 | tf_op jit(solution)/shard_map/ppermute | solution.py:304
  0.5 16.8 %collective-permute-start = (bf16[96,4096]{1,0:T(8,128)(2,1)}, bf16[96,4096]{1,0:T(8,128)(2,1)S(1)}, u32[]{:S(2)}, u32[]{:S(2)}) collective-permute-start(bf16[96,4096]{1,0:T(8,128)(2,1)} %own.1), channel_id=1, source_target_pairs={{0,2},{2,4},{4,6},{6,7},{7,5},{5,3},{3,1},{1,0},{10,8},{12,10},{14... | collective-permute-start | bytes 2359304 | tf_op jit(solution)/shard_map/ppermute | solution.py:303
  5.2 12.2 %copy-start = (bf16[128,4096]{1,0:T(8,128)(2,1)S(1)}, bf16[128,4096]{1,0:T(8,128)(2,1)}, u32[]{:S(2)}) copy-start(bf16[128,4096]{1,0:T(8,128)(2,1)} %val_own.1) | copy-start | bytes 3145732
  5.3 0.7 copy-start.1
  6.0 11.8 %copy-start.2 = (bf16[96,4096]{1,0:T(8,128)(2,1)S(1)}, bf16[96,4096]{1,0:T(8,128)(2,1)}, u32[]{:S(2)}) copy-start(bf16[96,4096]{1,0:T(8,128)(2,1)} %own.1) | copy-start | bytes 2359300
  17.2 2.4 %collective-permute-start.4 = (bf16[96,4096]{1,0:T(8,128)(2,1)S(1)}, bf16[96,4096]{1,0:T(8,128)(2,1)S(1)}, u32[]{:S(2)}, u32[]{:S(2)}) collective-permute-start(bf16[96,4096]{1,0:T(8,128)(2,1)S(1)} %collective-permute-done.one), channel_id=1, source_target_pairs={{0,8},{8,0},{1,9},{9,1},{2,10},{10,2},{3,11},{11,3},{4,12},{12,4},... | collective-permute-start | bytes 2359304 | tf_op jit(solution)/shard_map/ppermute | solution.py:315
  17.5 12.3 %collective-permute-start.5 = (bf16[128,4096]{1,0:T(8,128)(2,1)S(1)}, bf16[128,4096]{1,0:T(8,128)(2,1)S(1)}, u32[]{:S(2)}, u32[]{:S(2)}) collective-permute-start(bf16[128,4096]{1,0:T(8,128)(2,1)S(1)} %copy-done), channel_id=1, source_target_pairs={{0,8},{8,0},{1,9},{9,1},{2,10},{10,2},{3,11},{11,3},{4,12},{12,4},... | collective-permute-start | bytes 3145736 | tf_op jit(solution)/shard_map/ppermute | solution.py:304
  17.8 12.0 %collective-permute-start.3 = (bf16[96,4096]{1,0:T(8,128)(2,1)S(1)}, bf16[96,4096]{1,0:T(8,128)(2,1)S(1)}, u32[]{:S(2)}, u32[]{:S(2)}) collective-permute-start(bf16[96,4096]{1,0:T(8,128)(2,1)S(1)} %copy-done.2), channel_id=1, source_target_pairs={{2,0},{4,2},{6,4},{7,6},{5,7},{3,5},{1,3},{0,1},{8,10},{10,12},{12... | collective-permute-start | bytes 2359304 | tf_op jit(solution)/shard_map/ppermute | solution.py:306
  29.8 2.3 %collective-permute-start.6 = (bf16[96,4096]{1,0:T(8,128)(2,1)S(1)}, bf16[96,4096]{1,0:T(8,128)(2,1)S(1)}, u32[]{:S(2)}, u32[]{:S(2)}) collective-permute-start(bf16[96,4096]{1,0:T(8,128)(2,1)S(1)} %collective-permute-done.3.one), channel_id=1, source_target_pairs={{0,8},{8,0},{1,9},{9,1},{2,10},{10,2},{3,11},{11,3},{4,12},{12,4},... | collective-permute-start | bytes 2359304 | tf_op jit(solution)/shard_map/ppermute | solution.py:319
  29.8 12.0 %collective-permute-start.2 = (bf16[96,4096]{1,0:T(8,128)(2,1)S(1)}, bf16[96,4096]{1,0:T(8,128)(2,1)S(1)}, u32[]{:S(2)}, u32[]{:S(2)}) collective-permute-start(bf16[96,4096]{1,0:T(8,128)(2,1)S(1)} %collective-permute-done.one), channel_id=1, source_target_pairs={{0,2},{2,4},{4,6},{6,7},{7,5},{5,3},{3,1},{1,0},{10,8},{12,10},{14... | collective-permute-start | bytes 2359304 | tf_op jit(solution)/shard_map/ppermute | solution.py:315
  41.8 2.3 %collective-permute-start.9 = (bf16[96,4096]{1,0:T(8,128)(2,1)S(1)}, bf16[96,4096]{1,0:T(8,128)(2,1)S(1)}, u32[]{:S(2)}, u32[]{:S(2)}) collective-permute-start(bf16[96,4096]{1,0:T(8,128)(2,1)S(1)} %collective-permute-done.2.one), channel_id=1, source_target_pairs={{0,8},{8,0},{1,9},{9,1},{2,10},{10,2},{3,11},{11,3},{4,12},{12,4},... | collective-permute-start | bytes 2359304 | tf_op jit(solution)/shard_map/ppermute | solution.py:315
  41.8 12.0 %collective-permute-start.8 = (bf16[96,4096]{1,0:T(8,128)(2,1)S(1)}, bf16[96,4096]{1,0:T(8,128)(2,1)S(1)}, u32[]{:S(2)}, u32[]{:S(2)}) collective-permute-start(bf16[96,4096]{1,0:T(8,128)(2,1)S(1)} %collective-permute-done.3.one), channel_id=1, source_target_pairs={{2,0},{4,2},{6,4},{7,6},{5,7},{3,5},{1,3},{0,1},{8,10},{10,12},{12... | collective-permute-start | bytes 2359304 | tf_op jit(solution)/shard_map/ppermute | solution.py:318
  53.8 2.3 %collective-permute-start.10 = (bf16[96,4096]{1,0:T(8,128)(2,1)S(1)}, bf16[96,4096]{1,0:T(8,128)(2,1)S(1)}, u32[]{:S(2)}, u32[]{:S(2)}) collective-permute-start(bf16[96,4096]{1,0:T(8,128)(2,1)S(1)} %collective-permute-done.8.one), channel_id=1, source_target_pairs={{0,8},{8,0},{1,9},{9,1},{2,10},{10,2},{3,11},{11,3},{4,12},{12,4},... | collective-permute-start | bytes 2359304 | tf_op jit(solution)/shard_map/ppermute | solution.py:319
  53.8 12.0 %collective-permute-start.7 = (bf16[96,4096]{1,0:T(8,128)(2,1)S(1)}, bf16[96,4096]{1,0:T(8,128)(2,1)S(1)}, u32[]{:S(2)}, u32[]{:S(2)}) collective-permute-start(bf16[96,4096]{1,0:T(8,128)(2,1)S(1)} %collective-permute-done.2.one), channel_id=1, source_target_pairs={{0,2},{2,4},{4,6},{6,7},{7,5},{5,3},{3,1},{1,0},{10,8},{12,10},{14... | collective-permute-start | bytes 2359304 | tf_op jit(solution)/shard_map/ppermute | solution.py:315
  65.8 2.3 %collective-permute-start.13 = (bf16[96,4096]{1,0:T(8,128)(2,1)S(1)}, bf16[96,4096]{1,0:T(8,128)(2,1)S(1)}, u32[]{:S(2)}, u32[]{:S(2)}) collective-permute-start(bf16[96,4096]{1,0:T(8,128)(2,1)S(1)} %collective-permute-done.7.one), channel_id=1, source_target_pairs={{0,8},{8,0},{1,9},{9,1},{2,10},{10,2},{3,11},{11,3},{4,12},{12,4},... | collective-permute-start | bytes 2359304 | tf_op jit(solution)/shard_map/ppermute | solution.py:315
  65.8 12.0 %collective-permute-start.12 = (bf16[96,4096]{1,0:T(8,128)(2,1)S(1)}, bf16[96,4096]{1,0:T(8,128)(2,1)S(1)}, u32[]{:S(2)}, u32[]{:S(2)}) collective-permute-start(bf16[96,4096]{1,0:T(8,128)(2,1)S(1)} %collective-permute-done.8.one), channel_id=1, source_target_pairs={{2,0},{4,2},{6,4},{7,6},{5,7},{3,5},{1,3},{0,1},{8,10},{10,12},{12... | collective-permute-start | bytes 2359304 | tf_op jit(solution)/shard_map/ppermute | solution.py:318
  77.8 2.3 %collective-permute-start.14 = (bf16[96,4096]{1,0:T(8,128)(2,1)S(1)}, bf16[96,4096]{1,0:T(8,128)(2,1)S(1)}, u32[]{:S(2)}, u32[]{:S(2)}) collective-permute-start(bf16[96,4096]{1,0:T(8,128)(2,1)S(1)} %collective-permute-done.12.one), channel_id=1, source_target_pairs={{0,8},{8,0},{1,9},{9,1},{2,10},{10,2},{3,11},{11,3},{4,12},{12,4},... | collective-permute-start | bytes 2359304 | tf_op jit(solution)/shard_map/ppermute | solution.py:319
  77.8 12.0 %collective-permute-start.11 = (bf16[96,4096]{1,0:T(8,128)(2,1)S(1)}, bf16[96,4096]{1,0:T(8,128)(2,1)S(1)}, u32[]{:S(2)}, u32[]{:S(2)}) collective-permute-start(bf16[96,4096]{1,0:T(8,128)(2,1)S(1)} %collective-permute-done.7.one), channel_id=1, source_target_pairs={{0,2},{2,4},{4,6},{6,7},{7,5},{5,3},{3,1},{1,0},{10,8},{12,10},{14... | collective-permute-start | bytes 2359304 | tf_op jit(solution)/shard_map/ppermute | solution.py:315
  89.8 2.3 %collective-permute-start.15 = (bf16[96,4096]{1,0:T(8,128)(2,1)S(1)}, bf16[96,4096]{1,0:T(8,128)(2,1)S(1)}, u32[]{:S(2)}, u32[]{:S(2)}) collective-permute-start(bf16[96,4096]{1,0:T(8,128)(2,1)S(1)} %collective-permute-done.11.one), channel_id=1, source_target_pairs={{0,8},{8,0},{1,9},{9,1},{2,10},{10,2},{3,11},{11,3},{4,12},{12,4},... | collective-permute-start | bytes 2359304 | tf_op jit(solution)/shard_map/ppermute | solution.py:323
  96.7 1.4 %collective-permute-start.16 = (f32[256,128]{1,0:T(8,128)S(1)}, f32[256,128]{1,0:T(8,128)S(1)}, u32[]{:S(2)}, u32[]{:S(2)}) collective-permute-start(f32[256,128]{1,0:T(8,128)S(1)} %get-tuple-element.53), channel_id=1, source_target_pairs={{0,8},{8,0},{1,9},{9,1},{2,10},{10,2},{3,11},{11,3},{4,12},{12,4},... | collective-permute-start | bytes 393224 | tf_op jit(solution)/shard_map/ppermute | solution.py:325
  98.1 4.3 %collective-permute-start.17 = (bf16[256,128]{1,0:T(8,128)(2,1)S(1)}, bf16[256,128]{1,0:T(8,128)(2,1)S(1)}, u32[]{:S(2)}, u32[]{:S(2)}) collective-permute-start(bf16[256,128]{1,0:T(8,128)(2,1)S(1)} %get-tuple-element.57), channel_id=1, source_target_pairs={{0,1},{1,0},{2,3},{3,2},{4,5},{5,4},{6,7},{7,6},{8,9},{9,8},{10,11... | collective-permute-start | bytes 196616 | tf_op jit(solution)/shard_map/ppermute | solution.py:334
  99.5 4.6 %collective-permute-start.18 = (bf16[256,128]{1,0:T(8,128)(2,1)S(1)}, bf16[256,128]{1,0:T(8,128)(2,1)S(1)}, u32[]{:S(2)}, u32[]{:S(2)}) collective-permute-start(bf16[256,128]{1,0:T(8,128)(2,1)S(1)} %get-tuple-element.57), channel_id=1, source_target_pairs={{0,2},{1,3},{2,0},{3,1},{4,6},{5,7},{6,4},{7,5},{8,10},{9,11},{10,... | collective-permute-start | bytes 196616 | tf_op jit(solution)/shard_map/ppermute | solution.py:334
  101.1 5.2 %collective-permute-start.19 = (bf16[256,128]{1,0:T(8,128)(2,1)S(1)}, bf16[256,128]{1,0:T(8,128)(2,1)S(1)}, u32[]{:S(2)}, u32[]{:S(2)}) collective-permute-start(bf16[256,128]{1,0:T(8,128)(2,1)S(1)} %get-tuple-element.57), channel_id=1, source_target_pairs={{0,3},{1,2},{2,1},{3,0},{4,7},{5,6},{6,5},{7,4},{8,11},{9,10},{10,... | collective-permute-start | bytes 196616 | tf_op jit(solution)/shard_map/ppermute | solution.py:334
  106.3 5.8 %collective-permute-start.20 = (bf16[256,128]{1,0:T(8,128)(2,1)S(1)}, bf16[256,128]{1,0:T(8,128)(2,1)S(1)}, u32[]{:S(2)}, u32[]{:S(2)}) collective-permute-start(bf16[256,128]{1,0:T(8,128)(2,1)S(1)} %get-tuple-element.55), channel_id=1, source_target_pairs={{0,4},{1,5},{2,6},{3,7},{4,0},{5,1},{6,2},{7,3},{8,12},{9,13},{10,... | collective-permute-start | bytes 196616 | tf_op jit(solution)/shard_map/ppermute | solution.py:334

commit v6 on v5

--- a/solution.py
+++ b/solution.py
@@ -240,9 +240,9 @@
     return outs if last else outs[0]
 
 
-def score_kernel(table, mine, theirs, val_own, val_other, scores, sketch):
+def score_kernel(table, given, val_own, val_other, scores, sketch):
     core = table[table.shape[0] - 1]
-    sketch[...] = mine[...] + theirs[...].astype(jnp.float32)
+    sketch[...] = given[...].astype(jnp.float32)
     own, rank = scores.shape[0], sketch.shape[0] // scores.shape[0]
     half = rank // 2
     left = lax.broadcasted_iota(jnp.int32, (own, LANES), 1) < LANES // 2
@@ -273,15 +273,15 @@
     )
 
 
-def score(table, mine, theirs, val_own, val_other, own):
+def score(table, sketch, val_own, val_other, own):
     return pl.pallas_call(
         score_kernel,
         out_shape=jax.ShapeDtypeStruct((own, val_own.shape[0]), jnp.float32),
-        in_specs=[SMEM, VMEM, VMEM, VMEM, VMEM],
+        in_specs=[SMEM, VMEM, VMEM, VMEM],
         out_specs=VMEM,
-        scratch_shapes=[pltpu.VMEM(mine.shape, jnp.float32)],
+        scratch_shapes=[pltpu.VMEM(sketch.shape, jnp.float32)],
         compiler_params=pltpu.CompilerParams(vmem_limit_bytes=16 * 2**20),
-    )(table, mine, theirs, val_own, val_other)
+    )(table, sketch, val_own, val_other)
 
 
 def fast(order, tokens_in, out_grad, w_gate, w_up, proj_in, proj_out, lengths, val_sketch):
@@ -309,37 +309,36 @@
     )
     add = functools.partial(next_step, table=table, lengths=lengths, weights=weights)
 
-    entry = 2
+    waiting, entry = None, 2
     for k in range(1, n // 2):
         one_way, total = after((one_way, total))
-        next_one, swapped = send_one(one_way), swap(one_way)
-        total = add([one_way, swapped], entry, total)
+        next_one = send_one(one_way)
+        swapped_one = swap(one_way)
+        if waiting is not None:
+            total = add(waiting, entry, total)
+            entry += 2
         two_way, total, other_val = after((two_way, total, other_val))
         next_two = send_two(two_way) if k + 1 < n // 2 else None
-        total = add([two_way, swap(two_way)], entry + 2, total)
-        entry += 4
+        swapped_two = swap(two_way)
+        _, swapped_one = after((two_way, swapped_one))
+        total = add([one_way, swapped_one], entry, total)
+        entry += 2
+        waiting = (two_way, swapped_two)
         one_way, two_way = next_one, next_two
     one_way, total = after((one_way, total))
-    kept, sent = add([one_way, swap(one_way)], entry, total, last=True)
-
-    mine, theirs = kept, swap(sent)
-    bit = 1
-    while bit < n:
-        mine = mine + theirs
-        sent = mine.astype(jnp.bfloat16)
-        exchange = [bit]
-        if bit == 1 and n >= 8:
-            exchange = [1, 2, 3]
-        got = [
-            lax.ppermute(sent, "mp", [(i, i ^ flip) for i in range(n)]) for flip in exchange
-        ]
-        for part in got[:-1]:
-            mine = mine + part.astype(jnp.float32)
-        theirs = got[-1]
-        bit = exchange[-1] + 1 if len(exchange) > 1 else 2 * bit
-        if bit < n:
-            theirs = theirs.astype(jnp.float32)
-    return score(table, mine, theirs, val_sketch, other_val, seq_count // 2)
+    swapped_one = swap(one_way)
+    if waiting is not None:
+        total = add(waiting, entry, total)
+        entry += 2
+    kept, sent = add([one_way, swapped_one], entry, total, last=True)
+
+    part = kept + swap(sent)
+    size = part.shape[0] // n
+    part = lax.all_to_all(part.reshape(n, size, LANES), "mp", 0, 0)
+    part = jnp.sum(part, axis=0).astype(jnp.bfloat16)
+    part = jnp.broadcast_to(part[None], (n, size, LANES))
+    sketch = lax.all_to_all(part, "mp", 0, 0).reshape(n * size, LANES)
+    return score(table, sketch, val_sketch, other_val, seq_count // 2)
 
 
 def grad_rows(rows, cotangent, w_gate, w_up, proj_out):
@@ -401,6 +400,7 @@
         and width % LANES == 0
         and 2 * proj_in.shape[1] == LANES
         and lengths.shape[0] % 4 == 0
+        and lengths.shape[0] * LANES // 4 % (8 * n) == 0
         and val_sketch.shape[1] == proj_in.shape[1] * LANES // 2
     )
     work = fast if fits else plain

time: 114 us -> 106 us (0.930)
  waiting for transfers between devices: 47.7 us -> 20.6 us
  blocking collectives: 0 us -> 24.5 us
  starting transfers between devices: 17.8 us -> 11.7 us
    all_to_all x0 -> x2, blocking collectives: none -> 24.5 us  [the longest x1 15.1 us: fast(): part = lax.all_to_all(part.reshape(n, size, LANES), 'mp', 0, 0)]
    ppermute x15 -> x11, waiting for transfers between devices: 31.9 us -> 15 us  [the longest x3 14 us: fast(): next_one = send_one(one_way)]
    ppermute x2, waiting for transfers between devices: 10.2 us -> 2.21 us  [fast(): next_two = send_two(two_way) if k + 1 < n // 2 else None]
    ppermute x1, waiting for transfers between devices: 5.58 us -> 0.01 us  [fast(): two_way = send_two(later_tokens)]
    ppermute x1, waiting for transfers between devices: 0.01 us -> 3.42 us  [fast(): one_way = send_one(tokens_in)]
    ppermute x15 -> x11, starting transfers between devices: 10.5 us -> 7.99 us  [the longest x3 7.27 us: fast(): next_one = send_one(one_way)]
    ppermute x2, starting transfers between devices: 2.64 us -> 0.44 us  [fast(): next_two = send_two(two_way) if k + 1 < n // 2 else None]
    ppermute x1, starting transfers between devices: 1.32 us -> 0.01 us  [fast(): two_way = send_two(later_tokens)]
  transfers between devices with their start and end apart: 21 -> 17, of which waited for: 18 -> 6; matrix products, arithmetic and copies ran while one was open for 2% -> 2% of each run, Pallas kernels for 34% -> 38%
where the time goes in v6:
time: 106 us
  Pallas kernels  46.2 us (44%)
  blocking collectives  24.5 us (23%)
  waiting for transfers between devices  20.6 us (19%)
  starting transfers between devices  11.7 us (11%)
  local copies, waits for them, and re-layouts  2.88 us (3%)
    pallas_call x7, Pallas kernels, next_step(): pl.pallas_call(functools.partial(step_kernel, entry, last), out_shape=out...  33 us
    all_to_all x1, blocking collectives, fast(): part = lax.all_to_all(part.reshape(n, size, LANES), 'mp', 0, 0)  15.1 us
    ppermute x3, waiting for transfers between devices, fast(): next_one = send_one(one_way)  14 us
    pallas_call x1, Pallas kernels, first_step(): pl.pallas_call(first_kernel, out_shape=[jax.ShapeDtypeStruct((lengths.sha...  11.5 us
    all_to_all x1, blocking collectives, fast(): sketch = lax.all_to_all(part, 'mp', 0, 0).reshape(n * size, LANES)  9.42 us
    ppermute x3, starting transfers between devices, fast(): next_one = send_one(one_way)  7.27 us
    ppermute x1, waiting for transfers between devices, fast(): one_way = send_one(tokens_in)  3.42 us
    ppermute x1, starting transfers between devices, fast(): one_way = send_one(tokens_in)  2.57 us
  transfers between devices with their start and end apart: 17, of which 6 were waited for; matrix products, arithmetic and copies ran while one was open for 2% of the time, Pallas kernels for 38%

profile of v6, /device:TPU:0, one launch (start us, length us, event | category | flops | bytes accessed | tf_op | source)
XLA Modules:
  0.0 106.1 jit_solution(1219495147912245770)
XLA Ops:
  0.5 2.6 %collective-permute-start = (bf16[96,4096]{1,0:T(8,128)(2,1)}, bf16[96,4096]{1,0:T(8,128)(2,1)S(1)}, u32[]{:S(2)}, u32[]{:S(2)}) collective-permute-start(bf16[96,4096]{1,0:T(8,128)(2,1)} %own.1), channel_id=1, source_target_pairs={{0,2},{2,4},{4,6},{6,7},{7,5},{5,3},{3,1},{1,0},{10,8},{12,10},{14... | collective-permute-start | bytes 2359304 | tf_op jit(solution)/shard_map/ppermute | solution.py:303
  3.0 0.7 dynamic-slice_bitcast_fusion.table
  4.0 1.5 %copy.10.proj_in = bf16[4096,64]{1,0:T(8,128)(2,1)S(1)} copy(bf16[4096,64]{0,1:T(8,128)(2,1)} %param.13) | data formatting | bytes 1048576 | tf_op args[4]
  5.5 0.6 copy-done.1
  6.1 11.5 %shard_map.91 = (f32[512,128]{1,0:T(8,128)S(1)}, bf16[4096,1920]{1,0:T(8,128)(2,1)S(1)}, bf16[1536,896]{1,0:T(8,128)(2,1)S(1)}, bf16[1792,128]{1,0:T(8,128)(2,1)S(1)}) custom-call(s32[17]{0:T(128)S(1)} %dynamic-slice_bitcast_fusion.table, s32[8]{0:T(128)S(1)} %copy-done.1, bf16[96,4096]{1,0:T(8,128)(2,1)} %own.1, ...), custom_call_target="tpu_custom_call" | custom-call | flops 6039797760 | bytes 1572864 | tf_op jit(solution)/shard_map/pallas_call | solution.py:199
  17.6 3.4 %collective-permute-done.one = bf16[96,4096]{1,0:T(8,128)(2,1)S(1)} collective-permute-done((bf16[96,4096]{1,0:T(8,128)(2,1)}, bf16[96,4096]{1,0:T(8,128)(2,1)S(1)}, u32[]{:S(2)}, u32[]{:S(2)}) %collective-permute-start) | collective-permute-done | bytes 786464 | tf_op jit(solution)/shard_map/ppermute | solution.py:303
  21.0 2.4 %collective-permute-start.2 = (bf16[96,4096]{1,0:T(8,128)(2,1)S(1)}, bf16[96,4096]{1,0:T(8,128)(2,1)S(1)}, u32[]{:S(2)}, u32[]{:S(2)}) collective-permute-start(bf16[96,4096]{1,0:T(8,128)(2,1)S(1)} %collective-permute-done.one), channel_id=1, source_target_pairs={{0,2},{2,4},{4,6},{6,7},{7,5},{5,3},{3,1},{1,0},{10,8},{12,10},{14... | collective-permute-start | bytes 2359304 | tf_op jit(solution)/shard_map/ppermute | solution.py:315
  23.8 4.6 %shard_map.92.before = f32[512,128]{1,0:T(8,128)S(1)} custom-call(s32[17]{0:T(128)S(1)} %dynamic-slice_bitcast_fusion.table, s32[8]{0:T(128)S(1)} %copy-done.1, bf16[96,4096]{1,0:T(8,128)(2,1)S(1)} %collective-permute-done.one, bf16[96,4096]{1,0:T(8,128)(2,1)S(1)} %collective-permute-done.5.two, bf16[4096,1920]{1,0:T(8,128)(2,1)S(1)} %get-tuple-element.40.w, ...), custom_call_target="tpu_custom_call" | custom-call | flops 6039797760 | bytes 1572864 | tf_op jit(solution)/shard_map/pallas_call | solution.py:228
  28.5 11.6 %collective-permute-done.2.one = bf16[96,4096]{1,0:T(8,128)(2,1)S(1)} collective-permute-done((bf16[96,4096]{1,0:T(8,128)(2,1)S(1)}, bf16[96,4096]{1,0:T(8,128)(2,1)S(1)}, u32[]{:S(2)}, u32[]{:S(2)}) %collective-permute-start.2) | collective-permute-done | bytes 786464 | tf_op jit(solution)/shard_map/ppermute | solution.py:315
  40.1 2.5 %collective-permute-start.6 = (bf16[96,4096]{1,0:T(8,128)(2,1)S(1)}, bf16[96,4096]{1,0:T(8,128)(2,1)S(1)}, u32[]{:S(2)}, u32[]{:S(2)}) collective-permute-start(bf16[96,4096]{1,0:T(8,128)(2,1)S(1)} %collective-permute-done.2.one), channel_id=1, source_target_pairs={{0,2},{2,4},{4,6},{6,7},{7,5},{5,3},{3,1},{1,0},{10,8},{12,10},{14... | collective-permute-start | bytes 2359304 | tf_op jit(solution)/shard_map/ppermute | solution.py:315
  42.6 5.2 %shard_map.93.before = f32[512,128]{1,0:T(8,128)S(1)} custom-call(s32[17]{0:T(128)S(1)} %dynamic-slice_bitcast_fusion.table, s32[8]{0:T(128)S(1)} %copy-done.1, bf16[96,4096]{1,0:T(8,128)(2,1)} %collective-permute-done.3.one, bf16[96,4096]{1,0:T(8,128)(2,1)S(1)} %collective-permute-done.8.two, bf16[4096,1920]{1,0:T(8,128)(2,1)S(1)} %get-tuple-element.40.w, ...), custom_call_target="tpu_custom_call" | custom-call | flops 6039797760 | bytes 1572864 | tf_op jit(solution)/shard_map/pallas_call | solution.py:228
  48.0 4.6 %shard_map.94.before = f32[512,128]{1,0:T(8,128)S(1)} custom-call(s32[17]{0:T(128)S(1)} %dynamic-slice_bitcast_fusion.table, s32[8]{0:T(128)S(1)} %copy-done.1, bf16[96,4096]{1,0:T(8,128)(2,1)S(1)} %collective-permute-done.2.one, bf16[96,4096]{1,0:T(8,128)(2,1)S(1)} %collective-permute-done.9.two, bf16[4096,1920]{1,0:T(8,128)(2,1)S(1)} %get-tuple-element.40.w, ...), custom_call_target="tpu_custom_call" | custom-call | flops 6039797760 | bytes 1572864 | tf_op jit(solution)/shard_map/pallas_call | solution.py:228
  52.6 1.6 %collective-permute-done.6.one = bf16[96,4096]{1,0:T(8,128)(2,1)S(1)} collective-permute-done((bf16[96,4096]{1,0:T(8,128)(2,1)S(1)}, bf16[96,4096]{1,0:T(8,128)(2,1)S(1)}, u32[]{:S(2)}, u32[]{:S(2)}) %collective-permute-start.6) | collective-permute-done | bytes 786464 | tf_op jit(solution)/shard_map/ppermute | solution.py:315
  54.2 2.4 %collective-permute-start.10 = (bf16[96,4096]{1,0:T(8,128)(2,1)S(1)}, bf16[96,4096]{1,0:T(8,128)(2,1)S(1)}, u32[]{:S(2)}, u32[]{:S(2)}) collective-permute-start(bf16[96,4096]{1,0:T(8,128)(2,1)S(1)} %collective-permute-done.6.one), channel_id=1, source_target_pairs={{0,2},{2,4},{4,6},{6,7},{7,5},{5,3},{3,1},{1,0},{10,8},{12,10},{14... | collective-permute-start | bytes 2359304 | tf_op jit(solution)/shard_map/ppermute | solution.py:315
  56.6 4.6 %shard_map.95.before = f32[512,128]{1,0:T(8,128)S(1)} custom-call(s32[17]{0:T(128)S(1)} %dynamic-slice_bitcast_fusion.table, s32[8]{0:T(128)S(1)} %copy-done.1, bf16[96,4096]{1,0:T(8,128)(2,1)S(1)} %collective-permute-done.7.one, bf16[96,4096]{1,0:T(8,128)(2,1)S(1)} %collective-permute-done.12.two, bf16[4096,1920]{1,0:T(8,128)(2,1)S(1)} %get-tuple-element.40.w, ...), custom_call_target="tpu_custom_call" | custom-call | flops 6039797760 | bytes 1572864 | tf_op jit(solution)/shard_map/pallas_call | solution.py:228
  61.3 2.2 %collective-permute-done.11.one = bf16[96,4096]{1,0:T(8,128)(2,1)S(1)} collective-permute-done((bf16[96,4096]{1,0:T(8,128)(2,1)S(1)}, bf16[96,4096]{1,0:T(8,128)(2,1)S(1)}, u32[]{:S(2)}, u32[]{:S(2)}) %collective-permute-start.11) | collective-permute-done | bytes 786464 | tf_op jit(solution)/shard_map/ppermute | solution.py:321
  63.5 4.6 %shard_map.96.before = f32[512,128]{1,0:T(8,128)S(1)} custom-call(s32[17]{0:T(128)S(1)} %dynamic-slice_bitcast_fusion.table, s32[8]{0:T(128)S(1)} %copy-done.1, bf16[96,4096]{1,0:T(8,128)(2,1)S(1)} %collective-permute-done.6.one, bf16[96,4096]{1,0:T(8,128)(2,1)S(1)} %collective-permute-done.13.two, bf16[4096,1920]{1,0:T(8,128)(2,1)S(1)} %get-tuple-element.40.w, ...), custom_call_target="tpu_custom_call" | custom-call | flops 6039797760 | bytes 1572864 | tf_op jit(solution)/shard_map/pallas_call | solution.py:228
  68.1 0.8 collective-permute-done.10.one
  69.0 4.6 %shard_map.97.before = f32[512,128]{1,0:T(8,128)S(1)} custom-call(s32[17]{0:T(128)S(1)} %dynamic-slice_bitcast_fusion.table, s32[8]{0:T(128)S(1)} %copy-done.1, bf16[96,4096]{1,0:T(8,128)(2,1)S(1)} %collective-permute-done.11.one, bf16[96,4096]{1,0:T(8,128)(2,1)S(1)} %collective-permute-done.15.two, bf16[4096,1920]{1,0:T(8,128)(2,1)S(1)} %get-tuple-element.40.w, ...), custom_call_target="tpu_custom_call" | custom-call | flops 6039797760 | bytes 1572864 | tf_op jit(solution)/shard_map/pallas_call | solution.py:228
  73.7 4.6 %shard_map.98 = (f32[256,128]{1,0:T(8,128)S(1)}, f32[256,128]{1,0:T(8,128)S(1)}) custom-call(s32[17]{0:T(128)S(1)} %dynamic-slice_bitcast_fusion.table, s32[8]{0:T(128)S(1)} %copy-done.1, bf16[96,4096]{1,0:T(8,128)(2,1)S(1)} %collective-permute-done.10.one, bf16[96,4096]{1,0:T(8,128)(2,1)S(1)} %collective-permute-done.14.two, ...), custom_call_target="tpu_custom_call" | custom-call | flops 6039797760 | bytes 1572864 | tf_op jit(solution)/shard_map/pallas_call | solution.py:228
  78.8 1.0 collective-permute-done.16
  79.8 15.1 %all_to_all.10 = f32[8,32,128]{2,1,0:T(8,128)S(1)} all-to-all(f32[8,32,128]{2,1,0:T(8,128)S(1)} %bitcast.5), channel_id=1, replica_groups=mesh['groups'=2,'seq'=2,'mp'=8] {'mp'}, dimensions={0} | all-to-all | bytes 262144 | tf_op jit(solution)/shard_map/all_to_all | solution.py:337
  94.9 9.4 %all_to_all.11 = bf16[8,32,128]{2,1,0:T(8,128)(2,1)S(1)} all-to-all(bf16[8,32,128]{2,1,0:T(8,128)(2,1)S(1)} %broadcast_in_dim.2), channel_id=1, replica_groups=mesh['groups'=2,'seq'=2,'mp'=8] {'mp'}, dimensions={0} | all-to-all | bytes 131072 | tf_op jit(solution)/shard_map/all_to_all | solution.py:340
  104.3 1.8 %shard_map.99 = f32[4,128]{1,0:T(4,128)} custom-call(s32[17]{0:T(128)S(1)} %dynamic-slice_bitcast_fusion.table, bf16[256,128]{1,0:T(8,128)(2,1)S(1)} %bitcast.4, bf16[128,4096]{1,0:T(8,128)(2,1)S(1)} %copy-done, bf16[128,4096]{1,0:T(8,128)(2,1)S(1)} %collective-permute-done.4.val_other), custom_call_target="tpu_custom_call" | custom-call | tf_op jit(solution)/shard_map/pallas_call | solution.py:277
  (30 shorter events, 1.9 us)
Async XLA Ops:
  0.0 5.5 %collective-permute-start.1 = (bf16[96,4096]{1,0:T(8,128)(2,1)}, bf16[96,4096]{1,0:T(8,128)(2,1)}, u32[]{:S(2)}, u32[]{:S(2)}) collective-permute-start(bf16[96,4096]{1,0:T(8,128)(2,1)} %own.1), channel_id=1, source_target_pairs={{0,8},{8,0},{1,9},{9,1},{2,10},{10,2},{3,11},{11,3},{4,12},{12,4},... | collective-permute-start | bytes 2359304 | tf_op jit(solution)/shard_map/ppermute | solution.py:304
  0.5 20.6 %collective-permute-start = (bf16[96,4096]{1,0:T(8,128)(2,1)}, bf16[96,4096]{1,0:T(8,128)(2,1)S(1)}, u32[]{:S(2)}, u32[]{:S(2)}) collective-permute-start(bf16[96,4096]{1,0:T(8,128)(2,1)} %own.1), channel_id=1, source_target_pairs={{0,2},{2,4},{4,6},{6,7},{7,5},{5,3},{3,1},{1,0},{10,8},{12,10},{14... | collective-permute-start | bytes 2359304 | tf_op jit(solution)/shard_map/ppermute | solution.py:303
  3.7 19.7 %collective-permute-start.3 = (bf16[96,4096]{1,0:T(8,128)(2,1)}, bf16[96,4096]{1,0:T(8,128)(2,1)}, u32[]{:S(2)}, u32[]{:S(2)}) collective-permute-start(bf16[96,4096]{1,0:T(8,128)(2,1)} %own.1), channel_id=1, source_target_pairs={{2,0},{4,2},{6,4},{7,6},{5,7},{3,5},{1,3},{0,1},{8,10},{10,12},{12... | collective-permute-start | bytes 2359304 | tf_op jit(solution)/shard_map/ppermute | solution.py:306
  3.7 19.7 %collective-permute-start.4 = (bf16[128,4096]{1,0:T(8,128)(2,1)}, bf16[128,4096]{1,0:T(8,128)(2,1)S(1)}, u32[]{:S(2)}, u32[]{:S(2)}) collective-permute-start(bf16[128,4096]{1,0:T(8,128)(2,1)} %val_own.1), channel_id=1, source_target_pairs={{0,8},{8,0},{1,9},{9,1},{2,10},{10,2},{3,11},{11,3},{4,12},{12,4},... | collective-permute-start | bytes 3145736 | tf_op jit(solution)/shard_map/ppermute | solution.py:304
  5.5 0.7 copy-start.1
  21.0 2.8 %collective-permute-start.5 = (bf16[96,4096]{1,0:T(8,128)(2,1)S(1)}, bf16[96,4096]{1,0:T(8,128)(2,1)S(1)}, u32[]{:S(2)}, u32[]{:S(2)}) collective-permute-start(bf16[96,4096]{1,0:T(8,128)(2,1)S(1)} %collective-permute-done.one), channel_id=1, source_target_pairs={{0,8},{8,0},{1,9},{9,1},{2,10},{10,2},{3,11},{11,3},{4,12},{12,4},... | collective-permute-start | bytes 2359304 | tf_op jit(solution)/shard_map/ppermute | solution.py:316
  21.0 19.0 %collective-permute-start.2 = (bf16[96,4096]{1,0:T(8,128)(2,1)S(1)}, bf16[96,4096]{1,0:T(8,128)(2,1)S(1)}, u32[]{:S(2)}, u32[]{:S(2)}) collective-permute-start(bf16[96,4096]{1,0:T(8,128)(2,1)S(1)} %collective-permute-done.one), channel_id=1, source_target_pairs={{0,2},{2,4},{4,6},{6,7},{7,5},{5,3},{3,1},{1,0},{10,8},{12,10},{14... | collective-permute-start | bytes 2359304 | tf_op jit(solution)/shard_map/ppermute | solution.py:315
  23.4 19.1 %collective-permute-start.8 = (bf16[96,4096]{1,0:T(8,128)(2,1)}, bf16[96,4096]{1,0:T(8,128)(2,1)S(1)}, u32[]{:S(2)}, u32[]{:S(2)}) collective-permute-start(bf16[96,4096]{1,0:T(8,128)(2,1)} %collective-permute-done.3.one), channel_id=1, source_target_pairs={{0,8},{8,0},{1,9},{9,1},{2,10},{10,2},{3,11},{11,3},{4,12},{12,4},... | collective-permute-start | bytes 2359304 | tf_op jit(solution)/shard_map/ppermute | solution.py:322
  23.4 24.4 %collective-permute-start.7 = (bf16[96,4096]{1,0:T(8,128)(2,1)}, bf16[96,4096]{1,0:T(8,128)(2,1)S(1)}, u32[]{:S(2)}, u32[]{:S(2)}) collective-permute-start(bf16[96,4096]{1,0:T(8,128)(2,1)} %collective-permute-done.3.one), channel_id=1, source_target_pairs={{2,0},{4,2},{6,4},{7,6},{5,7},{3,5},{1,3},{0,1},{8,10},{10,12},{12... | collective-permute-start | bytes 2359304 | tf_op jit(solution)/shard_map/ppermute | solution.py:321
  40.1 7.9 %collective-permute-start.9 = (bf16[96,4096]{1,0:T(8,128)(2,1)S(1)}, bf16[96,4096]{1,0:T(8,128)(2,1)S(1)}, u32[]{:S(2)}, u32[]{:S(2)}) collective-permute-start(bf16[96,4096]{1,0:T(8,128)(2,1)S(1)} %collective-permute-done.2.one), channel_id=1, source_target_pairs={{0,8},{8,0},{1,9},{9,1},{2,10},{10,2},{3,11},{11,3},{4,12},{12,4},... | collective-permute-start | bytes 2359304 | tf_op jit(solution)/shard_map/ppermute | solution.py:316
  40.1 14.1 %collective-permute-start.6 = (bf16[96,4096]{1,0:T(8,128)(2,1)S(1)}, bf16[96,4096]{1,0:T(8,128)(2,1)S(1)}, u32[]{:S(2)}, u32[]{:S(2)}) collective-permute-start(bf16[96,4096]{1,0:T(8,128)(2,1)S(1)} %collective-permute-done.2.one), channel_id=1, source_target_pairs={{0,2},{2,4},{4,6},{6,7},{7,5},{5,3},{3,1},{1,0},{10,8},{12,10},{14... | collective-permute-start | bytes 2359304 | tf_op jit(solution)/shard_map/ppermute | solution.py:315
  47.8 8.8 %collective-permute-start.12 = (bf16[96,4096]{1,0:T(8,128)(2,1)S(1)}, bf16[96,4096]{1,0:T(8,128)(2,1)S(1)}, u32[]{:S(2)}, u32[]{:S(2)}) collective-permute-start(bf16[96,4096]{1,0:T(8,128)(2,1)S(1)} %collective-permute-done.7.one), channel_id=1, source_target_pairs={{0,8},{8,0},{1,9},{9,1},{2,10},{10,2},{3,11},{11,3},{4,12},{12,4},... | collective-permute-start | bytes 2359304 | tf_op jit(solution)/shard_map/ppermute | solution.py:322
  47.9 15.6 %collective-permute-start.11 = (bf16[96,4096]{1,0:T(8,128)(2,1)S(1)}, bf16[96,4096]{1,0:T(8,128)(2,1)S(1)}, u32[]{:S(2)}, u32[]{:S(2)}) collective-permute-start(bf16[96,4096]{1,0:T(8,128)(2,1)S(1)} %collective-permute-done.7.one), channel_id=1, source_target_pairs={{2,0},{4,2},{6,4},{7,6},{5,7},{3,5},{1,3},{0,1},{8,10},{10,12},{12... | collective-permute-start | bytes 2359304 | tf_op jit(solution)/shard_map/ppermute | solution.py:321
  54.1 9.3 %collective-permute-start.13 = (bf16[96,4096]{1,0:T(8,128)(2,1)S(1)}, bf16[96,4096]{1,0:T(8,128)(2,1)S(1)}, u32[]{:S(2)}, u32[]{:S(2)}) collective-permute-start(bf16[96,4096]{1,0:T(8,128)(2,1)S(1)} %collective-permute-done.6.one), channel_id=1, source_target_pairs={{0,8},{8,0},{1,9},{9,1},{2,10},{10,2},{3,11},{11,3},{4,12},{12,4},... | collective-permute-start | bytes 2359304 | tf_op jit(solution)/shard_map/ppermute | solution.py:316
  54.2 14.7 %collective-permute-start.10 = (bf16[96,4096]{1,0:T(8,128)(2,1)S(1)}, bf16[96,4096]{1,0:T(8,128)(2,1)S(1)}, u32[]{:S(2)}, u32[]{:S(2)}) collective-permute-start(bf16[96,4096]{1,0:T(8,128)(2,1)S(1)} %collective-permute-done.6.one), channel_id=1, source_target_pairs={{0,2},{2,4},{4,6},{6,7},{7,5},{5,3},{3,1},{1,0},{10,8},{12,10},{14... | collective-permute-start | bytes 2359304 | tf_op jit(solution)/shard_map/ppermute | solution.py:315
  63.5 5.6 %collective-permute-start.15 = (bf16[96,4096]{1,0:T(8,128)(2,1)S(1)}, bf16[96,4096]{1,0:T(8,128)(2,1)S(1)}, u32[]{:S(2)}, u32[]{:S(2)}) collective-permute-start(bf16[96,4096]{1,0:T(8,128)(2,1)S(1)} %collective-permute-done.11.one), channel_id=1, source_target_pairs={{0,8},{8,0},{1,9},{9,1},{2,10},{10,2},{3,11},{11,3},{4,12},{12,4},... | collective-permute-start | bytes 2359304 | tf_op jit(solution)/shard_map/ppermute | solution.py:322
  68.9 4.8 %collective-permute-start.14 = (bf16[96,4096]{1,0:T(8,128)(2,1)S(1)}, bf16[96,4096]{1,0:T(8,128)(2,1)S(1)}, u32[]{:S(2)}, u32[]{:S(2)}) collective-permute-start(bf16[96,4096]{1,0:T(8,128)(2,1)S(1)} %collective-permute-done.10.one), channel_id=1, source_target_pairs={{0,8},{8,0},{1,9},{9,1},{2,10},{10,2},{3,11},{11,3},{4,12},{12,4},... | collective-permute-start | bytes 2359304 | tf_op jit(solution)/shard_map/ppermute | solution.py:329
  73.7 30.6 %copy-start = (bf16[128,4096]{1,0:T(8,128)(2,1)S(1)}, bf16[128,4096]{1,0:T(8,128)(2,1)}, u32[]{:S(2)}) copy-start(bf16[128,4096]{1,0:T(8,128)(2,1)} %val_own.1) | copy-start | bytes 3145732
  78.3 1.4 %collective-permute-start.16 = (f32[256,128]{1,0:T(8,128)S(1)}, f32[256,128]{1,0:T(8,128)S(1)}, u32[]{:S(2)}, u32[]{:S(2)}) collective-permute-start(f32[256,128]{1,0:T(8,128)S(1)} %get-tuple-element.59), channel_id=1, source_target_pairs={{0,8},{8,0},{1,9},{9,1},{2,10},{10,2},{3,11},{11,3},{4,12},{12,4},... | collective-permute-start | bytes 393224 | tf_op jit(solution)/shard_map/ppermute | solution.py:335

commit v7 on v5

--- a/solution.py
+++ b/solution.py
@@ -99,39 +99,19 @@
     return main[:, :LANES] + main[:, LANES:] + rest
 
 
-def first_kernel(
-    table, lengths, own, other, gate_hbm, up_hbm, out_grad_hbm, proj_out_hbm, proj_in,
-    total, w, out_grad, diagonal, x, pre, both, sems, w_sems,
+def load_kernel(
+    table, lengths, gate_hbm, up_hbm, out_grad_hbm, proj_out_hbm, proj_in,
+    w, out_grad, diagonal, sems,
 ):
-    rows = own.shape[0]
-    width, hidden = gate_hbm.shape
-    depth = width // w_sems.shape[0]
-    parts = []
-    for k in range(w_sems.shape[0]):
-        here = pl.ds(k * depth, depth)
-        parts.append(
-            (
-                pltpu.make_async_copy(
-                    gate_hbm.at[here], w.at[here, pl.ds(0, hidden)], w_sems.at[k, 0]
-                ),
-                pltpu.make_async_copy(
-                    up_hbm.at[here], w.at[here, pl.ds(hidden, hidden)], w_sems.at[k, 1]
-                ),
-            )
-        )
-    blocks = [
-        pltpu.make_async_copy(own, x.at[pl.ds(0, rows)], sems.at[0]),
-        pltpu.make_async_copy(other, x.at[pl.ds(rows, rows)], sems.at[1]),
+    hidden = gate_hbm.shape[1]
+    upper = pltpu.make_async_copy(proj_out_hbm, diagonal.at[pl.ds(0, hidden)], sems.at[0])
+    copies = [
+        pltpu.make_async_copy(gate_hbm, w.at[:, pl.ds(0, hidden)], sems.at[1]),
+        pltpu.make_async_copy(up_hbm, w.at[:, pl.ds(hidden, hidden)], sems.at[2]),
+        pltpu.make_async_copy(out_grad_hbm, out_grad, sems.at[3]),
     ]
-    upper = pltpu.make_async_copy(proj_out_hbm, diagonal.at[pl.ds(0, hidden)], sems.at[2])
-    whole = pltpu.make_async_copy(out_grad_hbm, out_grad, sems.at[3])
-    for copy in blocks + [upper]:
+    for copy in [upper] + copies:
         copy.start()
-    for pair in parts:
-        for copy in pair:
-            copy.start()
-    whole.start()
-
     w[:, 2 * hidden :] = jnp.concatenate([proj_in[...], proj_in[...]], axis=1)
     upper.wait()
     values = diagonal[:hidden, :]
@@ -139,18 +119,8 @@
     none = jnp.zeros_like(values)
     diagonal[hidden:, :] = jnp.where(left, none, values)
     diagonal[:hidden, :] = jnp.where(left, values, none)
-    for copy in blocks:
+    for copy in copies:
         copy.wait()
-    for k, pair in enumerate(parts):
-        for copy in pair:
-            copy.wait()
-        here = slice(k * depth, (k + 1) * depth)
-        product = jnp.dot(x[:, here], w[here, :], preferred_element_type=jnp.float32)
-        pre[...] = product if k == 0 else pre[...] + product
-    whole.wait()
-    starts = [table[0], table[1]]
-    gradients(pre, cotangent_chunks(out_grad, starts, rows), both)
-    total[...] = sketch_of(starts, rows, lengths, pre, both, diagonal)
 
 
 def cotangent_chunks(out_grad, starts, rows):
@@ -162,14 +132,18 @@
     return chunks
 
 
-def step_kernel(entry, last, table, lengths, one, two, w, out_grad, diagonal, before, *refs):
+def step_kernel(entry, first, last, table, lengths, one, two, w, out_grad, diagonal, *refs):
     outs, (pre, both) = refs[:-2], refs[-2:]
+    if not first:
+        before, outs = outs[0], outs[1:]
     rows = one.shape[0]
     starts = [table[entry], table[entry + 1]]
     x = jnp.concatenate([one[...], two[...]], axis=0)
     pre[...] = jnp.dot(x, w[...], preferred_element_type=jnp.float32)
     gradients(pre, cotangent_chunks(out_grad, starts, rows), both)
-    total = before[...] + sketch_of(starts, rows, lengths, pre, both, diagonal)
+    total = sketch_of(starts, rows, lengths, pre, both, diagonal)
+    if not first:
+        total += before[...]
     if not last:
         outs[0][...] = total
         return
@@ -187,48 +161,39 @@
     )
 
 
-def first_step(table, lengths, own, other, w_gate, w_up, out_grad, proj_in, proj_out):
-    rows, width = own.shape
-    hidden = w_gate.shape[1]
-    columns = 2 * hidden + LANES
-    chunks = 4 if width % (4 * LANES) == 0 else 1
-    own, w_gate, w_up, out_grad, proj_out = [
+def load(table, lengths, w_gate, w_up, out_grad, proj_in, proj_out):
+    width, hidden = w_gate.shape
+    w_gate, w_up, out_grad, proj_out = [
         pltpu.with_memory_space_constraint(a, pltpu.HBM)
-        for a in (own, w_gate, w_up, out_grad, proj_out)
+        for a in (w_gate, w_up, out_grad, proj_out)
     ]
     return pl.pallas_call(
-        first_kernel,
+        load_kernel,
         out_shape=[
-            jax.ShapeDtypeStruct((lengths.shape[0] * LANES // 2, LANES), jnp.float32),
-            pltpu.VMEM((width, columns), jnp.bfloat16),
+            pltpu.VMEM((width, 2 * hidden + LANES), jnp.bfloat16),
             pltpu.VMEM(out_grad.shape, jnp.bfloat16),
             pltpu.VMEM((2 * hidden, LANES), jnp.bfloat16),
         ],
-        in_specs=[SMEM, SMEM] + [ANY] * 6 + [VMEM],
-        out_specs=[VMEM] * 4,
-        scratch_shapes=[
-            pltpu.VMEM((2 * rows, width), jnp.bfloat16),
-            pltpu.VMEM((2 * rows, columns), jnp.float32),
-            pltpu.VMEM((2 * rows, 2 * hidden), jnp.bfloat16),
-            pltpu.SemaphoreType.DMA((4,)),
-            pltpu.SemaphoreType.DMA((chunks, 2)),
-        ],
+        in_specs=[SMEM, SMEM] + [ANY] * 4 + [VMEM],
+        out_specs=[VMEM] * 3,
+        scratch_shapes=[pltpu.SemaphoreType.DMA((4,))],
         compiler_params=pltpu.CompilerParams(vmem_limit_bytes=16 * 2**20),
-        cost_estimate=costs(2 * rows, width, columns),
-    )(table, lengths, own, other, w_gate, w_up, out_grad, proj_out, proj_in)
-
-
-def next_step(blocks, entry, total, table, lengths, weights, last=False):
+    )(table, lengths, w_gate, w_up, out_grad, proj_out, proj_in)
+
+
+def add_step(blocks, entry, total, table, lengths, weights, last=False):
     rows, width = blocks[0].shape
     w, _, diagonal = weights
-    shape = total.shape
-    out_shape = [jax.ShapeDtypeStruct(shape, jnp.float32)]
+    first = total is None
+    operands = [*blocks, *weights] + ([] if first else [total])
+    out_rows = lengths.shape[0] * LANES // 2
+    out_shape = [jax.ShapeDtypeStruct((out_rows, LANES), jnp.float32)]
     if last:
-        out_shape = [jax.ShapeDtypeStruct((shape[0] // 2, LANES), jnp.float32)] * 2
+        out_shape = [jax.ShapeDtypeStruct((out_rows // 2, LANES), jnp.float32)] * 2
     outs = pl.pallas_call(
-        functools.partial(step_kernel, entry, last),
+        functools.partial(step_kernel, entry, first, last),
         out_shape=out_shape,
-        in_specs=[SMEM, SMEM] + [VMEM] * 6,
+        in_specs=[SMEM, SMEM] + [VMEM] * len(operands),
         out_specs=[VMEM] * len(out_shape),
         scratch_shapes=[
             pltpu.VMEM((2 * rows, w.shape[1]), jnp.float32),
@@ -236,7 +201,7 @@
         ],
         compiler_params=pltpu.CompilerParams(vmem_limit_bytes=16 * 2**20),
         cost_estimate=costs(2 * rows, width, w.shape[1]),
-    )(table, lengths, *blocks, *weights, total)
+    )(table, lengths, *operands)
     return outs if last else outs[0]
 
 
@@ -302,25 +267,36 @@
     after = lax.optimization_barrier
     one_way = send_one(tokens_in)
     other, other_val = swap(tokens_in), swap(val_sketch)
-    later_tokens, table = after((tokens_in, table))
+    w, out_grad, diagonal = load(table, lengths, w_gate, w_up, out_grad, proj_in, proj_out)
+    later_tokens, diagonal = after((tokens_in, diagonal))
     two_way = send_two(later_tokens)
-    total, *weights = first_step(
-        table, lengths, tokens_in, other, w_gate, w_up, out_grad, proj_in, proj_out
-    )
-    add = functools.partial(next_step, table=table, lengths=lengths, weights=weights)
-
-    entry = 2
+    add = functools.partial(
+        add_step, table=table, lengths=lengths, weights=[w, out_grad, diagonal]
+    )
+    total = add([tokens_in, other], 0, None)
+
+    waiting, entry = None, 2
     for k in range(1, n // 2):
         one_way, total = after((one_way, total))
-        next_one, swapped = send_one(one_way), swap(one_way)
-        total = add([one_way, swapped], entry, total)
+        next_one = send_one(one_way)
+        swapped_one = swap(one_way)
+        if waiting is not None:
+            total = add(waiting, entry, total)
+            entry += 2
         two_way, total, other_val = after((two_way, total, other_val))
         next_two = send_two(two_way) if k + 1 < n // 2 else None
-        total = add([two_way, swap(two_way)], entry + 2, total)
-        entry += 4
+        swapped_two = swap(two_way)
+        _, swapped_one = after((two_way, swapped_one))
+        total = add([one_way, swapped_one], entry, total)
+        entry += 2
+        waiting = (two_way, swapped_two)
         one_way, two_way = next_one, next_two
     one_way, total = after((one_way, total))
-    kept, sent = add([one_way, swap(one_way)], entry, total, last=True)
+    swapped_one = swap(one_way)
+    if waiting is not None:
+        total = add(waiting, entry, total)
+        entry += 2
+    kept, sent = add([one_way, swapped_one], entry, total, last=True)
 
     mine, theirs = kept, swap(sent)
     bit = 1

time: 114 us -> 92.8 us (0.81)
  waiting for transfers between devices: 47.7 us -> 24.2 us
  starting transfers between devices: 17.8 us -> 19.6 us
    ppermute x10, waiting for transfers between devices: 22 us -> 0.03 us  [the longest x4 0.01 us: fast(): swapped_one = swap(one_way)]
    ppermute x10, starting transfers between devices: 4.99 us -> 9.73 us  [the longest x3 5.21 us: fast(): next_one = send_one(one_way)]
    ppermute x1, waiting for transfers between devices: 5.58 us -> 8.48 us  [fast(): two_way = send_two(later_tokens)]
    ppermute x2, starting transfers between devices: 2.64 us -> 0.01 us  [fast(): next_two = send_two(two_way) if k + 1 < n // 2 else None]
    ppermute x4, waiting for transfers between devices: 8.69 us -> 6.18 us  [fast(): lax.ppermute(sent, 'mp', [(i, i ^ flip) for i in range(n)])]
    ppermute x2, waiting for transfers between devices: 10.2 us -> 8.19 us  [fast(): next_two = send_two(two_way) if k + 1 < n // 2 else None]
    ppermute x1, starting transfers between devices: 1.32 us -> 0.06 us  [fast(): two_way = send_two(later_tokens)]
    pallas_call x8 -> x9, Pallas kernels: 43.5 us -> 43.9 us  [the longest x8 37.2 us: add_step(): pl.pallas_call(functools.partial(step_kernel, entry, first, last), out_sh...]
  transfers between devices with their start and end apart: 21 -> 21, of which waited for: 18 -> 8; matrix products, arithmetic and copies ran while one was open for 2% -> 2% of each run, Pallas kernels for 34% -> 42%
where the time goes in v7:
time: 92.8 us; the launch traced here: 92.6 us
  Pallas kernels  45.7 us (49%)
  waiting for transfers between devices  24.2 us (26%)
  starting transfers between devices  19.6 us (21%)
  local copies, waits for them, and re-layouts  2.88 us (3%)
    pallas_call x8, Pallas kernels, add_step(): pl.pallas_call(functools.partial(step_kernel, entry, first, last), out_sh...  37.2 us
    ppermute x1, waiting for transfers between devices, fast(): two_way = send_two(later_tokens)  8.48 us
    ppermute x2, waiting for transfers between devices, fast(): next_two = send_two(two_way) if k + 1 < n // 2 else None  8.19 us
    pallas_call x1, Pallas kernels, load(): pl.pallas_call(load_kernel, out_shape=[pltpu.VMEM((width, 2 * hidden + LA...  6.7 us
    ppermute x4, starting transfers between devices, fast(): lax.ppermute(sent, 'mp', [(i, i ^ flip) for i in range(n)])  6.41 us
    ppermute x4, waiting for transfers between devices, fast(): lax.ppermute(sent, 'mp', [(i, i ^ flip) for i in range(n)])  6.18 us
    ppermute x3, starting transfers between devices, fast(): next_one = send_one(one_way)  5.21 us
    ppermute x4, starting transfers between devices, fast(): swapped_one = swap(one_way)  4.51 us
  transfers between devices with their start and end apart: 21, of which 8 were waited for; matrix products, arithmetic and copies ran while one was open for 2% of the time, Pallas kernels for 42%

profile of v7, /device:TPU:0, one launch (start us, length us, event | category | flops | bytes accessed | tf_op | source)
XLA Modules:
  0.0 92.6 jit_solution(3295393302569123381)
XLA Ops:
  0.5 2.6 %collective-permute-start = (bf16[96,4096]{1,0:T(8,128)(2,1)}, bf16[96,4096]{1,0:T(8,128)(2,1)S(1)}, u32[]{:S(2)}, u32[]{:S(2)}) collective-permute-start(bf16[96,4096]{1,0:T(8,128)(2,1)} %one.1), channel_id=1, source_target_pairs={{0,2},{2,4},{4,6},{6,7},{7,5},{5,3},{3,1},{1,0},{10,8},{12,10},{14... | collective-permute-start | bytes 2359304 | tf_op jit(solution)/shard_map/ppermute | solution.py:268
  3.0 1.5 %copy.10.proj_in = bf16[4096,64]{1,0:T(8,128)(2,1)S(1)} copy(bf16[4096,64]{0,1:T(8,128)(2,1)} %param.13) | data formatting | bytes 1048576 | tf_op args[4]
  5.9 6.7 %shard_map.91 = (bf16[4096,1920]{1,0:T(8,128)(2,1)S(1)}, bf16[1536,896]{1,0:T(8,128)(2,1)S(1)}, bf16[1792,128]{1,0:T(8,128)(2,1)S(1)}) custom-call(s32[17]{0:T(128)S(1)} %dynamic-slice_bitcast_fusion.table, s32[8]{0:T(128)S(1)} %copy-done.1, bf16[4096,896]{1,0:T(8,128)(2,1)} %gate_hbm.1, bf16[4096,896]{1,0:T(8,128)(2,1)} %up_hbm.1, ...), custom_call_target="tpu_custom_call" | custom-call | tf_op jit(solution)/shard_map/pallas_call | solution.py:170
  12.9 4.6 %shard_map.92.refs_0_ = f32[512,128]{1,0:T(8,128)S(1)} custom-call(s32[17]{0:T(128)S(1)} %dynamic-slice_bitcast_fusion.table, s32[8]{0:T(128)S(1)} %copy-done.2, bf16[96,4096]{1,0:T(8,128)(2,1)S(1)} %copy-done.3, bf16[96,4096]{1,0:T(8,128)(2,1)S(1)} %collective-permute-done.1.two, bf16[4096,1920]{1,0:T(8,128)(2,1)S(1)} %get-tuple-element.32.w, ...), custom_call_target="tpu_custom_call" | custom-call | flops 6039797760 | bytes 1572864 | tf_op jit(solution)/shard_map/pallas_call | solution.py:193
  18.0 1.9 %collective-permute-start.2 = (bf16[96,4096]{1,0:T(8,128)(2,1)S(1)}, bf16[96,4096]{1,0:T(8,128)(2,1)S(1)}, u32[]{:S(2)}, u32[]{:S(2)}) collective-permute-start(bf16[96,4096]{1,0:T(8,128)(2,1)S(1)} %collective-permute-done.one), channel_id=1, source_target_pairs={{0,2},{2,4},{4,6},{6,7},{7,5},{5,3},{3,1},{1,0},{10,8},{12,10},{14... | collective-permute-start | bytes 2359304 | tf_op jit(solution)/shard_map/ppermute | solution.py:281
  19.9 8.5 %collective-permute-done.3.one = bf16[96,4096]{1,0:T(8,128)(2,1)S(1)} collective-permute-done((bf16[96,4096]{1,0:T(8,128)(2,1)S(1)}, bf16[96,4096]{1,0:T(8,128)(2,1)S(1)}, u32[]{:S(2)}, u32[]{:S(2)}) %collective-permute-start.3) | collective-permute-done | bytes 786464 | tf_op jit(solution)/shard_map/ppermute | solution.py:272
  28.4 4.6 %shard_map.93.refs_0_ = f32[512,128]{1,0:T(8,128)S(1)} custom-call(s32[17]{0:T(128)S(1)} %dynamic-slice_bitcast_fusion.table, s32[8]{0:T(128)S(1)} %copy-done.2, bf16[96,4096]{1,0:T(8,128)(2,1)S(1)} %collective-permute-done.one, bf16[96,4096]{1,0:T(8,128)(2,1)S(1)} %collective-permute-done.5.two, bf16[4096,1920]{1,0:T(8,128)(2,1)S(1)} %get-tuple-element.32.w, ...), custom_call_target="tpu_custom_call" | custom-call | flops 6039797760 | bytes 1572864 | tf_op jit(solution)/shard_map/pallas_call | solution.py:193
  33.1 1.7 %collective-permute-start.9 = (bf16[96,4096]{1,0:T(8,128)(2,1)S(1)}, bf16[96,4096]{1,0:T(8,128)(2,1)S(1)}, u32[]{:S(2)}, u32[]{:S(2)}) collective-permute-start(bf16[96,4096]{1,0:T(8,128)(2,1)S(1)} %collective-permute-done.2.one), channel_id=1, source_target_pairs={{0,8},{8,0},{1,9},{9,1},{2,10},{10,2},{3,11},{11,3},{4,12},{12,4},... | collective-permute-start | bytes 2359304 | tf_op jit(solution)/shard_map/ppermute | solution.py:282
  34.8 1.6 %collective-permute-start.6 = (bf16[96,4096]{1,0:T(8,128)(2,1)S(1)}, bf16[96,4096]{1,0:T(8,128)(2,1)S(1)}, u32[]{:S(2)}, u32[]{:S(2)}) collective-permute-start(bf16[96,4096]{1,0:T(8,128)(2,1)S(1)} %collective-permute-done.2.one), channel_id=1, source_target_pairs={{0,2},{2,4},{4,6},{6,7},{7,5},{5,3},{3,1},{1,0},{10,8},{12,10},{14... | collective-permute-start | bytes 2359304 | tf_op jit(solution)/shard_map/ppermute | solution.py:281
  36.4 4.6 %shard_map.94.refs_0_ = f32[512,128]{1,0:T(8,128)S(1)} custom-call(s32[17]{0:T(128)S(1)} %dynamic-slice_bitcast_fusion.table, s32[8]{0:T(128)S(1)} %copy-done.2, bf16[96,4096]{1,0:T(8,128)(2,1)S(1)} %collective-permute-done.3.one, bf16[96,4096]{1,0:T(8,128)(2,1)S(1)} %collective-permute-done.8.two, bf16[4096,1920]{1,0:T(8,128)(2,1)S(1)} %get-tuple-element.32.w, ...), custom_call_target="tpu_custom_call" | custom-call | flops 6039797760 | bytes 1572864 | tf_op jit(solution)/shard_map/pallas_call | solution.py:193
  41.0 4.6 %collective-permute-done.7.one = bf16[96,4096]{1,0:T(8,128)(2,1)S(1)} collective-permute-done((bf16[96,4096]{1,0:T(8,128)(2,1)S(1)}, bf16[96,4096]{1,0:T(8,128)(2,1)S(1)}, u32[]{:S(2)}, u32[]{:S(2)}) %collective-permute-start.7) | collective-permute-done | bytes 786464 | tf_op jit(solution)/shard_map/ppermute | solution.py:287
  45.6 4.6 %shard_map.95.refs_0_ = f32[512,128]{1,0:T(8,128)S(1)} custom-call(s32[17]{0:T(128)S(1)} %dynamic-slice_bitcast_fusion.table, s32[8]{0:T(128)S(1)} %copy-done.2, bf16[96,4096]{1,0:T(8,128)(2,1)S(1)} %collective-permute-done.2.one, bf16[96,4096]{1,0:T(8,128)(2,1)S(1)} %collective-permute-done.9.two, bf16[4096,1920]{1,0:T(8,128)(2,1)S(1)} %get-tuple-element.32.w, ...), custom_call_target="tpu_custom_call" | custom-call | flops 6039797760 | bytes 1572864 | tf_op jit(solution)/shard_map/pallas_call | solution.py:193
  50.2 1.8 %collective-permute-start.13 = (bf16[96,4096]{1,0:T(8,128)(2,1)S(1)}, bf16[96,4096]{1,0:T(8,128)(2,1)S(1)}, u32[]{:S(2)}, u32[]{:S(2)}) collective-permute-start(bf16[96,4096]{1,0:T(8,128)(2,1)S(1)} %collective-permute-done.6.one), channel_id=1, source_target_pairs={{0,8},{8,0},{1,9},{9,1},{2,10},{10,2},{3,11},{11,3},{4,12},{12,4},... | collective-permute-start | bytes 2359304 | tf_op jit(solution)/shard_map/ppermute | solution.py:282
  52.0 1.7 %collective-permute-start.10 = (bf16[96,4096]{1,0:T(8,128)(2,1)S(1)}, bf16[96,4096]{1,0:T(8,128)(2,1)S(1)}, u32[]{:S(2)}, u32[]{:S(2)}) collective-permute-start(bf16[96,4096]{1,0:T(8,128)(2,1)S(1)} %collective-permute-done.6.one), channel_id=1, source_target_pairs={{0,2},{2,4},{4,6},{6,7},{7,5},{5,3},{3,1},{1,0},{10,8},{12,10},{14... | collective-permute-start | bytes 2359304 | tf_op jit(solution)/shard_map/ppermute | solution.py:281
  53.7 4.6 %shard_map.96.refs_0_ = f32[512,128]{1,0:T(8,128)S(1)} custom-call(s32[17]{0:T(128)S(1)} %dynamic-slice_bitcast_fusion.table, s32[8]{0:T(128)S(1)} %copy-done.2, bf16[96,4096]{1,0:T(8,128)(2,1)S(1)} %collective-permute-done.7.one, bf16[96,4096]{1,0:T(8,128)(2,1)S(1)} %collective-permute-done.12.two, bf16[4096,1920]{1,0:T(8,128)(2,1)S(1)} %get-tuple-element.32.w, ...), custom_call_target="tpu_custom_call" | custom-call | flops 6039797760 | bytes 1572864 | tf_op jit(solution)/shard_map/pallas_call | solution.py:193
  58.4 3.6 %collective-permute-done.11.one = bf16[96,4096]{1,0:T(8,128)(2,1)S(1)} collective-permute-done((bf16[96,4096]{1,0:T(8,128)(2,1)S(1)}, bf16[96,4096]{1,0:T(8,128)(2,1)S(1)}, u32[]{:S(2)}, u32[]{:S(2)}) %collective-permute-start.11) | collective-permute-done | bytes 786464 | tf_op jit(solution)/shard_map/ppermute | solution.py:287
  62.0 4.6 %shard_map.97.refs_0_ = f32[512,128]{1,0:T(8,128)S(1)} custom-call(s32[17]{0:T(128)S(1)} %dynamic-slice_bitcast_fusion.table, s32[8]{0:T(128)S(1)} %copy-done.2, bf16[96,4096]{1,0:T(8,128)(2,1)S(1)} %collective-permute-done.6.one, bf16[96,4096]{1,0:T(8,128)(2,1)S(1)} %collective-permute-done.13.two, bf16[4096,1920]{1,0:T(8,128)(2,1)S(1)} %get-tuple-element.32.w, ...), custom_call_target="tpu_custom_call" | custom-call | flops 6039797760 | bytes 1572864 | tf_op jit(solution)/shard_map/pallas_call | solution.py:193
  67.2 4.6 %shard_map.98.refs_0_ = f32[512,128]{1,0:T(8,128)S(1)} custom-call(s32[17]{0:T(128)S(1)} %dynamic-slice_bitcast_fusion.table, s32[8]{0:T(128)S(1)} %copy-done.2, bf16[96,4096]{1,0:T(8,128)(2,1)S(1)} %collective-permute-done.11.one, bf16[96,4096]{1,0:T(8,128)(2,1)S(1)} %collective-permute-done.15.two, bf16[4096,1920]{1,0:T(8,128)(2,1)S(1)} %get-tuple-element.32.w, ...), custom_call_target="tpu_custom_call" | custom-call | flops 6039797760 | bytes 1572864 | tf_op jit(solution)/shard_map/pallas_call | solution.py:193
  71.8 4.8 %shard_map.99 = (f32[256,128]{1,0:T(8,128)S(1)}, f32[256,128]{1,0:T(8,128)S(1)}) custom-call(s32[17]{0:T(128)S(1)} %dynamic-slice_bitcast_fusion.table, s32[8]{0:T(128)S(1)} %copy-done.2, bf16[96,4096]{1,0:T(8,128)(2,1)S(1)} %collective-permute-done.10.one, bf16[96,4096]{1,0:T(8,128)(2,1)S(1)} %collective-permute-done.14.two, ...), custom_call_target="tpu_custom_call" | custom-call | flops 6039797760 | bytes 1572864 | tf_op jit(solution)/shard_map/pallas_call | solution.py:193
  78.7 1.6 %collective-permute-start.18 = (bf16[256,128]{1,0:T(8,128)(2,1)S(1)}, bf16[256,128]{1,0:T(8,128)(2,1)S(1)}, u32[]{:S(2)}, u32[]{:S(2)}) collective-permute-start(bf16[256,128]{1,0:T(8,128)(2,1)S(1)} %get-tuple-element.61), channel_id=1, source_target_pairs={{0,2},{1,3},{2,0},{3,1},{4,6},{5,7},{6,4},{7,5},{8,10},{9,11},{10,... | collective-permute-start | bytes 196616 | tf_op jit(solution)/shard_map/ppermute | solution.py:310
  83.0 2.5 %collective-permute-done.19 = bf16[256,128]{1,0:T(8,128)(2,1)S(1)} collective-permute-done((bf16[256,128]{1,0:T(8,128)(2,1)S(1)}, bf16[256,128]{1,0:T(8,128)(2,1)S(1)}, u32[]{:S(2)}, u32[]{:S(2)}) %collective-permute-start.19) | collective-permute-done | bytes 65568 | tf_op jit(solution)/shard_map/ppermute | solution.py:310
  85.5 2.9 %collective-permute-start.20 = (bf16[256,128]{1,0:T(8,128)(2,1)S(1)}, bf16[256,128]{1,0:T(8,128)(2,1)S(1)}, u32[]{:S(2)}, u32[]{:S(2)}) collective-permute-start(bf16[256,128]{1,0:T(8,128)(2,1)S(1)} %get-tuple-element.59), channel_id=1, source_target_pairs={{0,4},{1,5},{2,6},{3,7},{4,0},{5,1},{6,2},{7,3},{8,12},{9,13},{10,... | collective-permute-start | bytes 196616 | tf_op jit(solution)/shard_map/ppermute | solution.py:310
  88.4 2.4 %collective-permute-done.20.theirs = bf16[256,128]{1,0:T(8,128)(2,1)S(1)} collective-permute-done((bf16[256,128]{1,0:T(8,128)(2,1)S(1)}, bf16[256,128]{1,0:T(8,128)(2,1)S(1)}, u32[]{:S(2)}, u32[]{:S(2)}) %collective-permute-start.20) | collective-permute-done | bytes 65568 | tf_op jit(solution)/shard_map/ppermute | solution.py:310
  90.7 1.8 %shard_map.100 = f32[4,128]{1,0:T(4,128)} custom-call(s32[17]{0:T(128)S(1)} %dynamic-slice_bitcast_fusion.table, f32[256,128]{1,0:T(8,128)S(1)} %get-tuple-element.60.mine, bf16[256,128]{1,0:T(8,128)(2,1)S(1)} %collective-permute-done.20.theirs, bf16[128,4096]{1,0:T(8,128)(2,1)S(1)} %copy-done, bf16[128,4096]{1,0:T(8,128)(2,1)S(1)} %collective-permute-done.4.val_other), custom_call_target="tpu_custom_call" | custom-call | tf_op jit(solution)/shard_map/pallas_call | solution.py:242
  (40 shorter events, 7.9 us)
Async XLA Ops:
  0.0 12.9 %collective-permute-start.1 = (bf16[96,4096]{1,0:T(8,128)(2,1)}, bf16[96,4096]{1,0:T(8,128)(2,1)S(1)}, u32[]{:S(2)}, u32[]{:S(2)}) collective-permute-start(bf16[96,4096]{1,0:T(8,128)(2,1)} %one.1), channel_id=1, source_target_pairs={{0,8},{8,0},{1,9},{9,1},{2,10},{10,2},{3,11},{11,3},{4,12},{12,4},... | collective-permute-start | bytes 2359304 | tf_op jit(solution)/shard_map/ppermute | solution.py:269
  0.5 17.1 %collective-permute-start = (bf16[96,4096]{1,0:T(8,128)(2,1)}, bf16[96,4096]{1,0:T(8,128)(2,1)S(1)}, u32[]{:S(2)}, u32[]{:S(2)}) collective-permute-start(bf16[96,4096]{1,0:T(8,128)(2,1)} %one.1), channel_id=1, source_target_pairs={{0,2},{2,4},{4,6},{6,7},{7,5},{5,3},{3,1},{1,0},{10,8},{12,10},{14... | collective-permute-start | bytes 2359304 | tf_op jit(solution)/shard_map/ppermute | solution.py:268
  5.9 6.7 %copy-start.3 = (bf16[96,4096]{1,0:T(8,128)(2,1)S(1)}, bf16[96,4096]{1,0:T(8,128)(2,1)}, u32[]{:S(2)}) copy-start(bf16[96,4096]{1,0:T(8,128)(2,1)} %one.1) | copy-start | bytes 2359300
  5.9 6.8 %copy-start = (bf16[128,4096]{1,0:T(8,128)(2,1)S(1)}, bf16[128,4096]{1,0:T(8,128)(2,1)}, u32[]{:S(2)}) copy-start(bf16[128,4096]{1,0:T(8,128)(2,1)} %val_own.1) | copy-start | bytes 3145732
  5.9 7.0 %copy-start.2 = (s32[8]{0:T(128)S(1)}, s32[8]{0:T(128)}, u32[]{:S(2)}) copy-start(s32[8]{0:T(128)} %lengths.17) | copy-start | bytes 100
  12.6 15.8 %collective-permute-start.3 = (bf16[96,4096]{1,0:T(8,128)(2,1)S(1)}, bf16[96,4096]{1,0:T(8,128)(2,1)S(1)}, u32[]{:S(2)}, u32[]{:S(2)}) collective-permute-start(bf16[96,4096]{1,0:T(8,128)(2,1)S(1)} %copy-done.3), channel_id=1, source_target_pairs={{2,0},{4,2},{6,4},{7,6},{5,7},{3,5},{1,3},{0,1},{8,10},{10,12},{12... | collective-permute-start | bytes 2359304 | tf_op jit(solution)/shard_map/ppermute | solution.py:272
  12.7 15.7 %collective-permute-start.4 = (bf16[128,4096]{1,0:T(8,128)(2,1)S(1)}, bf16[128,4096]{1,0:T(8,128)(2,1)S(1)}, u32[]{:S(2)}, u32[]{:S(2)}) collective-permute-start(bf16[128,4096]{1,0:T(8,128)(2,1)S(1)} %copy-done), channel_id=1, source_target_pairs={{0,8},{8,0},{1,9},{9,1},{2,10},{10,2},{3,11},{11,3},{4,12},{12,4},... | collective-permute-start | bytes 3145736 | tf_op jit(solution)/shard_map/ppermute | solution.py:269
  17.6 10.8 %collective-permute-start.5 = (bf16[96,4096]{1,0:T(8,128)(2,1)S(1)}, bf16[96,4096]{1,0:T(8,128)(2,1)S(1)}, u32[]{:S(2)}, u32[]{:S(2)}) collective-permute-start(bf16[96,4096]{1,0:T(8,128)(2,1)S(1)} %collective-permute-done.one), channel_id=1, source_target_pairs={{0,8},{8,0},{1,9},{9,1},{2,10},{10,2},{3,11},{11,3},{4,12},{12,4},... | collective-permute-start | bytes 2359304 | tf_op jit(solution)/shard_map/ppermute | solution.py:282
  18.0 15.1 %collective-permute-start.2 = (bf16[96,4096]{1,0:T(8,128)(2,1)S(1)}, bf16[96,4096]{1,0:T(8,128)(2,1)S(1)}, u32[]{:S(2)}, u32[]{:S(2)}) collective-permute-start(bf16[96,4096]{1,0:T(8,128)(2,1)S(1)} %collective-permute-done.one), channel_id=1, source_target_pairs={{0,2},{2,4},{4,6},{6,7},{7,5},{5,3},{3,1},{1,0},{10,8},{12,10},{14... | collective-permute-start | bytes 2359304 | tf_op jit(solution)/shard_map/ppermute | solution.py:281
  28.4 7.9 %collective-permute-start.8 = (bf16[96,4096]{1,0:T(8,128)(2,1)S(1)}, bf16[96,4096]{1,0:T(8,128)(2,1)S(1)}, u32[]{:S(2)}, u32[]{:S(2)}) collective-permute-start(bf16[96,4096]{1,0:T(8,128)(2,1)S(1)} %collective-permute-done.3.one), channel_id=1, source_target_pairs={{0,8},{8,0},{1,9},{9,1},{2,10},{10,2},{3,11},{11,3},{4,12},{12,4},... | collective-permute-start | bytes 2359304 | tf_op jit(solution)/shard_map/ppermute | solution.py:288
  28.4 17.1 %collective-permute-start.7 = (bf16[96,4096]{1,0:T(8,128)(2,1)S(1)}, bf16[96,4096]{1,0:T(8,128)(2,1)S(1)}, u32[]{:S(2)}, u32[]{:S(2)}) collective-permute-start(bf16[96,4096]{1,0:T(8,128)(2,1)S(1)} %collective-permute-done.3.one), channel_id=1, source_target_pairs={{2,0},{4,2},{6,4},{7,6},{5,7},{3,5},{1,3},{0,1},{8,10},{10,12},{12... | collective-permute-start | bytes 2359304 | tf_op jit(solution)/shard_map/ppermute | solution.py:287
  33.1 12.5 %collective-permute-start.9 = (bf16[96,4096]{1,0:T(8,128)(2,1)S(1)}, bf16[96,4096]{1,0:T(8,128)(2,1)S(1)}, u32[]{:S(2)}, u32[]{:S(2)}) collective-permute-start(bf16[96,4096]{1,0:T(8,128)(2,1)S(1)} %collective-permute-done.2.one), channel_id=1, source_target_pairs={{0,8},{8,0},{1,9},{9,1},{2,10},{10,2},{3,11},{11,3},{4,12},{12,4},... | collective-permute-start | bytes 2359304 | tf_op jit(solution)/shard_map/ppermute | solution.py:282
  34.8 15.4 %collective-permute-start.6 = (bf16[96,4096]{1,0:T(8,128)(2,1)S(1)}, bf16[96,4096]{1,0:T(8,128)(2,1)S(1)}, u32[]{:S(2)}, u32[]{:S(2)}) collective-permute-start(bf16[96,4096]{1,0:T(8,128)(2,1)S(1)} %collective-permute-done.2.one), channel_id=1, source_target_pairs={{0,2},{2,4},{4,6},{6,7},{7,5},{5,3},{3,1},{1,0},{10,8},{12,10},{14... | collective-permute-start | bytes 2359304 | tf_op jit(solution)/shard_map/ppermute | solution.py:281
  45.5 8.2 %collective-permute-start.12 = (bf16[96,4096]{1,0:T(8,128)(2,1)S(1)}, bf16[96,4096]{1,0:T(8,128)(2,1)S(1)}, u32[]{:S(2)}, u32[]{:S(2)}) collective-permute-start(bf16[96,4096]{1,0:T(8,128)(2,1)S(1)} %collective-permute-done.7.one), channel_id=1, source_target_pairs={{0,8},{8,0},{1,9},{9,1},{2,10},{10,2},{3,11},{11,3},{4,12},{12,4},... | collective-permute-start | bytes 2359304 | tf_op jit(solution)/shard_map/ppermute | solution.py:288
  45.6 16.4 %collective-permute-start.11 = (bf16[96,4096]{1,0:T(8,128)(2,1)S(1)}, bf16[96,4096]{1,0:T(8,128)(2,1)S(1)}, u32[]{:S(2)}, u32[]{:S(2)}) collective-permute-start(bf16[96,4096]{1,0:T(8,128)(2,1)S(1)} %collective-permute-done.7.one), channel_id=1, source_target_pairs={{2,0},{4,2},{6,4},{7,6},{5,7},{3,5},{1,3},{0,1},{8,10},{10,12},{12... | collective-permute-start | bytes 2359304 | tf_op jit(solution)/shard_map/ppermute | solution.py:287
  50.2 11.8 %collective-permute-start.13 = (bf16[96,4096]{1,0:T(8,128)(2,1)S(1)}, bf16[96,4096]{1,0:T(8,128)(2,1)S(1)}, u32[]{:S(2)}, u32[]{:S(2)}) collective-permute-start(bf16[96,4096]{1,0:T(8,128)(2,1)S(1)} %collective-permute-done.6.one), channel_id=1, source_target_pairs={{0,8},{8,0},{1,9},{9,1},{2,10},{10,2},{3,11},{11,3},{4,12},{12,4},... | collective-permute-start | bytes 2359304 | tf_op jit(solution)/shard_map/ppermute | solution.py:282
  52.0 14.6 %collective-permute-start.10 = (bf16[96,4096]{1,0:T(8,128)(2,1)S(1)}, bf16[96,4096]{1,0:T(8,128)(2,1)S(1)}, u32[]{:S(2)}, u32[]{:S(2)}) collective-permute-start(bf16[96,4096]{1,0:T(8,128)(2,1)S(1)} %collective-permute-done.6.one), channel_id=1, source_target_pairs={{0,2},{2,4},{4,6},{6,7},{7,5},{5,3},{3,1},{1,0},{10,8},{12,10},{14... | collective-permute-start | bytes 2359304 | tf_op jit(solution)/shard_map/ppermute | solution.py:281
  62.0 5.2 %collective-permute-start.15 = (bf16[96,4096]{1,0:T(8,128)(2,1)S(1)}, bf16[96,4096]{1,0:T(8,128)(2,1)S(1)}, u32[]{:S(2)}, u32[]{:S(2)}) collective-permute-start(bf16[96,4096]{1,0:T(8,128)(2,1)S(1)} %collective-permute-done.11.one), channel_id=1, source_target_pairs={{0,8},{8,0},{1,9},{9,1},{2,10},{10,2},{3,11},{11,3},{4,12},{12,4},... | collective-permute-start | bytes 2359304 | tf_op jit(solution)/shard_map/ppermute | solution.py:288
  66.6 5.2 %collective-permute-start.14 = (bf16[96,4096]{1,0:T(8,128)(2,1)S(1)}, bf16[96,4096]{1,0:T(8,128)(2,1)S(1)}, u32[]{:S(2)}, u32[]{:S(2)}) collective-permute-start(bf16[96,4096]{1,0:T(8,128)(2,1)S(1)} %collective-permute-done.10.one), channel_id=1, source_target_pairs={{0,8},{8,0},{1,9},{9,1},{2,10},{10,2},{3,11},{11,3},{4,12},{12,4},... | collective-permute-start | bytes 2359304 | tf_op jit(solution)/shard_map/ppermute | solution.py:295
  76.7 1.4 %collective-permute-start.16 = (f32[256,128]{1,0:T(8,128)S(1)}, f32[256,128]{1,0:T(8,128)S(1)}, u32[]{:S(2)}, u32[]{:S(2)}) collective-permute-start(f32[256,128]{1,0:T(8,128)S(1)} %get-tuple-element.57), channel_id=1, source_target_pairs={{0,8},{8,0},{1,9},{9,1},{2,10},{10,2},{3,11},{11,3},{4,12},{12,4},... | collective-permute-start | bytes 393224 | tf_op jit(solution)/shard_map/ppermute | solution.py:301
  78.1 4.3 %collective-permute-start.17 = (bf16[256,128]{1,0:T(8,128)(2,1)S(1)}, bf16[256,128]{1,0:T(8,128)(2,1)S(1)}, u32[]{:S(2)}, u32[]{:S(2)}) collective-permute-start(bf16[256,128]{1,0:T(8,128)(2,1)S(1)} %get-tuple-element.61), channel_id=1, source_target_pairs={{0,1},{1,0},{2,3},{3,2},{4,5},{5,4},{6,7},{7,6},{8,9},{9,8},{10,11... | collective-permute-start | bytes 196616 | tf_op jit(solution)/shard_map/ppermute | solution.py:310
  78.7 4.3 %collective-permute-start.18 = (bf16[256,128]{1,0:T(8,128)(2,1)S(1)}, bf16[256,128]{1,0:T(8,128)(2,1)S(1)}, u32[]{:S(2)}, u32[]{:S(2)}) collective-permute-start(bf16[256,128]{1,0:T(8,128)(2,1)S(1)} %get-tuple-element.61), channel_id=1, source_target_pairs={{0,2},{1,3},{2,0},{3,1},{4,6},{5,7},{6,4},{7,5},{8,10},{9,11},{10,... | collective-permute-start | bytes 196616 | tf_op jit(solution)/shard_map/ppermute | solution.py:310
  80.3 5.2 %collective-permute-start.19 = (bf16[256,128]{1,0:T(8,128)(2,1)S(1)}, bf16[256,128]{1,0:T(8,128)(2,1)S(1)}, u32[]{:S(2)}, u32[]{:S(2)}) collective-permute-start(bf16[256,128]{1,0:T(8,128)(2,1)S(1)} %get-tuple-element.61), channel_id=1, source_target_pairs={{0,3},{1,2},{2,1},{3,0},{4,7},{5,6},{6,5},{7,4},{8,11},{9,10},{10,... | collective-permute-start | bytes 196616 | tf_op jit(solution)/shard_map/ppermute | solution.py:310
  85.5 5.2 %collective-permute-start.20 = (bf16[256,128]{1,0:T(8,128)(2,1)S(1)}, bf16[256,128]{1,0:T(8,128)(2,1)S(1)}, u32[]{:S(2)}, u32[]{:S(2)}) collective-permute-start(bf16[256,128]{1,0:T(8,128)(2,1)S(1)} %get-tuple-element.59), channel_id=1, source_target_pairs={{0,4},{1,5},{2,6},{3,7},{4,0},{5,1},{6,2},{7,3},{8,12},{9,13},{10,... | collective-permute-start | bytes 196616 | tf_op jit(solution)/shard_map/ppermute | solution.py:310
  (1 other events, 0.7 us)

commit v8 on v7

--- a/solution.py
+++ b/solution.py
@@ -52,24 +52,41 @@
     return high, (value - high.astype(jnp.float32)).astype(jnp.bfloat16)
 
 
-def gradients(pre, cotangents, both):
+def chunks_of(hidden):
+    tiles = hidden // LANES
+    if tiles < 4:
+        return [(0, hidden)]
+    size = tiles // 2
+    sizes = [size, tiles - 1 - size, 1]
+    firsts = [0, size, tiles - 1]
+    return [(f * LANES, c * LANES) for f, c in zip(firsts, sizes)]
+
+
+def columns_of(hidden):
+    spans, at = [], 0
+    for i, (_, count) in enumerate(chunks_of(hidden)):
+        width = 2 * count + (LANES if i == 0 else 0)
+        spans.append((at, width))
+        at += width
+    return spans
+
+
+def gradients(pre, cotangents, both, first, count):
     hidden = both.shape[1] // 2
     for i, cotangent in enumerate(cotangents):
         here = slice(i * CHUNK, (i + 1) * CHUNK)
-        gate = pre[here, :hidden]
-        up = pre[here, hidden : 2 * hidden]
+        gate = pre[here, :count]
+        up = pre[here, count : 2 * count]
         sig = 0.5 * (1.0 + jnp.tanh(0.5 * gate))
-        scaled = cotangent().astype(jnp.float32) * sig
-        both[here, hidden:] = (scaled * gate).astype(jnp.bfloat16)
-        both[here, :hidden] = (scaled * up * (1.0 + gate * (1.0 - sig))).astype(jnp.bfloat16)
-
-
-def sketch_of(starts, rows, lengths, pre, both, diagonal):
-    grads = jnp.dot(both[...], diagonal[...], preferred_element_type=jnp.float32)
-    grads_high, grads_low = split(grads)
-    grads_both = jnp.concatenate([grads_high, grads_low], axis=1)
+        scaled = cotangent(first, count).astype(jnp.float32) * sig
+        both[here, hidden + first : hidden + first + count] = (scaled * gate).astype(jnp.bfloat16)
+        both[here, first : first + count] = (
+            scaled * up * (1.0 + gate * (1.0 - sig))
+        ).astype(jnp.bfloat16)
+
+
+def weighted_acts(starts, rows, lengths, acts):
     seq_count = lengths.shape[0]
-    acts = pre[:, both.shape[1] :]
     position = []
     for start in starts:
         position.append(start + lax.broadcasted_iota(jnp.int32, (rows, LANES), 0))
@@ -86,39 +103,51 @@
         high, rest = split(weighted)
         highs.append(high)
         lows.append(rest)
+    return jnp.concatenate(highs, axis=1), jnp.concatenate(lows, axis=1)
+
+
+def sketch_of(acts_high, acts_low, both, diagonal):
+    grads = jnp.dot(both[...], diagonal[...], preferred_element_type=jnp.float32)
+    grads_high, grads_low = split(grads)
+    grads_both = jnp.concatenate([grads_high, grads_low], axis=1)
     over_rows = (((0,), (0,)), ((), ()))
-    main = lax.dot_general(
-        jnp.concatenate(highs, axis=1),
-        grads_both,
-        over_rows,
-        preferred_element_type=jnp.float32,
-    )
-    rest = lax.dot_general(
-        jnp.concatenate(lows, axis=1), grads_high, over_rows, preferred_element_type=jnp.float32
-    )
+    main = lax.dot_general(acts_high, grads_both, over_rows, preferred_element_type=jnp.float32)
+    rest = lax.dot_general(acts_low, grads_high, over_rows, preferred_element_type=jnp.float32)
     return main[:, :LANES] + main[:, LANES:] + rest
 
 
-def load_kernel(
-    table, lengths, gate_hbm, up_hbm, out_grad_hbm, proj_out_hbm, proj_in,
-    w, out_grad, diagonal, sems,
-):
-    hidden = gate_hbm.shape[1]
+def small_kernel(table, lengths, out_grad_hbm, proj_out_hbm, out_grad, diagonal, sems):
+    hidden = proj_out_hbm.shape[0]
     upper = pltpu.make_async_copy(proj_out_hbm, diagonal.at[pl.ds(0, hidden)], sems.at[0])
-    copies = [
-        pltpu.make_async_copy(gate_hbm, w.at[:, pl.ds(0, hidden)], sems.at[1]),
-        pltpu.make_async_copy(up_hbm, w.at[:, pl.ds(hidden, hidden)], sems.at[2]),
-        pltpu.make_async_copy(out_grad_hbm, out_grad, sems.at[3]),
-    ]
-    for copy in [upper] + copies:
-        copy.start()
-    w[:, 2 * hidden :] = jnp.concatenate([proj_in[...], proj_in[...]], axis=1)
+    whole = pltpu.make_async_copy(out_grad_hbm, out_grad, sems.at[1])
+    upper.start()
+    whole.start()
     upper.wait()
     values = diagonal[:hidden, :]
     left = lax.broadcasted_iota(jnp.int32, values.shape, 1) < LANES // 2
     none = jnp.zeros_like(values)
     diagonal[hidden:, :] = jnp.where(left, none, values)
     diagonal[:hidden, :] = jnp.where(left, values, none)
+    whole.wait()
+
+
+def load_kernel(lengths, diagonal, gate_hbm, up_hbm, proj_in, w, sems):
+    hidden = gate_hbm.shape[1]
+    copies = []
+    for i, (first, count) in enumerate(chunks_of(hidden)):
+        at = columns_of(hidden)[i][0]
+        for j, source in enumerate((gate_hbm, up_hbm)):
+            copies.append(
+                pltpu.make_async_copy(
+                    source.at[:, pl.ds(first, count)],
+                    w.at[:, pl.ds(at + j * count, count)],
+                    sems.at[i, j],
+                )
+            )
+    for copy in copies:
+        copy.start()
+    at, width = columns_of(hidden)[0]
+    w[:, at + width - LANES : at + width] = jnp.concatenate([proj_in[...], proj_in[...]], axis=1)
     for copy in copies:
         copy.wait()
 
@@ -128,20 +157,28 @@
     for start in starts:
         for row in range(0, rows, CHUNK):
             here = pl.ds(pl.multiple_of(start + row, CHUNK), CHUNK)
-            chunks.append(lambda here=here: out_grad[here, :])
+            chunks.append(
+                lambda first, count, here=here: out_grad[here, first : first + count]
+            )
     return chunks
 
 
 def step_kernel(entry, first, last, table, lengths, one, two, w, out_grad, diagonal, *refs):
-    outs, (pre, both) = refs[:-2], refs[-2:]
+    hidden = out_grad.shape[1]
+    chunks = chunks_of(hidden)
+    outs, pres, both = refs[: -1 - len(chunks)], refs[-1 - len(chunks) : -1], refs[-1]
     if not first:
         before, outs = outs[0], outs[1:]
     rows = one.shape[0]
     starts = [table[entry], table[entry + 1]]
-    x = jnp.concatenate([one[...], two[...]], axis=0)
-    pre[...] = jnp.dot(x, w[...], preferred_element_type=jnp.float32)
-    gradients(pre, cotangent_chunks(out_grad, starts, rows), both)
-    total = sketch_of(starts, rows, lengths, pre, both, diagonal)
+    cotangents = cotangent_chunks(out_grad, starts, rows)
+    for i, (at, width) in enumerate(columns_of(hidden)):
+        x = jnp.concatenate([one[...], two[...]], axis=0)
+        pres[i][...] = jnp.dot(x, w[:, at : at + width], preferred_element_type=jnp.float32)
+        if i == 0:
+            acts = weighted_acts(starts, rows, lengths, pres[0][:, width - LANES :])
+        gradients(pres[i], cotangents, both, *chunks[i])
+    total = sketch_of(*acts, both, diagonal)
     if not first:
         total += before[...]
     if not last:
@@ -161,24 +198,35 @@
     )
 
 
-def load(table, lengths, w_gate, w_up, out_grad, proj_in, proj_out):
-    width, hidden = w_gate.shape
-    w_gate, w_up, out_grad, proj_out = [
-        pltpu.with_memory_space_constraint(a, pltpu.HBM)
-        for a in (w_gate, w_up, out_grad, proj_out)
+def load_small(table, lengths, out_grad, proj_out):
+    out_grad, proj_out = [
+        pltpu.with_memory_space_constraint(a, pltpu.HBM) for a in (out_grad, proj_out)
     ]
+    hidden = out_grad.shape[1]
     return pl.pallas_call(
-        load_kernel,
+        small_kernel,
         out_shape=[
-            pltpu.VMEM((width, 2 * hidden + LANES), jnp.bfloat16),
             pltpu.VMEM(out_grad.shape, jnp.bfloat16),
             pltpu.VMEM((2 * hidden, LANES), jnp.bfloat16),
         ],
-        in_specs=[SMEM, SMEM] + [ANY] * 4 + [VMEM],
-        out_specs=[VMEM] * 3,
-        scratch_shapes=[pltpu.SemaphoreType.DMA((4,))],
+        in_specs=[SMEM, SMEM, ANY, ANY],
+        out_specs=[VMEM] * 2,
+        scratch_shapes=[pltpu.SemaphoreType.DMA((2,))],
         compiler_params=pltpu.CompilerParams(vmem_limit_bytes=16 * 2**20),
-    )(table, lengths, w_gate, w_up, out_grad, proj_out, proj_in)
+    )(table, lengths, out_grad, proj_out)
+
+
+def load(lengths, diagonal, w_gate, w_up, proj_in):
+    width, hidden = w_gate.shape
+    w_gate, w_up = [pltpu.with_memory_space_constraint(a, pltpu.HBM) for a in (w_gate, w_up)]
+    return pl.pallas_call(
+        load_kernel,
+        out_shape=pltpu.VMEM((width, 2 * hidden + LANES), jnp.bfloat16),
+        in_specs=[SMEM, VMEM, ANY, ANY, VMEM],
+        out_specs=VMEM,
+        scratch_shapes=[pltpu.SemaphoreType.DMA((len(chunks_of(hidden)), 2))],
+        compiler_params=pltpu.CompilerParams(vmem_limit_bytes=16 * 2**20),
+    )(lengths, diagonal, w_gate, w_up, proj_in)
 
 
 def add_step(blocks, entry, total, table, lengths, weights, last=False):
@@ -196,7 +244,10 @@
         in_specs=[SMEM, SMEM] + [VMEM] * len(operands),
         out_specs=[VMEM] * len(out_shape),
         scratch_shapes=[
-            pltpu.VMEM((2 * rows, w.shape[1]), jnp.float32),
+            *[
+                pltpu.VMEM((2 * rows, columns), jnp.float32)
+                for _, columns in columns_of(diagonal.shape[0] // 2)
+            ],
             pltpu.VMEM((2 * rows, diagonal.shape[0]), jnp.bfloat16),
         ],
         compiler_params=pltpu.CompilerParams(vmem_limit_bytes=16 * 2**20),
@@ -267,9 +318,10 @@
     after = lax.optimization_barrier
     one_way = send_one(tokens_in)
     other, other_val = swap(tokens_in), swap(val_sketch)
-    w, out_grad, diagonal = load(table, lengths, w_gate, w_up, out_grad, proj_in, proj_out)
+    out_grad, diagonal = load_small(table, lengths, out_grad, proj_out)
     later_tokens, diagonal = after((tokens_in, diagonal))
     two_way = send_two(later_tokens)
+    w = load(lengths, diagonal, w_gate, w_up, proj_in)
     add = functools.partial(
         add_step, table=table, lengths=lengths, weights=[w, out_grad, diagonal]
     )

time: 92.8 us -> 99.7 us (1.074)
  Pallas kernels: 45.7 us -> 50 us
  local copies, waits for them, and re-layouts: 2.88 us -> 5.2 us
  starting transfers between devices: 19.6 us -> 21.1 us
  waiting for transfers between devices: 24.2 us -> 22.8 us
    ppermute x3, waiting for transfers between devices: 0.01 us -> 11.5 us  [fast(): next_one = send_one(one_way)]
    ppermute x1, waiting for transfers between devices: 8.48 us -> 0.01 us  [fast(): two_way = send_two(later_tokens)]
    ppermute x2, waiting for transfers between devices: 8.19 us -> 2.46 us  [fast(): next_two = send_two(two_way) if k + 1 < n // 2 else None]
    ppermute x4, starting transfers between devices: 4.51 us -> 0.41 us  [fast(): swapped_one = swap(one_way)]
    ppermute x2, starting transfers between devices: 0.01 us -> 2.9 us  [fast(): next_two = send_two(two_way) if k + 1 < n // 2 else None]
    pallas_call x8, Pallas kernels: 37.2 us -> 39.6 us  [add_step(): pl.pallas_call(functools.partial(step_kernel, entry, first, last), out_sh...]
    unnamed x9 -> x13, local copies, waits for them, and re-layouts: 2.18 us -> 4.51 us
    pallas_call x1 -> x2, Pallas kernels: 6.7 us -> 8.59 us  [the longest x1 6.11 us: load(): pl.pallas_call(load_kernel, out_shape=pltpu.VMEM((width, 2 * hidden + LAN...]
  transfers between devices with their start and end apart: 21 -> 21, of which waited for: 8 -> 8; matrix products, arithmetic and copies ran while one was open for 2% -> 2% of each run, Pallas kernels for 42% -> 44%
where the time goes in v8:
time: 99.7 us; the launch traced here: 99.3 us
  Pallas kernels  50 us (50%)
  waiting for transfers between devices  22.8 us (23%)
  starting transfers between devices  21.1 us (21%)
  local copies, waits for them, and re-layouts  5.2 us (5%)
    pallas_call x8, Pallas kernels, add_step(): pl.pallas_call(functools.partial(step_kernel, entry, first, last), out_sh...  39.6 us
    ppermute x3, waiting for transfers between devices, fast(): next_one = send_one(one_way)  11.5 us
    ppermute x4, waiting for transfers between devices, fast(): lax.ppermute(sent, 'mp', [(i, i ^ flip) for i in range(n)])  7.87 us
    ppermute x4, starting transfers between devices, fast(): lax.ppermute(sent, 'mp', [(i, i ^ flip) for i in range(n)])  6.77 us
    pallas_call x1, Pallas kernels, load(): pl.pallas_call(load_kernel, out_shape=pltpu.VMEM((width, 2 * hidden + LAN...  6.11 us
    ppermute x3, starting transfers between devices, fast(): next_one = send_one(one_way)  5.58 us
    unnamed x13, local copies, waits for them, and re-layouts  4.51 us
    ppermute x2, starting transfers between devices, fast(): next_two = send_two(two_way) if k + 1 < n // 2 else None  2.9 us
  transfers between devices with their start and end apart: 21, of which 8 were waited for; matrix products, arithmetic and copies ran while one was open for 2% of the time, Pallas kernels for 44%

profile of v8, /device:TPU:0, one launch (start us, length us, event | category | flops | bytes accessed | tf_op | source)
XLA Modules:
  0.0 99.3 jit_solution(16081534990067492990)
XLA Ops:
  0.5 2.6 %collective-permute-start = (bf16[96,4096]{1,0:T(8,128)(2,1)}, bf16[96,4096]{1,0:T(8,128)(2,1)S(1)}, u32[]{:S(2)}, u32[]{:S(2)}) collective-permute-start(bf16[96,4096]{1,0:T(8,128)(2,1)} %one.1), channel_id=1, source_target_pairs={{0,2},{2,4},{4,6},{6,7},{7,5},{5,3},{3,1},{1,0},{10,8},{12,10},{14... | collective-permute-start | bytes 2359304 | tf_op jit(solution)/shard_map/ppermute | solution.py:319
  4.4 2.5 %shard_map.91 = (bf16[1536,896]{1,0:T(8,128)(2,1)S(1)}, bf16[1792,128]{1,0:T(8,128)(2,1)S(1)}) custom-call(s32[17]{0:T(128)S(1)} %dynamic-slice_bitcast_fusion.table, s32[8]{0:T(128)S(1)} %copy-done.1, bf16[1536,896]{1,0:T(8,128)(2,1)} %out_grad_hbm.1, bf16[896,128]{1,0:T(8,128)(2,1)} %proj_out_hbm.1), custom_call_target="tpu_custom_call" | custom-call | tf_op jit(solution)/shard_map/pallas_call | solution.py:206
  6.9 1.5 %copy-done.3 = bf16[1536,896]{1,0:T(8,128)(2,1)} copy-done((bf16[1536,896]{1,0:T(8,128)(2,1)}, bf16[1536,896]{1,0:T(8,128)(2,1)S(1)}, u32[]{:S(2)}) %copy-start.3) | copy-done | bytes 2752536
  10.8 6.1 %shard_map.92.w = bf16[4096,1920]{1,0:T(8,128)(2,1)S(1)} custom-call(s32[8]{0:T(128)S(1)} %copy-done.2, bf16[1792,128]{1,0:T(8,128)(2,1)S(1)} %get-tuple-element.32.diagonal, bf16[4096,896]{1,0:T(8,128)(2,1)} %gate_hbm.1, bf16[4096,896]{1,0:T(8,128)(2,1)} %up_hbm.1, bf16[4096,64]{1,0:T(8,128)(2,1)S(1)} %copy.10.proj_in), custom_call_target="tpu_custom_call" | custom-call | tf_op jit(solution)/shard_map/pallas_call | solution.py:222
  17.1 5.4 %shard_map.93.refs_0_ = f32[512,128]{1,0:T(8,128)S(1)} custom-call(s32[17]{0:T(128)S(1)} %dynamic-slice_bitcast_fusion.table, s32[8]{0:T(128)S(1)} %copy-done.2, bf16[96,4096]{1,0:T(8,128)(2,1)S(1)} %copy-done.5, bf16[96,4096]{1,0:T(8,128)(2,1)} %collective-permute-done.1.two, bf16[4096,1920]{1,0:T(8,128)(2,1)S(1)} %shard_map.92.w, ...), custom_call_target="tpu_custom_call" | custom-call | flops 6039797760 | bytes 1572864 | tf_op jit(solution)/shard_map/pallas_call | solution.py:241
  22.8 2.0 %collective-permute-start.2 = (bf16[96,4096]{1,0:T(8,128)(2,1)S(1)}, bf16[96,4096]{1,0:T(8,128)(2,1)S(1)}, u32[]{:S(2)}, u32[]{:S(2)}) collective-permute-start(bf16[96,4096]{1,0:T(8,128)(2,1)S(1)} %collective-permute-done.one), channel_id=1, source_target_pairs={{0,2},{2,4},{4,6},{6,7},{7,5},{5,3},{3,1},{1,0},{10,8},{12,10},{14... | collective-permute-start | bytes 2359304 | tf_op jit(solution)/shard_map/ppermute | solution.py:333
  26.2 4.8 %shard_map.94.refs_0_ = f32[512,128]{1,0:T(8,128)S(1)} custom-call(s32[17]{0:T(128)S(1)} %dynamic-slice_bitcast_fusion.table, s32[8]{0:T(128)S(1)} %copy-done.2, bf16[96,4096]{1,0:T(8,128)(2,1)S(1)} %collective-permute-done.one, bf16[96,4096]{1,0:T(8,128)(2,1)S(1)} %collective-permute-done.5.two, bf16[4096,1920]{1,0:T(8,128)(2,1)S(1)} %shard_map.92.w, ...), custom_call_target="tpu_custom_call" | custom-call | flops 6039797760 | bytes 1572864 | tf_op jit(solution)/shard_map/pallas_call | solution.py:241
  30.9 10.5 %collective-permute-done.2.one = bf16[96,4096]{1,0:T(8,128)(2,1)S(1)} collective-permute-done((bf16[96,4096]{1,0:T(8,128)(2,1)S(1)}, bf16[96,4096]{1,0:T(8,128)(2,1)S(1)}, u32[]{:S(2)}, u32[]{:S(2)}) %collective-permute-start.2) | collective-permute-done | bytes 786464 | tf_op jit(solution)/shard_map/ppermute | solution.py:333
  41.4 2.5 %collective-permute-start.6 = (bf16[96,4096]{1,0:T(8,128)(2,1)S(1)}, bf16[96,4096]{1,0:T(8,128)(2,1)S(1)}, u32[]{:S(2)}, u32[]{:S(2)}) collective-permute-start(bf16[96,4096]{1,0:T(8,128)(2,1)S(1)} %collective-permute-done.2.one), channel_id=1, source_target_pairs={{0,2},{2,4},{4,6},{6,7},{7,5},{5,3},{3,1},{1,0},{10,8},{12,10},{14... | collective-permute-start | bytes 2359304 | tf_op jit(solution)/shard_map/ppermute | solution.py:333
  43.9 5.4 %shard_map.95.refs_0_ = f32[512,128]{1,0:T(8,128)S(1)} custom-call(s32[17]{0:T(128)S(1)} %dynamic-slice_bitcast_fusion.table, s32[8]{0:T(128)S(1)} %copy-done.2, bf16[96,4096]{1,0:T(8,128)(2,1)} %collective-permute-done.3.one, bf16[96,4096]{1,0:T(8,128)(2,1)S(1)} %collective-permute-done.8.two, bf16[4096,1920]{1,0:T(8,128)(2,1)S(1)} %shard_map.92.w, ...), custom_call_target="tpu_custom_call" | custom-call | flops 6039797760 | bytes 1572864 | tf_op jit(solution)/shard_map/pallas_call | solution.py:241
  50.3 1.6 %collective-permute-start.11 = (bf16[96,4096]{1,0:T(8,128)(2,1)S(1)}, bf16[96,4096]{1,0:T(8,128)(2,1)S(1)}, u32[]{:S(2)}, u32[]{:S(2)}) collective-permute-start(bf16[96,4096]{1,0:T(8,128)(2,1)S(1)} %collective-permute-done.7.one), channel_id=1, source_target_pairs={{2,0},{4,2},{6,4},{7,6},{5,7},{3,5},{1,3},{0,1},{8,10},{10,12},{12... | collective-permute-start | bytes 2359304 | tf_op jit(solution)/shard_map/ppermute | solution.py:339
  51.9 4.8 %shard_map.96.refs_0_ = f32[512,128]{1,0:T(8,128)S(1)} custom-call(s32[17]{0:T(128)S(1)} %dynamic-slice_bitcast_fusion.table, s32[8]{0:T(128)S(1)} %copy-done.2, bf16[96,4096]{1,0:T(8,128)(2,1)S(1)} %collective-permute-done.2.one, bf16[96,4096]{1,0:T(8,128)(2,1)S(1)} %collective-permute-done.9.two, bf16[4096,1920]{1,0:T(8,128)(2,1)S(1)} %shard_map.92.w, ...), custom_call_target="tpu_custom_call" | custom-call | flops 6039797760 | bytes 1572864 | tf_op jit(solution)/shard_map/pallas_call | solution.py:241
  57.9 4.8 %shard_map.97.refs_0_ = f32[512,128]{1,0:T(8,128)S(1)} custom-call(s32[17]{0:T(128)S(1)} %dynamic-slice_bitcast_fusion.table, s32[8]{0:T(128)S(1)} %copy-done.2, bf16[96,4096]{1,0:T(8,128)(2,1)S(1)} %collective-permute-done.7.one, bf16[96,4096]{1,0:T(8,128)(2,1)S(1)} %collective-permute-done.12.two, bf16[4096,1920]{1,0:T(8,128)(2,1)S(1)} %shard_map.92.w, ...), custom_call_target="tpu_custom_call" | custom-call | flops 6039797760 | bytes 1572864 | tf_op jit(solution)/shard_map/pallas_call | solution.py:241
  62.6 2.5 %collective-permute-done.11.one = bf16[96,4096]{1,0:T(8,128)(2,1)S(1)} collective-permute-done((bf16[96,4096]{1,0:T(8,128)(2,1)S(1)}, bf16[96,4096]{1,0:T(8,128)(2,1)S(1)}, u32[]{:S(2)}, u32[]{:S(2)}) %collective-permute-start.11) | collective-permute-done | bytes 786464 | tf_op jit(solution)/shard_map/ppermute | solution.py:339
  65.6 4.8 %shard_map.98.refs_0_ = f32[512,128]{1,0:T(8,128)S(1)} custom-call(s32[17]{0:T(128)S(1)} %dynamic-slice_bitcast_fusion.table, s32[8]{0:T(128)S(1)} %copy-done.2, bf16[96,4096]{1,0:T(8,128)(2,1)S(1)} %collective-permute-done.6.one, bf16[96,4096]{1,0:T(8,128)(2,1)S(1)} %collective-permute-done.13.two, bf16[4096,1920]{1,0:T(8,128)(2,1)S(1)} %shard_map.92.w, ...), custom_call_target="tpu_custom_call" | custom-call | flops 6039797760 | bytes 1572864 | tf_op jit(solution)/shard_map/pallas_call | solution.py:241
  71.4 4.8 %shard_map.99.refs_0_ = f32[512,128]{1,0:T(8,128)S(1)} custom-call(s32[17]{0:T(128)S(1)} %dynamic-slice_bitcast_fusion.table, s32[8]{0:T(128)S(1)} %copy-done.2, bf16[96,4096]{1,0:T(8,128)(2,1)S(1)} %collective-permute-done.11.one, bf16[96,4096]{1,0:T(8,128)(2,1)S(1)} %collective-permute-done.15.two, bf16[4096,1920]{1,0:T(8,128)(2,1)S(1)} %shard_map.92.w, ...), custom_call_target="tpu_custom_call" | custom-call | flops 6039797760 | bytes 1572864 | tf_op jit(solution)/shard_map/pallas_call | solution.py:241
  76.2 5.0 %shard_map.100 = (f32[256,128]{1,0:T(8,128)S(1)}, f32[256,128]{1,0:T(8,128)S(1)}) custom-call(s32[17]{0:T(128)S(1)} %dynamic-slice_bitcast_fusion.table, s32[8]{0:T(128)S(1)} %copy-done.2, bf16[96,4096]{1,0:T(8,128)(2,1)S(1)} %collective-permute-done.10.one, bf16[96,4096]{1,0:T(8,128)(2,1)S(1)} %collective-permute-done.14.two, ...), custom_call_target="tpu_custom_call" | custom-call | flops 6039797760 | bytes 1572864 | tf_op jit(solution)/shard_map/pallas_call | solution.py:241
  82.8 2.1 %collective-permute-start.17 = (bf16[256,128]{1,0:T(8,128)(2,1)S(1)}, bf16[256,128]{1,0:T(8,128)(2,1)S(1)}, u32[]{:S(2)}, u32[]{:S(2)}) collective-permute-start(bf16[256,128]{1,0:T(8,128)(2,1)S(1)} %get-tuple-element.59), channel_id=1, source_target_pairs={{0,1},{1,0},{2,3},{3,2},{4,5},{5,4},{6,7},{7,6},{8,9},{9,8},{10,11... | collective-permute-start | bytes 196616 | tf_op jit(solution)/shard_map/ppermute | solution.py:362
  84.9 1.6 %collective-permute-start.18 = (bf16[256,128]{1,0:T(8,128)(2,1)S(1)}, bf16[256,128]{1,0:T(8,128)(2,1)S(1)}, u32[]{:S(2)}, u32[]{:S(2)}) collective-permute-start(bf16[256,128]{1,0:T(8,128)(2,1)S(1)} %get-tuple-element.59), channel_id=1, source_target_pairs={{0,2},{1,3},{2,0},{3,1},{4,6},{5,7},{6,4},{7,5},{8,10},{9,11},{10,... | collective-permute-start | bytes 196616 | tf_op jit(solution)/shard_map/ppermute | solution.py:362
  87.5 2.2 %collective-permute-done.18 = bf16[256,128]{1,0:T(8,128)(2,1)S(1)} collective-permute-done((bf16[256,128]{1,0:T(8,128)(2,1)S(1)}, bf16[256,128]{1,0:T(8,128)(2,1)S(1)}, u32[]{:S(2)}, u32[]{:S(2)}) %collective-permute-start.18) | collective-permute-done | bytes 65568 | tf_op jit(solution)/shard_map/ppermute | solution.py:362
  89.7 2.0 %collective-permute-done.19 = bf16[256,128]{1,0:T(8,128)(2,1)S(1)} collective-permute-done((bf16[256,128]{1,0:T(8,128)(2,1)S(1)}, bf16[256,128]{1,0:T(8,128)(2,1)S(1)}, u32[]{:S(2)}, u32[]{:S(2)}) %collective-permute-start.19) | collective-permute-done | bytes 65568 | tf_op jit(solution)/shard_map/ppermute | solution.py:362
  91.7 3.1 %collective-permute-start.20 = (bf16[256,128]{1,0:T(8,128)(2,1)S(1)}, bf16[256,128]{1,0:T(8,128)(2,1)S(1)}, u32[]{:S(2)}, u32[]{:S(2)}) collective-permute-start(bf16[256,128]{1,0:T(8,128)(2,1)S(1)} %get-tuple-element.57), channel_id=1, source_target_pairs={{0,4},{1,5},{2,6},{3,7},{4,0},{5,1},{6,2},{7,3},{8,12},{9,13},{10,... | collective-permute-start | bytes 196616 | tf_op jit(solution)/shard_map/ppermute | solution.py:362
  94.8 2.7 %collective-permute-done.20.theirs = bf16[256,128]{1,0:T(8,128)(2,1)S(1)} collective-permute-done((bf16[256,128]{1,0:T(8,128)(2,1)S(1)}, bf16[256,128]{1,0:T(8,128)(2,1)S(1)}, u32[]{:S(2)}, u32[]{:S(2)}) %collective-permute-start.20) | collective-permute-done | bytes 65568 | tf_op jit(solution)/shard_map/ppermute | solution.py:362
  97.5 1.8 %shard_map.101 = f32[4,128]{1,0:T(4,128)} custom-call(s32[17]{0:T(128)S(1)} %dynamic-slice_bitcast_fusion.table, f32[256,128]{1,0:T(8,128)S(1)} %get-tuple-element.58.mine, bf16[256,128]{1,0:T(8,128)(2,1)S(1)} %collective-permute-done.20.theirs, bf16[128,4096]{1,0:T(8,128)(2,1)S(1)} %copy-done, bf16[128,4096]{1,0:T(8,128)(2,1)S(1)} %collective-permute-done.4.val_other), custom_call_target="tpu_custom_call" | custom-call | tf_op jit(solution)/shard_map/pallas_call | solution.py:293
  (45 shorter events, 12.4 us)
Async XLA Ops:
  0.0 16.9 %collective-permute-start.1 = (bf16[96,4096]{1,0:T(8,128)(2,1)}, bf16[96,4096]{1,0:T(8,128)(2,1)}, u32[]{:S(2)}, u32[]{:S(2)}) collective-permute-start(bf16[96,4096]{1,0:T(8,128)(2,1)} %one.1), channel_id=1, source_target_pairs={{0,8},{8,0},{1,9},{9,1},{2,10},{10,2},{3,11},{11,3},{4,12},{12,4},... | collective-permute-start | bytes 2359304 | tf_op jit(solution)/shard_map/ppermute | solution.py:320
  0.5 22.0 %collective-permute-start = (bf16[96,4096]{1,0:T(8,128)(2,1)}, bf16[96,4096]{1,0:T(8,128)(2,1)S(1)}, u32[]{:S(2)}, u32[]{:S(2)}) collective-permute-start(bf16[96,4096]{1,0:T(8,128)(2,1)} %one.1), channel_id=1, source_target_pairs={{0,2},{2,4},{4,6},{6,7},{7,5},{5,3},{3,1},{1,0},{10,8},{12,10},{14... | collective-permute-start | bytes 2359304 | tf_op jit(solution)/shard_map/ppermute | solution.py:319
  8.4 16.5 %collective-permute-start.3 = (bf16[96,4096]{1,0:T(8,128)(2,1)}, bf16[96,4096]{1,0:T(8,128)(2,1)}, u32[]{:S(2)}, u32[]{:S(2)}) collective-permute-start(bf16[96,4096]{1,0:T(8,128)(2,1)} %one.1), channel_id=1, source_target_pairs={{2,0},{4,2},{6,4},{7,6},{5,7},{3,5},{1,3},{0,1},{8,10},{10,12},{12... | collective-permute-start | bytes 2359304 | tf_op jit(solution)/shard_map/ppermute | solution.py:323
  8.4 16.5 %collective-permute-start.4 = (bf16[128,4096]{1,0:T(8,128)(2,1)}, bf16[128,4096]{1,0:T(8,128)(2,1)S(1)}, u32[]{:S(2)}, u32[]{:S(2)}) collective-permute-start(bf16[128,4096]{1,0:T(8,128)(2,1)} %val_own.1), channel_id=1, source_target_pairs={{0,8},{8,0},{1,9},{9,1},{2,10},{10,2},{3,11},{11,3},{4,12},{12,4},... | collective-permute-start | bytes 3145736 | tf_op jit(solution)/shard_map/ppermute | solution.py:320
  10.8 6.1 %copy-start.4 = (bf16[1536,896]{1,0:T(8,128)(2,1)S(1)}, bf16[1536,896]{1,0:T(8,128)(2,1)}, u32[]{:S(2)}) copy-start(bf16[1536,896]{1,0:T(8,128)(2,1)} %copy-done.3) | copy-start | bytes 8257540
  10.8 6.3 %copy-start.5 = (bf16[96,4096]{1,0:T(8,128)(2,1)S(1)}, bf16[96,4096]{1,0:T(8,128)(2,1)}, u32[]{:S(2)}) copy-start(bf16[96,4096]{1,0:T(8,128)(2,1)} %one.1) | copy-start | bytes 2359300
  22.5 3.7 %collective-permute-start.5 = (bf16[96,4096]{1,0:T(8,128)(2,1)S(1)}, bf16[96,4096]{1,0:T(8,128)(2,1)S(1)}, u32[]{:S(2)}, u32[]{:S(2)}) collective-permute-start(bf16[96,4096]{1,0:T(8,128)(2,1)S(1)} %collective-permute-done.one), channel_id=1, source_target_pairs={{0,8},{8,0},{1,9},{9,1},{2,10},{10,2},{3,11},{11,3},{4,12},{12,4},... | collective-permute-start | bytes 2359304 | tf_op jit(solution)/shard_map/ppermute | solution.py:334
  22.8 18.6 %collective-permute-start.2 = (bf16[96,4096]{1,0:T(8,128)(2,1)S(1)}, bf16[96,4096]{1,0:T(8,128)(2,1)S(1)}, u32[]{:S(2)}, u32[]{:S(2)}) collective-permute-start(bf16[96,4096]{1,0:T(8,128)(2,1)S(1)} %collective-permute-done.one), channel_id=1, source_target_pairs={{0,2},{2,4},{4,6},{6,7},{7,5},{5,3},{3,1},{1,0},{10,8},{12,10},{14... | collective-permute-start | bytes 2359304 | tf_op jit(solution)/shard_map/ppermute | solution.py:333
  24.9 19.0 %collective-permute-start.8 = (bf16[96,4096]{1,0:T(8,128)(2,1)}, bf16[96,4096]{1,0:T(8,128)(2,1)S(1)}, u32[]{:S(2)}, u32[]{:S(2)}) collective-permute-start(bf16[96,4096]{1,0:T(8,128)(2,1)} %collective-permute-done.3.one), channel_id=1, source_target_pairs={{0,8},{8,0},{1,9},{9,1},{2,10},{10,2},{3,11},{11,3},{4,12},{12,4},... | collective-permute-start | bytes 2359304 | tf_op jit(solution)/shard_map/ppermute | solution.py:340
  24.9 24.4 %collective-permute-start.7 = (bf16[96,4096]{1,0:T(8,128)(2,1)}, bf16[96,4096]{1,0:T(8,128)(2,1)S(1)}, u32[]{:S(2)}, u32[]{:S(2)}) collective-permute-start(bf16[96,4096]{1,0:T(8,128)(2,1)} %collective-permute-done.3.one), channel_id=1, source_target_pairs={{2,0},{4,2},{6,4},{7,6},{5,7},{3,5},{1,3},{0,1},{8,10},{10,12},{12... | collective-permute-start | bytes 2359304 | tf_op jit(solution)/shard_map/ppermute | solution.py:339
  41.4 10.5 %collective-permute-start.9 = (bf16[96,4096]{1,0:T(8,128)(2,1)S(1)}, bf16[96,4096]{1,0:T(8,128)(2,1)S(1)}, u32[]{:S(2)}, u32[]{:S(2)}) collective-permute-start(bf16[96,4096]{1,0:T(8,128)(2,1)S(1)} %collective-permute-done.2.one), channel_id=1, source_target_pairs={{0,8},{8,0},{1,9},{9,1},{2,10},{10,2},{3,11},{11,3},{4,12},{12,4},... | collective-permute-start | bytes 2359304 | tf_op jit(solution)/shard_map/ppermute | solution.py:334
  41.4 15.3 %collective-permute-start.6 = (bf16[96,4096]{1,0:T(8,128)(2,1)S(1)}, bf16[96,4096]{1,0:T(8,128)(2,1)S(1)}, u32[]{:S(2)}, u32[]{:S(2)}) collective-permute-start(bf16[96,4096]{1,0:T(8,128)(2,1)S(1)} %collective-permute-done.2.one), channel_id=1, source_target_pairs={{0,2},{2,4},{4,6},{6,7},{7,5},{5,3},{3,1},{1,0},{10,8},{12,10},{14... | collective-permute-start | bytes 2359304 | tf_op jit(solution)/shard_map/ppermute | solution.py:333
  49.3 8.6 %collective-permute-start.12 = (bf16[96,4096]{1,0:T(8,128)(2,1)S(1)}, bf16[96,4096]{1,0:T(8,128)(2,1)S(1)}, u32[]{:S(2)}, u32[]{:S(2)}) collective-permute-start(bf16[96,4096]{1,0:T(8,128)(2,1)S(1)} %collective-permute-done.7.one), channel_id=1, source_target_pairs={{0,8},{8,0},{1,9},{9,1},{2,10},{10,2},{3,11},{11,3},{4,12},{12,4},... | collective-permute-start | bytes 2359304 | tf_op jit(solution)/shard_map/ppermute | solution.py:340
  50.3 14.8 %collective-permute-start.11 = (bf16[96,4096]{1,0:T(8,128)(2,1)S(1)}, bf16[96,4096]{1,0:T(8,128)(2,1)S(1)}, u32[]{:S(2)}, u32[]{:S(2)}) collective-permute-start(bf16[96,4096]{1,0:T(8,128)(2,1)S(1)} %collective-permute-done.7.one), channel_id=1, source_target_pairs={{2,0},{4,2},{6,4},{7,6},{5,7},{3,5},{1,3},{0,1},{8,10},{10,12},{12... | collective-permute-start | bytes 2359304 | tf_op jit(solution)/shard_map/ppermute | solution.py:339
  56.7 8.9 %collective-permute-start.13 = (bf16[96,4096]{1,0:T(8,128)(2,1)S(1)}, bf16[96,4096]{1,0:T(8,128)(2,1)S(1)}, u32[]{:S(2)}, u32[]{:S(2)}) collective-permute-start(bf16[96,4096]{1,0:T(8,128)(2,1)S(1)} %collective-permute-done.6.one), channel_id=1, source_target_pairs={{0,8},{8,0},{1,9},{9,1},{2,10},{10,2},{3,11},{11,3},{4,12},{12,4},... | collective-permute-start | bytes 2359304 | tf_op jit(solution)/shard_map/ppermute | solution.py:334
  56.8 14.6 %collective-permute-start.10 = (bf16[96,4096]{1,0:T(8,128)(2,1)S(1)}, bf16[96,4096]{1,0:T(8,128)(2,1)S(1)}, u32[]{:S(2)}, u32[]{:S(2)}) collective-permute-start(bf16[96,4096]{1,0:T(8,128)(2,1)S(1)} %collective-permute-done.6.one), channel_id=1, source_target_pairs={{0,2},{2,4},{4,6},{6,7},{7,5},{5,3},{3,1},{1,0},{10,8},{12,10},{14... | collective-permute-start | bytes 2359304 | tf_op jit(solution)/shard_map/ppermute | solution.py:333
  65.1 6.3 %collective-permute-start.15 = (bf16[96,4096]{1,0:T(8,128)(2,1)S(1)}, bf16[96,4096]{1,0:T(8,128)(2,1)S(1)}, u32[]{:S(2)}, u32[]{:S(2)}) collective-permute-start(bf16[96,4096]{1,0:T(8,128)(2,1)S(1)} %collective-permute-done.11.one), channel_id=1, source_target_pairs={{0,8},{8,0},{1,9},{9,1},{2,10},{10,2},{3,11},{11,3},{4,12},{12,4},... | collective-permute-start | bytes 2359304 | tf_op jit(solution)/shard_map/ppermute | solution.py:340
  71.4 4.8 %collective-permute-start.14 = (bf16[96,4096]{1,0:T(8,128)(2,1)S(1)}, bf16[96,4096]{1,0:T(8,128)(2,1)S(1)}, u32[]{:S(2)}, u32[]{:S(2)}) collective-permute-start(bf16[96,4096]{1,0:T(8,128)(2,1)S(1)} %collective-permute-done.10.one), channel_id=1, source_target_pairs={{0,8},{8,0},{1,9},{9,1},{2,10},{10,2},{3,11},{11,3},{4,12},{12,4},... | collective-permute-start | bytes 2359304 | tf_op jit(solution)/shard_map/ppermute | solution.py:347
  76.2 21.3 %copy-start = (bf16[128,4096]{1,0:T(8,128)(2,1)S(1)}, bf16[128,4096]{1,0:T(8,128)(2,1)}, u32[]{:S(2)}) copy-start(bf16[128,4096]{1,0:T(8,128)(2,1)} %val_own.1) | copy-start | bytes 3145732
  81.2 1.6 %collective-permute-start.16 = (f32[256,128]{1,0:T(8,128)S(1)}, f32[256,128]{1,0:T(8,128)S(1)}, u32[]{:S(2)}, u32[]{:S(2)}) collective-permute-start(f32[256,128]{1,0:T(8,128)S(1)} %get-tuple-element.55), channel_id=1, source_target_pairs={{0,8},{8,0},{1,9},{9,1},{2,10},{10,2},{3,11},{11,3},{4,12},{12,4},... | collective-permute-start | bytes 393224 | tf_op jit(solution)/shard_map/ppermute | solution.py:353
  82.8 4.7 %collective-permute-start.17 = (bf16[256,128]{1,0:T(8,128)(2,1)S(1)}, bf16[256,128]{1,0:T(8,128)(2,1)S(1)}, u32[]{:S(2)}, u32[]{:S(2)}) collective-permute-start(bf16[256,128]{1,0:T(8,128)(2,1)S(1)} %get-tuple-element.59), channel_id=1, source_target_pairs={{0,1},{1,0},{2,3},{3,2},{4,5},{5,4},{6,7},{7,6},{8,9},{9,8},{10,11... | collective-permute-start | bytes 196616 | tf_op jit(solution)/shard_map/ppermute | solution.py:362
  84.9 4.8 %collective-permute-start.18 = (bf16[256,128]{1,0:T(8,128)(2,1)S(1)}, bf16[256,128]{1,0:T(8,128)(2,1)S(1)}, u32[]{:S(2)}, u32[]{:S(2)}) collective-permute-start(bf16[256,128]{1,0:T(8,128)(2,1)S(1)} %get-tuple-element.59), channel_id=1, source_target_pairs={{0,2},{1,3},{2,0},{3,1},{4,6},{5,7},{6,4},{7,5},{8,10},{9,11},{10,... | collective-permute-start | bytes 196616 | tf_op jit(solution)/shard_map/ppermute | solution.py:362
  86.5 5.2 %collective-permute-start.19 = (bf16[256,128]{1,0:T(8,128)(2,1)S(1)}, bf16[256,128]{1,0:T(8,128)(2,1)S(1)}, u32[]{:S(2)}, u32[]{:S(2)}) collective-permute-start(bf16[256,128]{1,0:T(8,128)(2,1)S(1)} %get-tuple-element.59), channel_id=1, source_target_pairs={{0,3},{1,2},{2,1},{3,0},{4,7},{5,6},{6,5},{7,4},{8,11},{9,10},{10,... | collective-permute-start | bytes 196616 | tf_op jit(solution)/shard_map/ppermute | solution.py:362
  91.7 5.8 %collective-permute-start.20 = (bf16[256,128]{1,0:T(8,128)(2,1)S(1)}, bf16[256,128]{1,0:T(8,128)(2,1)S(1)}, u32[]{:S(2)}, u32[]{:S(2)}) collective-permute-start(bf16[256,128]{1,0:T(8,128)(2,1)S(1)} %get-tuple-element.57), channel_id=1, source_target_pairs={{0,4},{1,5},{2,6},{3,7},{4,0},{5,1},{6,2},{7,3},{8,12},{9,13},{10,... | collective-permute-start | bytes 196616 | tf_op jit(solution)/shard_map/ppermute | solution.py:362
  (3 other events, 2.9 us)

commit v9 on v7

--- a/solution.py
+++ b/solution.py
@@ -99,26 +99,31 @@
     return main[:, :LANES] + main[:, LANES:] + rest
 
 
-def load_kernel(
-    table, lengths, gate_hbm, up_hbm, out_grad_hbm, proj_out_hbm, proj_in,
-    w, out_grad, diagonal, sems,
-):
-    hidden = gate_hbm.shape[1]
+def small_kernel(table, lengths, out_grad_hbm, proj_out_hbm, out_grad, diagonal, sems):
+    hidden = proj_out_hbm.shape[0]
     upper = pltpu.make_async_copy(proj_out_hbm, diagonal.at[pl.ds(0, hidden)], sems.at[0])
-    copies = [
-        pltpu.make_async_copy(gate_hbm, w.at[:, pl.ds(0, hidden)], sems.at[1]),
-        pltpu.make_async_copy(up_hbm, w.at[:, pl.ds(hidden, hidden)], sems.at[2]),
-        pltpu.make_async_copy(out_grad_hbm, out_grad, sems.at[3]),
-    ]
-    for copy in [upper] + copies:
-        copy.start()
-    w[:, 2 * hidden :] = jnp.concatenate([proj_in[...], proj_in[...]], axis=1)
+    whole = pltpu.make_async_copy(out_grad_hbm, out_grad, sems.at[1])
+    upper.start()
+    whole.start()
     upper.wait()
     values = diagonal[:hidden, :]
     left = lax.broadcasted_iota(jnp.int32, values.shape, 1) < LANES // 2
     none = jnp.zeros_like(values)
     diagonal[hidden:, :] = jnp.where(left, none, values)
     diagonal[:hidden, :] = jnp.where(left, values, none)
+    whole.wait()
+
+
+def load_kernel(lengths, diagonal, gate_hbm, up_hbm, proj_in, w, total, sems):
+    hidden = gate_hbm.shape[1]
+    copies = [
+        pltpu.make_async_copy(gate_hbm, w.at[:, pl.ds(0, hidden)], sems.at[0]),
+        pltpu.make_async_copy(up_hbm, w.at[:, pl.ds(hidden, hidden)], sems.at[1]),
+    ]
+    for copy in copies:
+        copy.start()
+    w[:, 2 * hidden :] = jnp.concatenate([proj_in[...], proj_in[...]], axis=1)
+    total[...] = jnp.zeros_like(total)
     for copy in copies:
         copy.wait()
 
@@ -132,18 +137,14 @@
     return chunks
 
 
-def step_kernel(entry, first, last, table, lengths, one, two, w, out_grad, diagonal, *refs):
+def step_kernel(entry, last, table, lengths, one, two, w, out_grad, diagonal, before, *refs):
     outs, (pre, both) = refs[:-2], refs[-2:]
-    if not first:
-        before, outs = outs[0], outs[1:]
     rows = one.shape[0]
     starts = [table[entry], table[entry + 1]]
     x = jnp.concatenate([one[...], two[...]], axis=0)
     pre[...] = jnp.dot(x, w[...], preferred_element_type=jnp.float32)
     gradients(pre, cotangent_chunks(out_grad, starts, rows), both)
-    total = sketch_of(starts, rows, lengths, pre, both, diagonal)
-    if not first:
-        total += before[...]
+    total = before[...] + sketch_of(starts, rows, lengths, pre, both, diagonal)
     if not last:
         outs[0][...] = total
         return
@@ -161,37 +162,50 @@
     )
 
 
-def load(table, lengths, w_gate, w_up, out_grad, proj_in, proj_out):
+def load_small(table, lengths, out_grad, proj_out):
+    out_grad, proj_out = [
+        pltpu.with_memory_space_constraint(a, pltpu.HBM) for a in (out_grad, proj_out)
+    ]
+    hidden = out_grad.shape[1]
+    return pl.pallas_call(
+        small_kernel,
+        out_shape=[
+            pltpu.VMEM(out_grad.shape, jnp.bfloat16),
+            pltpu.VMEM((2 * hidden, LANES), jnp.bfloat16),
+        ],
+        in_specs=[SMEM, SMEM, ANY, ANY],
+        out_specs=[VMEM] * 2,
+        scratch_shapes=[pltpu.SemaphoreType.DMA((2,))],
+        compiler_params=pltpu.CompilerParams(vmem_limit_bytes=16 * 2**20),
+    )(table, lengths, out_grad, proj_out)
+
+
+def load(lengths, diagonal, w_gate, w_up, proj_in):
     width, hidden = w_gate.shape
-    w_gate, w_up, out_grad, proj_out = [
-        pltpu.with_memory_space_constraint(a, pltpu.HBM)
-        for a in (w_gate, w_up, out_grad, proj_out)
-    ]
+    w_gate, w_up = [pltpu.with_memory_space_constraint(a, pltpu.HBM) for a in (w_gate, w_up)]
     return pl.pallas_call(
         load_kernel,
         out_shape=[
             pltpu.VMEM((width, 2 * hidden + LANES), jnp.bfloat16),
-            pltpu.VMEM(out_grad.shape, jnp.bfloat16),
-            pltpu.VMEM((2 * hidden, LANES), jnp.bfloat16),
+            jax.ShapeDtypeStruct((lengths.shape[0] * LANES // 2, LANES), jnp.float32),
         ],
-        in_specs=[SMEM, SMEM] + [ANY] * 4 + [VMEM],
-        out_specs=[VMEM] * 3,
-        scratch_shapes=[pltpu.SemaphoreType.DMA((4,))],
+        in_specs=[SMEM, VMEM, ANY, ANY, VMEM],
+        out_specs=[VMEM] * 2,
+        scratch_shapes=[pltpu.SemaphoreType.DMA((2,))],
         compiler_params=pltpu.CompilerParams(vmem_limit_bytes=16 * 2**20),
-    )(table, lengths, w_gate, w_up, out_grad, proj_out, proj_in)
+    )(lengths, diagonal, w_gate, w_up, proj_in)
 
 
 def add_step(blocks, entry, total, table, lengths, weights, last=False):
     rows, width = blocks[0].shape
     w, _, diagonal = weights
-    first = total is None
-    operands = [*blocks, *weights] + ([] if first else [total])
+    operands = [*blocks, *weights, total]
     out_rows = lengths.shape[0] * LANES // 2
     out_shape = [jax.ShapeDtypeStruct((out_rows, LANES), jnp.float32)]
     if last:
         out_shape = [jax.ShapeDtypeStruct((out_rows // 2, LANES), jnp.float32)] * 2
     outs = pl.pallas_call(
-        functools.partial(step_kernel, entry, first, last),
+        functools.partial(step_kernel, entry, last),
         out_shape=out_shape,
         in_specs=[SMEM, SMEM] + [VMEM] * len(operands),
         out_specs=[VMEM] * len(out_shape),
@@ -267,36 +281,30 @@
     after = lax.optimization_barrier
     one_way = send_one(tokens_in)
     other, other_val = swap(tokens_in), swap(val_sketch)
-    w, out_grad, diagonal = load(table, lengths, w_gate, w_up, out_grad, proj_in, proj_out)
+    out_grad, diagonal = load_small(table, lengths, out_grad, proj_out)
     later_tokens, diagonal = after((tokens_in, diagonal))
     two_way = send_two(later_tokens)
+    w, total = load(lengths, diagonal, w_gate, w_up, proj_in)
     add = functools.partial(
         add_step, table=table, lengths=lengths, weights=[w, out_grad, diagonal]
     )
-    total = add([tokens_in, other], 0, None)
-
-    waiting, entry = None, 2
+
+    waiting, entry = (tokens_in, other), 0
     for k in range(1, n // 2):
         one_way, total = after((one_way, total))
         next_one = send_one(one_way)
         swapped_one = swap(one_way)
-        if waiting is not None:
-            total = add(waiting, entry, total)
-            entry += 2
+        total = add(waiting, entry, total)
         two_way, total, other_val = after((two_way, total, other_val))
         next_two = send_two(two_way) if k + 1 < n // 2 else None
-        swapped_two = swap(two_way)
-        _, swapped_one = after((two_way, swapped_one))
-        total = add([one_way, swapped_one], entry, total)
-        entry += 2
-        waiting = (two_way, swapped_two)
+        total = add([one_way, swapped_one], entry + 2, total)
+        entry += 4
+        waiting = (two_way, swap(two_way))
         one_way, two_way = next_one, next_two
     one_way, total = after((one_way, total))
     swapped_one = swap(one_way)
-    if waiting is not None:
-        total = add(waiting, entry, total)
-        entry += 2
-    kept, sent = add([one_way, swapped_one], entry, total, last=True)
+    total = add(waiting, entry, total)
+    kept, sent = add([one_way, swapped_one], entry + 2, total, last=True)
 
     mine, theirs = kept, swap(sent)
     bit = 1

time: 92.8 us -> 91.7 us (0.988)
  waiting for transfers between devices: 24.2 us -> 16.2 us
  Pallas kernels: 45.7 us -> 49 us
  local copies, waits for them, and re-layouts: 2.88 us -> 5.05 us
  starting transfers between devices: 19.6 us -> 21 us
    ppermute x1, waiting for transfers between devices: 8.48 us -> 0.01 us  [fast(): two_way = send_two(later_tokens)]
    ppermute x2, waiting for transfers between devices: 8.19 us -> 1.57 us  [fast(): next_two = send_two(two_way) if k + 1 < n // 2 else None]
    ppermute x3, waiting for transfers between devices: 0.01 us -> 5.65 us  [fast(): next_one = send_one(one_way)]
    pallas_call x8 -> x9, Pallas kernels: 37.2 us -> 41.1 us  [the longest x8 38.7 us: add_step(): pl.pallas_call(functools.partial(step_kernel, entry, last), out_shape=out...]
    ppermute x4, starting transfers between devices: 4.51 us -> 0.81 us  [fast(): swapped_one = swap(one_way)]
    ppermute x3, starting transfers between devices: 0.01 us -> 2.54 us  [fast(): waiting = (two_way, swap(two_way))]
    unnamed x9 -> x15, local copies, waits for them, and re-layouts: 2.18 us -> 4.36 us
    ppermute x2, starting transfers between devices: 0.01 us -> 2.16 us  [fast(): next_two = send_two(two_way) if k + 1 < n // 2 else None]
  transfers between devices with their start and end apart: 21 -> 21, of which waited for: 8 -> 9; matrix products, arithmetic and copies ran while one was open for 2% -> 2% of each run, Pallas kernels for 42% -> 46%
where the time goes in v9:
time: 91.7 us; the launch traced here: 91.4 us
  Pallas kernels  49 us (53%)
  starting transfers between devices  21 us (23%)
  waiting for transfers between devices  16.2 us (18%)
  local copies, waits for them, and re-layouts  5.05 us (6%)
    pallas_call x8, Pallas kernels, add_step(): pl.pallas_call(functools.partial(step_kernel, entry, last), out_shape=out...  38.7 us
    ppermute x4, waiting for transfers between devices, fast(): lax.ppermute(sent, 'mp', [(i, i ^ flip) for i in range(n)])  7.96 us
    ppermute x4, starting transfers between devices, fast(): lax.ppermute(sent, 'mp', [(i, i ^ flip) for i in range(n)])  6.23 us
    pallas_call x1, Pallas kernels, load(): pl.pallas_call(load_kernel, out_shape=[pltpu.VMEM((width, 2 * hidden + LA...  6.01 us
    ppermute x3, waiting for transfers between devices, fast(): next_one = send_one(one_way)  5.65 us
    ppermute x3, starting transfers between devices, fast(): next_one = send_one(one_way)  4.54 us
    unnamed x15, local copies, waits for them, and re-layouts  4.36 us
    ppermute x1, starting transfers between devices, fast(): one_way = send_one(tokens_in)  3.02 us
  transfers between devices with their start and end apart: 21, of which 9 were waited for; matrix products, arithmetic and copies ran while one was open for 2% of the time, Pallas kernels for 46%

profile of v9, /device:TPU:0, one launch (start us, length us, event | category | flops | bytes accessed | tf_op | source)
XLA Modules:
  0.0 91.4 jit_solution(1786579513739586845)
XLA Ops:
  0.0 3.0 %collective-permute-start = (bf16[96,4096]{1,0:T(8,128)(2,1)}, bf16[96,4096]{1,0:T(8,128)(2,1)S(1)}, u32[]{:S(2)}, u32[]{:S(2)}) collective-permute-start(bf16[96,4096]{1,0:T(8,128)(2,1)} %one.1), channel_id=1, source_target_pairs={{0,2},{2,4},{4,6},{6,7},{7,5},{5,3},{3,1},{1,0},{10,8},{12,10},{14... | collective-permute-start | bytes 2359304 | tf_op jit(solution)/shard_map/ppermute | solution.py:282
  4.9 2.5 %shard_map.91 = (bf16[1536,896]{1,0:T(8,128)(2,1)S(1)}, bf16[1792,128]{1,0:T(8,128)(2,1)S(1)}) custom-call(s32[17]{0:T(128)S(1)} %dynamic-slice_bitcast_fusion.table, s32[8]{0:T(128)S(1)} %copy-done.1, bf16[1536,896]{1,0:T(8,128)(2,1)} %out_grad_hbm.1, bf16[896,128]{1,0:T(8,128)(2,1)} %proj_out_hbm.1), custom_call_target="tpu_custom_call" | custom-call | tf_op jit(solution)/shard_map/pallas_call | solution.py:170
  9.5 1.5 %copy.10.proj_in = bf16[4096,64]{1,0:T(8,128)(2,1)S(1)} copy(bf16[4096,64]{0,1:T(8,128)(2,1)} %param.13) | data formatting | bytes 1048576 | tf_op args[4]
  11.6 6.0 %shard_map.92 = (bf16[4096,1920]{1,0:T(8,128)(2,1)S(1)}, f32[512,128]{1,0:T(8,128)S(1)}) custom-call(s32[8]{0:T(128)S(1)} %copy-done.2, bf16[1792,128]{1,0:T(8,128)(2,1)S(1)} %get-tuple-element.31.diagonal, bf16[4096,896]{1,0:T(8,128)(2,1)} %gate_hbm.1, bf16[4096,896]{1,0:T(8,128)(2,1)} %up_hbm.1, bf16[4096,64]{1,0:T(8,128)(2,1)S(1)} %copy.10.proj_in), custom_call_target="tpu_custom_call" | custom-call | tf_op jit(solution)/shard_map/pallas_call | solution.py:186
  18.5 1.6 %collective-permute-start.1 = (bf16[96,4096]{1,0:T(8,128)(2,1)S(1)}, bf16[96,4096]{1,0:T(8,128)(2,1)S(1)}, u32[]{:S(2)}, u32[]{:S(2)}) collective-permute-start(bf16[96,4096]{1,0:T(8,128)(2,1)S(1)} %collective-permute-done.one), channel_id=1, source_target_pairs={{0,2},{2,4},{4,6},{6,7},{7,5},{5,3},{3,1},{1,0},{10,8},{12,10},{14... | collective-permute-start | bytes 2359304 | tf_op jit(solution)/shard_map/ppermute | solution.py:295
  20.1 5.3 %shard_map.93.before = f32[512,128]{1,0:T(8,128)S(1)} custom-call(s32[17]{0:T(128)S(1)} %dynamic-slice_bitcast_fusion.table, s32[8]{0:T(128)S(1)} %copy-done.3, bf16[96,4096]{1,0:T(8,128)(2,1)S(1)} %copy-done.6, bf16[96,4096]{1,0:T(8,128)(2,1)} %collective-permute-done.4.two, bf16[4096,1920]{1,0:T(8,128)(2,1)S(1)} %get-tuple-element.34.w, ...), custom_call_target="tpu_custom_call" | custom-call | flops 6039797760 | bytes 1572864 | tf_op jit(solution)/shard_map/pallas_call | solution.py:207
  26.5 4.7 %shard_map.94.before = f32[512,128]{1,0:T(8,128)S(1)} custom-call(s32[17]{0:T(128)S(1)} %dynamic-slice_bitcast_fusion.table, s32[8]{0:T(128)S(1)} %copy-done.3, bf16[96,4096]{1,0:T(8,128)(2,1)S(1)} %collective-permute-done.one, bf16[96,4096]{1,0:T(8,128)(2,1)S(1)} %collective-permute-done.2.two, bf16[4096,1920]{1,0:T(8,128)(2,1)S(1)} %get-tuple-element.34.w, ...), custom_call_target="tpu_custom_call" | custom-call | flops 6039797760 | bytes 1572864 | tf_op jit(solution)/shard_map/pallas_call | solution.py:207
  32.1 1.7 %collective-permute-start.6 = (bf16[96,4096]{1,0:T(8,128)(2,1)S(1)}, bf16[96,4096]{1,0:T(8,128)(2,1)S(1)}, u32[]{:S(2)}, u32[]{:S(2)}) collective-permute-start(bf16[96,4096]{1,0:T(8,128)(2,1)S(1)} %collective-permute-done.1.one), channel_id=1, source_target_pairs={{0,2},{2,4},{4,6},{6,7},{7,5},{5,3},{3,1},{1,0},{10,8},{12,10},{14... | collective-permute-start | bytes 2359304 | tf_op jit(solution)/shard_map/ppermute | solution.py:295
  33.8 5.3 %shard_map.95.before = f32[512,128]{1,0:T(8,128)S(1)} custom-call(s32[17]{0:T(128)S(1)} %dynamic-slice_bitcast_fusion.table, s32[8]{0:T(128)S(1)} %copy-done.3, bf16[96,4096]{1,0:T(8,128)(2,1)} %collective-permute-done.3.one, bf16[96,4096]{1,0:T(8,128)(2,1)S(1)} %collective-permute-done.9.two, bf16[4096,1920]{1,0:T(8,128)(2,1)S(1)} %get-tuple-element.34.w, ...), custom_call_target="tpu_custom_call" | custom-call | flops 6039797760 | bytes 1572864 | tf_op jit(solution)/shard_map/pallas_call | solution.py:207
  39.1 1.6 %collective-permute-done.8.one = bf16[96,4096]{1,0:T(8,128)(2,1)S(1)} collective-permute-done((bf16[96,4096]{1,0:T(8,128)(2,1)}, bf16[96,4096]{1,0:T(8,128)(2,1)S(1)}, u32[]{:S(2)}, u32[]{:S(2)}) %collective-permute-start.8) | collective-permute-done | bytes 786464 | tf_op jit(solution)/shard_map/ppermute | solution.py:299
  42.8 4.7 %shard_map.96.before = f32[512,128]{1,0:T(8,128)S(1)} custom-call(s32[17]{0:T(128)S(1)} %dynamic-slice_bitcast_fusion.table, s32[8]{0:T(128)S(1)} %copy-done.3, bf16[96,4096]{1,0:T(8,128)(2,1)S(1)} %collective-permute-done.1.one, bf16[96,4096]{1,0:T(8,128)(2,1)S(1)} %collective-permute-done.7.two, bf16[4096,1920]{1,0:T(8,128)(2,1)S(1)} %get-tuple-element.34.w, ...), custom_call_target="tpu_custom_call" | custom-call | flops 6039797760 | bytes 1572864 | tf_op jit(solution)/shard_map/pallas_call | solution.py:207
  47.4 2.8 %collective-permute-done.6.one = bf16[96,4096]{1,0:T(8,128)(2,1)S(1)} collective-permute-done((bf16[96,4096]{1,0:T(8,128)(2,1)S(1)}, bf16[96,4096]{1,0:T(8,128)(2,1)S(1)}, u32[]{:S(2)}, u32[]{:S(2)}) %collective-permute-start.6) | collective-permute-done | bytes 786464 | tf_op jit(solution)/shard_map/ppermute | solution.py:295
  51.6 4.7 %shard_map.97.before = f32[512,128]{1,0:T(8,128)S(1)} custom-call(s32[17]{0:T(128)S(1)} %dynamic-slice_bitcast_fusion.table, s32[8]{0:T(128)S(1)} %copy-done.3, bf16[96,4096]{1,0:T(8,128)(2,1)S(1)} %collective-permute-done.8.one, bf16[96,4096]{1,0:T(8,128)(2,1)S(1)} %collective-permute-done.13.two, bf16[4096,1920]{1,0:T(8,128)(2,1)S(1)} %get-tuple-element.34.w, ...), custom_call_target="tpu_custom_call" | custom-call | flops 6039797760 | bytes 1572864 | tf_op jit(solution)/shard_map/pallas_call | solution.py:207
  57.7 4.6 %shard_map.98.before = f32[512,128]{1,0:T(8,128)S(1)} custom-call(s32[17]{0:T(128)S(1)} %dynamic-slice_bitcast_fusion.table, s32[8]{0:T(128)S(1)} %copy-done.3, bf16[96,4096]{1,0:T(8,128)(2,1)S(1)} %collective-permute-done.6.one, bf16[96,4096]{1,0:T(8,128)(2,1)S(1)} %collective-permute-done.11.two, bf16[4096,1920]{1,0:T(8,128)(2,1)S(1)} %get-tuple-element.34.w, ...), custom_call_target="tpu_custom_call" | custom-call | flops 6039797760 | bytes 1572864 | tf_op jit(solution)/shard_map/pallas_call | solution.py:207
  62.3 1.8 %collective-permute-done.10.one = bf16[96,4096]{1,0:T(8,128)(2,1)S(1)} collective-permute-done((bf16[96,4096]{1,0:T(8,128)(2,1)S(1)}, bf16[96,4096]{1,0:T(8,128)(2,1)S(1)}, u32[]{:S(2)}, u32[]{:S(2)}) %collective-permute-start.10) | collective-permute-done | bytes 786464 | tf_op jit(solution)/shard_map/ppermute | solution.py:295
  64.2 4.7 %shard_map.99.before = f32[512,128]{1,0:T(8,128)S(1)} custom-call(s32[17]{0:T(128)S(1)} %dynamic-slice_bitcast_fusion.table, s32[8]{0:T(128)S(1)} %copy-done.3, bf16[96,4096]{1,0:T(8,128)(2,1)S(1)} %collective-permute-done.12.one, bf16[96,4096]{1,0:T(8,128)(2,1)S(1)} %collective-permute-done.15.two, bf16[4096,1920]{1,0:T(8,128)(2,1)S(1)} %get-tuple-element.34.w, ...), custom_call_target="tpu_custom_call" | custom-call | flops 6039797760 | bytes 1572864 | tf_op jit(solution)/shard_map/pallas_call | solution.py:207
  68.9 4.9 %shard_map.100 = (f32[256,128]{1,0:T(8,128)S(1)}, f32[256,128]{1,0:T(8,128)S(1)}) custom-call(s32[17]{0:T(128)S(1)} %dynamic-slice_bitcast_fusion.table, s32[8]{0:T(128)S(1)} %copy-done.3, bf16[96,4096]{1,0:T(8,128)(2,1)S(1)} %collective-permute-done.10.one, bf16[96,4096]{1,0:T(8,128)(2,1)S(1)} %collective-permute-done.14.two, ...), custom_call_target="tpu_custom_call" | custom-call | flops 6039797760 | bytes 1572864 | tf_op jit(solution)/shard_map/pallas_call | solution.py:207
  75.3 1.6 %collective-permute-start.17 = (bf16[256,128]{1,0:T(8,128)(2,1)S(1)}, bf16[256,128]{1,0:T(8,128)(2,1)S(1)}, u32[]{:S(2)}, u32[]{:S(2)}) collective-permute-start(bf16[256,128]{1,0:T(8,128)(2,1)S(1)} %get-tuple-element.57), channel_id=1, source_target_pairs={{0,1},{1,0},{2,3},{3,2},{4,5},{5,4},{6,7},{7,6},{8,9},{9,8},{10,11... | collective-permute-start | bytes 196616 | tf_op jit(solution)/shard_map/ppermute | solution.py:318
  77.0 1.6 %collective-permute-start.18 = (bf16[256,128]{1,0:T(8,128)(2,1)S(1)}, bf16[256,128]{1,0:T(8,128)(2,1)S(1)}, u32[]{:S(2)}, u32[]{:S(2)}) collective-permute-start(bf16[256,128]{1,0:T(8,128)(2,1)S(1)} %get-tuple-element.57), channel_id=1, source_target_pairs={{0,2},{1,3},{2,0},{3,1},{4,6},{5,7},{6,4},{7,5},{8,10},{9,11},{10,... | collective-permute-start | bytes 196616 | tf_op jit(solution)/shard_map/ppermute | solution.py:318
  79.8 1.8 %collective-permute-done.18 = bf16[256,128]{1,0:T(8,128)(2,1)S(1)} collective-permute-done((bf16[256,128]{1,0:T(8,128)(2,1)S(1)}, bf16[256,128]{1,0:T(8,128)(2,1)S(1)}, u32[]{:S(2)}, u32[]{:S(2)}) %collective-permute-start.18) | collective-permute-done | bytes 65568 | tf_op jit(solution)/shard_map/ppermute | solution.py:318
  81.6 2.1 %collective-permute-done.19 = bf16[256,128]{1,0:T(8,128)(2,1)S(1)} collective-permute-done((bf16[256,128]{1,0:T(8,128)(2,1)S(1)}, bf16[256,128]{1,0:T(8,128)(2,1)S(1)}, u32[]{:S(2)}, u32[]{:S(2)}) %collective-permute-start.19) | collective-permute-done | bytes 65568 | tf_op jit(solution)/shard_map/ppermute | solution.py:318
  83.8 2.7 %collective-permute-start.20 = (bf16[256,128]{1,0:T(8,128)(2,1)S(1)}, bf16[256,128]{1,0:T(8,128)(2,1)S(1)}, u32[]{:S(2)}, u32[]{:S(2)}) collective-permute-start(bf16[256,128]{1,0:T(8,128)(2,1)S(1)} %get-tuple-element.55), channel_id=1, source_target_pairs={{0,4},{1,5},{2,6},{3,7},{4,0},{5,1},{6,2},{7,3},{8,12},{9,13},{10,... | collective-permute-start | bytes 196616 | tf_op jit(solution)/shard_map/ppermute | solution.py:318
  86.4 3.2 %collective-permute-done.20.theirs = bf16[256,128]{1,0:T(8,128)(2,1)S(1)} collective-permute-done((bf16[256,128]{1,0:T(8,128)(2,1)S(1)}, bf16[256,128]{1,0:T(8,128)(2,1)S(1)}, u32[]{:S(2)}, u32[]{:S(2)}) %collective-permute-start.20) | collective-permute-done | bytes 65568 | tf_op jit(solution)/shard_map/ppermute | solution.py:318
  89.6 1.8 %shard_map.101 = f32[4,128]{1,0:T(4,128)} custom-call(s32[17]{0:T(128)S(1)} %dynamic-slice_bitcast_fusion.table, f32[256,128]{1,0:T(8,128)S(1)} %get-tuple-element.56.mine, bf16[256,128]{1,0:T(8,128)(2,1)S(1)} %collective-permute-done.20.theirs, bf16[128,4096]{1,0:T(8,128)(2,1)S(1)} %copy-done, bf16[128,4096]{1,0:T(8,128)(2,1)S(1)} %collective-permute-done.5.val_other), custom_call_target="tpu_custom_call" | custom-call | tf_op jit(solution)/shard_map/pallas_call | solution.py:256
  (47 shorter events, 15.2 us)
Async XLA Ops:
  0.0 17.7 %collective-permute-start = (bf16[96,4096]{1,0:T(8,128)(2,1)}, bf16[96,4096]{1,0:T(8,128)(2,1)S(1)}, u32[]{:S(2)}, u32[]{:S(2)}) collective-permute-start(bf16[96,4096]{1,0:T(8,128)(2,1)} %one.1), channel_id=1, source_target_pairs={{0,2},{2,4},{4,6},{6,7},{7,5},{5,3},{3,1},{1,0},{10,8},{12,10},{14... | collective-permute-start | bytes 2359304 | tf_op jit(solution)/shard_map/ppermute | solution.py:282
  3.0 17.0 %collective-permute-start.4 = (bf16[96,4096]{1,0:T(8,128)(2,1)}, bf16[96,4096]{1,0:T(8,128)(2,1)}, u32[]{:S(2)}, u32[]{:S(2)}) collective-permute-start(bf16[96,4096]{1,0:T(8,128)(2,1)} %one.1), channel_id=1, source_target_pairs={{0,8},{8,0},{1,9},{9,1},{2,10},{10,2},{3,11},{11,3},{4,12},{12,4},... | collective-permute-start | bytes 2359304 | tf_op jit(solution)/shard_map/ppermute | solution.py:283
  3.0 22.3 %collective-permute-start.5 = (bf16[128,4096]{1,0:T(8,128)(2,1)}, bf16[128,4096]{1,0:T(8,128)(2,1)S(1)}, u32[]{:S(2)}, u32[]{:S(2)}) collective-permute-start(bf16[128,4096]{1,0:T(8,128)(2,1)} %val_own.1), channel_id=1, source_target_pairs={{0,8},{8,0},{1,9},{9,1},{2,10},{10,2},{3,11},{11,3},{4,12},{12,4},... | collective-permute-start | bytes 3145736 | tf_op jit(solution)/shard_map/ppermute | solution.py:283
  8.9 16.4 %collective-permute-start.3 = (bf16[96,4096]{1,0:T(8,128)(2,1)}, bf16[96,4096]{1,0:T(8,128)(2,1)}, u32[]{:S(2)}, u32[]{:S(2)}) collective-permute-start(bf16[96,4096]{1,0:T(8,128)(2,1)} %one.1), channel_id=1, source_target_pairs={{2,0},{4,2},{6,4},{7,6},{5,7},{3,5},{1,3},{0,1},{8,10},{10,12},{12... | collective-permute-start | bytes 2359304 | tf_op jit(solution)/shard_map/ppermute | solution.py:286
  11.6 8.4 %copy-start.5 = (bf16[1536,896]{1,0:T(8,128)(2,1)S(1)}, bf16[1536,896]{1,0:T(8,128)(2,1)}, u32[]{:S(2)}) copy-start(bf16[1536,896]{1,0:T(8,128)(2,1)} %copy-done.4) | copy-start | bytes 8257540
  11.6 8.4 %copy-start.6 = (bf16[96,4096]{1,0:T(8,128)(2,1)S(1)}, bf16[96,4096]{1,0:T(8,128)(2,1)}, u32[]{:S(2)}) copy-start(bf16[96,4096]{1,0:T(8,128)(2,1)} %one.1) | copy-start | bytes 2359300
  17.7 8.8 %collective-permute-start.2 = (bf16[96,4096]{1,0:T(8,128)(2,1)S(1)}, bf16[96,4096]{1,0:T(8,128)(2,1)S(1)}, u32[]{:S(2)}, u32[]{:S(2)}) collective-permute-start(bf16[96,4096]{1,0:T(8,128)(2,1)S(1)} %collective-permute-done.one), channel_id=1, source_target_pairs={{0,8},{8,0},{1,9},{9,1},{2,10},{10,2},{3,11},{11,3},{4,12},{12,4},... | collective-permute-start | bytes 2359304 | tf_op jit(solution)/shard_map/ppermute | solution.py:296
  18.5 13.7 %collective-permute-start.1 = (bf16[96,4096]{1,0:T(8,128)(2,1)S(1)}, bf16[96,4096]{1,0:T(8,128)(2,1)S(1)}, u32[]{:S(2)}, u32[]{:S(2)}) collective-permute-start(bf16[96,4096]{1,0:T(8,128)(2,1)S(1)} %collective-permute-done.one), channel_id=1, source_target_pairs={{0,2},{2,4},{4,6},{6,7},{7,5},{5,3},{3,1},{1,0},{10,8},{12,10},{14... | collective-permute-start | bytes 2359304 | tf_op jit(solution)/shard_map/ppermute | solution.py:295
  25.4 8.5 %collective-permute-start.9 = (bf16[96,4096]{1,0:T(8,128)(2,1)}, bf16[96,4096]{1,0:T(8,128)(2,1)S(1)}, u32[]{:S(2)}, u32[]{:S(2)}) collective-permute-start(bf16[96,4096]{1,0:T(8,128)(2,1)} %collective-permute-done.3.one), channel_id=1, source_target_pairs={{0,8},{8,0},{1,9},{9,1},{2,10},{10,2},{3,11},{11,3},{4,12},{12,4},... | collective-permute-start | bytes 2359304 | tf_op jit(solution)/shard_map/ppermute | solution.py:302
  25.4 15.2 %collective-permute-start.8 = (bf16[96,4096]{1,0:T(8,128)(2,1)}, bf16[96,4096]{1,0:T(8,128)(2,1)S(1)}, u32[]{:S(2)}, u32[]{:S(2)}) collective-permute-start(bf16[96,4096]{1,0:T(8,128)(2,1)} %collective-permute-done.3.one), channel_id=1, source_target_pairs={{2,0},{4,2},{6,4},{7,6},{5,7},{3,5},{1,3},{0,1},{8,10},{10,12},{12... | collective-permute-start | bytes 2359304 | tf_op jit(solution)/shard_map/ppermute | solution.py:299
  32.1 10.6 %collective-permute-start.7 = (bf16[96,4096]{1,0:T(8,128)(2,1)S(1)}, bf16[96,4096]{1,0:T(8,128)(2,1)S(1)}, u32[]{:S(2)}, u32[]{:S(2)}) collective-permute-start(bf16[96,4096]{1,0:T(8,128)(2,1)S(1)} %collective-permute-done.1.one), channel_id=1, source_target_pairs={{0,8},{8,0},{1,9},{9,1},{2,10},{10,2},{3,11},{11,3},{4,12},{12,4},... | collective-permute-start | bytes 2359304 | tf_op jit(solution)/shard_map/ppermute | solution.py:296
  32.1 18.1 %collective-permute-start.6 = (bf16[96,4096]{1,0:T(8,128)(2,1)S(1)}, bf16[96,4096]{1,0:T(8,128)(2,1)S(1)}, u32[]{:S(2)}, u32[]{:S(2)}) collective-permute-start(bf16[96,4096]{1,0:T(8,128)(2,1)S(1)} %collective-permute-done.1.one), channel_id=1, source_target_pairs={{0,2},{2,4},{4,6},{6,7},{7,5},{5,3},{3,1},{1,0},{10,8},{12,10},{14... | collective-permute-start | bytes 2359304 | tf_op jit(solution)/shard_map/ppermute | solution.py:295
  40.7 10.9 %collective-permute-start.13 = (bf16[96,4096]{1,0:T(8,128)(2,1)S(1)}, bf16[96,4096]{1,0:T(8,128)(2,1)S(1)}, u32[]{:S(2)}, u32[]{:S(2)}) collective-permute-start(bf16[96,4096]{1,0:T(8,128)(2,1)S(1)} %collective-permute-done.8.one), channel_id=1, source_target_pairs={{0,8},{8,0},{1,9},{9,1},{2,10},{10,2},{3,11},{11,3},{4,12},{12,4},... | collective-permute-start | bytes 2359304 | tf_op jit(solution)/shard_map/ppermute | solution.py:302
  41.7 14.5 %collective-permute-start.12 = (bf16[96,4096]{1,0:T(8,128)(2,1)S(1)}, bf16[96,4096]{1,0:T(8,128)(2,1)S(1)}, u32[]{:S(2)}, u32[]{:S(2)}) collective-permute-start(bf16[96,4096]{1,0:T(8,128)(2,1)S(1)} %collective-permute-done.8.one), channel_id=1, source_target_pairs={{2,0},{4,2},{6,4},{7,6},{5,7},{3,5},{1,3},{0,1},{8,10},{10,12},{12... | collective-permute-start | bytes 2359304 | tf_op jit(solution)/shard_map/ppermute | solution.py:299
  50.3 7.4 %collective-permute-start.11 = (bf16[96,4096]{1,0:T(8,128)(2,1)S(1)}, bf16[96,4096]{1,0:T(8,128)(2,1)S(1)}, u32[]{:S(2)}, u32[]{:S(2)}) collective-permute-start(bf16[96,4096]{1,0:T(8,128)(2,1)S(1)} %collective-permute-done.6.one), channel_id=1, source_target_pairs={{0,8},{8,0},{1,9},{9,1},{2,10},{10,2},{3,11},{11,3},{4,12},{12,4},... | collective-permute-start | bytes 2359304 | tf_op jit(solution)/shard_map/ppermute | solution.py:296
  50.3 13.9 %collective-permute-start.10 = (bf16[96,4096]{1,0:T(8,128)(2,1)S(1)}, bf16[96,4096]{1,0:T(8,128)(2,1)S(1)}, u32[]{:S(2)}, u32[]{:S(2)}) collective-permute-start(bf16[96,4096]{1,0:T(8,128)(2,1)S(1)} %collective-permute-done.6.one), channel_id=1, source_target_pairs={{0,2},{2,4},{4,6},{6,7},{7,5},{5,3},{3,1},{1,0},{10,8},{12,10},{14... | collective-permute-start | bytes 2359304 | tf_op jit(solution)/shard_map/ppermute | solution.py:295
  56.2 8.0 %collective-permute-start.15 = (bf16[96,4096]{1,0:T(8,128)(2,1)S(1)}, bf16[96,4096]{1,0:T(8,128)(2,1)S(1)}, u32[]{:S(2)}, u32[]{:S(2)}) collective-permute-start(bf16[96,4096]{1,0:T(8,128)(2,1)S(1)} %collective-permute-done.12.one), channel_id=1, source_target_pairs={{0,8},{8,0},{1,9},{9,1},{2,10},{10,2},{3,11},{11,3},{4,12},{12,4},... | collective-permute-start | bytes 2359304 | tf_op jit(solution)/shard_map/ppermute | solution.py:302
  64.2 4.7 %collective-permute-start.14 = (bf16[96,4096]{1,0:T(8,128)(2,1)S(1)}, bf16[96,4096]{1,0:T(8,128)(2,1)S(1)}, u32[]{:S(2)}, u32[]{:S(2)}) collective-permute-start(bf16[96,4096]{1,0:T(8,128)(2,1)S(1)} %collective-permute-done.10.one), channel_id=1, source_target_pairs={{0,8},{8,0},{1,9},{9,1},{2,10},{10,2},{3,11},{11,3},{4,12},{12,4},... | collective-permute-start | bytes 2359304 | tf_op jit(solution)/shard_map/ppermute | solution.py:305
  68.8 20.7 %copy-start = (bf16[128,4096]{1,0:T(8,128)(2,1)S(1)}, bf16[128,4096]{1,0:T(8,128)(2,1)}, u32[]{:S(2)}) copy-start(bf16[128,4096]{1,0:T(8,128)(2,1)} %val_own.1) | copy-start | bytes 3145732
  73.8 1.6 %collective-permute-start.16 = (f32[256,128]{1,0:T(8,128)S(1)}, f32[256,128]{1,0:T(8,128)S(1)}, u32[]{:S(2)}, u32[]{:S(2)}) collective-permute-start(f32[256,128]{1,0:T(8,128)S(1)} %get-tuple-element.53), channel_id=1, source_target_pairs={{0,8},{8,0},{1,9},{9,1},{2,10},{10,2},{3,11},{11,3},{4,12},{12,4},... | collective-permute-start | bytes 393224 | tf_op jit(solution)/shard_map/ppermute | solution.py:309
  75.3 4.4 %collective-permute-start.17 = (bf16[256,128]{1,0:T(8,128)(2,1)S(1)}, bf16[256,128]{1,0:T(8,128)(2,1)S(1)}, u32[]{:S(2)}, u32[]{:S(2)}) collective-permute-start(bf16[256,128]{1,0:T(8,128)(2,1)S(1)} %get-tuple-element.57), channel_id=1, source_target_pairs={{0,1},{1,0},{2,3},{3,2},{4,5},{5,4},{6,7},{7,6},{8,9},{9,8},{10,11... | collective-permute-start | bytes 196616 | tf_op jit(solution)/shard_map/ppermute | solution.py:318
  77.0 4.6 %collective-permute-start.18 = (bf16[256,128]{1,0:T(8,128)(2,1)S(1)}, bf16[256,128]{1,0:T(8,128)(2,1)S(1)}, u32[]{:S(2)}, u32[]{:S(2)}) collective-permute-start(bf16[256,128]{1,0:T(8,128)(2,1)S(1)} %get-tuple-element.57), channel_id=1, source_target_pairs={{0,2},{1,3},{2,0},{3,1},{4,6},{5,7},{6,4},{7,5},{8,10},{9,11},{10,... | collective-permute-start | bytes 196616 | tf_op jit(solution)/shard_map/ppermute | solution.py:318
  78.5 5.2 %collective-permute-start.19 = (bf16[256,128]{1,0:T(8,128)(2,1)S(1)}, bf16[256,128]{1,0:T(8,128)(2,1)S(1)}, u32[]{:S(2)}, u32[]{:S(2)}) collective-permute-start(bf16[256,128]{1,0:T(8,128)(2,1)S(1)} %get-tuple-element.57), channel_id=1, source_target_pairs={{0,3},{1,2},{2,1},{3,0},{4,7},{5,6},{6,5},{7,4},{8,11},{9,10},{10,... | collective-permute-start | bytes 196616 | tf_op jit(solution)/shard_map/ppermute | solution.py:318
  83.8 5.8 %collective-permute-start.20 = (bf16[256,128]{1,0:T(8,128)(2,1)S(1)}, bf16[256,128]{1,0:T(8,128)(2,1)S(1)}, u32[]{:S(2)}, u32[]{:S(2)}) collective-permute-start(bf16[256,128]{1,0:T(8,128)(2,1)S(1)} %get-tuple-element.55), channel_id=1, source_target_pairs={{0,4},{1,5},{2,6},{3,7},{4,0},{5,1},{6,2},{7,3},{8,12},{9,13},{10,... | collective-permute-start | bytes 196616 | tf_op jit(solution)/shard_map/ppermute | solution.py:318
  (4 other events, 11.3 us)

commit v10 on v9

--- a/solution.py
+++ b/solution.py
@@ -88,15 +88,15 @@
         lows.append(rest)
     over_rows = (((0,), (0,)), ((), ()))
     main = lax.dot_general(
+        grads_both,
         jnp.concatenate(highs, axis=1),
-        grads_both,
         over_rows,
         preferred_element_type=jnp.float32,
     )
     rest = lax.dot_general(
-        jnp.concatenate(lows, axis=1), grads_high, over_rows, preferred_element_type=jnp.float32
-    )
-    return main[:, :LANES] + main[:, LANES:] + rest
+        grads_high, jnp.concatenate(lows, axis=1), over_rows, preferred_element_type=jnp.float32
+    )
+    return main[:LANES, :] + main[LANES:, :] + rest
 
 
 def small_kernel(table, lengths, out_grad_hbm, proj_out_hbm, out_grad, diagonal, sems):
@@ -137,11 +137,12 @@
     return chunks
 
 
-def step_kernel(entry, last, table, lengths, one, two, w, out_grad, diagonal, before, *refs):
-    outs, (pre, both) = refs[:-2], refs[-2:]
-    rows = one.shape[0]
-    starts = [table[entry], table[entry + 1]]
-    x = jnp.concatenate([one[...], two[...]], axis=0)
+def step_kernel(count, entry, last, table, lengths, *refs):
+    blocks, (w, out_grad, diagonal, before) = refs[:count], refs[count : count + 4]
+    outs, (pre, both) = refs[count + 4 : -2], refs[-2:]
+    rows = blocks[0].shape[0]
+    starts = [table[entry + i] for i in range(count)]
+    x = jnp.concatenate([block[...] for block in blocks], axis=0)
     pre[...] = jnp.dot(x, w[...], preferred_element_type=jnp.float32)
     gradients(pre, cotangent_chunks(out_grad, starts, rows), both)
     total = before[...] + sketch_of(starts, rows, lengths, pre, both, diagonal)
@@ -150,15 +151,15 @@
         return
     kept, sent = outs
     core = table[table.shape[0] - 1]
-    half = total.shape[0] // 2
-    upper, lower = total[:half, :], total[half:, :]
+    half = total.shape[1] // 2
+    upper, lower = total[:, :half], total[:, half:]
     kept[...] = jnp.where(core == 0, upper, lower)
     sent[...] = jnp.where(core == 0, lower, upper)
 
 
 def costs(rows, width, columns):
     return pl.CostEstimate(
-        flops=4 * rows * width * columns, bytes_accessed=2 * rows * width, transcendentals=0
+        flops=40 * rows * width * columns, bytes_accessed=2 * rows * width, transcendentals=0
     )
 
 
@@ -187,7 +188,7 @@
         load_kernel,
         out_shape=[
             pltpu.VMEM((width, 2 * hidden + LANES), jnp.bfloat16),
-            jax.ShapeDtypeStruct((lengths.shape[0] * LANES // 2, LANES), jnp.float32),
+            jax.ShapeDtypeStruct((LANES, lengths.shape[0] * LANES // 2), jnp.float32),
         ],
         in_specs=[SMEM, VMEM, ANY, ANY, VMEM],
         out_specs=[VMEM] * 2,
@@ -197,31 +198,30 @@
 
 
 def add_step(blocks, entry, total, table, lengths, weights, last=False):
-    rows, width = blocks[0].shape
+    count, (rows, width) = len(blocks), blocks[0].shape
     w, _, diagonal = weights
     operands = [*blocks, *weights, total]
-    out_rows = lengths.shape[0] * LANES // 2
-    out_shape = [jax.ShapeDtypeStruct((out_rows, LANES), jnp.float32)]
+    out_shape = [jax.ShapeDtypeStruct(total.shape, jnp.float32)]
     if last:
-        out_shape = [jax.ShapeDtypeStruct((out_rows // 2, LANES), jnp.float32)] * 2
+        out_shape = [jax.ShapeDtypeStruct((LANES, total.shape[1] // 2), jnp.float32)] * 2
     outs = pl.pallas_call(
-        functools.partial(step_kernel, entry, last),
+        functools.partial(step_kernel, count, entry, last),
         out_shape=out_shape,
         in_specs=[SMEM, SMEM] + [VMEM] * len(operands),
         out_specs=[VMEM] * len(out_shape),
         scratch_shapes=[
-            pltpu.VMEM((2 * rows, w.shape[1]), jnp.float32),
-            pltpu.VMEM((2 * rows, diagonal.shape[0]), jnp.bfloat16),
+            pltpu.VMEM((count * rows, w.shape[1]), jnp.float32),
+            pltpu.VMEM((count * rows, diagonal.shape[0]), jnp.bfloat16),
         ],
         compiler_params=pltpu.CompilerParams(vmem_limit_bytes=16 * 2**20),
-        cost_estimate=costs(2 * rows, width, w.shape[1]),
+        cost_estimate=costs(count * rows, width, w.shape[1]),
     )(table, lengths, *operands)
     return outs if last else outs[0]
 
 
 def score_kernel(table, mine, theirs, val_own, val_other, scores, sketch):
     core = table[table.shape[0] - 1]
-    sketch[...] = mine[...] + theirs[...].astype(jnp.float32)
+    sketch[...] = (mine[...] + theirs[...].astype(jnp.float32)).T
     own, rank = scores.shape[0], sketch.shape[0] // scores.shape[0]
     half = rank // 2
     left = lax.broadcasted_iota(jnp.int32, (own, LANES), 1) < LANES // 2
@@ -258,7 +258,7 @@
         out_shape=jax.ShapeDtypeStruct((own, val_own.shape[0]), jnp.float32),
         in_specs=[SMEM, VMEM, VMEM, VMEM, VMEM],
         out_specs=VMEM,
-        scratch_shapes=[pltpu.VMEM(mine.shape, jnp.float32)],
+        scratch_shapes=[pltpu.VMEM(mine.shape[::-1], jnp.float32)],
         compiler_params=pltpu.CompilerParams(vmem_limit_bytes=16 * 2**20),
     )(table, mine, theirs, val_own, val_other)
 
@@ -289,22 +289,24 @@
         add_step, table=table, lengths=lengths, weights=[w, out_grad, diagonal]
     )
 
-    waiting, entry = (tokens_in, other), 0
-    for k in range(1, n // 2):
-        one_way, total = after((one_way, total))
-        next_one = send_one(one_way)
-        swapped_one = swap(one_way)
-        total = add(waiting, entry, total)
-        two_way, total, other_val = after((two_way, total, other_val))
-        next_two = send_two(two_way) if k + 1 < n // 2 else None
-        total = add([one_way, swapped_one], entry + 2, total)
-        entry += 4
-        waiting = (two_way, swap(two_way))
-        one_way, two_way = next_one, next_two
-    one_way, total = after((one_way, total))
-    swapped_one = swap(one_way)
-    total = add(waiting, entry, total)
-    kept, sent = add([one_way, swapped_one], entry + 2, total, last=True)
+    streams = [(one_way, send_one), (two_way, send_two)]
+    waiting, entry = [[tokens_in, other]], 0
+    arrivals = n - 1
+    for i in range(arrivals):
+        block, send = streams[i % 2]
+        if i == 1:
+            block, total, other_val = after((block, total, other_val))
+        else:
+            block, total = after((block, total))
+        streams[i % 2] = (send(block) if i + 2 < arrivals else None, send)
+        if i == arrivals - 1:
+            total = add([block], entry, total)
+            kept, sent = add([swap(block)], entry + 1, total, last=True)
+            break
+        waiting.append([block, swap(block)])
+        while waiting and (len(waiting) > 1 or i >= arrivals - 2):
+            total = add(waiting.pop(0), entry, total)
+            entry += 2
 
     mine, theirs = kept, swap(sent)
     bit = 1

time: 91.7 us -> 94.1 us (1.026)
  Pallas kernels: 49 us -> 53.2 us
  starting transfers between devices: 21 us -> 19.5 us
    pallas_call x8 -> x9, Pallas kernels: 38.7 us -> 42.8 us  [add_step(): pl.pallas_call(functools.partial(step_kernel, count, entry, last), out_sh...]
    ppermute x12, starting transfers between devices: 10.1 us -> 8.04 us  [the longest x5 6.58 us: fast(): streams[i % 2] = (send(block) if i + 2 < arrivals else None, send)]
  transfers between devices with their start and end apart: 21 -> 21, of which waited for: 9 -> 9; matrix products, arithmetic and copies ran while one was open for 2% -> 2% of each run, Pallas kernels for 46% -> 50%
where the time goes in v10:
time: 94.1 us; the launch traced here: 93.7 us
  Pallas kernels  53.2 us (57%)
  starting transfers between devices  19.5 us (21%)
  waiting for transfers between devices  15.7 us (17%)
  local copies, waits for them, and re-layouts  5.05 us (5%)
    pallas_call x9, Pallas kernels, add_step(): pl.pallas_call(functools.partial(step_kernel, count, entry, last), out_sh...  42.8 us
    ppermute x4, waiting for transfers between devices, fast(): lax.ppermute(sent, 'mp', [(i, i ^ flip) for i in range(n)])  7.89 us
    ppermute x5, waiting for transfers between devices, fast(): streams[i % 2] = (send(block) if i + 2 < arrivals else None, send)  6.78 us
    ppermute x5, starting transfers between devices, fast(): streams[i % 2] = (send(block) if i + 2 < arrivals else None, send)  6.58 us
    ppermute x4, starting transfers between devices, fast(): lax.ppermute(sent, 'mp', [(i, i ^ flip) for i in range(n)])  6.11 us
    pallas_call x1, Pallas kernels, load(): pl.pallas_call(load_kernel, out_shape=[pltpu.VMEM((width, 2 * hidden + LA...  6.01 us
    unnamed x15, local copies, waits for them, and re-layouts  4.36 us
    ppermute x1, starting transfers between devices, fast(): one_way = send_one(tokens_in)  3.02 us
  transfers between devices with their start and end apart: 21, of which 9 were waited for; matrix products, arithmetic and copies ran while one was open for 2% of the time, Pallas kernels for 50%

profile of v10, /device:TPU:0, one launch (start us, length us, event | category | flops | bytes accessed | tf_op | source)
XLA Modules:
  0.0 93.7 jit_solution(800954784749477389)
XLA Ops:
  0.0 3.0 %collective-permute-start = (bf16[96,4096]{1,0:T(8,128)(2,1)}, bf16[96,4096]{1,0:T(8,128)(2,1)S(1)}, u32[]{:S(2)}, u32[]{:S(2)}) collective-permute-start(bf16[96,4096]{1,0:T(8,128)(2,1)} %refs_0_.1), channel_id=1, source_target_pairs={{0,2},{2,4},{4,6},{6,7},{7,5},{5,3},{3,1},{1,0},{10,8},{12,10},{14... | collective-permute-start | bytes 2359304 | tf_op jit(solution)/shard_map/ppermute | solution.py:282
  4.4 2.5 %shard_map.91 = (bf16[1536,896]{1,0:T(8,128)(2,1)S(1)}, bf16[1792,128]{1,0:T(8,128)(2,1)S(1)}) custom-call(s32[17]{0:T(128)S(1)} %dynamic-slice_bitcast_fusion.table, s32[8]{0:T(128)S(1)} %copy-done.1, bf16[1536,896]{1,0:T(8,128)(2,1)} %out_grad_hbm.1, bf16[896,128]{1,0:T(8,128)(2,1)} %proj_out_hbm.1), custom_call_target="tpu_custom_call" | custom-call | tf_op jit(solution)/shard_map/pallas_call | solution.py:171
  6.9 1.5 %copy-done.4 = bf16[1536,896]{1,0:T(8,128)(2,1)} copy-done((bf16[1536,896]{1,0:T(8,128)(2,1)}, bf16[1536,896]{1,0:T(8,128)(2,1)S(1)}, u32[]{:S(2)}) %copy-start.4) | copy-done | bytes 2752536
  10.2 1.5 %copy.10.proj_in = bf16[4096,64]{1,0:T(8,128)(2,1)S(1)} copy(bf16[4096,64]{0,1:T(8,128)(2,1)} %param.13) | data formatting | bytes 1048576 | tf_op args[4]
  12.4 6.0 %shard_map.92 = (bf16[4096,1920]{1,0:T(8,128)(2,1)S(1)}, f32[128,512]{1,0:T(8,128)S(1)}) custom-call(s32[8]{0:T(128)S(1)} %copy-done.2, bf16[1792,128]{1,0:T(8,128)(2,1)S(1)} %get-tuple-element.29.diagonal.refs_4_.refs_3_, bf16[4096,896]{1,0:T(8,128)(2,1)} %gate_hbm.1, bf16[4096,896]{1,0:T(8,128)(2,1)} %up_hbm.1, bf16[4096,64]{1,0:T(8,128)(2,1)S(1)} %copy.10.proj_in), custom_call_target="tpu_custom_call" | custom-call | tf_op jit(solution)/shard_map/pallas_call | solution.py:187
  18.5 1.6 %collective-permute-start.1 = (bf16[96,4096]{1,0:T(8,128)(2,1)S(1)}, bf16[96,4096]{1,0:T(8,128)(2,1)S(1)}, u32[]{:S(2)}, u32[]{:S(2)}) collective-permute-start(bf16[96,4096]{1,0:T(8,128)(2,1)S(1)} %collective-permute-done.refs_0_), channel_id=1, source_target_pairs={{0,2},{2,4},{4,6},{6,7},{7,5},{5,3},{3,1},{1,0},{10,8},{12,10},{14... | collective-permute-start | bytes 2359304 | tf_op jit(solution)/shard_map/ppermute | solution.py:301
  20.1 5.3 %shard_map.93.refs_5_ = f32[128,512]{1,0:T(8,128)S(1)} custom-call(s32[17]{0:T(128)S(1)} %dynamic-slice_bitcast_fusion.table, s32[8]{0:T(128)S(1)} %copy-done.3, bf16[96,4096]{1,0:T(8,128)(2,1)S(1)} %copy-done.6, bf16[96,4096]{1,0:T(8,128)(2,1)} %collective-permute-done.4.refs_1_, bf16[4096,1920]{1,0:T(8,128)(2,1)S(1)} %get-tuple-element.32.refs_2_.refs_1_, ...), custom_call_target="tpu_custom_call" | custom-call | flops 60397977600 | bytes 1572864 | tf_op jit(solution)/shard_map/pallas_call | solution.py:207
  26.6 4.7 %shard_map.94.refs_5_ = f32[128,512]{1,0:T(8,128)S(1)} custom-call(s32[17]{0:T(128)S(1)} %dynamic-slice_bitcast_fusion.table, s32[8]{0:T(128)S(1)} %copy-done.3, bf16[96,4096]{1,0:T(8,128)(2,1)S(1)} %collective-permute-done.refs_0_, bf16[96,4096]{1,0:T(8,128)(2,1)S(1)} %collective-permute-done.2.refs_1_, ...), custom_call_target="tpu_custom_call" | custom-call | flops 60397977600 | bytes 1572864 | tf_op jit(solution)/shard_map/pallas_call | solution.py:207
  32.2 1.6 %collective-permute-start.6 = (bf16[96,4096]{1,0:T(8,128)(2,1)S(1)}, bf16[96,4096]{1,0:T(8,128)(2,1)}, u32[]{:S(2)}, u32[]{:S(2)}) collective-permute-start(bf16[96,4096]{1,0:T(8,128)(2,1)S(1)} %collective-permute-done.1.refs_0_), channel_id=1, source_target_pairs={{0,2},{2,4},{4,6},{6,7},{7,5},{5,3},{3,1},{1,0},{10,8},{12,10},{14... | collective-permute-start | bytes 2359304 | tf_op jit(solution)/shard_map/ppermute | solution.py:301
  33.8 5.3 %shard_map.95.refs_5_ = f32[128,512]{1,0:T(8,128)S(1)} custom-call(s32[17]{0:T(128)S(1)} %dynamic-slice_bitcast_fusion.table, s32[8]{0:T(128)S(1)} %copy-done.3, bf16[96,4096]{1,0:T(8,128)(2,1)} %collective-permute-done.3.refs_0_, bf16[96,4096]{1,0:T(8,128)(2,1)S(1)} %collective-permute-done.9.refs_1_, ...), custom_call_target="tpu_custom_call" | custom-call | flops 60397977600 | bytes 1572864 | tf_op jit(solution)/shard_map/pallas_call | solution.py:207
  39.1 2.4 %collective-permute-done.8.refs_0_ = bf16[96,4096]{1,0:T(8,128)(2,1)S(1)} collective-permute-done((bf16[96,4096]{1,0:T(8,128)(2,1)}, bf16[96,4096]{1,0:T(8,128)(2,1)S(1)}, u32[]{:S(2)}, u32[]{:S(2)}) %collective-permute-start.8) | collective-permute-done | bytes 786464 | tf_op jit(solution)/shard_map/ppermute | solution.py:301
  42.9 4.7 %shard_map.96.refs_5_ = f32[128,512]{1,0:T(8,128)S(1)} custom-call(s32[17]{0:T(128)S(1)} %dynamic-slice_bitcast_fusion.table, s32[8]{0:T(128)S(1)} %copy-done.3, bf16[96,4096]{1,0:T(8,128)(2,1)S(1)} %collective-permute-done.1.refs_0_, bf16[96,4096]{1,0:T(8,128)(2,1)S(1)} %collective-permute-done.7.refs_1_, ...), custom_call_target="tpu_custom_call" | custom-call | flops 60397977600 | bytes 1572864 | tf_op jit(solution)/shard_map/pallas_call | solution.py:207
  47.6 2.6 %collective-permute-done.6.refs_0_ = bf16[96,4096]{1,0:T(8,128)(2,1)} collective-permute-done((bf16[96,4096]{1,0:T(8,128)(2,1)S(1)}, bf16[96,4096]{1,0:T(8,128)(2,1)}, u32[]{:S(2)}, u32[]{:S(2)}) %collective-permute-start.6) | collective-permute-done | bytes 786464 | tf_op jit(solution)/shard_map/ppermute | solution.py:301
  50.2 1.3 %collective-permute-start.10 = (bf16[96,4096]{1,0:T(8,128)(2,1)}, bf16[96,4096]{1,0:T(8,128)(2,1)}, u32[]{:S(2)}, u32[]{:S(2)}) collective-permute-start(bf16[96,4096]{1,0:T(8,128)(2,1)} %collective-permute-done.6.refs_0_), channel_id=1, source_target_pairs={{0,2},{2,4},{4,6},{6,7},{7,5},{5,3},{3,1},{1,0},{10,8},{12,10},{14... | collective-permute-start | bytes 2359304 | tf_op jit(solution)/shard_map/ppermute | solution.py:301
  51.5 4.7 %shard_map.97.refs_5_ = f32[128,512]{1,0:T(8,128)S(1)} custom-call(s32[17]{0:T(128)S(1)} %dynamic-slice_bitcast_fusion.table, s32[8]{0:T(128)S(1)} %copy-done.3, bf16[96,4096]{1,0:T(8,128)(2,1)S(1)} %collective-permute-done.8.refs_0_, bf16[96,4096]{1,0:T(8,128)(2,1)S(1)} %collective-permute-done.12.refs_1_, ...), custom_call_target="tpu_custom_call" | custom-call | flops 60397977600 | bytes 1572864 | tf_op jit(solution)/shard_map/pallas_call | solution.py:207
  57.8 5.3 %shard_map.98.refs_5_ = f32[128,512]{1,0:T(8,128)S(1)} custom-call(s32[17]{0:T(128)S(1)} %dynamic-slice_bitcast_fusion.table, s32[8]{0:T(128)S(1)} %copy-done.3, bf16[96,4096]{1,0:T(8,128)(2,1)} %collective-permute-done.6.refs_0_, bf16[96,4096]{1,0:T(8,128)(2,1)S(1)} %collective-permute-done.14.refs_1_, ...), custom_call_target="tpu_custom_call" | custom-call | flops 60397977600 | bytes 1572864 | tf_op jit(solution)/shard_map/pallas_call | solution.py:207
  63.0 4.7 %shard_map.99.refs_4_ = f32[128,512]{1,0:T(8,128)S(1)} custom-call(s32[17]{0:T(128)S(1)} %dynamic-slice_bitcast_fusion.table, s32[8]{0:T(128)S(1)} %copy-done.3, bf16[96,4096]{1,0:T(8,128)(2,1)S(1)} %collective-permute-done.11.refs_0_, bf16[96,4096]{1,0:T(8,128)(2,1)S(1)} %collective-permute-done.13.refs_1_, ...), custom_call_target="tpu_custom_call" | custom-call | flops 60397977600 | bytes 1572864 | tf_op jit(solution)/shard_map/pallas_call | solution.py:207
  67.8 4.4 %shard_map.100.refs_4_ = f32[128,512]{1,0:T(8,128)S(1)} custom-call(s32[17]{0:T(128)S(1)} %dynamic-slice_bitcast_fusion.table, s32[8]{0:T(128)S(1)} %copy-done.3, bf16[96,4096]{1,0:T(8,128)(2,1)} %collective-permute-done.10.refs_0_, bf16[4096,1920]{1,0:T(8,128)(2,1)S(1)} %get-tuple-element.32.refs_2_.refs_1_, bf16[1536,896]{1,0:T(8,128)(2,1)S(1)} %copy-done.5, ...), custom_call_target="tpu_custom_call" | custom-call | flops 30198988800 | bytes 786432 | tf_op jit(solution)/shard_map/pallas_call | solution.py:207
  72.2 4.0 %shard_map.101 = (f32[128,256]{1,0:T(8,128)S(1)}, f32[128,256]{1,0:T(8,128)S(1)}) custom-call(s32[17]{0:T(128)S(1)} %dynamic-slice_bitcast_fusion.table, s32[8]{0:T(128)S(1)} %copy-done.3, bf16[96,4096]{1,0:T(8,128)(2,1)S(1)} %collective-permute-done.15.refs_0_, bf16[4096,1920]{1,0:T(8,128)(2,1)S(1)} %get-tuple-element.32.refs_2_.refs_1_, ...), custom_call_target="tpu_custom_call" | custom-call | flops 30198988800 | bytes 786432 | tf_op jit(solution)/shard_map/pallas_call | solution.py:207
  78.9 1.5 %collective-permute-start.18 = (bf16[128,256]{1,0:T(8,128)(2,1)S(1)}, bf16[128,256]{1,0:T(8,128)(2,1)S(1)}, u32[]{:S(2)}, u32[]{:S(2)}) collective-permute-start(bf16[128,256]{1,0:T(8,128)(2,1)S(1)} %get-tuple-element.53), channel_id=1, source_target_pairs={{0,2},{1,3},{2,0},{3,1},{4,6},{5,7},{6,4},{7,5},{8,10},{9,11},{10,... | collective-permute-start | bytes 196616 | tf_op jit(solution)/shard_map/ppermute | solution.py:320
  83.2 2.4 %collective-permute-done.19 = bf16[128,256]{1,0:T(8,128)(2,1)S(1)} collective-permute-done((bf16[128,256]{1,0:T(8,128)(2,1)S(1)}, bf16[128,256]{1,0:T(8,128)(2,1)S(1)}, u32[]{:S(2)}, u32[]{:S(2)}) %collective-permute-start.19) | collective-permute-done | bytes 65568 | tf_op jit(solution)/shard_map/ppermute | solution.py:320
  85.6 2.5 %collective-permute-start.20 = (bf16[128,256]{1,0:T(8,128)(2,1)S(1)}, bf16[128,256]{1,0:T(8,128)(2,1)S(1)}, u32[]{:S(2)}, u32[]{:S(2)}) collective-permute-start(bf16[128,256]{1,0:T(8,128)(2,1)S(1)} %get-tuple-element.51), channel_id=1, source_target_pairs={{0,4},{1,5},{2,6},{3,7},{4,0},{5,1},{6,2},{7,3},{8,12},{9,13},{10,... | collective-permute-start | bytes 196616 | tf_op jit(solution)/shard_map/ppermute | solution.py:320
  88.1 3.7 %collective-permute-done.20.theirs = bf16[128,256]{1,0:T(8,128)(2,1)S(1)} collective-permute-done((bf16[128,256]{1,0:T(8,128)(2,1)S(1)}, bf16[128,256]{1,0:T(8,128)(2,1)S(1)}, u32[]{:S(2)}, u32[]{:S(2)}) %collective-permute-start.20) | collective-permute-done | bytes 65568 | tf_op jit(solution)/shard_map/ppermute | solution.py:320
  91.8 1.9 %shard_map.102 = f32[4,128]{1,0:T(4,128)} custom-call(s32[17]{0:T(128)S(1)} %dynamic-slice_bitcast_fusion.table, f32[128,256]{1,0:T(8,128)S(1)} %get-tuple-element.52.mine, bf16[128,256]{1,0:T(8,128)(2,1)S(1)} %collective-permute-done.20.theirs, bf16[128,4096]{1,0:T(8,128)(2,1)S(1)} %copy-done, bf16[128,4096]{1,0:T(8,128)(2,1)S(1)} %collective-permute-done.5.val_other), custom_call_target="tpu_custom_call" | custom-call | tf_op jit(solution)/shard_map/pallas_call | solution.py:256
  (48 shorter events, 14.6 us)
Async XLA Ops:
  0.0 18.4 %collective-permute-start = (bf16[96,4096]{1,0:T(8,128)(2,1)}, bf16[96,4096]{1,0:T(8,128)(2,1)S(1)}, u32[]{:S(2)}, u32[]{:S(2)}) collective-permute-start(bf16[96,4096]{1,0:T(8,128)(2,1)} %refs_0_.1), channel_id=1, source_target_pairs={{0,2},{2,4},{4,6},{6,7},{7,5},{5,3},{3,1},{1,0},{10,8},{12,10},{14... | collective-permute-start | bytes 2359304 | tf_op jit(solution)/shard_map/ppermute | solution.py:282
  3.0 17.1 %collective-permute-start.4 = (bf16[96,4096]{1,0:T(8,128)(2,1)}, bf16[96,4096]{1,0:T(8,128)(2,1)}, u32[]{:S(2)}, u32[]{:S(2)}) collective-permute-start(bf16[96,4096]{1,0:T(8,128)(2,1)} %refs_0_.1), channel_id=1, source_target_pairs={{0,8},{8,0},{1,9},{9,1},{2,10},{10,2},{3,11},{11,3},{4,12},{12,4},... | collective-permute-start | bytes 2359304 | tf_op jit(solution)/shard_map/ppermute | solution.py:283
  8.4 17.0 %collective-permute-start.3 = (bf16[96,4096]{1,0:T(8,128)(2,1)}, bf16[96,4096]{1,0:T(8,128)(2,1)}, u32[]{:S(2)}, u32[]{:S(2)}) collective-permute-start(bf16[96,4096]{1,0:T(8,128)(2,1)} %refs_0_.1), channel_id=1, source_target_pairs={{2,0},{4,2},{6,4},{7,6},{5,7},{3,5},{1,3},{0,1},{8,10},{10,12},{12... | collective-permute-start | bytes 2359304 | tf_op jit(solution)/shard_map/ppermute | solution.py:286
  9.5 16.0 %collective-permute-start.5 = (bf16[128,4096]{1,0:T(8,128)(2,1)}, bf16[128,4096]{1,0:T(8,128)(2,1)S(1)}, u32[]{:S(2)}, u32[]{:S(2)}) collective-permute-start(bf16[128,4096]{1,0:T(8,128)(2,1)} %val_own.1), channel_id=1, source_target_pairs={{0,8},{8,0},{1,9},{9,1},{2,10},{10,2},{3,11},{11,3},{4,12},{12,4},... | collective-permute-start | bytes 3145736 | tf_op jit(solution)/shard_map/ppermute | solution.py:283
  12.4 7.8 %copy-start.5 = (bf16[1536,896]{1,0:T(8,128)(2,1)S(1)}, bf16[1536,896]{1,0:T(8,128)(2,1)}, u32[]{:S(2)}) copy-start(bf16[1536,896]{1,0:T(8,128)(2,1)} %copy-done.4) | copy-start | bytes 8257540
  12.4 7.8 %copy-start.6 = (bf16[96,4096]{1,0:T(8,128)(2,1)S(1)}, bf16[96,4096]{1,0:T(8,128)(2,1)}, u32[]{:S(2)}) copy-start(bf16[96,4096]{1,0:T(8,128)(2,1)} %refs_0_.1) | copy-start | bytes 2359300
  18.4 8.2 %collective-permute-start.2 = (bf16[96,4096]{1,0:T(8,128)(2,1)S(1)}, bf16[96,4096]{1,0:T(8,128)(2,1)S(1)}, u32[]{:S(2)}, u32[]{:S(2)}) collective-permute-start(bf16[96,4096]{1,0:T(8,128)(2,1)S(1)} %collective-permute-done.refs_0_), channel_id=1, source_target_pairs={{0,8},{8,0},{1,9},{9,1},{2,10},{10,2},{3,11},{11,3},{4,12},{12,4},... | collective-permute-start | bytes 2359304 | tf_op jit(solution)/shard_map/ppermute | solution.py:306
  18.5 13.7 %collective-permute-start.1 = (bf16[96,4096]{1,0:T(8,128)(2,1)S(1)}, bf16[96,4096]{1,0:T(8,128)(2,1)S(1)}, u32[]{:S(2)}, u32[]{:S(2)}) collective-permute-start(bf16[96,4096]{1,0:T(8,128)(2,1)S(1)} %collective-permute-done.refs_0_), channel_id=1, source_target_pairs={{0,2},{2,4},{4,6},{6,7},{7,5},{5,3},{3,1},{1,0},{10,8},{12,10},{14... | collective-permute-start | bytes 2359304 | tf_op jit(solution)/shard_map/ppermute | solution.py:301
  25.4 8.4 %collective-permute-start.9 = (bf16[96,4096]{1,0:T(8,128)(2,1)}, bf16[96,4096]{1,0:T(8,128)(2,1)S(1)}, u32[]{:S(2)}, u32[]{:S(2)}) collective-permute-start(bf16[96,4096]{1,0:T(8,128)(2,1)} %collective-permute-done.3.refs_0_), channel_id=1, source_target_pairs={{0,8},{8,0},{1,9},{9,1},{2,10},{10,2},{3,11},{11,3},{4,12},{12,4},... | collective-permute-start | bytes 2359304 | tf_op jit(solution)/shard_map/ppermute | solution.py:306
  25.5 16.0 %collective-permute-start.8 = (bf16[96,4096]{1,0:T(8,128)(2,1)}, bf16[96,4096]{1,0:T(8,128)(2,1)S(1)}, u32[]{:S(2)}, u32[]{:S(2)}) collective-permute-start(bf16[96,4096]{1,0:T(8,128)(2,1)} %collective-permute-done.3.refs_0_), channel_id=1, source_target_pairs={{2,0},{4,2},{6,4},{7,6},{5,7},{3,5},{1,3},{0,1},{8,10},{10,12},{12... | collective-permute-start | bytes 2359304 | tf_op jit(solution)/shard_map/ppermute | solution.py:301
  32.2 10.7 %collective-permute-start.7 = (bf16[96,4096]{1,0:T(8,128)(2,1)S(1)}, bf16[96,4096]{1,0:T(8,128)(2,1)S(1)}, u32[]{:S(2)}, u32[]{:S(2)}) collective-permute-start(bf16[96,4096]{1,0:T(8,128)(2,1)S(1)} %collective-permute-done.1.refs_0_), channel_id=1, source_target_pairs={{0,8},{8,0},{1,9},{9,1},{2,10},{10,2},{3,11},{11,3},{4,12},{12,4},... | collective-permute-start | bytes 2359304 | tf_op jit(solution)/shard_map/ppermute | solution.py:306
  32.2 18.0 %collective-permute-start.6 = (bf16[96,4096]{1,0:T(8,128)(2,1)S(1)}, bf16[96,4096]{1,0:T(8,128)(2,1)}, u32[]{:S(2)}, u32[]{:S(2)}) collective-permute-start(bf16[96,4096]{1,0:T(8,128)(2,1)S(1)} %collective-permute-done.1.refs_0_), channel_id=1, source_target_pairs={{0,2},{2,4},{4,6},{6,7},{7,5},{5,3},{3,1},{1,0},{10,8},{12,10},{14... | collective-permute-start | bytes 2359304 | tf_op jit(solution)/shard_map/ppermute | solution.py:301
  41.5 10.0 %collective-permute-start.12 = (bf16[96,4096]{1,0:T(8,128)(2,1)S(1)}, bf16[96,4096]{1,0:T(8,128)(2,1)S(1)}, u32[]{:S(2)}, u32[]{:S(2)}) collective-permute-start(bf16[96,4096]{1,0:T(8,128)(2,1)S(1)} %collective-permute-done.8.refs_0_), channel_id=1, source_target_pairs={{0,8},{8,0},{1,9},{9,1},{2,10},{10,2},{3,11},{11,3},{4,12},{12,4},... | collective-permute-start | bytes 2359304 | tf_op jit(solution)/shard_map/ppermute | solution.py:306
  42.0 15.0 %collective-permute-start.11 = (bf16[96,4096]{1,0:T(8,128)(2,1)S(1)}, bf16[96,4096]{1,0:T(8,128)(2,1)S(1)}, u32[]{:S(2)}, u32[]{:S(2)}) collective-permute-start(bf16[96,4096]{1,0:T(8,128)(2,1)S(1)} %collective-permute-done.8.refs_0_), channel_id=1, source_target_pairs={{2,0},{4,2},{6,4},{7,6},{5,7},{3,5},{1,3},{0,1},{8,10},{10,12},{12... | collective-permute-start | bytes 2359304 | tf_op jit(solution)/shard_map/ppermute | solution.py:301
  50.2 7.6 %collective-permute-start.14 = (bf16[96,4096]{1,0:T(8,128)(2,1)}, bf16[96,4096]{1,0:T(8,128)(2,1)S(1)}, u32[]{:S(2)}, u32[]{:S(2)}) collective-permute-start(bf16[96,4096]{1,0:T(8,128)(2,1)} %collective-permute-done.6.refs_0_), channel_id=1, source_target_pairs={{0,8},{8,0},{1,9},{9,1},{2,10},{10,2},{3,11},{11,3},{4,12},{12,4},... | collective-permute-start | bytes 2359304 | tf_op jit(solution)/shard_map/ppermute | solution.py:306
  50.2 17.5 %collective-permute-start.10 = (bf16[96,4096]{1,0:T(8,128)(2,1)}, bf16[96,4096]{1,0:T(8,128)(2,1)}, u32[]{:S(2)}, u32[]{:S(2)}) collective-permute-start(bf16[96,4096]{1,0:T(8,128)(2,1)} %collective-permute-done.6.refs_0_), channel_id=1, source_target_pairs={{0,2},{2,4},{4,6},{6,7},{7,5},{5,3},{3,1},{1,0},{10,8},{12,10},{14... | collective-permute-start | bytes 2359304 | tf_op jit(solution)/shard_map/ppermute | solution.py:301
  57.0 6.1 %collective-permute-start.13 = (bf16[96,4096]{1,0:T(8,128)(2,1)S(1)}, bf16[96,4096]{1,0:T(8,128)(2,1)S(1)}, u32[]{:S(2)}, u32[]{:S(2)}) collective-permute-start(bf16[96,4096]{1,0:T(8,128)(2,1)S(1)} %collective-permute-done.11.refs_0_), channel_id=1, source_target_pairs={{0,8},{8,0},{1,9},{9,1},{2,10},{10,2},{3,11},{11,3},{4,12},{12,4},... | collective-permute-start | bytes 2359304 | tf_op jit(solution)/shard_map/ppermute | solution.py:306
  67.7 4.5 %collective-permute-start.15 = (bf16[96,4096]{1,0:T(8,128)(2,1)}, bf16[96,4096]{1,0:T(8,128)(2,1)S(1)}, u32[]{:S(2)}, u32[]{:S(2)}) collective-permute-start(bf16[96,4096]{1,0:T(8,128)(2,1)} %collective-permute-done.10.refs_0_), channel_id=1, source_target_pairs={{0,8},{8,0},{1,9},{9,1},{2,10},{10,2},{3,11},{11,3},{4,12},{12,4},... | collective-permute-start | bytes 2359304 | tf_op jit(solution)/shard_map/ppermute | solution.py:304
  72.2 19.6 %copy-start = (bf16[128,4096]{1,0:T(8,128)(2,1)S(1)}, bf16[128,4096]{1,0:T(8,128)(2,1)}, u32[]{:S(2)}) copy-start(bf16[128,4096]{1,0:T(8,128)(2,1)} %val_own.1) | copy-start | bytes 3145732
  76.2 1.5 %collective-permute-start.16 = (f32[128,256]{1,0:T(8,128)S(1)}, f32[128,256]{1,0:T(8,128)S(1)}, u32[]{:S(2)}, u32[]{:S(2)}) collective-permute-start(f32[128,256]{1,0:T(8,128)S(1)} %get-tuple-element.49), channel_id=1, source_target_pairs={{0,8},{8,0},{1,9},{9,1},{2,10},{10,2},{3,11},{11,3},{4,12},{12,4},... | collective-permute-start | bytes 393224 | tf_op jit(solution)/shard_map/ppermute | solution.py:311
  77.8 4.4 %collective-permute-start.17 = (bf16[128,256]{1,0:T(8,128)(2,1)S(1)}, bf16[128,256]{1,0:T(8,128)(2,1)S(1)}, u32[]{:S(2)}, u32[]{:S(2)}) collective-permute-start(bf16[128,256]{1,0:T(8,128)(2,1)S(1)} %get-tuple-element.53), channel_id=1, source_target_pairs={{0,1},{1,0},{2,3},{3,2},{4,5},{5,4},{6,7},{7,6},{8,9},{9,8},{10,11... | collective-permute-start | bytes 196616 | tf_op jit(solution)/shard_map/ppermute | solution.py:320
  78.9 4.3 %collective-permute-start.18 = (bf16[128,256]{1,0:T(8,128)(2,1)S(1)}, bf16[128,256]{1,0:T(8,128)(2,1)S(1)}, u32[]{:S(2)}, u32[]{:S(2)}) collective-permute-start(bf16[128,256]{1,0:T(8,128)(2,1)S(1)} %get-tuple-element.53), channel_id=1, source_target_pairs={{0,2},{1,3},{2,0},{3,1},{4,6},{5,7},{6,4},{7,5},{8,10},{9,11},{10,... | collective-permute-start | bytes 196616 | tf_op jit(solution)/shard_map/ppermute | solution.py:320
  80.4 5.2 %collective-permute-start.19 = (bf16[128,256]{1,0:T(8,128)(2,1)S(1)}, bf16[128,256]{1,0:T(8,128)(2,1)S(1)}, u32[]{:S(2)}, u32[]{:S(2)}) collective-permute-start(bf16[128,256]{1,0:T(8,128)(2,1)S(1)} %get-tuple-element.53), channel_id=1, source_target_pairs={{0,3},{1,2},{2,1},{3,0},{4,7},{5,6},{6,5},{7,4},{8,11},{9,10},{10,... | collective-permute-start | bytes 196616 | tf_op jit(solution)/shard_map/ppermute | solution.py:320
  85.6 6.2 %collective-permute-start.20 = (bf16[128,256]{1,0:T(8,128)(2,1)S(1)}, bf16[128,256]{1,0:T(8,128)(2,1)S(1)}, u32[]{:S(2)}, u32[]{:S(2)}) collective-permute-start(bf16[128,256]{1,0:T(8,128)(2,1)S(1)} %get-tuple-element.51), channel_id=1, source_target_pairs={{0,4},{1,5},{2,6},{3,7},{4,0},{5,1},{6,2},{7,3},{8,12},{9,13},{10,... | collective-permute-start | bytes 196616 | tf_op jit(solution)/shard_map/ppermute | solution.py:320
  (4 other events, 10.6 us)

commit v11 on v9

--- a/solution.py
+++ b/solution.py
@@ -226,22 +226,23 @@
     half = rank // 2
     left = lax.broadcasted_iota(jnp.int32, (own, LANES), 1) < LANES // 2
     squares = jnp.zeros((own, LANES), jnp.float32)
-    found = jnp.zeros((4 * own, scores.shape[1]), jnp.float32)
-    for side, val in ((core, val_own), (1 - core, val_other)):
+    rows = []
+    for side in (core, 1 - core):
         gates, ups = [], []
         for a in range(half):
             slab = sketch[pl.ds(side * half + a, own, stride=rank), :]
             squares += slab * slab
             gates.append(jnp.where(left, slab, 0.0))
             ups.append(jnp.where(left, 0.0, slab))
-        gate_high, gate_low = split(jnp.concatenate(gates, axis=1))
-        up_high, up_low = split(jnp.concatenate(ups, axis=1))
-        found += lax.dot_general(
-            jnp.concatenate([gate_high, gate_low, up_high, up_low], axis=0),
-            val[...],
-            (((1,), (1,)), ((), ())),
-            preferred_element_type=jnp.float32,
-        )
+        rows += [*split(jnp.concatenate(gates, axis=1)), *split(jnp.concatenate(ups, axis=1))]
+    products = lax.dot_general(
+        jnp.concatenate(rows, axis=0),
+        jnp.concatenate([val_own[...], val_other[...]], axis=0),
+        (((1,), (1,)), ((), ())),
+        preferred_element_type=jnp.float32,
+    )
+    columns = scores.shape[1]
+    found = products[: 4 * own, :columns] + products[4 * own :, columns:]
     count = rank * LANES // 2
     gate_mean = jnp.sum(jnp.where(left, squares, 0.0), axis=1, keepdims=True) / count
     up_mean = jnp.sum(jnp.where(left, 0.0, squares), axis=1, keepdims=True) / count
@@ -313,14 +314,14 @@
         sent = mine.astype(jnp.bfloat16)
         exchange = [bit]
         if bit == 1 and n >= 8:
-            exchange = [1, 2, 3]
+            exchange = [3, 2, 1]
         got = [
             lax.ppermute(sent, "mp", [(i, i ^ flip) for i in range(n)]) for flip in exchange
         ]
         for part in got[:-1]:
             mine = mine + part.astype(jnp.float32)
         theirs = got[-1]
-        bit = exchange[-1] + 1 if len(exchange) > 1 else 2 * bit
+        bit = 4 if len(exchange) > 1 else 2 * bit
         if bit < n:
             theirs = theirs.astype(jnp.float32)
     return score(table, mine, theirs, val_sketch, other_val, seq_count // 2)

time: 91.7 us -> 90.2 us (0.984)
  waiting for transfers between devices: 16.2 us -> 14.6 us
    ppermute x4, waiting for transfers between devices: 7.96 us -> 6.36 us  [fast(): lax.ppermute(sent, 'mp', [(i, i ^ flip) for i in range(n)])]
  transfers between devices with their start and end apart: 21 -> 21, of which waited for: 9 -> 9; matrix products, arithmetic and copies ran while one was open for 2% -> 2% of each run, Pallas kernels for 46% -> 47%
where the time goes in v11:
time: 90.2 us; the launch traced here: 89.9 us
  Pallas kernels  49 us (54%)
  starting transfers between devices  21 us (23%)
  waiting for transfers between devices  14.6 us (16%)
  local copies, waits for them, and re-layouts  5.05 us (6%)
    pallas_call x8, Pallas kernels, add_step(): pl.pallas_call(functools.partial(step_kernel, entry, last), out_shape=out...  38.7 us
    ppermute x4, waiting for transfers between devices, fast(): lax.ppermute(sent, 'mp', [(i, i ^ flip) for i in range(n)])  6.36 us
    ppermute x4, starting transfers between devices, fast(): lax.ppermute(sent, 'mp', [(i, i ^ flip) for i in range(n)])  6.22 us
    pallas_call x1, Pallas kernels, load(): pl.pallas_call(load_kernel, out_shape=[pltpu.VMEM((width, 2 * hidden + LA...  6.01 us
    ppermute x3, waiting for transfers between devices, fast(): next_one = send_one(one_way)  5.65 us
    ppermute x3, starting transfers between devices, fast(): next_one = send_one(one_way)  4.54 us
    unnamed x15, local copies, waits for them, and re-layouts  4.36 us
    ppermute x1, starting transfers between devices, fast(): one_way = send_one(tokens_in)  3.02 us
  transfers between devices with their start and end apart: 21, of which 9 were waited for; matrix products, arithmetic and copies ran while one was open for 2% of the time, Pallas kernels for 47%

profile of v11, /device:TPU:0, one launch (start us, length us, event | category | flops | bytes accessed | tf_op | source)
XLA Modules:
  0.0 89.9 jit_solution(18373266114521918228)
XLA Ops:
  0.0 3.0 %collective-permute-start = (bf16[96,4096]{1,0:T(8,128)(2,1)}, bf16[96,4096]{1,0:T(8,128)(2,1)S(1)}, u32[]{:S(2)}, u32[]{:S(2)}) collective-permute-start(bf16[96,4096]{1,0:T(8,128)(2,1)} %one.1), channel_id=1, source_target_pairs={{0,2},{2,4},{4,6},{6,7},{7,5},{5,3},{3,1},{1,0},{10,8},{12,10},{14... | collective-permute-start | bytes 2359304 | tf_op jit(solution)/shard_map/ppermute | solution.py:283
  4.9 2.5 %shard_map.91 = (bf16[1536,896]{1,0:T(8,128)(2,1)S(1)}, bf16[1792,128]{1,0:T(8,128)(2,1)S(1)}) custom-call(s32[17]{0:T(128)S(1)} %dynamic-slice_bitcast_fusion.table, s32[8]{0:T(128)S(1)} %copy-done.1, bf16[1536,896]{1,0:T(8,128)(2,1)} %out_grad_hbm.1, bf16[896,128]{1,0:T(8,128)(2,1)} %proj_out_hbm.1), custom_call_target="tpu_custom_call" | custom-call | tf_op jit(solution)/shard_map/pallas_call | solution.py:170
  7.4 1.5 %copy-done.4 = bf16[1536,896]{1,0:T(8,128)(2,1)} copy-done((bf16[1536,896]{1,0:T(8,128)(2,1)}, bf16[1536,896]{1,0:T(8,128)(2,1)S(1)}, u32[]{:S(2)}) %copy-start.4) | copy-done | bytes 2752536
  9.5 1.5 %copy.10.proj_in = bf16[4096,64]{1,0:T(8,128)(2,1)S(1)} copy(bf16[4096,64]{0,1:T(8,128)(2,1)} %param.13) | data formatting | bytes 1048576 | tf_op args[4]
  11.6 6.0 %shard_map.92 = (bf16[4096,1920]{1,0:T(8,128)(2,1)S(1)}, f32[512,128]{1,0:T(8,128)S(1)}) custom-call(s32[8]{0:T(128)S(1)} %copy-done.2, bf16[1792,128]{1,0:T(8,128)(2,1)S(1)} %get-tuple-element.31.diagonal, bf16[4096,896]{1,0:T(8,128)(2,1)} %gate_hbm.1, bf16[4096,896]{1,0:T(8,128)(2,1)} %up_hbm.1, bf16[4096,64]{1,0:T(8,128)(2,1)S(1)} %copy.10.proj_in), custom_call_target="tpu_custom_call" | custom-call | tf_op jit(solution)/shard_map/pallas_call | solution.py:186
  18.5 1.6 %collective-permute-start.1 = (bf16[96,4096]{1,0:T(8,128)(2,1)S(1)}, bf16[96,4096]{1,0:T(8,128)(2,1)S(1)}, u32[]{:S(2)}, u32[]{:S(2)}) collective-permute-start(bf16[96,4096]{1,0:T(8,128)(2,1)S(1)} %collective-permute-done.one), channel_id=1, source_target_pairs={{0,2},{2,4},{4,6},{6,7},{7,5},{5,3},{3,1},{1,0},{10,8},{12,10},{14... | collective-permute-start | bytes 2359304 | tf_op jit(solution)/shard_map/ppermute | solution.py:296
  20.1 5.3 %shard_map.93.before = f32[512,128]{1,0:T(8,128)S(1)} custom-call(s32[17]{0:T(128)S(1)} %dynamic-slice_bitcast_fusion.table, s32[8]{0:T(128)S(1)} %copy-done.3, bf16[96,4096]{1,0:T(8,128)(2,1)S(1)} %copy-done.6, bf16[96,4096]{1,0:T(8,128)(2,1)} %collective-permute-done.4.two, bf16[4096,1920]{1,0:T(8,128)(2,1)S(1)} %get-tuple-element.34.w, ...), custom_call_target="tpu_custom_call" | custom-call | flops 6039797760 | bytes 1572864 | tf_op jit(solution)/shard_map/pallas_call | solution.py:207
  26.5 4.7 %shard_map.94.before = f32[512,128]{1,0:T(8,128)S(1)} custom-call(s32[17]{0:T(128)S(1)} %dynamic-slice_bitcast_fusion.table, s32[8]{0:T(128)S(1)} %copy-done.3, bf16[96,4096]{1,0:T(8,128)(2,1)S(1)} %collective-permute-done.one, bf16[96,4096]{1,0:T(8,128)(2,1)S(1)} %collective-permute-done.2.two, bf16[4096,1920]{1,0:T(8,128)(2,1)S(1)} %get-tuple-element.34.w, ...), custom_call_target="tpu_custom_call" | custom-call | flops 6039797760 | bytes 1572864 | tf_op jit(solution)/shard_map/pallas_call | solution.py:207
  32.1 1.7 %collective-permute-start.6 = (bf16[96,4096]{1,0:T(8,128)(2,1)S(1)}, bf16[96,4096]{1,0:T(8,128)(2,1)S(1)}, u32[]{:S(2)}, u32[]{:S(2)}) collective-permute-start(bf16[96,4096]{1,0:T(8,128)(2,1)S(1)} %collective-permute-done.1.one), channel_id=1, source_target_pairs={{0,2},{2,4},{4,6},{6,7},{7,5},{5,3},{3,1},{1,0},{10,8},{12,10},{14... | collective-permute-start | bytes 2359304 | tf_op jit(solution)/shard_map/ppermute | solution.py:296
  33.8 5.3 %shard_map.95.before = f32[512,128]{1,0:T(8,128)S(1)} custom-call(s32[17]{0:T(128)S(1)} %dynamic-slice_bitcast_fusion.table, s32[8]{0:T(128)S(1)} %copy-done.3, bf16[96,4096]{1,0:T(8,128)(2,1)} %collective-permute-done.3.one, bf16[96,4096]{1,0:T(8,128)(2,1)S(1)} %collective-permute-done.9.two, bf16[4096,1920]{1,0:T(8,128)(2,1)S(1)} %get-tuple-element.34.w, ...), custom_call_target="tpu_custom_call" | custom-call | flops 6039797760 | bytes 1572864 | tf_op jit(solution)/shard_map/pallas_call | solution.py:207
  39.1 1.6 %collective-permute-done.8.one = bf16[96,4096]{1,0:T(8,128)(2,1)S(1)} collective-permute-done((bf16[96,4096]{1,0:T(8,128)(2,1)}, bf16[96,4096]{1,0:T(8,128)(2,1)S(1)}, u32[]{:S(2)}, u32[]{:S(2)}) %collective-permute-start.8) | collective-permute-done | bytes 786464 | tf_op jit(solution)/shard_map/ppermute | solution.py:300
  42.8 4.7 %shard_map.96.before = f32[512,128]{1,0:T(8,128)S(1)} custom-call(s32[17]{0:T(128)S(1)} %dynamic-slice_bitcast_fusion.table, s32[8]{0:T(128)S(1)} %copy-done.3, bf16[96,4096]{1,0:T(8,128)(2,1)S(1)} %collective-permute-done.1.one, bf16[96,4096]{1,0:T(8,128)(2,1)S(1)} %collective-permute-done.7.two, bf16[4096,1920]{1,0:T(8,128)(2,1)S(1)} %get-tuple-element.34.w, ...), custom_call_target="tpu_custom_call" | custom-call | flops 6039797760 | bytes 1572864 | tf_op jit(solution)/shard_map/pallas_call | solution.py:207
  47.4 2.8 %collective-permute-done.6.one = bf16[96,4096]{1,0:T(8,128)(2,1)S(1)} collective-permute-done((bf16[96,4096]{1,0:T(8,128)(2,1)S(1)}, bf16[96,4096]{1,0:T(8,128)(2,1)S(1)}, u32[]{:S(2)}, u32[]{:S(2)}) %collective-permute-start.6) | collective-permute-done | bytes 786464 | tf_op jit(solution)/shard_map/ppermute | solution.py:296
  51.6 4.7 %shard_map.97.before = f32[512,128]{1,0:T(8,128)S(1)} custom-call(s32[17]{0:T(128)S(1)} %dynamic-slice_bitcast_fusion.table, s32[8]{0:T(128)S(1)} %copy-done.3, bf16[96,4096]{1,0:T(8,128)(2,1)S(1)} %collective-permute-done.8.one, bf16[96,4096]{1,0:T(8,128)(2,1)S(1)} %collective-permute-done.13.two, bf16[4096,1920]{1,0:T(8,128)(2,1)S(1)} %get-tuple-element.34.w, ...), custom_call_target="tpu_custom_call" | custom-call | flops 6039797760 | bytes 1572864 | tf_op jit(solution)/shard_map/pallas_call | solution.py:207
  56.2 1.5 %collective-permute-start.15 = (bf16[96,4096]{1,0:T(8,128)(2,1)S(1)}, bf16[96,4096]{1,0:T(8,128)(2,1)S(1)}, u32[]{:S(2)}, u32[]{:S(2)}) collective-permute-start(bf16[96,4096]{1,0:T(8,128)(2,1)S(1)} %collective-permute-done.12.one), channel_id=1, source_target_pairs={{0,8},{8,0},{1,9},{9,1},{2,10},{10,2},{3,11},{11,3},{4,12},{12,4},... | collective-permute-start | bytes 2359304 | tf_op jit(solution)/shard_map/ppermute | solution.py:303
  57.7 4.6 %shard_map.98.before = f32[512,128]{1,0:T(8,128)S(1)} custom-call(s32[17]{0:T(128)S(1)} %dynamic-slice_bitcast_fusion.table, s32[8]{0:T(128)S(1)} %copy-done.3, bf16[96,4096]{1,0:T(8,128)(2,1)S(1)} %collective-permute-done.6.one, bf16[96,4096]{1,0:T(8,128)(2,1)S(1)} %collective-permute-done.11.two, bf16[4096,1920]{1,0:T(8,128)(2,1)S(1)} %get-tuple-element.34.w, ...), custom_call_target="tpu_custom_call" | custom-call | flops 6039797760 | bytes 1572864 | tf_op jit(solution)/shard_map/pallas_call | solution.py:207
  62.3 1.8 %collective-permute-done.10.one = bf16[96,4096]{1,0:T(8,128)(2,1)S(1)} collective-permute-done((bf16[96,4096]{1,0:T(8,128)(2,1)S(1)}, bf16[96,4096]{1,0:T(8,128)(2,1)S(1)}, u32[]{:S(2)}, u32[]{:S(2)}) %collective-permute-start.10) | collective-permute-done | bytes 786464 | tf_op jit(solution)/shard_map/ppermute | solution.py:296
  64.2 4.7 %shard_map.99.before = f32[512,128]{1,0:T(8,128)S(1)} custom-call(s32[17]{0:T(128)S(1)} %dynamic-slice_bitcast_fusion.table, s32[8]{0:T(128)S(1)} %copy-done.3, bf16[96,4096]{1,0:T(8,128)(2,1)S(1)} %collective-permute-done.12.one, bf16[96,4096]{1,0:T(8,128)(2,1)S(1)} %collective-permute-done.15.two, bf16[4096,1920]{1,0:T(8,128)(2,1)S(1)} %get-tuple-element.34.w, ...), custom_call_target="tpu_custom_call" | custom-call | flops 6039797760 | bytes 1572864 | tf_op jit(solution)/shard_map/pallas_call | solution.py:207
  68.9 4.9 %shard_map.100 = (f32[256,128]{1,0:T(8,128)S(1)}, f32[256,128]{1,0:T(8,128)S(1)}) custom-call(s32[17]{0:T(128)S(1)} %dynamic-slice_bitcast_fusion.table, s32[8]{0:T(128)S(1)} %copy-done.3, bf16[96,4096]{1,0:T(8,128)(2,1)S(1)} %collective-permute-done.10.one, bf16[96,4096]{1,0:T(8,128)(2,1)S(1)} %collective-permute-done.14.two, ...), custom_call_target="tpu_custom_call" | custom-call | flops 6039797760 | bytes 1572864 | tf_op jit(solution)/shard_map/pallas_call | solution.py:207
  75.3 2.6 %collective-permute-start.17 = (bf16[256,128]{1,0:T(8,128)(2,1)S(1)}, bf16[256,128]{1,0:T(8,128)(2,1)S(1)}, u32[]{:S(2)}, u32[]{:S(2)}) collective-permute-start(bf16[256,128]{1,0:T(8,128)(2,1)S(1)} %get-tuple-element.57), channel_id=1, source_target_pairs={{0,3},{1,2},{2,1},{3,0},{4,7},{5,6},{6,5},{7,4},{8,11},{9,10},{10,... | collective-permute-start | bytes 196616 | tf_op jit(solution)/shard_map/ppermute | solution.py:319
  78.9 1.9 %collective-permute-done.17 = bf16[256,128]{1,0:T(8,128)(2,1)S(1)} collective-permute-done((bf16[256,128]{1,0:T(8,128)(2,1)S(1)}, bf16[256,128]{1,0:T(8,128)(2,1)S(1)}, u32[]{:S(2)}, u32[]{:S(2)}) %collective-permute-start.17) | collective-permute-done | bytes 65568 | tf_op jit(solution)/shard_map/ppermute | solution.py:319
  82.7 2.7 %collective-permute-start.20 = (bf16[256,128]{1,0:T(8,128)(2,1)S(1)}, bf16[256,128]{1,0:T(8,128)(2,1)S(1)}, u32[]{:S(2)}, u32[]{:S(2)}) collective-permute-start(bf16[256,128]{1,0:T(8,128)(2,1)S(1)} %get-tuple-element.55), channel_id=1, source_target_pairs={{0,4},{1,5},{2,6},{3,7},{4,0},{5,1},{6,2},{7,3},{8,12},{9,13},{10,... | collective-permute-start | bytes 196616 | tf_op jit(solution)/shard_map/ppermute | solution.py:319
  85.4 2.6 %collective-permute-done.20.theirs = bf16[256,128]{1,0:T(8,128)(2,1)S(1)} collective-permute-done((bf16[256,128]{1,0:T(8,128)(2,1)S(1)}, bf16[256,128]{1,0:T(8,128)(2,1)S(1)}, u32[]{:S(2)}, u32[]{:S(2)}) %collective-permute-start.20) | collective-permute-done | bytes 65568 | tf_op jit(solution)/shard_map/ppermute | solution.py:319
  88.0 1.9 %shard_map.101 = f32[4,128]{1,0:T(4,128)} custom-call(s32[17]{0:T(128)S(1)} %dynamic-slice_bitcast_fusion.table, f32[256,128]{1,0:T(8,128)S(1)} %get-tuple-element.56.mine, bf16[256,128]{1,0:T(8,128)(2,1)S(1)} %collective-permute-done.20.theirs, bf16[128,4096]{1,0:T(8,128)(2,1)S(1)} %copy-done, bf16[128,4096]{1,0:T(8,128)(2,1)S(1)} %collective-permute-done.5.val_other), custom_call_target="tpu_custom_call" | custom-call | tf_op jit(solution)/shard_map/pallas_call | solution.py:257
  (47 shorter events, 13.9 us)
Async XLA Ops:
  0.0 17.7 %collective-permute-start = (bf16[96,4096]{1,0:T(8,128)(2,1)}, bf16[96,4096]{1,0:T(8,128)(2,1)S(1)}, u32[]{:S(2)}, u32[]{:S(2)}) collective-permute-start(bf16[96,4096]{1,0:T(8,128)(2,1)} %one.1), channel_id=1, source_target_pairs={{0,2},{2,4},{4,6},{6,7},{7,5},{5,3},{3,1},{1,0},{10,8},{12,10},{14... | collective-permute-start | bytes 2359304 | tf_op jit(solution)/shard_map/ppermute | solution.py:283
  3.0 17.0 %collective-permute-start.4 = (bf16[96,4096]{1,0:T(8,128)(2,1)}, bf16[96,4096]{1,0:T(8,128)(2,1)}, u32[]{:S(2)}, u32[]{:S(2)}) collective-permute-start(bf16[96,4096]{1,0:T(8,128)(2,1)} %one.1), channel_id=1, source_target_pairs={{0,8},{8,0},{1,9},{9,1},{2,10},{10,2},{3,11},{11,3},{4,12},{12,4},... | collective-permute-start | bytes 2359304 | tf_op jit(solution)/shard_map/ppermute | solution.py:284
  3.0 22.3 %collective-permute-start.5 = (bf16[128,4096]{1,0:T(8,128)(2,1)}, bf16[128,4096]{1,0:T(8,128)(2,1)S(1)}, u32[]{:S(2)}, u32[]{:S(2)}) collective-permute-start(bf16[128,4096]{1,0:T(8,128)(2,1)} %val_own.1), channel_id=1, source_target_pairs={{0,8},{8,0},{1,9},{9,1},{2,10},{10,2},{3,11},{11,3},{4,12},{12,4},... | collective-permute-start | bytes 3145736 | tf_op jit(solution)/shard_map/ppermute | solution.py:284
  8.9 16.4 %collective-permute-start.3 = (bf16[96,4096]{1,0:T(8,128)(2,1)}, bf16[96,4096]{1,0:T(8,128)(2,1)}, u32[]{:S(2)}, u32[]{:S(2)}) collective-permute-start(bf16[96,4096]{1,0:T(8,128)(2,1)} %one.1), channel_id=1, source_target_pairs={{2,0},{4,2},{6,4},{7,6},{5,7},{3,5},{1,3},{0,1},{8,10},{10,12},{12... | collective-permute-start | bytes 2359304 | tf_op jit(solution)/shard_map/ppermute | solution.py:287
  11.6 8.4 %copy-start.5 = (bf16[1536,896]{1,0:T(8,128)(2,1)S(1)}, bf16[1536,896]{1,0:T(8,128)(2,1)}, u32[]{:S(2)}) copy-start(bf16[1536,896]{1,0:T(8,128)(2,1)} %copy-done.4) | copy-start | bytes 8257540
  11.6 8.4 %copy-start.6 = (bf16[96,4096]{1,0:T(8,128)(2,1)S(1)}, bf16[96,4096]{1,0:T(8,128)(2,1)}, u32[]{:S(2)}) copy-start(bf16[96,4096]{1,0:T(8,128)(2,1)} %one.1) | copy-start | bytes 2359300
  17.7 8.8 %collective-permute-start.2 = (bf16[96,4096]{1,0:T(8,128)(2,1)S(1)}, bf16[96,4096]{1,0:T(8,128)(2,1)S(1)}, u32[]{:S(2)}, u32[]{:S(2)}) collective-permute-start(bf16[96,4096]{1,0:T(8,128)(2,1)S(1)} %collective-permute-done.one), channel_id=1, source_target_pairs={{0,8},{8,0},{1,9},{9,1},{2,10},{10,2},{3,11},{11,3},{4,12},{12,4},... | collective-permute-start | bytes 2359304 | tf_op jit(solution)/shard_map/ppermute | solution.py:297
  18.5 13.7 %collective-permute-start.1 = (bf16[96,4096]{1,0:T(8,128)(2,1)S(1)}, bf16[96,4096]{1,0:T(8,128)(2,1)S(1)}, u32[]{:S(2)}, u32[]{:S(2)}) collective-permute-start(bf16[96,4096]{1,0:T(8,128)(2,1)S(1)} %collective-permute-done.one), channel_id=1, source_target_pairs={{0,2},{2,4},{4,6},{6,7},{7,5},{5,3},{3,1},{1,0},{10,8},{12,10},{14... | collective-permute-start | bytes 2359304 | tf_op jit(solution)/shard_map/ppermute | solution.py:296
  25.4 8.5 %collective-permute-start.9 = (bf16[96,4096]{1,0:T(8,128)(2,1)}, bf16[96,4096]{1,0:T(8,128)(2,1)S(1)}, u32[]{:S(2)}, u32[]{:S(2)}) collective-permute-start(bf16[96,4096]{1,0:T(8,128)(2,1)} %collective-permute-done.3.one), channel_id=1, source_target_pairs={{0,8},{8,0},{1,9},{9,1},{2,10},{10,2},{3,11},{11,3},{4,12},{12,4},... | collective-permute-start | bytes 2359304 | tf_op jit(solution)/shard_map/ppermute | solution.py:303
  25.4 15.2 %collective-permute-start.8 = (bf16[96,4096]{1,0:T(8,128)(2,1)}, bf16[96,4096]{1,0:T(8,128)(2,1)S(1)}, u32[]{:S(2)}, u32[]{:S(2)}) collective-permute-start(bf16[96,4096]{1,0:T(8,128)(2,1)} %collective-permute-done.3.one), channel_id=1, source_target_pairs={{2,0},{4,2},{6,4},{7,6},{5,7},{3,5},{1,3},{0,1},{8,10},{10,12},{12... | collective-permute-start | bytes 2359304 | tf_op jit(solution)/shard_map/ppermute | solution.py:300
  32.1 10.6 %collective-permute-start.7 = (bf16[96,4096]{1,0:T(8,128)(2,1)S(1)}, bf16[96,4096]{1,0:T(8,128)(2,1)S(1)}, u32[]{:S(2)}, u32[]{:S(2)}) collective-permute-start(bf16[96,4096]{1,0:T(8,128)(2,1)S(1)} %collective-permute-done.1.one), channel_id=1, source_target_pairs={{0,8},{8,0},{1,9},{9,1},{2,10},{10,2},{3,11},{11,3},{4,12},{12,4},... | collective-permute-start | bytes 2359304 | tf_op jit(solution)/shard_map/ppermute | solution.py:297
  32.1 18.1 %collective-permute-start.6 = (bf16[96,4096]{1,0:T(8,128)(2,1)S(1)}, bf16[96,4096]{1,0:T(8,128)(2,1)S(1)}, u32[]{:S(2)}, u32[]{:S(2)}) collective-permute-start(bf16[96,4096]{1,0:T(8,128)(2,1)S(1)} %collective-permute-done.1.one), channel_id=1, source_target_pairs={{0,2},{2,4},{4,6},{6,7},{7,5},{5,3},{3,1},{1,0},{10,8},{12,10},{14... | collective-permute-start | bytes 2359304 | tf_op jit(solution)/shard_map/ppermute | solution.py:296
  40.7 10.9 %collective-permute-start.13 = (bf16[96,4096]{1,0:T(8,128)(2,1)S(1)}, bf16[96,4096]{1,0:T(8,128)(2,1)S(1)}, u32[]{:S(2)}, u32[]{:S(2)}) collective-permute-start(bf16[96,4096]{1,0:T(8,128)(2,1)S(1)} %collective-permute-done.8.one), channel_id=1, source_target_pairs={{0,8},{8,0},{1,9},{9,1},{2,10},{10,2},{3,11},{11,3},{4,12},{12,4},... | collective-permute-start | bytes 2359304 | tf_op jit(solution)/shard_map/ppermute | solution.py:303
  41.7 14.5 %collective-permute-start.12 = (bf16[96,4096]{1,0:T(8,128)(2,1)S(1)}, bf16[96,4096]{1,0:T(8,128)(2,1)S(1)}, u32[]{:S(2)}, u32[]{:S(2)}) collective-permute-start(bf16[96,4096]{1,0:T(8,128)(2,1)S(1)} %collective-permute-done.8.one), channel_id=1, source_target_pairs={{2,0},{4,2},{6,4},{7,6},{5,7},{3,5},{1,3},{0,1},{8,10},{10,12},{12... | collective-permute-start | bytes 2359304 | tf_op jit(solution)/shard_map/ppermute | solution.py:300
  50.3 7.4 %collective-permute-start.11 = (bf16[96,4096]{1,0:T(8,128)(2,1)S(1)}, bf16[96,4096]{1,0:T(8,128)(2,1)S(1)}, u32[]{:S(2)}, u32[]{:S(2)}) collective-permute-start(bf16[96,4096]{1,0:T(8,128)(2,1)S(1)} %collective-permute-done.6.one), channel_id=1, source_target_pairs={{0,8},{8,0},{1,9},{9,1},{2,10},{10,2},{3,11},{11,3},{4,12},{12,4},... | collective-permute-start | bytes 2359304 | tf_op jit(solution)/shard_map/ppermute | solution.py:297
  50.3 13.9 %collective-permute-start.10 = (bf16[96,4096]{1,0:T(8,128)(2,1)S(1)}, bf16[96,4096]{1,0:T(8,128)(2,1)S(1)}, u32[]{:S(2)}, u32[]{:S(2)}) collective-permute-start(bf16[96,4096]{1,0:T(8,128)(2,1)S(1)} %collective-permute-done.6.one), channel_id=1, source_target_pairs={{0,2},{2,4},{4,6},{6,7},{7,5},{5,3},{3,1},{1,0},{10,8},{12,10},{14... | collective-permute-start | bytes 2359304 | tf_op jit(solution)/shard_map/ppermute | solution.py:296
  56.2 8.0 %collective-permute-start.15 = (bf16[96,4096]{1,0:T(8,128)(2,1)S(1)}, bf16[96,4096]{1,0:T(8,128)(2,1)S(1)}, u32[]{:S(2)}, u32[]{:S(2)}) collective-permute-start(bf16[96,4096]{1,0:T(8,128)(2,1)S(1)} %collective-permute-done.12.one), channel_id=1, source_target_pairs={{0,8},{8,0},{1,9},{9,1},{2,10},{10,2},{3,11},{11,3},{4,12},{12,4},... | collective-permute-start | bytes 2359304 | tf_op jit(solution)/shard_map/ppermute | solution.py:303
  64.2 4.7 %collective-permute-start.14 = (bf16[96,4096]{1,0:T(8,128)(2,1)S(1)}, bf16[96,4096]{1,0:T(8,128)(2,1)S(1)}, u32[]{:S(2)}, u32[]{:S(2)}) collective-permute-start(bf16[96,4096]{1,0:T(8,128)(2,1)S(1)} %collective-permute-done.10.one), channel_id=1, source_target_pairs={{0,8},{8,0},{1,9},{9,1},{2,10},{10,2},{3,11},{11,3},{4,12},{12,4},... | collective-permute-start | bytes 2359304 | tf_op jit(solution)/shard_map/ppermute | solution.py:306
  68.8 19.1 %copy-start = (bf16[128,4096]{1,0:T(8,128)(2,1)S(1)}, bf16[128,4096]{1,0:T(8,128)(2,1)}, u32[]{:S(2)}) copy-start(bf16[128,4096]{1,0:T(8,128)(2,1)} %val_own.1) | copy-start | bytes 3145732
  73.8 1.6 %collective-permute-start.16 = (f32[256,128]{1,0:T(8,128)S(1)}, f32[256,128]{1,0:T(8,128)S(1)}, u32[]{:S(2)}, u32[]{:S(2)}) collective-permute-start(f32[256,128]{1,0:T(8,128)S(1)} %get-tuple-element.53), channel_id=1, source_target_pairs={{0,8},{8,0},{1,9},{9,1},{2,10},{10,2},{3,11},{11,3},{4,12},{12,4},... | collective-permute-start | bytes 393224 | tf_op jit(solution)/shard_map/ppermute | solution.py:310
  75.3 5.4 %collective-permute-start.17 = (bf16[256,128]{1,0:T(8,128)(2,1)S(1)}, bf16[256,128]{1,0:T(8,128)(2,1)S(1)}, u32[]{:S(2)}, u32[]{:S(2)}) collective-permute-start(bf16[256,128]{1,0:T(8,128)(2,1)S(1)} %get-tuple-element.57), channel_id=1, source_target_pairs={{0,3},{1,2},{2,1},{3,0},{4,7},{5,6},{6,5},{7,4},{8,11},{9,10},{10,... | collective-permute-start | bytes 196616 | tf_op jit(solution)/shard_map/ppermute | solution.py:319
  78.0 4.3 %collective-permute-start.18 = (bf16[256,128]{1,0:T(8,128)(2,1)S(1)}, bf16[256,128]{1,0:T(8,128)(2,1)S(1)}, u32[]{:S(2)}, u32[]{:S(2)}) collective-permute-start(bf16[256,128]{1,0:T(8,128)(2,1)S(1)} %get-tuple-element.57), channel_id=1, source_target_pairs={{0,2},{1,3},{2,0},{3,1},{4,6},{5,7},{6,4},{7,5},{8,10},{9,11},{10,... | collective-permute-start | bytes 196616 | tf_op jit(solution)/shard_map/ppermute | solution.py:319
  78.4 4.3 %collective-permute-start.19 = (bf16[256,128]{1,0:T(8,128)(2,1)S(1)}, bf16[256,128]{1,0:T(8,128)(2,1)S(1)}, u32[]{:S(2)}, u32[]{:S(2)}) collective-permute-start(bf16[256,128]{1,0:T(8,128)(2,1)S(1)} %get-tuple-element.57), channel_id=1, source_target_pairs={{0,1},{1,0},{2,3},{3,2},{4,5},{5,4},{6,7},{7,6},{8,9},{9,8},{10,11... | collective-permute-start | bytes 196616 | tf_op jit(solution)/shard_map/ppermute | solution.py:319
  82.7 5.2 %collective-permute-start.20 = (bf16[256,128]{1,0:T(8,128)(2,1)S(1)}, bf16[256,128]{1,0:T(8,128)(2,1)S(1)}, u32[]{:S(2)}, u32[]{:S(2)}) collective-permute-start(bf16[256,128]{1,0:T(8,128)(2,1)S(1)} %get-tuple-element.55), channel_id=1, source_target_pairs={{0,4},{1,5},{2,6},{3,7},{4,0},{5,1},{6,2},{7,3},{8,12},{9,13},{10,... | collective-permute-start | bytes 196616 | tf_op jit(solution)/shard_map/ppermute | solution.py:319
  (4 other events, 11.3 us)

commit v12 on v11

--- a/solution.py
+++ b/solution.py
@@ -236,11 +236,11 @@
             ups.append(jnp.where(left, 0.0, slab))
         rows += [*split(jnp.concatenate(gates, axis=1)), *split(jnp.concatenate(ups, axis=1))]
     products = lax.dot_general(
+        jnp.concatenate([val_own[...], val_other[...]], axis=0),
         jnp.concatenate(rows, axis=0),
-        jnp.concatenate([val_own[...], val_other[...]], axis=0),
         (((1,), (1,)), ((), ())),
         preferred_element_type=jnp.float32,
-    )
+    ).T
     columns = scores.shape[1]
     found = products[: 4 * own, :columns] + products[4 * own :, columns:]
     count = rank * LANES // 2

time: 90.2 us -> 90.2 us (level)
  no operation moved by 1% of the time
where the time goes in v12:
time: 90.2 us; the launch traced here: 89.9 us
  Pallas kernels  49.1 us (54%)
  starting transfers between devices  21 us (23%)
  waiting for transfers between devices  14.6 us (16%)
  local copies, waits for them, and re-layouts  5.05 us (6%)
    pallas_call x8, Pallas kernels, add_step(): pl.pallas_call(functools.partial(step_kernel, entry, last), out_shape=out...  38.7 us
    ppermute x4, waiting for transfers between devices, fast(): lax.ppermute(sent, 'mp', [(i, i ^ flip) for i in range(n)])  6.36 us
    ppermute x4, starting transfers between devices, fast(): lax.ppermute(sent, 'mp', [(i, i ^ flip) for i in range(n)])  6.22 us
    pallas_call x1, Pallas kernels, load(): pl.pallas_call(load_kernel, out_shape=[pltpu.VMEM((width, 2 * hidden + LA...  6.01 us
    ppermute x3, waiting for transfers between devices, fast(): next_one = send_one(one_way)  5.65 us
    ppermute x3, starting transfers between devices, fast(): next_one = send_one(one_way)  4.54 us
    unnamed x15, local copies, waits for them, and re-layouts  4.36 us
    ppermute x1, starting transfers between devices, fast(): one_way = send_one(tokens_in)  3.02 us
  transfers between devices with their start and end apart: 21, of which 9 were waited for; matrix products, arithmetic and copies ran while one was open for 2% of the time, Pallas kernels for 47%

profile of v12, /device:TPU:0, one launch (start us, length us, event | category | flops | bytes accessed | tf_op | source)
XLA Modules:
  0.0 89.9 jit_solution(4695741745841711408)
XLA Ops:
  0.0 3.0 %collective-permute-start = (bf16[96,4096]{1,0:T(8,128)(2,1)}, bf16[96,4096]{1,0:T(8,128)(2,1)S(1)}, u32[]{:S(2)}, u32[]{:S(2)}) collective-permute-start(bf16[96,4096]{1,0:T(8,128)(2,1)} %one.1), channel_id=1, source_target_pairs={{0,2},{2,4},{4,6},{6,7},{7,5},{5,3},{3,1},{1,0},{10,8},{12,10},{14... | collective-permute-start | bytes 2359304 | tf_op jit(solution)/shard_map/ppermute | solution.py:283
  4.9 2.5 %shard_map.91 = (bf16[1536,896]{1,0:T(8,128)(2,1)S(1)}, bf16[1792,128]{1,0:T(8,128)(2,1)S(1)}) custom-call(s32[17]{0:T(128)S(1)} %dynamic-slice_bitcast_fusion.table, s32[8]{0:T(128)S(1)} %copy-done.1, bf16[1536,896]{1,0:T(8,128)(2,1)} %out_grad_hbm.1, bf16[896,128]{1,0:T(8,128)(2,1)} %proj_out_hbm.1), custom_call_target="tpu_custom_call" | custom-call | tf_op jit(solution)/shard_map/pallas_call | solution.py:170
  7.4 1.5 %copy-done.4 = bf16[1536,896]{1,0:T(8,128)(2,1)} copy-done((bf16[1536,896]{1,0:T(8,128)(2,1)}, bf16[1536,896]{1,0:T(8,128)(2,1)S(1)}, u32[]{:S(2)}) %copy-start.4) | copy-done | bytes 2752536
  9.5 1.5 %copy.10.proj_in = bf16[4096,64]{1,0:T(8,128)(2,1)S(1)} copy(bf16[4096,64]{0,1:T(8,128)(2,1)} %param.13) | data formatting | bytes 1048576 | tf_op args[4]
  11.6 6.0 %shard_map.92 = (bf16[4096,1920]{1,0:T(8,128)(2,1)S(1)}, f32[512,128]{1,0:T(8,128)S(1)}) custom-call(s32[8]{0:T(128)S(1)} %copy-done.2, bf16[1792,128]{1,0:T(8,128)(2,1)S(1)} %get-tuple-element.31.diagonal, bf16[4096,896]{1,0:T(8,128)(2,1)} %gate_hbm.1, bf16[4096,896]{1,0:T(8,128)(2,1)} %up_hbm.1, bf16[4096,64]{1,0:T(8,128)(2,1)S(1)} %copy.10.proj_in), custom_call_target="tpu_custom_call" | custom-call | tf_op jit(solution)/shard_map/pallas_call | solution.py:186
  18.5 1.6 %collective-permute-start.1 = (bf16[96,4096]{1,0:T(8,128)(2,1)S(1)}, bf16[96,4096]{1,0:T(8,128)(2,1)S(1)}, u32[]{:S(2)}, u32[]{:S(2)}) collective-permute-start(bf16[96,4096]{1,0:T(8,128)(2,1)S(1)} %collective-permute-done.one), channel_id=1, source_target_pairs={{0,2},{2,4},{4,6},{6,7},{7,5},{5,3},{3,1},{1,0},{10,8},{12,10},{14... | collective-permute-start | bytes 2359304 | tf_op jit(solution)/shard_map/ppermute | solution.py:296
  20.1 5.3 %shard_map.93.before = f32[512,128]{1,0:T(8,128)S(1)} custom-call(s32[17]{0:T(128)S(1)} %dynamic-slice_bitcast_fusion.table, s32[8]{0:T(128)S(1)} %copy-done.3, bf16[96,4096]{1,0:T(8,128)(2,1)S(1)} %copy-done.6, bf16[96,4096]{1,0:T(8,128)(2,1)} %collective-permute-done.4.two, bf16[4096,1920]{1,0:T(8,128)(2,1)S(1)} %get-tuple-element.34.w, ...), custom_call_target="tpu_custom_call" | custom-call | flops 6039797760 | bytes 1572864 | tf_op jit(solution)/shard_map/pallas_call | solution.py:207
  26.5 4.7 %shard_map.94.before = f32[512,128]{1,0:T(8,128)S(1)} custom-call(s32[17]{0:T(128)S(1)} %dynamic-slice_bitcast_fusion.table, s32[8]{0:T(128)S(1)} %copy-done.3, bf16[96,4096]{1,0:T(8,128)(2,1)S(1)} %collective-permute-done.one, bf16[96,4096]{1,0:T(8,128)(2,1)S(1)} %collective-permute-done.2.two, bf16[4096,1920]{1,0:T(8,128)(2,1)S(1)} %get-tuple-element.34.w, ...), custom_call_target="tpu_custom_call" | custom-call | flops 6039797760 | bytes 1572864 | tf_op jit(solution)/shard_map/pallas_call | solution.py:207
  32.1 1.7 %collective-permute-start.6 = (bf16[96,4096]{1,0:T(8,128)(2,1)S(1)}, bf16[96,4096]{1,0:T(8,128)(2,1)S(1)}, u32[]{:S(2)}, u32[]{:S(2)}) collective-permute-start(bf16[96,4096]{1,0:T(8,128)(2,1)S(1)} %collective-permute-done.1.one), channel_id=1, source_target_pairs={{0,2},{2,4},{4,6},{6,7},{7,5},{5,3},{3,1},{1,0},{10,8},{12,10},{14... | collective-permute-start | bytes 2359304 | tf_op jit(solution)/shard_map/ppermute | solution.py:296
  33.8 5.3 %shard_map.95.before = f32[512,128]{1,0:T(8,128)S(1)} custom-call(s32[17]{0:T(128)S(1)} %dynamic-slice_bitcast_fusion.table, s32[8]{0:T(128)S(1)} %copy-done.3, bf16[96,4096]{1,0:T(8,128)(2,1)} %collective-permute-done.3.one, bf16[96,4096]{1,0:T(8,128)(2,1)S(1)} %collective-permute-done.9.two, bf16[4096,1920]{1,0:T(8,128)(2,1)S(1)} %get-tuple-element.34.w, ...), custom_call_target="tpu_custom_call" | custom-call | flops 6039797760 | bytes 1572864 | tf_op jit(solution)/shard_map/pallas_call | solution.py:207
  39.1 1.6 %collective-permute-done.8.one = bf16[96,4096]{1,0:T(8,128)(2,1)S(1)} collective-permute-done((bf16[96,4096]{1,0:T(8,128)(2,1)}, bf16[96,4096]{1,0:T(8,128)(2,1)S(1)}, u32[]{:S(2)}, u32[]{:S(2)}) %collective-permute-start.8) | collective-permute-done | bytes 786464 | tf_op jit(solution)/shard_map/ppermute | solution.py:300
  42.8 4.7 %shard_map.96.before = f32[512,128]{1,0:T(8,128)S(1)} custom-call(s32[17]{0:T(128)S(1)} %dynamic-slice_bitcast_fusion.table, s32[8]{0:T(128)S(1)} %copy-done.3, bf16[96,4096]{1,0:T(8,128)(2,1)S(1)} %collective-permute-done.1.one, bf16[96,4096]{1,0:T(8,128)(2,1)S(1)} %collective-permute-done.7.two, bf16[4096,1920]{1,0:T(8,128)(2,1)S(1)} %get-tuple-element.34.w, ...), custom_call_target="tpu_custom_call" | custom-call | flops 6039797760 | bytes 1572864 | tf_op jit(solution)/shard_map/pallas_call | solution.py:207
  47.4 2.8 %collective-permute-done.6.one = bf16[96,4096]{1,0:T(8,128)(2,1)S(1)} collective-permute-done((bf16[96,4096]{1,0:T(8,128)(2,1)S(1)}, bf16[96,4096]{1,0:T(8,128)(2,1)S(1)}, u32[]{:S(2)}, u32[]{:S(2)}) %collective-permute-start.6) | collective-permute-done | bytes 786464 | tf_op jit(solution)/shard_map/ppermute | solution.py:296
  51.6 4.7 %shard_map.97.before = f32[512,128]{1,0:T(8,128)S(1)} custom-call(s32[17]{0:T(128)S(1)} %dynamic-slice_bitcast_fusion.table, s32[8]{0:T(128)S(1)} %copy-done.3, bf16[96,4096]{1,0:T(8,128)(2,1)S(1)} %collective-permute-done.8.one, bf16[96,4096]{1,0:T(8,128)(2,1)S(1)} %collective-permute-done.13.two, bf16[4096,1920]{1,0:T(8,128)(2,1)S(1)} %get-tuple-element.34.w, ...), custom_call_target="tpu_custom_call" | custom-call | flops 6039797760 | bytes 1572864 | tf_op jit(solution)/shard_map/pallas_call | solution.py:207
  56.2 1.5 %collective-permute-start.15 = (bf16[96,4096]{1,0:T(8,128)(2,1)S(1)}, bf16[96,4096]{1,0:T(8,128)(2,1)S(1)}, u32[]{:S(2)}, u32[]{:S(2)}) collective-permute-start(bf16[96,4096]{1,0:T(8,128)(2,1)S(1)} %collective-permute-done.12.one), channel_id=1, source_target_pairs={{0,8},{8,0},{1,9},{9,1},{2,10},{10,2},{3,11},{11,3},{4,12},{12,4},... | collective-permute-start | bytes 2359304 | tf_op jit(solution)/shard_map/ppermute | solution.py:303
  57.7 4.6 %shard_map.98.before = f32[512,128]{1,0:T(8,128)S(1)} custom-call(s32[17]{0:T(128)S(1)} %dynamic-slice_bitcast_fusion.table, s32[8]{0:T(128)S(1)} %copy-done.3, bf16[96,4096]{1,0:T(8,128)(2,1)S(1)} %collective-permute-done.6.one, bf16[96,4096]{1,0:T(8,128)(2,1)S(1)} %collective-permute-done.11.two, bf16[4096,1920]{1,0:T(8,128)(2,1)S(1)} %get-tuple-element.34.w, ...), custom_call_target="tpu_custom_call" | custom-call | flops 6039797760 | bytes 1572864 | tf_op jit(solution)/shard_map/pallas_call | solution.py:207
  62.3 1.8 %collective-permute-done.10.one = bf16[96,4096]{1,0:T(8,128)(2,1)S(1)} collective-permute-done((bf16[96,4096]{1,0:T(8,128)(2,1)S(1)}, bf16[96,4096]{1,0:T(8,128)(2,1)S(1)}, u32[]{:S(2)}, u32[]{:S(2)}) %collective-permute-start.10) | collective-permute-done | bytes 786464 | tf_op jit(solution)/shard_map/ppermute | solution.py:296
  64.2 4.7 %shard_map.99.before = f32[512,128]{1,0:T(8,128)S(1)} custom-call(s32[17]{0:T(128)S(1)} %dynamic-slice_bitcast_fusion.table, s32[8]{0:T(128)S(1)} %copy-done.3, bf16[96,4096]{1,0:T(8,128)(2,1)S(1)} %collective-permute-done.12.one, bf16[96,4096]{1,0:T(8,128)(2,1)S(1)} %collective-permute-done.15.two, bf16[4096,1920]{1,0:T(8,128)(2,1)S(1)} %get-tuple-element.34.w, ...), custom_call_target="tpu_custom_call" | custom-call | flops 6039797760 | bytes 1572864 | tf_op jit(solution)/shard_map/pallas_call | solution.py:207
  68.9 4.9 %shard_map.100 = (f32[256,128]{1,0:T(8,128)S(1)}, f32[256,128]{1,0:T(8,128)S(1)}) custom-call(s32[17]{0:T(128)S(1)} %dynamic-slice_bitcast_fusion.table, s32[8]{0:T(128)S(1)} %copy-done.3, bf16[96,4096]{1,0:T(8,128)(2,1)S(1)} %collective-permute-done.10.one, bf16[96,4096]{1,0:T(8,128)(2,1)S(1)} %collective-permute-done.14.two, ...), custom_call_target="tpu_custom_call" | custom-call | flops 6039797760 | bytes 1572864 | tf_op jit(solution)/shard_map/pallas_call | solution.py:207
  75.3 2.6 %collective-permute-start.17 = (bf16[256,128]{1,0:T(8,128)(2,1)S(1)}, bf16[256,128]{1,0:T(8,128)(2,1)S(1)}, u32[]{:S(2)}, u32[]{:S(2)}) collective-permute-start(bf16[256,128]{1,0:T(8,128)(2,1)S(1)} %get-tuple-element.57), channel_id=1, source_target_pairs={{0,3},{1,2},{2,1},{3,0},{4,7},{5,6},{6,5},{7,4},{8,11},{9,10},{10,... | collective-permute-start | bytes 196616 | tf_op jit(solution)/shard_map/ppermute | solution.py:319
  78.9 1.9 %collective-permute-done.17 = bf16[256,128]{1,0:T(8,128)(2,1)S(1)} collective-permute-done((bf16[256,128]{1,0:T(8,128)(2,1)S(1)}, bf16[256,128]{1,0:T(8,128)(2,1)S(1)}, u32[]{:S(2)}, u32[]{:S(2)}) %collective-permute-start.17) | collective-permute-done | bytes 65568 | tf_op jit(solution)/shard_map/ppermute | solution.py:319
  82.7 2.7 %collective-permute-start.20 = (bf16[256,128]{1,0:T(8,128)(2,1)S(1)}, bf16[256,128]{1,0:T(8,128)(2,1)S(1)}, u32[]{:S(2)}, u32[]{:S(2)}) collective-permute-start(bf16[256,128]{1,0:T(8,128)(2,1)S(1)} %get-tuple-element.55), channel_id=1, source_target_pairs={{0,4},{1,5},{2,6},{3,7},{4,0},{5,1},{6,2},{7,3},{8,12},{9,13},{10,... | collective-permute-start | bytes 196616 | tf_op jit(solution)/shard_map/ppermute | solution.py:319
  85.4 2.6 %collective-permute-done.20.theirs = bf16[256,128]{1,0:T(8,128)(2,1)S(1)} collective-permute-done((bf16[256,128]{1,0:T(8,128)(2,1)S(1)}, bf16[256,128]{1,0:T(8,128)(2,1)S(1)}, u32[]{:S(2)}, u32[]{:S(2)}) %collective-permute-start.20) | collective-permute-done | bytes 65568 | tf_op jit(solution)/shard_map/ppermute | solution.py:319
  88.0 1.9 %shard_map.101 = f32[4,128]{1,0:T(4,128)} custom-call(s32[17]{0:T(128)S(1)} %dynamic-slice_bitcast_fusion.table, f32[256,128]{1,0:T(8,128)S(1)} %get-tuple-element.56.mine, bf16[256,128]{1,0:T(8,128)(2,1)S(1)} %collective-permute-done.20.theirs, bf16[128,4096]{1,0:T(8,128)(2,1)S(1)} %copy-done, bf16[128,4096]{1,0:T(8,128)(2,1)S(1)} %collective-permute-done.5.val_other), custom_call_target="tpu_custom_call" | custom-call | tf_op jit(solution)/shard_map/pallas_call | solution.py:257
  (47 shorter events, 13.9 us)
Async XLA Ops:
  0.0 17.7 %collective-permute-start = (bf16[96,4096]{1,0:T(8,128)(2,1)}, bf16[96,4096]{1,0:T(8,128)(2,1)S(1)}, u32[]{:S(2)}, u32[]{:S(2)}) collective-permute-start(bf16[96,4096]{1,0:T(8,128)(2,1)} %one.1), channel_id=1, source_target_pairs={{0,2},{2,4},{4,6},{6,7},{7,5},{5,3},{3,1},{1,0},{10,8},{12,10},{14... | collective-permute-start | bytes 2359304 | tf_op jit(solution)/shard_map/ppermute | solution.py:283
  3.0 17.0 %collective-permute-start.4 = (bf16[96,4096]{1,0:T(8,128)(2,1)}, bf16[96,4096]{1,0:T(8,128)(2,1)}, u32[]{:S(2)}, u32[]{:S(2)}) collective-permute-start(bf16[96,4096]{1,0:T(8,128)(2,1)} %one.1), channel_id=1, source_target_pairs={{0,8},{8,0},{1,9},{9,1},{2,10},{10,2},{3,11},{11,3},{4,12},{12,4},... | collective-permute-start | bytes 2359304 | tf_op jit(solution)/shard_map/ppermute | solution.py:284
  3.0 22.3 %collective-permute-start.5 = (bf16[128,4096]{1,0:T(8,128)(2,1)}, bf16[128,4096]{1,0:T(8,128)(2,1)S(1)}, u32[]{:S(2)}, u32[]{:S(2)}) collective-permute-start(bf16[128,4096]{1,0:T(8,128)(2,1)} %val_own.1), channel_id=1, source_target_pairs={{0,8},{8,0},{1,9},{9,1},{2,10},{10,2},{3,11},{11,3},{4,12},{12,4},... | collective-permute-start | bytes 3145736 | tf_op jit(solution)/shard_map/ppermute | solution.py:284
  8.9 16.4 %collective-permute-start.3 = (bf16[96,4096]{1,0:T(8,128)(2,1)}, bf16[96,4096]{1,0:T(8,128)(2,1)}, u32[]{:S(2)}, u32[]{:S(2)}) collective-permute-start(bf16[96,4096]{1,0:T(8,128)(2,1)} %one.1), channel_id=1, source_target_pairs={{2,0},{4,2},{6,4},{7,6},{5,7},{3,5},{1,3},{0,1},{8,10},{10,12},{12... | collective-permute-start | bytes 2359304 | tf_op jit(solution)/shard_map/ppermute | solution.py:287
  11.6 8.4 %copy-start.5 = (bf16[1536,896]{1,0:T(8,128)(2,1)S(1)}, bf16[1536,896]{1,0:T(8,128)(2,1)}, u32[]{:S(2)}) copy-start(bf16[1536,896]{1,0:T(8,128)(2,1)} %copy-done.4) | copy-start | bytes 8257540
  11.6 8.4 %copy-start.6 = (bf16[96,4096]{1,0:T(8,128)(2,1)S(1)}, bf16[96,4096]{1,0:T(8,128)(2,1)}, u32[]{:S(2)}) copy-start(bf16[96,4096]{1,0:T(8,128)(2,1)} %one.1) | copy-start | bytes 2359300
  17.7 8.8 %collective-permute-start.2 = (bf16[96,4096]{1,0:T(8,128)(2,1)S(1)}, bf16[96,4096]{1,0:T(8,128)(2,1)S(1)}, u32[]{:S(2)}, u32[]{:S(2)}) collective-permute-start(bf16[96,4096]{1,0:T(8,128)(2,1)S(1)} %collective-permute-done.one), channel_id=1, source_target_pairs={{0,8},{8,0},{1,9},{9,1},{2,10},{10,2},{3,11},{11,3},{4,12},{12,4},... | collective-permute-start | bytes 2359304 | tf_op jit(solution)/shard_map/ppermute | solution.py:297
  18.5 13.7 %collective-permute-start.1 = (bf16[96,4096]{1,0:T(8,128)(2,1)S(1)}, bf16[96,4096]{1,0:T(8,128)(2,1)S(1)}, u32[]{:S(2)}, u32[]{:S(2)}) collective-permute-start(bf16[96,4096]{1,0:T(8,128)(2,1)S(1)} %collective-permute-done.one), channel_id=1, source_target_pairs={{0,2},{2,4},{4,6},{6,7},{7,5},{5,3},{3,1},{1,0},{10,8},{12,10},{14... | collective-permute-start | bytes 2359304 | tf_op jit(solution)/shard_map/ppermute | solution.py:296
  25.4 8.5 %collective-permute-start.9 = (bf16[96,4096]{1,0:T(8,128)(2,1)}, bf16[96,4096]{1,0:T(8,128)(2,1)S(1)}, u32[]{:S(2)}, u32[]{:S(2)}) collective-permute-start(bf16[96,4096]{1,0:T(8,128)(2,1)} %collective-permute-done.3.one), channel_id=1, source_target_pairs={{0,8},{8,0},{1,9},{9,1},{2,10},{10,2},{3,11},{11,3},{4,12},{12,4},... | collective-permute-start | bytes 2359304 | tf_op jit(solution)/shard_map/ppermute | solution.py:303
  25.4 15.2 %collective-permute-start.8 = (bf16[96,4096]{1,0:T(8,128)(2,1)}, bf16[96,4096]{1,0:T(8,128)(2,1)S(1)}, u32[]{:S(2)}, u32[]{:S(2)}) collective-permute-start(bf16[96,4096]{1,0:T(8,128)(2,1)} %collective-permute-done.3.one), channel_id=1, source_target_pairs={{2,0},{4,2},{6,4},{7,6},{5,7},{3,5},{1,3},{0,1},{8,10},{10,12},{12... | collective-permute-start | bytes 2359304 | tf_op jit(solution)/shard_map/ppermute | solution.py:300
  32.1 10.6 %collective-permute-start.7 = (bf16[96,4096]{1,0:T(8,128)(2,1)S(1)}, bf16[96,4096]{1,0:T(8,128)(2,1)S(1)}, u32[]{:S(2)}, u32[]{:S(2)}) collective-permute-start(bf16[96,4096]{1,0:T(8,128)(2,1)S(1)} %collective-permute-done.1.one), channel_id=1, source_target_pairs={{0,8},{8,0},{1,9},{9,1},{2,10},{10,2},{3,11},{11,3},{4,12},{12,4},... | collective-permute-start | bytes 2359304 | tf_op jit(solution)/shard_map/ppermute | solution.py:297
  32.1 18.1 %collective-permute-start.6 = (bf16[96,4096]{1,0:T(8,128)(2,1)S(1)}, bf16[96,4096]{1,0:T(8,128)(2,1)S(1)}, u32[]{:S(2)}, u32[]{:S(2)}) collective-permute-start(bf16[96,4096]{1,0:T(8,128)(2,1)S(1)} %collective-permute-done.1.one), channel_id=1, source_target_pairs={{0,2},{2,4},{4,6},{6,7},{7,5},{5,3},{3,1},{1,0},{10,8},{12,10},{14... | collective-permute-start | bytes 2359304 | tf_op jit(solution)/shard_map/ppermute | solution.py:296
  40.7 10.9 %collective-permute-start.13 = (bf16[96,4096]{1,0:T(8,128)(2,1)S(1)}, bf16[96,4096]{1,0:T(8,128)(2,1)S(1)}, u32[]{:S(2)}, u32[]{:S(2)}) collective-permute-start(bf16[96,4096]{1,0:T(8,128)(2,1)S(1)} %collective-permute-done.8.one), channel_id=1, source_target_pairs={{0,8},{8,0},{1,9},{9,1},{2,10},{10,2},{3,11},{11,3},{4,12},{12,4},... | collective-permute-start | bytes 2359304 | tf_op jit(solution)/shard_map/ppermute | solution.py:303
  41.7 14.5 %collective-permute-start.12 = (bf16[96,4096]{1,0:T(8,128)(2,1)S(1)}, bf16[96,4096]{1,0:T(8,128)(2,1)S(1)}, u32[]{:S(2)}, u32[]{:S(2)}) collective-permute-start(bf16[96,4096]{1,0:T(8,128)(2,1)S(1)} %collective-permute-done.8.one), channel_id=1, source_target_pairs={{2,0},{4,2},{6,4},{7,6},{5,7},{3,5},{1,3},{0,1},{8,10},{10,12},{12... | collective-permute-start | bytes 2359304 | tf_op jit(solution)/shard_map/ppermute | solution.py:300
  50.3 7.4 %collective-permute-start.11 = (bf16[96,4096]{1,0:T(8,128)(2,1)S(1)}, bf16[96,4096]{1,0:T(8,128)(2,1)S(1)}, u32[]{:S(2)}, u32[]{:S(2)}) collective-permute-start(bf16[96,4096]{1,0:T(8,128)(2,1)S(1)} %collective-permute-done.6.one), channel_id=1, source_target_pairs={{0,8},{8,0},{1,9},{9,1},{2,10},{10,2},{3,11},{11,3},{4,12},{12,4},... | collective-permute-start | bytes 2359304 | tf_op jit(solution)/shard_map/ppermute | solution.py:297
  50.3 13.9 %collective-permute-start.10 = (bf16[96,4096]{1,0:T(8,128)(2,1)S(1)}, bf16[96,4096]{1,0:T(8,128)(2,1)S(1)}, u32[]{:S(2)}, u32[]{:S(2)}) collective-permute-start(bf16[96,4096]{1,0:T(8,128)(2,1)S(1)} %collective-permute-done.6.one), channel_id=1, source_target_pairs={{0,2},{2,4},{4,6},{6,7},{7,5},{5,3},{3,1},{1,0},{10,8},{12,10},{14... | collective-permute-start | bytes 2359304 | tf_op jit(solution)/shard_map/ppermute | solution.py:296
  56.2 8.0 %collective-permute-start.15 = (bf16[96,4096]{1,0:T(8,128)(2,1)S(1)}, bf16[96,4096]{1,0:T(8,128)(2,1)S(1)}, u32[]{:S(2)}, u32[]{:S(2)}) collective-permute-start(bf16[96,4096]{1,0:T(8,128)(2,1)S(1)} %collective-permute-done.12.one), channel_id=1, source_target_pairs={{0,8},{8,0},{1,9},{9,1},{2,10},{10,2},{3,11},{11,3},{4,12},{12,4},... | collective-permute-start | bytes 2359304 | tf_op jit(solution)/shard_map/ppermute | solution.py:303
  64.2 4.7 %collective-permute-start.14 = (bf16[96,4096]{1,0:T(8,128)(2,1)S(1)}, bf16[96,4096]{1,0:T(8,128)(2,1)S(1)}, u32[]{:S(2)}, u32[]{:S(2)}) collective-permute-start(bf16[96,4096]{1,0:T(8,128)(2,1)S(1)} %collective-permute-done.10.one), channel_id=1, source_target_pairs={{0,8},{8,0},{1,9},{9,1},{2,10},{10,2},{3,11},{11,3},{4,12},{12,4},... | collective-permute-start | bytes 2359304 | tf_op jit(solution)/shard_map/ppermute | solution.py:306
  68.8 19.1 %copy-start = (bf16[128,4096]{1,0:T(8,128)(2,1)S(1)}, bf16[128,4096]{1,0:T(8,128)(2,1)}, u32[]{:S(2)}) copy-start(bf16[128,4096]{1,0:T(8,128)(2,1)} %val_own.1) | copy-start | bytes 3145732
  73.8 1.6 %collective-permute-start.16 = (f32[256,128]{1,0:T(8,128)S(1)}, f32[256,128]{1,0:T(8,128)S(1)}, u32[]{:S(2)}, u32[]{:S(2)}) collective-permute-start(f32[256,128]{1,0:T(8,128)S(1)} %get-tuple-element.53), channel_id=1, source_target_pairs={{0,8},{8,0},{1,9},{9,1},{2,10},{10,2},{3,11},{11,3},{4,12},{12,4},... | collective-permute-start | bytes 393224 | tf_op jit(solution)/shard_map/ppermute | solution.py:310
  75.3 5.4 %collective-permute-start.17 = (bf16[256,128]{1,0:T(8,128)(2,1)S(1)}, bf16[256,128]{1,0:T(8,128)(2,1)S(1)}, u32[]{:S(2)}, u32[]{:S(2)}) collective-permute-start(bf16[256,128]{1,0:T(8,128)(2,1)S(1)} %get-tuple-element.57), channel_id=1, source_target_pairs={{0,3},{1,2},{2,1},{3,0},{4,7},{5,6},{6,5},{7,4},{8,11},{9,10},{10,... | collective-permute-start | bytes 196616 | tf_op jit(solution)/shard_map/ppermute | solution.py:319
  78.0 4.3 %collective-permute-start.18 = (bf16[256,128]{1,0:T(8,128)(2,1)S(1)}, bf16[256,128]{1,0:T(8,128)(2,1)S(1)}, u32[]{:S(2)}, u32[]{:S(2)}) collective-permute-start(bf16[256,128]{1,0:T(8,128)(2,1)S(1)} %get-tuple-element.57), channel_id=1, source_target_pairs={{0,2},{1,3},{2,0},{3,1},{4,6},{5,7},{6,4},{7,5},{8,10},{9,11},{10,... | collective-permute-start | bytes 196616 | tf_op jit(solution)/shard_map/ppermute | solution.py:319
  78.4 4.3 %collective-permute-start.19 = (bf16[256,128]{1,0:T(8,128)(2,1)S(1)}, bf16[256,128]{1,0:T(8,128)(2,1)S(1)}, u32[]{:S(2)}, u32[]{:S(2)}) collective-permute-start(bf16[256,128]{1,0:T(8,128)(2,1)S(1)} %get-tuple-element.57), channel_id=1, source_target_pairs={{0,1},{1,0},{2,3},{3,2},{4,5},{5,4},{6,7},{7,6},{8,9},{9,8},{10,11... | collective-permute-start | bytes 196616 | tf_op jit(solution)/shard_map/ppermute | solution.py:319
  82.7 5.2 %collective-permute-start.20 = (bf16[256,128]{1,0:T(8,128)(2,1)S(1)}, bf16[256,128]{1,0:T(8,128)(2,1)S(1)}, u32[]{:S(2)}, u32[]{:S(2)}) collective-permute-start(bf16[256,128]{1,0:T(8,128)(2,1)S(1)} %get-tuple-element.55), channel_id=1, source_target_pairs={{0,4},{1,5},{2,6},{3,7},{4,0},{5,1},{6,2},{7,3},{8,12},{9,13},{10,... | collective-permute-start | bytes 196616 | tf_op jit(solution)/shard_map/ppermute | solution.py:319
  (4 other events, 11.3 us)
